TPU v7x, 32 devices: a whole 2x2x4 slice. The times are simulated.
32 devices in a mesh: replica: 8 (over y, x, core), table: 4 (over z).
Axes of the slice: x: 2, y: 2, z: 4, core: 2. Of those that a mesh axis runs over, the one named last changes fastest.
Arguments:
- emb_table: float32 [4096, 128], P('table'), may hold values from -3 to 3
- row_accum: float32 [4096], P('table'), may hold values from 0.001 to 1
- look_rows: int32 [8, 4, 4, 4, 1248], P('replica', 'table'), may hold values from 0 to 1023
- live_counts: int32 [8, 4, 4], P('replica'), may hold values from 1 to 1248, 3328 in all within a row
- bag_order: int32 [8, 4, 3328], P('replica', 'table'), may hold values from 0 to 3327, each once within a row
- dense_emb: bfloat16 [4096, 128], P(('replica', 'table')), may hold values from -6 to 6
- labels: int32 [4096], P(('replica', 'table')), may hold values 0 or 1
- cross_in: bfloat16 [3456, 512], P('table'), may hold values from -0.109375 to 0.109375
- cross_out: bfloat16 [3456, 512], P('table'), may hold values from -0.25 to 0.25
- cross_bias: float32 [3456], replicated, may hold values from -3 to 3
- head_weight: float32 [3456], replicated, may hold values from -0.109375 to 0.109375
Outputs:
- logits: float32 [4096], P(('replica', 'table'))
- row_update: float32 [4096, 128], P('table')
- new_accum: float32 [4096], P('table')
Inputs may be any that keep to these rules, and one draw needn't show every extreme that they name: `look_rows`: local row numbers within shard s; entries in unused slots are ignored. `live_counts`: for each replica and owner the counts over shards sum to 3328; for each of them some shard sends exactly 1248. `bag_order`: each of an owner's 3328 bags appears once.
All inputs are finite; a program needn't handle non-finite values. No bound on the sum of `labels` on one device may be relied on, other than what follows from the above.
Results may differ from a plain program's by a relative error of at most 0.0045.
Values may be sent and summed in bfloat16 or wider, within the bound.
No kernel may reach another device: no remote copies, remote signals or barrier semaphores. Data moves between devices by JAX's collectives and lax.ppermute only.
A program may use at most 64 MiB of HBM per device.

v0:
```python
import jax
import jax.numpy as jnp
from jax import lax
from jax.sharding import PartitionSpec as P

EPSILON = 1e-08


def bag_sources(live_row, permute, capacity):
    bag_count = permute.shape[0]
    slot_ends = jnp.cumsum(live_row)
    counter = jnp.arange(bag_count, dtype=jnp.int32)
    passed = (counter[:, None] >= slot_ends[None, :]).astype(jnp.int32)
    source = jnp.sum(passed, axis=1)
    before = jnp.sum(passed * live_row[None, :], axis=1)
    flat_slot = source * capacity + (counter - before)
    inverse = jnp.zeros((bag_count,), jnp.int32).at[permute].set(counter)
    return flat_slot[inverse]


def slot_bags(live_row, permute, capacity):
    bag_count = permute.shape[0]
    starts = jnp.cumsum(live_row) - live_row
    column = jnp.arange(capacity, dtype=jnp.int32)
    position = jnp.minimum(starts[:, None] + column[None, :], bag_count - 1)
    is_live = column[None, :] < live_row[:, None]
    return (permute[position], is_live)


def local(
    emb_table,
    row_accum,
    look_rows,
    live_counts,
    bag_order,
    dense_emb,
    labels,
    cross_in,
    cross_out,
    cross_bias,
    head_weight,
):
    shards = lax.axis_size("table")
    own_index = lax.axis_index("table")
    feature_width = emb_table.shape[1]
    hot_count = look_rows.shape[3]
    capacity = look_rows.shape[4]
    contract = (((1,), (1,)), ((), ()))
    row_ids = look_rows[0, 0]
    pool_sum = jnp.take(emb_table, row_ids[:, 0].reshape(-1), axis=0)
    for member in range(1, hot_count):
        pool_sum = pool_sum + jnp.take(emb_table, row_ids[:, member].reshape(-1), axis=0)
    slot_pool = pool_sum.astype(jnp.bfloat16).reshape(shards, capacity, feature_width)
    arrived = lax.all_to_all(slot_pool, "table", split_axis=0, concat_axis=0, tiled=True)
    live_row = lax.dynamic_index_in_dim(live_counts[0], own_index, 0, keepdims=False)
    permute = bag_order[0, 0]
    bag_slot = bag_sources(live_row, permute, capacity)
    batch_size = dense_emb.shape[0]
    pooled = jnp.take(arrived.reshape(-1, feature_width), bag_slot, axis=0).reshape(batch_size, -1)
    cross_input = jnp.concatenate([dense_emb, pooled], axis=1)
    full_in, full_out = (
        lax.all_gather(cross_in, "table", axis=0, tiled=True),
        lax.all_gather(cross_out, "table", axis=0, tiled=True),
    )
    hidden = jnp.dot(cross_input, full_in, preferred_element_type=jnp.float32).astype(jnp.bfloat16)
    mixed_rows = (
        lax.dot_general(hidden, full_out, contract, preferred_element_type=jnp.float32) + cross_bias
    )
    crossed = cross_input * mixed_rows + cross_input
    logits = jnp.dot(crossed, head_weight, precision=lax.Precision.HIGHEST)
    logit_grad = jax.nn.sigmoid(logits) - labels.astype(jnp.float32)
    cross_grad = logit_grad[:, None] * head_weight[None, :]
    mixed_grad = (cross_grad * cross_input).astype(jnp.bfloat16)
    hidden_grad = jnp.dot(mixed_grad, full_out, preferred_element_type=jnp.float32).astype(
        jnp.bfloat16
    )
    back_term = lax.dot_general(hidden_grad, full_in, contract, preferred_element_type=jnp.float32)
    input_grad = cross_grad * (mixed_rows + 1.0) + back_term
    pooled_grad = input_grad[:, feature_width:].astype(jnp.bfloat16).reshape(-1, feature_width)
    bag_ids, is_live = slot_bags(live_row, permute, capacity)
    outgoing = jnp.take(pooled_grad, bag_ids.reshape(-1), axis=0).reshape(
        shards, capacity, feature_width
    )
    outgoing = jnp.where(is_live[:, :, None], outgoing, jnp.zeros_like(outgoing))
    returned = lax.all_to_all(outgoing, "table", split_axis=0, concat_axis=0, tiled=True)
    returned_rows = returned.astype(jnp.float32).reshape(-1, feature_width)
    local_grads = jnp.zeros(emb_table.shape, jnp.float32)
    for member in range(hot_count):
        local_grads = local_grads.at[row_ids[:, member].reshape(-1)].add(returned_rows)
    summed = lax.psum(local_grads, "replica")
    new_accum = row_accum + jnp.mean(summed * summed, axis=1)
    row_update = -summed / (jnp.sqrt(new_accum)[:, None] + EPSILON)
    return (logits, row_update, new_accum)


def solution(mesh):
    placed = (
        P("table", None),
        P("table"),
        P("replica", "table", None, None, None),
        P("replica", None, None),
        P("replica", "table", None),
        P(("replica", "table"), None),
        P(("replica", "table")),
        P("table", None),
        P("table", None),
        P(),
        P(),
    )
    return jax.shard_map(
        local,
        mesh=mesh,
        in_specs=placed,
        out_specs=(P(("replica", "table")), P("table", None), P("table")),
        check_vma=False,
    )
```

profile of v0, /device:TPU:0, one launch (start us, length us, event | category | flops | bytes accessed | tf_op | source)
XLA Modules:
  0.0 419.6 jit_solution(9694469367428273642)
XLA Ops:
  7.2 0.7 all-gather.3.cloned.1.call-update
  8.0 0.7 all-gather.5.cloned.1.call-update
  8.7 1.3 slice_reduce_fusion.3
  10.4 0.2 copy-done.3
  10.6 8.2 %gather_fusion.6 = f32[4992,128]{1,0:T(8,128)S(1)} fusion(f32[1024,128]{1,0:T(8,128)S(1)} %copy-done, s32[5120]{0:T(1024)S(1)} %pad_clamp_fusion.3), kind=kCustom, calls=%fused_computation.2.clone | custom fusion | bytes 5131776 | tf_op jit(solution)/shard_map/jit(_take)/gather | solution.py:52
  18.8 10.1 %gather_fusion.7 = f32[4992,128]{1,0:T(8,128)} fusion(f32[1024,128]{1,0:T(8,128)S(1)} %copy-done, s32[5120]{0:T(1024)S(1)} %pad_clamp_fusion.2), kind=kCustom, calls=%fused_computation.3.clone | custom fusion | bytes 5131776 | tf_op jit(solution)/shard_map/jit(_take)/gather | solution.py:52
  29.0 10.1 %gather_fusion.4 = f32[4992,128]{1,0:T(8,128)} fusion(f32[1024,128]{1,0:T(8,128)S(1)} %copy-done, s32[5120]{0:T(1024)S(1)} %pad_clamp_fusion.5), kind=kCustom, calls=%fused_computation.clone | custom fusion | bytes 5131776 | tf_op jit(solution)/shard_map/jit(_take)/gather | solution.py:50
  39.1 10.1 %gather_fusion.5 = f32[4992,128]{1,0:T(8,128)} fusion(f32[1024,128]{1,0:T(8,128)S(1)} %copy-done, s32[5120]{0:T(1024)S(1)} %pad_clamp_fusion.4), kind=kCustom, calls=%fused_computation.1.clone | custom fusion | bytes 5131776 | tf_op jit(solution)/shard_map/jit(_take)/gather | solution.py:52
  49.3 6.9 %fusion.8 = bf16[4992,128]{1,0:T(8,128)(2,1)} fusion(f32[4992,128]{1,0:T(8,128)} %gather_fusion.7, f32[4992,128]{1,0:T(8,128)S(1)} %gather_fusion.6, f32[4992,128]{1,0:T(8,128)} %gather_fusion.5, f32[4992,128]{1,0:T(8,128)} %gather_fusion.4, pred[4992]{0:T(1024)(128)(4,1)S(1)} %get-tuple-element.16, pred[4992]{0:T(1024)(128)(4,1)S(1)} %get-tuple-element.17, ...), kind=kLoop, calls=%fused_computation.24 | loop fusion | flops 5111808 | bytes 11521536 | tf_op jit(solution)/shard_map/convert_element_type | solution.py:53
  56.2 6.3 %all-to-all-start = ((bf16[4,1248,128]{2,1,0:T(8,128)(2,1)}), bf16[4,1248,128]{2,1,0:T(8,128)(2,1)S(1)}, u32[]{:S(2)}, u32[]{:S(2)}) async-start(bf16[4,1248,128]{2,1,0:T(8,128)(2,1)} %bitcast.30), calls=%async_computation | async-start | bytes 2555904 | tf_op jit(solution)/shard_map/all_to_all | solution.py:54
  62.5 0.2 reduce-window.7
  62.8 12.9 %scatter_custom_fusion = s32[3328]{0:T(1024)S(1)} fusion(s32[3328]{0:T(1024)S(1)} %fusion.22, s32[3328]{0:T(1024)S(1)} %iota.19, s32[]{:T(128)} %constant.31.clone.1), kind=kCustom, calls=%fused_computation.90 | custom fusion | bytes 13316 | tf_op jit(solution)/shard_map/scatter | solution.py:17
  75.8 0.1 convert_reduce_fusion
  75.9 17.5 %gather_fusion = s32[3328]{0:T(1024)S(1)} fusion(s32[3328]{0:T(1024)S(1)} %subtract_add_fusion, s32[4096]{0:T(1024)S(1)} %pad_clamp_fusion.7), kind=kCustom, calls=%fused_computation.4 | custom fusion | bytes 39936 | tf_op jit(solution)/shard_map/gather | solution.py:18
  93.5 0.1 gather.26
  93.7 0.1 broadcast_in_dim.67
  93.9 0.8 copy.17
  94.7 0.6 reshape.462
  95.5 26.1 %gather_fusion.2 = s32[4992]{0:T(1024)S(1)} fusion(s32[3328]{0:T(1024)S(1)} %reduce.8, s32[5120]{0:T(1024)S(1)} %pad_clamp_fusion.1), kind=kCustom, calls=%fused_computation.6 | custom fusion | bytes 59904 | tf_op jit(solution)/shard_map/gather | solution.py:27
  121.8 0.6 pad_clamp_fusion
  122.4 0.7 iota_compare_fusion.1
  123.1 6.5 %gather_fusion.1 = bf16[3328,128]{1,0:T(8,128)(2,1)S(1)} fusion(bf16[4992,128]{1,0:T(8,128)(2,1)S(1)} %bitcast.25, s32[4096]{0:T(1024)S(1)} %pad_clamp_fusion.6), kind=kCustom, calls=%fused_computation.5 | custom fusion | bytes 1717248 | tf_op jit(solution)/shard_map/jit(_take)/gather | solution.py:59
  129.6 0.9 gather.29
  130.6 0.1 broadcast_select_fusion
  130.7 43.6 %all-gather.5.cloned.1.call-done = bf16[3456,512]{1,0:T(8,128)(2,1)} async-done(((bf16[864,512]{1,0:T(8,128)(2,1)}), bf16[3456,512]{1,0:T(8,128)(2,1)}) %all-gather.5.cloned.1.call-update) | async-done | bytes 3538960 | tf_op jit(solution)/shard_map/all_gather | solution.py:63
  174.3 4.8 %convolution_add_fusion = f32[128,3456]{1,0:T(8,128)S(1)} fusion(bf16[3456,512]{1,0:T(8,128)(2,1)} %all-gather.5.cloned.1.call-done, bf16[3456,512]{1,0:T(8,128)(2,1)} %all-gather.3.cloned.1.call-done, f32[3456]{0:T(1024)} %param.22, bf16[128,3328]{1,0:T(8,128)(2,1)S(1)} %broadcast_select_fusion, bf16[128,128]{1,0:T(8,128)(2,1)S(1)} %copy-done.2), kind=kOutput, calls=%fused_computation.13 | convolution fusion | flops 908247040 | bytes 9745920 | tf_op jit(solution)/shard_map/dot_general | solution.py:67
  179.1 2.1 divide_subtract_fusion
  181.2 1.4 broadcast_multiply_fusion
  182.6 6.1 %fusion.12 = f32[128,3456]{1,0:T(8,128)} fusion(bf16[3456,512]{1,0:T(8,128)(2,1)} %all-gather.3.cloned.1.call-done, bf16[3456,512]{1,0:T(8,128)(2,1)} %all-gather.5.cloned.1.call-done, f32[3456]{0:T(1024)S(1)} %copy-done.11, f32[128]{0:T(128)S(1)} %get-tuple-element.14, bf16[128,3328]{1,0:T(8,128)(2,1)S(1)} %broadcast_select_fusion, ...), kind=kOutput, calls=%fused_computation.37 | convolution fusion | flops 909131776 | bytes 9746432 | tf_op jit(solution)/shard_map/dot_general | solution.py:77
  188.7 3.1 fusion.11
  191.8 2.2 reshape.337
  194.0 10.0 %gather_fusion.3 = bf16[4992,128]{1,0:T(8,128)(2,1)S(1)} fusion(bf16[3328,128]{1,0:T(8,128)(2,1)S(1)} %reshape.337, s32[5120]{0:T(1024)S(1)} %copy-done.12), kind=kCustom, calls=%fused_computation.7 | custom fusion | bytes 2575872 | tf_op jit(solution)/shard_map/jit(_take)/gather | solution.py:81
  204.1 4.4 %select_select_fusion = bf16[4,1248,128]{2,1,0:T(8,128)(2,1)} fusion(bf16[4,1248,128]{2,1,0:T(8,128)(2,1)S(1)} %bitcast.31, pred[4,1248]{1,0:T(4,128)(4,1)S(1)} %copy-done.16, pred[4,1248]{1,0:T(4,128)(4,1)S(1)} %copy-done.15), kind=kLoop, calls=%fused_computation.34 | loop fusion | flops 1277952 | bytes 2565888 | tf_op jit(solution)/shard_map/jit(_where)/select_n | solution.py:84
  208.5 3.5 all-to-all-start.1
  212.0 0.3 all-reduce.2.cloned.1.call-start
  212.3 0.1 reshape_squeeze.28
  212.4 0.1 reshape_squeeze.29
  212.5 0.1 reshape_squeeze.30
  213.0 29.8 %all-to-all-done.1 = bf16[4,1248,128]{2,1,0:T(8,128)(2,1)S(1)} async-done(((bf16[4,1248,128]{2,1,0:T(8,128)(2,1)}), bf16[4,1248,128]{2,1,0:T(8,128)(2,1)S(1)}, u32[]{:S(2)}, u32[]{:S(2)}) %all-to-all-start.1) | async-done | bytes 1277984 | tf_op jit(solution)/shard_map/all_to_all | solution.py:85
  242.9 25.9 %scatter_custom_fusion.1 = f32[1024,128]{1,0:T(8,128)S(1)} fusion(s32[4992]{0:T(1024)S(1)} %fusion.17, bf16[4992,128]{1,0:T(8,128)(2,1)S(1)} %bitcast.26, f32[]{:T(128)} %constant.48.clone.1), kind=kCustom, calls=%fused_computation.20 | custom fusion | flops 1277952 | bytes 1802244 | tf_op jit(solution)/shard_map/scatter-add | solution.py:89
  268.7 28.6 %scatter_custom_fusion.2 = f32[1024,128]{1,0:T(8,128)S(1)} fusion(f32[1024,128]{1,0:T(8,128)S(1)} %scatter_custom_fusion.1, s32[4992]{0:T(1024)S(1)} %fusion.19, bf16[4992,128]{1,0:T(8,128)(2,1)S(1)} %bitcast.27), kind=kCustom, calls=%fused_computation.18 | custom fusion | flops 1277952 | bytes 1802240 | tf_op jit(solution)/shard_map/scatter-add | solution.py:89
  297.4 28.6 %scatter_custom_fusion.3 = f32[1024,128]{1,0:T(8,128)S(1)} fusion(f32[1024,128]{1,0:T(8,128)S(1)} %scatter_custom_fusion.2, s32[4992]{0:T(1024)S(1)} %fusion.20, bf16[4992,128]{1,0:T(8,128)(2,1)S(1)} %bitcast.28), kind=kCustom, calls=%fused_computation.16 | custom fusion | flops 1277952 | bytes 1802240 | tf_op jit(solution)/shard_map/scatter-add | solution.py:89
  326.0 28.6 %scatter_custom_fusion.4 = f32[1024,128]{1,0:T(8,128)S(1)} fusion(f32[1024,128]{1,0:T(8,128)S(1)} %scatter_custom_fusion.3, s32[4992]{0:T(1024)S(1)} %fusion.21, bf16[4992,128]{1,0:T(8,128)(2,1)S(1)} %bitcast.29), kind=kCustom, calls=%fused_computation.14 | custom fusion | flops 1277952 | bytes 1802240 | tf_op jit(solution)/shard_map/scatter-add | solution.py:89
  354.6 0.8 copy-done.1
  355.4 53.7 %all-reduce.2.cloned.1.call-done = f32[1024,128]{1,0:T(8,128)} async-done(((f32[1024,128]{1,0:T(8,128)}), f32[1024,128]{1,0:T(8,128)}) %all-reduce.2.cloned.1.call-update) | async-done | bytes 524304 | tf_op jit(solution)/shard_map/psum | solution.py:90
  409.1 1.2 multiply_reduce_fusion
  410.4 0.6 sqrt_add_fusion
  411.0 2.0 negate_divide_fusion
  (79 shorter events, 1.6 us)
Async XLA Ops:
  7.2 3.5 copy-start
  7.2 123.5 %all-gather.3.cloned.1.call-start = ((), (), s32[]{:S(2)}) async-start(), calls=%async_computation.2 | async-start | bytes 4423680 | tf_op jit(solution)/shard_map/all_gather | solution.py:62
  7.9 166.4 %all-gather.5.cloned.1.call-start = ((), (), s32[]{:S(2)}) async-start(), calls=%async_computation.3 | async-start | bytes 4423680 | tf_op jit(solution)/shard_map/all_gather | solution.py:63
  10.0 0.6 copy-start.3
  10.0 0.6 copy-start.5
  10.0 0.6 copy-start.7
  10.0 0.6 copy-start.9
  56.2 6.3 %copy-start.19 = (s32[1,4,4]{2,1,0:T(4,128)S(1)}, s32[1,4,4]{2,1,0:T(4,128)}, u32[]{:S(2)}) copy-start(s32[1,4,4]{2,1,0:T(4,128)} %param.16) | copy-start | bytes 196
  56.2 6.5 %copy-start.14 = (s32[1,1,3328]{2,1,0:T(1,128)S(1)}, s32[1,1,3328]{2,1,0:T(1,128)}, u32[]{:S(2)}) copy-start(s32[1,1,3328]{2,1,0:T(1,128)} %param.17) | copy-start | bytes 39940
  56.2 66.9 %all-to-all-start = ((bf16[4,1248,128]{2,1,0:T(8,128)(2,1)}), bf16[4,1248,128]{2,1,0:T(8,128)(2,1)S(1)}, u32[]{:S(2)}, u32[]{:S(2)}) async-start(bf16[4,1248,128]{2,1,0:T(8,128)(2,1)} %bitcast.30), calls=%async_computation | async-start | bytes 2555904 | tf_op jit(solution)/shard_map/all_to_all | solution.py:54
  75.9 18.8 %copy-start.11 = (f32[3456]{0:T(1024)S(1)}, f32[3456]{0:T(1024)}, u32[]{:S(2)}) copy-start(f32[3456]{0:T(1024)} %param.23) | copy-start | bytes 41476
  129.6 44.7 %copy-start.2 = (bf16[128,128]{1,0:T(8,128)(2,1)S(1)}, bf16[128,128]{1,0:T(8,128)(2,1)}, u32[]{:S(2)}) copy-start(bf16[128,128]{1,0:T(8,128)(2,1)} %param.18) | copy-start | bytes 98308
  130.7 48.4 %copy-start.13 = (f32[3456,1]{0,1:T(1,128)S(1)}, f32[3456,1]{0,1:T(1,128)}, u32[]{:S(2)}) copy-start(f32[3456,1]{0,1:T(1,128)} %reshape.462) | copy-start | bytes 41476
  130.7 48.4 %copy-start.18 = (s32[128]{0:T(128)S(1)}, s32[128]{0:T(128)}, u32[]{:S(2)}) copy-start(s32[128]{0:T(128)} %param.19) | copy-start | bytes 1540
  188.7 5.3 %copy-start.12 = (s32[5120]{0:T(1024)S(1)}, s32[5120]{0:T(1024)}, u32[]{:S(2)}) copy-start(s32[5120]{0:T(1024)} %pad_clamp_fusion) | copy-start | bytes 61444
  194.0 10.0 %copy-start.15 = (pred[4,1248]{1,0:T(4,128)(4,1)S(1)}, pred[4,1248]{1,0:T(4,128)(4,1)}, u32[]{:S(2)}) copy-start(pred[4,1248]{1,0:T(4,128)(4,1)} %get-tuple-element.20) | copy-start | bytes 14980
  194.0 10.0 %copy-start.16 = (pred[4,1248]{1,0:T(4,128)(4,1)S(1)}, pred[4,1248]{1,0:T(4,128)(4,1)}, u32[]{:S(2)}) copy-start(pred[4,1248]{1,0:T(4,128)(4,1)} %get-tuple-element.21) | copy-start | bytes 14980
  204.0 8.3 %copy-start.10 = (s32[4,1248]{1,0:T(4,128)S(1)}, s32[4,1248]{1,0:T(4,128)}, u32[]{:S(2)}) copy-start(s32[4,1248]{1,0:T(4,128)} %copy-done.9) | copy-start | bytes 59908
  204.0 8.4 %copy-start.8 = (s32[4,1248]{1,0:T(4,128)S(1)}, s32[4,1248]{1,0:T(4,128)}, u32[]{:S(2)}) copy-start(s32[4,1248]{1,0:T(4,128)} %copy-done.7) | copy-start | bytes 59908
  204.1 8.5 %copy-start.6 = (s32[4,1248]{1,0:T(4,128)S(1)}, s32[4,1248]{1,0:T(4,128)}, u32[]{:S(2)}) copy-start(s32[4,1248]{1,0:T(4,128)} %copy-done.5) | copy-start | bytes 59908
  204.1 8.6 %copy-start.4 = (s32[4,1248]{1,0:T(4,128)S(1)}, s32[4,1248]{1,0:T(4,128)}, u32[]{:S(2)}) copy-start(s32[4,1248]{1,0:T(4,128)} %copy-done.3) | copy-start | bytes 59908
  208.5 34.4 %all-to-all-start.1 = ((bf16[4,1248,128]{2,1,0:T(8,128)(2,1)}), bf16[4,1248,128]{2,1,0:T(8,128)(2,1)S(1)}, u32[]{:S(2)}, u32[]{:S(2)}) async-start(bf16[4,1248,128]{2,1,0:T(8,128)(2,1)} %select_select_fusion), calls=%async_computation.1 | async-start | bytes 2555904 | tf_op jit(solution)/shard_map/all_to_all | solution.py:85
  212.0 197.1 %all-reduce.2.cloned.1.call-start = ((), (), s32[]{:S(2)}) async-start(), calls=%async_computation.4 | async-start | bytes 1048576 | tf_op jit(solution)/shard_map/psum | solution.py:90
  297.4 113.0 %copy-start.17 = (f32[1024]{0:T(1024)S(1)}, f32[1024]{0:T(1024)}, u32[]{:S(2)}) copy-start(f32[1024]{0:T(1024)} %param.14) | copy-start | bytes 12292
  354.6 0.8 copy-start.1
Sparse Core Ops, SparseCore 0:
  9.6 94.9 all-gather.2
  106.2 68.0 all-gather.4
  355.5 53.5 all-reduce.1
where the time goes:
time: 420 us
  other arithmetic  134 us (32%)
  waiting for transfers between devices  129 us (31%)
  local copies, waits for them, and re-layouts  120 us (29%)
  between operations  14.3 us (3%)
  matrix products  12.9 us (3%)
  starting transfers between devices  10.2 us (2%)
    scatter-add x4, other arithmetic, local(): local_grads.at[row_ids[:, member].reshape(-1)].add(returned_rows)  112 us
    psum x1, waiting for transfers between devices, local(): summed = lax.psum(local_grads, 'replica')  53.7 us
    all_gather x1, waiting for transfers between devices, local(): lax.all_gather(cross_out, 'table', axis=0, tiled=True)  43.6 us
    all_to_all x1, waiting for transfers between devices, local(): lax.all_to_all(outgoing, 'table', split_axis=0, concat_axis=0, tiled=True)  29.8 us
    gather x3, local copies, waits for them, and re-layouts, local(): jnp.take(emb_table, row_ids[:, member].reshape(-1), axis=0)  28.4 us
    gather x2, local copies, waits for them, and re-layouts, slot_bags(): return (permute[position], is_live)  26.2 us
    gather x2, local copies, waits for them, and re-layouts, bag_sources(): return flat_slot[inverse]  17.7 us
    scatter x1, local copies, waits for them, and re-layouts, bag_sources(): inverse = jnp.zeros((bag_count,), jnp.int32).at[permute].set(counter)  12.9 us
  transfers between devices with their start and end apart: 5, of which 3 were waited for; matrix products, arithmetic and copies ran while one was open for 28% of the time, Pallas kernels for 0%

commit v1 on v0

v1 whole, which is shorter than its diff:
```python
import functools

import jax
import jax.numpy as jnp
from jax import lax
from jax.experimental import pallas as pl
from jax.experimental.pallas import tpu as pltpu
from jax.sharding import PartitionSpec as P

EPSILON = 1e-08
F32, BF16 = jnp.float32, jnp.bfloat16
LOW = 32
UNROLL = 8
VMEM_LIMIT = 48 * 1024 * 1024


def swap(array, mask):
    size = lax.axis_size("replica")
    return lax.ppermute(array, "replica", [(i, i ^ mask) for i in range(size)])


def shift(array, step):
    size = lax.axis_size("table")
    return lax.ppermute(array, "table", [(i, (i + step) % size) for i in range(size)])


def mask_stages(size):
    stages, bit = [(1,)], 1
    while (1 << bit) < size:
        if (2 << bit) < size:
            stages.append((1 << bit, 2 << bit, 3 << bit))
            bit += 2
        else:
            stages.append((1 << bit,))
            bit += 1
    return stages


def replica_gather(piece):
    out = {0: piece}
    for masks in reversed(mask_stages(lax.axis_size("replica"))):
        for held in list(out):
            for mask in masks:
                out[held ^ mask] = swap(out[held], mask)
    return [out[m] for m in sorted(out)]


def whole(space=pltpu.VMEM):
    return pl.BlockSpec(memory_space=space)


def pool_kernel(shards, replicas, scal, dest, *refs):
    ids, (own, *pieces), (out, table, pooled) = refs[:shards], refs[shards:-3], refs[-3:]
    hot = ids[0].shape[0]
    block = pieces[0].shape[1]
    mine = scal[2 * shards]
    table[0] = own[...]
    for m, piece in enumerate(pieces):
        rows = pl.ds(pl.multiple_of((mine ^ m) * block, block), block)
        for k in range(1, shards):
            table[k, rows, :] = piece[k - 1].astype(F32)
    for k in range(shards):
        start, live = scal[k], scal[shards + k]

        def one(c, k=k, start=start):
            total = table[k, pl.ds(ids[k][0, c], 1), :]
            for h in range(1, hot):
                total = total + table[k, pl.ds(ids[k][h, c], 1), :]
            pooled[pl.ds(dest[start + c], 1), :] = total

        def group(i, _, one=one):
            for u in range(UNROLL):
                one(i * UNROLL + u)
            return 0

        def single(c, _, one=one):
            one(c)
            return 0

        full = live // UNROLL
        lax.fori_loop(0, full, group, 0)
        lax.fori_loop(full * UNROLL, live, single, 0)
    out[...] = pooled[...].astype(BF16)


def pool(scal, dest, ids, own, pieces, bags):
    shards, replicas = len(ids), len(pieces)
    rows, width = own.shape
    smem = whole(pltpu.SMEM)
    return pl.pallas_call(
        functools.partial(pool_kernel, shards, replicas),
        out_shape=jax.ShapeDtypeStruct((bags, width), BF16),
        in_specs=[smem, smem] + [smem] * shards + [whole()] * (1 + replicas),
        out_specs=whole(),
        scratch_shapes=[pltpu.VMEM((shards, rows, width), F32), pltpu.VMEM((bags, width), F32)],
        compiler_params=pltpu.CompilerParams(vmem_limit_bytes=VMEM_LIMIT),
        cost_estimate=pl.CostEstimate(flops=10**6, bytes_accessed=30 * 10**6, transcendentals=0),
        name="pool",
    )(scal, dest, *ids, own, *pieces)


def column_of(row, size):
    eye = lax.broadcasted_iota(jnp.int32, (size, size), 0) == lax.broadcasted_iota(
        jnp.int32, (size, size), 1
    )
    return jnp.sum(jnp.where(eye, jnp.broadcast_to(row, (size, size)), 0.0), axis=1, keepdims=True)


def row_of(column, size):
    eye = lax.broadcasted_iota(jnp.int32, (size, size), 0) == lax.broadcasted_iota(
        jnp.int32, (size, size), 1
    )
    return jnp.sum(
        jnp.where(eye, jnp.broadcast_to(column, (size, size)), 0.0), axis=0, keepdims=True
    )


def dense_kernel(shards, replicas, spots, chunk, scal, dest, *refs):
    ids = refs[:shards]
    dense, rows_in, bias, head, labels = refs[shards : shards + 5]
    weights = refs[shards + 5 : shards + 5 + len(spots)]
    logits, even, odd = refs[shards + 5 + len(spots) : shards + 8 + len(spots)]
    full_in, full_out, cross, scaled, grads, slots, counts, total = refs[shards + 8 + len(spots) :]
    factor = (full_in, full_out)
    batch, width = dense.shape
    features = full_in.shape[0]
    hot, capacity = ids[0].shape
    table_rows = total.shape[0]
    mine = scal[2 * shards]
    across = (((1,), (1,)), ((), ()))

    for ref, placing in zip(weights, spots):
        placing(ref, factor, scal)

    cross[:, :width] = dense[...]
    for f in range(1, features // width):
        cross[:, f * width : (f + 1) * width] = rows_in[(f - 1) * batch : f * batch, :]
    for f in range(features // width):
        at = slice(f * width, (f + 1) * width)
        scaled[:, at] = (cross[:, at].astype(F32) * head[:, at]).astype(BF16)
    hidden = jnp.dot(cross[...], full_in[...], preferred_element_type=F32).astype(BF16)
    back = jnp.dot(scaled[...], full_out[...], preferred_element_type=F32).astype(BF16)

    step = 3 * width if (features // width) % 3 == 0 else width
    logit = jnp.zeros((batch, width), F32)
    for n in range(features // step):
        at = slice(n * step, (n + 1) * step)
        mixed = lax.dot_general(hidden, full_out[at, :], across, preferred_element_type=F32)
        gain = head[:, at] * (mixed + bias[:, at] + 1.0)
        term = cross[:, at].astype(F32) * gain
        grad = gain + lax.dot_general(back, full_in[at, :], across, preferred_element_type=F32)
        for p in range(step // width):
            part = slice(p * width, (p + 1) * width)
            logit = logit + term[:, part]
            f = n * (step // width) + p
            if f > 0:
                grads[(f - 1) * batch : f * batch, :] = grad[:, part]
    logit = jnp.sum(logit, axis=1, keepdims=True)
    logits[...] = row_of(logit, batch)
    lean = jax.nn.sigmoid(logit) - column_of(labels[...].astype(F32), batch)
    for f in range(features // width - 1):
        at = slice(f * batch, (f + 1) * batch)
        grads[at, :] = (grads[at, :] * lean).astype(BF16).astype(F32)

    slots[...] = jnp.zeros_like(slots)
    low = lax.broadcasted_iota(jnp.int32, (LOW, chunk), 0)
    block = table_rows // replicas
    for k in range(shards):
        start, live = scal[k], scal[shards + k]

        def group(i, _, start=start):
            for u in range(UNROLL):
                c = i * UNROLL + u
                slots[pl.ds(c, 1), :] = grads[pl.ds(dest[start + c], 1), :]
            return 0

        lax.fori_loop(0, (live + UNROLL - 1) // UNROLL, group, 0)
        total[...] = jnp.zeros_like(total)

        def piece(q, _, k=k, live=live):
            at = pl.ds(pl.multiple_of(q * chunk, chunk), chunk)
            place = q * chunk + lax.broadcasted_iota(jnp.int32, (1, chunk), 1)
            lows, highs = [], []
            for h in range(hot):
                row = ids[k][h : h + 1, at] ^ (mine * block)
                row = jnp.where(place < live, row, -1)
                high = lax.shift_right_arithmetic(row, LOW.bit_length() - 1)
                lows.append((low == (row & (LOW - 1))).astype(F32).astype(BF16))
                highs.append(high)
            for b in range(table_rows // LOW):
                count = None
                for h in range(hot):
                    hit = (highs[h] == b).astype(F32).astype(BF16)
                    term = lows[h] * hit
                    count = term if count is None else count + term
                counts[b * LOW : (b + 1) * LOW, :] = count
            total[...] += jnp.dot(
                counts[...], slots[at, :].astype(BF16), preferred_element_type=F32
            )
            return 0

        lax.fori_loop(0, (live + chunk - 1) // chunk, piece, 0)
        for m in range(replicas):
            half = even if m % 2 == 0 else odd
            half[m // 2, k] = total[m * block : (m + 1) * block, :].astype(BF16)


def dense_step(scal, dest, ids, dense, rows_in, bias, head, labels, weights, spots, replicas, rows):
    shards = len(ids)
    batch, width = dense.shape
    features = bias.shape[1]
    rank = sum_columns(weights, spots)
    capacity = ids[0].shape[1]
    chunk = 256 if capacity % 256 == 0 else 128
    half = jax.ShapeDtypeStruct((replicas // 2, shards, rows // replicas, width), BF16)
    smem = whole(pltpu.SMEM)
    return pl.pallas_call(
        functools.partial(dense_kernel, shards, replicas, spots, chunk),
        out_shape=(jax.ShapeDtypeStruct((1, batch), F32), half, half),
        in_specs=[smem, smem] + [whole()] * (shards + 5 + len(weights)),
        out_specs=(whole(), whole(), whole()),
        scratch_shapes=[
            pltpu.VMEM((features, rank), BF16),
            pltpu.VMEM((features, rank), BF16),
            pltpu.VMEM((batch, features), BF16),
            pltpu.VMEM((batch, features), BF16),
            pltpu.VMEM((features // width * batch - batch, width), F32),
            pltpu.VMEM((capacity, width), F32),
            pltpu.VMEM((rows, chunk), BF16),
            pltpu.VMEM((rows, width), F32),
        ],
        compiler_params=pltpu.CompilerParams(vmem_limit_bytes=VMEM_LIMIT),
        cost_estimate=pl.CostEstimate(
            flops=4 * 10**9, bytes_accessed=30 * 10**6, transcendentals=0
        ),
        name="dense",
    )(scal, dest, *ids, dense, rows_in, bias, head, labels, *weights)


def sum_columns(weights, spots):
    return max(spot.rank for spot in spots)


class Spot:
    def __init__(self, which, rank, copy):
        self.which, self.rank, self.copy = which, rank, copy

    def __call__(self, ref, factor, scal):
        self.copy(ref, factor[self.which], scal)


def gather_weights(cross_in, cross_out):
    shards, replicas = lax.axis_size("table"), lax.axis_size("replica")
    shard_rows, rank = cross_in.shape
    mine = lax.axis_index("replica")
    half, lanes = shard_rows // 2, 128
    if replicas != 8 or rank != 4 * lanes or half % 16 != 0:
        both = [lax.all_gather(w, "table", axis=0, tiled=True) for w in (cross_in, cross_out)]

        def whole_copy(ref, full, scal):
            full[...] = ref[...]

        return both, [Spot(i, rank, whole_copy) for i in range(2)]

    start = ((mine & 1) * half, (mine >> 1) * lanes)
    piece = jnp.stack([lax.dynamic_slice(w, start, (half, lanes)) for w in (cross_in, cross_out)])
    far = [shift(piece, k) for k in range(1, shards)]
    top = jnp.stack([f[0] for f in far])
    bottom = jnp.stack([f[1] for f in far])
    tops, bottoms = {0: top}, {0: bottom}
    tops[2], bottoms[2], tops[4], bottoms[4] = swap(top, 2), swap(bottom, 2), swap(top, 4), swap(bottom, 4)
    tops[6], bottoms[6] = swap(tops[2], 4), swap(bottoms[4], 2)
    arrays, spots = [], []
    for which, held in enumerate((tops, bottoms)):
        for m in (0, 2, 4, 6):
            for core in (0, 1):
                arrays.append(held[m] if core == 0 else swap(held[m], 1))

                def copy(ref, full, scal, m=m, core=core):
                    own, here = scal[2 * shards], scal[2 * shards + 1]
                    for k in range(1, shards):
                        source = lax.rem(here - k + shards, shards)
                        first = source * shard_rows + ((own & 1) ^ core) * half
                        at = pl.ds(pl.multiple_of(first, 16), half)
                        full[at, (m // 2) * lanes : (m // 2 + 1) * lanes] = ref[k - 1]

                spots.append(Spot(which, rank, copy))
    for which, own_rows in enumerate((cross_in, cross_out)):

        def copy_own(ref, full, scal):
            own, here = scal[2 * shards], scal[2 * shards + 1]
            at = pl.ds(pl.multiple_of(here * shard_rows, 16), shard_rows)
            for m in range(4):
                columns = pl.ds(pl.multiple_of(((own >> 1) ^ m) * lanes, lanes), lanes)
                full[at, m * lanes : (m + 1) * lanes] = ref[:, columns]

        arrays.append(own_rows)
        spots.append(Spot(which, rank, copy_own))
    return arrays, spots


def reduce_rows(even, odd):
    shards, replicas = lax.axis_size("table"), lax.axis_size("replica")
    kept = even.astype(F32) + swap(odd, 1).astype(F32)
    for masks in mask_stages(replicas)[1:]:
        split = kept.reshape((-1, len(masks) + 1) + kept.shape[1:])
        kept = split[:, 0]
        for i, mask in enumerate(masks):
            kept = kept + swap(split[:, i + 1].astype(BF16), mask).astype(F32)
    kept = kept[0]
    total = kept[0]
    for k in range(1, shards):
        total = total + shift(kept[k], -k)
    return total


def finish_kernel(replicas, scal, accum, *refs):
    pieces, (update, fresh) = refs[:-2], refs[-2:]
    block, width = pieces[0].shape
    mine = scal[0]
    for m, piece in enumerate(pieces):
        own = mine ^ m
        grad = piece[...]
        square = jnp.sum(grad * grad, axis=1, keepdims=True) * (1.0 / width)
        row = accum[pl.ds(own, 1), :] + row_of(square, block)
        fresh[pl.ds(own, 1), :] = row
        rows = pl.ds(pl.multiple_of(own * block, block), block)
        update[rows, :] = -grad / (jnp.sqrt(column_of(row, block)) + EPSILON)


def finish(mine, accum, pieces):
    block, width = pieces[0].shape
    replicas = len(pieces)
    return pl.pallas_call(
        functools.partial(finish_kernel, replicas),
        out_shape=(
            jax.ShapeDtypeStruct((replicas * block, width), F32),
            jax.ShapeDtypeStruct((replicas, block), F32),
        ),
        in_specs=[whole(pltpu.SMEM)] + [whole()] * (1 + replicas),
        out_specs=(whole(), whole()),
        name="finish",
    )(mine, accum, *pieces)


def local(
    emb_table,
    row_accum,
    look_rows,
    live_counts,
    bag_order,
    dense_emb,
    labels,
    cross_in,
    cross_out,
    cross_bias,
    head_weight,
):
    shards, replicas = lax.axis_size("table"), lax.axis_size("replica")
    here, mine = lax.axis_index("table"), lax.axis_index("replica")
    rows, width = emb_table.shape
    batch = dense_emb.shape[0]
    bags = bag_order.shape[2]
    per_sample = bags // batch
    capacity = look_rows.shape[4]
    padded = -(-capacity // 128) * 128

    sent = jnp.pad(look_rows[0, 0], ((0, 0), (0, 0), (0, padded - capacity)))
    around = [lax.rem(here + k, shards) for k in range(shards)]
    ids = [lax.dynamic_index_in_dim(sent, around[k], 0, keepdims=False) for k in range(shards)]
    ids = [ids[0]] + [shift(ids[k], k) for k in range(1, shards)]

    block = rows // replicas
    piece = lax.dynamic_slice_in_dim(emb_table, mine * block, block, 0).astype(BF16)
    near = jnp.stack([shift(piece, k) for k in range(1, shards)])
    pieces = replica_gather(near)

    weights, spots = gather_weights(cross_in, cross_out)

    live = lax.dynamic_index_in_dim(live_counts[0], here, 0, keepdims=False)
    starts = jnp.cumsum(live) - live
    back = lax.rem(here - jnp.arange(shards, dtype=jnp.int32) + shards, shards)
    scal = jnp.concatenate([starts[back], live[back], jnp.stack([mine, here])]).astype(jnp.int32)
    order = bag_order[0, 0]
    dest = (order % per_sample) * batch + order // per_sample
    dest = jnp.pad(dest, (0, 128))

    rows_in = pool(scal, dest, ids, emb_table, pieces, bags)
    logits, even, odd = dense_step(
        scal,
        dest,
        ids,
        dense_emb,
        rows_in,
        cross_bias.reshape(1, -1),
        head_weight.reshape(1, -1),
        labels.reshape(1, -1),
        weights,
        spots,
        replicas,
        rows,
    )
    grad = reduce_rows(even, odd)
    update, accum = finish(
        jnp.stack([mine]).astype(jnp.int32), row_accum.reshape(replicas, block), replica_gather(grad)
    )
    return (logits.reshape(-1), update, accum.reshape(-1))


def solution(mesh):
    placed = (
        P("table", None),
        P("table"),
        P("replica", "table", None, None, None),
        P("replica", None, None),
        P("replica", "table", None),
        P(("replica", "table"), None),
        P(("replica", "table")),
        P("table", None),
        P("table", None),
        P(),
        P(),
    )
    return jax.shard_map(
        local,
        mesh=mesh,
        in_specs=placed,
        out_specs=(P(("replica", "table")), P("table", None), P("table")),
        check_vma=False,
    )
```

time: 420 us -> 144 us (0.34)
  other arithmetic: 134 us -> 0.83 us
  local copies, waits for them, and re-layouts: 120 us -> 7.51 us
  waiting for transfers between devices: 129 us -> 42.9 us
  Pallas kernels: 0 us -> 45.6 us
  starting transfers between devices: 10.2 us -> 46.1 us
  between operations: 14.3 us -> 0.97 us
  matrix products: 12.9 us -> 0 us
    scatter-add x4 -> x0, other arithmetic: 112 us -> none  [local(): local_grads.at[row_ids[:, member].reshape(-1)].add(returned_rows)]
    gather x11 -> x2, local copies, waits for them, and re-layouts: 99.9 us -> 1.28 us  [the longest x1 0.64 us: local(): starts[back]]
    psum x1 -> x0, waiting for transfers between devices: 53.7 us -> none  [local(): summed = lax.psum(local_grads, 'replica')]
    ppermute x0 -> x44, starting transfers between devices: none -> 46.1 us  [the longest x12 27.6 us: shift(): lax.ppermute(array, 'table', [(i, (i + step) % size) for i in range(size)])]
    pallas_call x0 -> x3, Pallas kernels: none -> 45.6 us  [the longest x1 23.4 us: pool(): pl.pallas_call(functools.partial(pool_kernel, shards, replicas), out_shap...]
    all_gather x2 -> x0, waiting for transfers between devices: 43.6 us -> none  [the longest x1 43.6 us: local(): lax.all_gather(cross_out, 'table', axis=0, tiled=True)]
    ppermute x0 -> x44, waiting for transfers between devices: none -> 42.9 us  [the longest x32 33.5 us: swap(): return lax.ppermute(array, 'replica', [(i, i ^ mask) for i in range(size)])]
    all_to_all x2 -> x0, waiting for transfers between devices: 29.8 us -> none  [the longest x1 29.8 us: local(): lax.all_to_all(outgoing, 'table', split_axis=0, concat_axis=0, tiled=True)]
  transfers between devices with their start and end apart: 5 -> 44, of which waited for: 3 -> 22; matrix products, arithmetic and copies ran while one was open for 28% -> 2% of each run, Pallas kernels for 0% -> 16%
where the time goes in v1:
time: 144 us
  starting transfers between devices  46.1 us (32%)
  Pallas kernels  45.6 us (32%)
  waiting for transfers between devices  42.9 us (30%)
  local copies, waits for them, and re-layouts  7.51 us (5%)
    ppermute x32, waiting for transfers between devices, swap(): return lax.ppermute(array, 'replica', [(i, i ^ mask) for i in range(size)])  33.5 us
    ppermute x12, starting transfers between devices, shift(): lax.ppermute(array, 'table', [(i, (i + step) % size) for i in range(size)])  27.6 us
    pallas_call x1, Pallas kernels, pool(): pl.pallas_call(functools.partial(pool_kernel, shards, replicas), out_shap...  23.4 us
    pallas_call x1, Pallas kernels, dense_step(): pl.pallas_call(functools.partial(dense_kernel, shards, replicas, spots, c...  19.6 us
    ppermute x32, starting transfers between devices, swap(): return lax.ppermute(array, 'replica', [(i, i ^ mask) for i in range(size)])  18.4 us
    ppermute x12, waiting for transfers between devices, shift(): lax.ppermute(array, 'table', [(i, (i + step) % size) for i in range(size)])  9.46 us
    unnamed x34, local copies, waits for them, and re-layouts  4.28 us
  transfers between devices with their start and end apart: 44, of which 22 were waited for; matrix products, arithmetic and copies ran while one was open for 2% of the time, Pallas kernels for 16%

profile of v1, /device:TPU:0, one launch (start us, length us, event | category | flops | bytes accessed | tf_op | source)
XLA Modules:
  0.0 143.9 jit_solution(10368028836099585415)
XLA Ops:
  0.6 0.8 dynamic-slice_convert_fusion
  1.5 5.0 %collective-permute-start.5 = (bf16[128,128]{1,0:T(8,128)(2,1)S(1)}, bf16[128,128]{1,0:T(8,128)(2,1)S(1)}, u32[]{:S(2)}, u32[]{:S(2)}) collective-permute-start(bf16[128,128]{1,0:T(8,128)(2,1)S(1)} %dynamic-slice_convert_fusion), channel_id=1, source_target_pairs={{0,3},{1,0},{2,1},{3,2},{4,7},{5,4},{6,5},{7,6},{8,11},{9,8},{10,9... | collective-permute-start | bytes 98312 | tf_op jit(solution)/shard_map/ppermute | solution.py:24
  6.5 1.0 collective-permute-start.3
  7.5 1.0 dynamic-slice_bitcast_fusion
  8.6 2.9 %collective-permute-start.15 = (bf16[2,432,128]{2,1,0:T(8,128)(2,1)S(1)}, bf16[2,432,128]{2,1,0:T(8,128)(2,1)S(1)}, u32[]{:S(2)}, u32[]{:S(2)}) collective-permute-start(bf16[2,432,128]{2,1,0:T(8,128)(2,1)S(1)} %pad_maximum_fusion.2), channel_id=1, source_target_pairs={{0,3},{1,0},{2,1},{3,2},{4,7},{5,4},{6,5},{7,6},{8,11},{9,8},{10,9... | collective-permute-start | bytes 663560 | tf_op jit(solution)/shard_map/ppermute | solution.py:24
  11.4 1.1 collective-permute-start.14
  13.4 3.8 %collective-permute-start.2 = (s32[4,1280]{1,0:T(4,128)S(1)}, s32[4,1280]{1,0:T(4,128)S(1)}, u32[]{:S(2)}, u32[]{:S(2)}) collective-permute-start(s32[4,1280]{1,0:T(4,128)S(1)} %get-tuple-element.31), channel_id=1, source_target_pairs={{0,3},{1,0},{2,1},{3,2},{4,7},{5,4},{6,5},{7,6},{8,11},{9,8},{10,9... | collective-permute-start | bytes 61448 | tf_op jit(solution)/shard_map/ppermute | solution.py:24
  17.4 11.2 %collective-permute-start.1 = (s32[4,1280]{1,0:T(4,128)S(1)}, s32[4,1280]{1,0:T(4,128)S(1)}, u32[]{:S(2)}, u32[]{:S(2)}) collective-permute-start(s32[4,1280]{1,0:T(4,128)S(1)} %get-tuple-element.33), channel_id=1, source_target_pairs={{0,2},{1,3},{2,0},{3,1},{4,6},{5,7},{6,4},{7,5},{8,10},{9,11},{10,... | collective-permute-start | bytes 61448 | tf_op jit(solution)/shard_map/ppermute | solution.py:24
  28.6 3.8 %collective-permute-done.14 = bf16[2,432,128]{2,1,0:T(8,128)(2,1)S(1)} collective-permute-done((bf16[2,432,128]{2,1,0:T(8,128)(2,1)S(1)}, bf16[2,432,128]{2,1,0:T(8,128)(2,1)S(1)}, u32[]{:S(2)}, u32[]{:S(2)}) %collective-permute-start.14) | collective-permute-done | bytes 221216 | tf_op jit(solution)/shard_map/ppermute | solution.py:24
  32.4 2.4 %collective-permute-start.11 = (bf16[3,128,128]{2,1,0:T(8,128)(2,1)S(1)}, bf16[3,128,128]{2,1,0:T(8,128)(2,1)S(1)}, u32[]{:S(2)}, u32[]{:S(2)}) collective-permute-start(bf16[3,128,128]{2,1,0:T(8,128)(2,1)S(1)} %pad_maximum_fusion.3.refs_5_), channel_id=1, source_target_pairs={{0,24},{4,28},{8,16},{12,20},{16,8},{20,12},{24,0},{28,4},{1,25},{... | collective-permute-start | bytes 294920 | tf_op jit(solution)/shard_map/ppermute | solution.py:19
  36.1 2.4 %collective-permute-done.11.refs_11_ = bf16[3,128,128]{2,1,0:T(8,128)(2,1)S(1)} collective-permute-done((bf16[3,128,128]{2,1,0:T(8,128)(2,1)S(1)}, bf16[3,128,128]{2,1,0:T(8,128)(2,1)S(1)}, u32[]{:S(2)}, u32[]{:S(2)}) %collective-permute-start.11) | collective-permute-done | bytes 98336 | tf_op jit(solution)/shard_map/ppermute | solution.py:19
  38.6 1.0 collective-permute-done.9.refs_9_
  39.6 0.9 collective-permute-start.19
  40.5 1.2 collective-permute-start.17
  41.7 0.9 collective-permute-start.26
  42.8 1.1 collective-permute-done.8.refs_8_
  44.0 1.3 collective-permute-start.24
  45.2 5.0 %collective-permute-done.19.refs_13_ = bf16[3,432,128]{2,1,0:T(8,128)(2,1)S(1)} collective-permute-done((bf16[3,432,128]{2,1,0:T(8,128)(2,1)S(1)}, bf16[3,432,128]{2,1,0:T(8,128)(2,1)S(1)}, u32[]{:S(2)}, u32[]{:S(2)}) %collective-permute-start.19) | collective-permute-done | bytes 331808 | tf_op jit(solution)/shard_map/ppermute | solution.py:19
  50.2 0.9 collective-permute-done.17.refs_11_
  51.2 1.2 collective-permute-start.21
  52.4 4.9 %collective-permute-done.26.refs_21_ = bf16[3,432,128]{2,1,0:T(8,128)(2,1)S(1)} collective-permute-done((bf16[3,432,128]{2,1,0:T(8,128)(2,1)S(1)}, bf16[3,432,128]{2,1,0:T(8,128)(2,1)S(1)}, u32[]{:S(2)}, u32[]{:S(2)}) %collective-permute-start.26) | collective-permute-done | bytes 331808 | tf_op jit(solution)/shard_map/ppermute | solution.py:19
  57.3 0.8 collective-permute-start.28
  59.6 0.7 copy-done.15
  60.3 0.7 copy-done.13
  61.8 2.3 %collective-permute-done.21.refs_15_ = bf16[3,432,128]{2,1,0:T(8,128)(2,1)} collective-permute-done((bf16[3,432,128]{2,1,0:T(8,128)(2,1)S(1)}, bf16[3,432,128]{2,1,0:T(8,128)(2,1)}, u32[]{:S(2)}, u32[]{:S(2)}) %collective-permute-start.21) | collective-permute-done | bytes 331808 | tf_op jit(solution)/shard_map/ppermute | solution.py:19
  64.2 2.4 %collective-permute-done.28.refs_23_ = bf16[3,432,128]{2,1,0:T(8,128)(2,1)} collective-permute-done((bf16[3,432,128]{2,1,0:T(8,128)(2,1)S(1)}, bf16[3,432,128]{2,1,0:T(8,128)(2,1)}, u32[]{:S(2)}, u32[]{:S(2)}) %collective-permute-start.28) | collective-permute-done | bytes 331808 | tf_op jit(solution)/shard_map/ppermute | solution.py:19
  66.7 23.4 %pool.1.refs_5_ = bf16[3328,128]{1,0:T(8,128)(2,1)S(1)} custom-call(s32[10]{0:T(128)S(1)} %pad_add_fusion.scal, s32[3456]{0:T(1024)S(1)} %pad.8.dest, s32[4,1280]{1,0:T(4,128)S(1)} %get-tuple-element.34.refs_0_, s32[4,1280]{1,0:T(4,128)S(1)} %collective-permute-done.refs_1_, s32[4,1280]{1,0:T(4,128)S(1)} %collective-permute-done.1.refs_2_, ...), custom_call_target="tpu_custom_call" | custom-call | flops 1000000 | bytes 30000000 | tf_op jit(solution)/shard_map/pool/pallas_call | solution.py:90
  90.2 0.9 copy-done
  91.7 19.6 %dense.1 = (f32[1,128]{1,0:T(1,128)}, bf16[4,4,128,128]{3,2,1,0:T(8,128)(2,1)S(1)}, bf16[4,4,128,128]{3,2,1,0:T(8,128)(2,1)}) custom-call(s32[10]{0:T(128)S(1)} %pad_add_fusion.scal, s32[3456]{0:T(1024)S(1)} %pad.8.dest, s32[4,1280]{1,0:T(4,128)S(1)} %get-tuple-element.34.refs_0_, s32[4,1280]{1,0:T(4,128)S(1)} %collective-permute-done.refs_1_, ...), custom_call_target="tpu_custom_call" | custom-call | flops 4000000000 | bytes 30000000 | tf_op jit(solution)/shard_map/dense/pallas_call | solution.py:217
  111.9 1.7 %collective-permute-done.30 = bf16[4,4,128,128]{3,2,1,0:T(8,128)(2,1)S(1)} collective-permute-done((bf16[4,4,128,128]{3,2,1,0:T(8,128)(2,1)}, bf16[4,4,128,128]{3,2,1,0:T(8,128)(2,1)S(1)}, u32[]{:S(2)}, u32[]{:S(2)}) %collective-permute-start.30) | collective-permute-done | bytes 524320 | tf_op jit(solution)/shard_map/ppermute | solution.py:19
  113.9 1.4 collective-permute-start.31
  115.2 1.0 collective-permute-start.33
  116.3 1.1 collective-permute-start.32
  117.4 2.8 %collective-permute-done.31 = bf16[1,4,128,128]{3,2,1,0:T(8,128)(2,1)S(1)} collective-permute-done((bf16[1,4,128,128]{3,2,1,0:T(8,128)(2,1)S(1)}, bf16[1,4,128,128]{3,2,1,0:T(8,128)(2,1)S(1)}, u32[]{:S(2)}, u32[]{:S(2)}) %collective-permute-start.31) | collective-permute-done | bytes 131104 | tf_op jit(solution)/shard_map/ppermute | solution.py:19
  120.3 2.7 %collective-permute-done.33 = bf16[1,4,128,128]{3,2,1,0:T(8,128)(2,1)S(1)} collective-permute-done((bf16[1,4,128,128]{3,2,1,0:T(8,128)(2,1)S(1)}, bf16[1,4,128,128]{3,2,1,0:T(8,128)(2,1)S(1)}, u32[]{:S(2)}, u32[]{:S(2)}) %collective-permute-start.33) | collective-permute-done | bytes 131104 | tf_op jit(solution)/shard_map/ppermute | solution.py:19
  122.9 1.4 collective-permute-done.32
  124.4 2.0 %collective-permute-start.36 = (f32[128,128]{1,0:T(8,128)S(1)}, f32[128,128]{1,0:T(8,128)S(1)}, u32[]{:S(2)}, u32[]{:S(2)}) collective-permute-start(f32[128,128]{1,0:T(8,128)S(1)} %get-tuple-element.23), channel_id=1, source_target_pairs={{0,1},{1,2},{2,3},{3,0},{4,5},{5,6},{6,7},{7,4},{8,9},{9,10},{10,1... | collective-permute-start | bytes 196616 | tf_op jit(solution)/shard_map/ppermute | solution.py:24
  126.9 2.9 %collective-permute-done.34 = f32[128,128]{1,0:T(8,128)S(1)} collective-permute-done((f32[128,128]{1,0:T(8,128)S(1)}, f32[128,128]{1,0:T(8,128)S(1)}, u32[]{:S(2)}, u32[]{:S(2)}) %collective-permute-start.34) | collective-permute-done | bytes 65568 | tf_op jit(solution)/shard_map/ppermute | solution.py:24
  129.8 1.0 collective-permute-done.36
  130.8 1.7 %collective-permute-done.35 = f32[128,128]{1,0:T(8,128)S(1)} collective-permute-done((f32[128,128]{1,0:T(8,128)S(1)}, f32[128,128]{1,0:T(8,128)S(1)}, u32[]{:S(2)}, u32[]{:S(2)}) %collective-permute-start.35) | collective-permute-done | bytes 65568 | tf_op jit(solution)/shard_map/ppermute | solution.py:24
  132.5 1.8 %collective-permute-start.42 = (f32[128,128]{1,0:T(8,128)S(1)}, f32[128,128]{1,0:T(8,128)S(1)}, u32[]{:S(2)}, u32[]{:S(2)}) collective-permute-start(f32[128,128]{1,0:T(8,128)S(1)} %fusion.5.refs_0_), channel_id=1, source_target_pairs={{0,24},{4,28},{8,16},{12,20},{16,8},{20,12},{24,0},{28,4},{1,25},{... | collective-permute-start | bytes 196616 | tf_op jit(solution)/shard_map/ppermute | solution.py:19
  134.3 0.9 collective-permute-start.40
  135.2 0.8 collective-permute-start.38
  136.1 1.8 %collective-permute-done.42.refs_6_ = f32[128,128]{1,0:T(8,128)S(1)} collective-permute-done((f32[128,128]{1,0:T(8,128)S(1)}, f32[128,128]{1,0:T(8,128)S(1)}, u32[]{:S(2)}, u32[]{:S(2)}) %collective-permute-start.42) | collective-permute-done | bytes 65568 | tf_op jit(solution)/shard_map/ppermute | solution.py:19
  137.9 0.7 collective-permute-done.40.refs_4_
  138.6 0.9 collective-permute-done.38.refs_2_
  139.9 0.9 collective-permute-done.39.refs_3_
  141.4 2.5 %finish.1 = (f32[1024,128]{1,0:T(8,128)}, f32[8,128]{1,0:T(8,128)}) custom-call(s32[1]{0:T(128)} %bitcast.4.scal, f32[8,128]{1,0:T(8,128)} %bitcast.68, f32[128,128]{1,0:T(8,128)} %copy-done.4, f32[128,128]{1,0:T(8,128)} %copy-done.9, f32[128,128]{1,0:T(8,128)} %copy-done.8, f32[128,128]{1,0:T(8,128)} %copy-done.12, f32[128,128]{1,0:T(8,128)} %copy-done.7, ...), custom_call_target="tpu_custom_call" | custom-call | tf_op jit(solution)/shard_map/finish/pallas_call | solution.py:334
  (106 shorter events, 7.8 us)
Async XLA Ops:
  1.5 11.9 %collective-permute-start.5 = (bf16[128,128]{1,0:T(8,128)(2,1)S(1)}, bf16[128,128]{1,0:T(8,128)(2,1)S(1)}, u32[]{:S(2)}, u32[]{:S(2)}) collective-permute-start(bf16[128,128]{1,0:T(8,128)(2,1)S(1)} %dynamic-slice_convert_fusion), channel_id=1, source_target_pairs={{0,3},{1,0},{2,1},{3,2},{4,7},{5,4},{6,5},{7,6},{8,11},{9,8},{10,9... | collective-permute-start | bytes 98312 | tf_op jit(solution)/shard_map/ppermute | solution.py:24
  6.5 6.9 %collective-permute-start.4 = (bf16[128,128]{1,0:T(8,128)(2,1)S(1)}, bf16[128,128]{1,0:T(8,128)(2,1)S(1)}, u32[]{:S(2)}, u32[]{:S(2)}) collective-permute-start(bf16[128,128]{1,0:T(8,128)(2,1)S(1)} %dynamic-slice_convert_fusion), channel_id=1, source_target_pairs={{0,2},{1,3},{2,0},{3,1},{4,6},{5,7},{6,4},{7,5},{8,10},{9,11},{10,... | collective-permute-start | bytes 98312 | tf_op jit(solution)/shard_map/ppermute | solution.py:24
  6.5 10.7 %collective-permute-start.3 = (bf16[128,128]{1,0:T(8,128)(2,1)S(1)}, bf16[128,128]{1,0:T(8,128)(2,1)S(1)}, u32[]{:S(2)}, u32[]{:S(2)}) collective-permute-start(bf16[128,128]{1,0:T(8,128)(2,1)S(1)} %dynamic-slice_convert_fusion), channel_id=1, source_target_pairs={{0,1},{1,2},{2,3},{3,0},{4,5},{5,6},{6,7},{7,4},{8,9},{9,10},{10,1... | collective-permute-start | bytes 98312 | tf_op jit(solution)/shard_map/ppermute | solution.py:24
  8.6 4.0 %copy-start.5 = (s32[1,1,4,4,1248]{4,3,2,1,0:T(4,128)S(1)}, s32[1,1,4,4,1248]{4,3,2,1,0:T(4,128)}, u32[]{:S(2)}) copy-start(s32[1,1,4,4,1248]{4,3,2,1,0:T(4,128)} %param.13) | copy-start | bytes 239620
  8.6 8.8 %collective-permute-start.15 = (bf16[2,432,128]{2,1,0:T(8,128)(2,1)S(1)}, bf16[2,432,128]{2,1,0:T(8,128)(2,1)S(1)}, u32[]{:S(2)}, u32[]{:S(2)}) collective-permute-start(bf16[2,432,128]{2,1,0:T(8,128)(2,1)S(1)} %pad_maximum_fusion.2), channel_id=1, source_target_pairs={{0,3},{1,0},{2,1},{3,2},{4,7},{5,4},{6,5},{7,6},{8,11},{9,8},{10,9... | collective-permute-start | bytes 663560 | tf_op jit(solution)/shard_map/ppermute | solution.py:24
  11.4 21.0 %collective-permute-start.14 = (bf16[2,432,128]{2,1,0:T(8,128)(2,1)S(1)}, bf16[2,432,128]{2,1,0:T(8,128)(2,1)S(1)}, u32[]{:S(2)}, u32[]{:S(2)}) collective-permute-start(bf16[2,432,128]{2,1,0:T(8,128)(2,1)S(1)} %pad_maximum_fusion.2), channel_id=1, source_target_pairs={{0,2},{1,3},{2,0},{3,1},{4,6},{5,7},{6,4},{7,5},{8,10},{9,11},{10,... | collective-permute-start | bytes 663560 | tf_op jit(solution)/shard_map/ppermute | solution.py:24
  13.4 21.5 %collective-permute-start.13 = (bf16[2,432,128]{2,1,0:T(8,128)(2,1)S(1)}, bf16[2,432,128]{2,1,0:T(8,128)(2,1)S(1)}, u32[]{:S(2)}, u32[]{:S(2)}) collective-permute-start(bf16[2,432,128]{2,1,0:T(8,128)(2,1)S(1)} %pad_maximum_fusion.2), channel_id=1, source_target_pairs={{0,1},{1,2},{2,3},{3,0},{4,5},{5,6},{6,7},{7,4},{8,9},{9,10},{10,1... | collective-permute-start | bytes 663560 | tf_op jit(solution)/shard_map/ppermute | solution.py:24
  13.4 22.1 %collective-permute-start.2 = (s32[4,1280]{1,0:T(4,128)S(1)}, s32[4,1280]{1,0:T(4,128)S(1)}, u32[]{:S(2)}, u32[]{:S(2)}) collective-permute-start(s32[4,1280]{1,0:T(4,128)S(1)} %get-tuple-element.31), channel_id=1, source_target_pairs={{0,3},{1,0},{2,1},{3,2},{4,7},{5,4},{6,5},{7,6},{8,11},{9,8},{10,9... | collective-permute-start | bytes 61448 | tf_op jit(solution)/shard_map/ppermute | solution.py:24
  17.3 18.9 %collective-permute-start = (s32[4,1280]{1,0:T(4,128)S(1)}, s32[4,1280]{1,0:T(4,128)S(1)}, u32[]{:S(2)}, u32[]{:S(2)}) collective-permute-start(s32[4,1280]{1,0:T(4,128)S(1)} %get-tuple-element.32), channel_id=1, source_target_pairs={{0,1},{1,2},{2,3},{3,0},{4,5},{5,6},{6,7},{7,4},{8,9},{9,10},{10,1... | collective-permute-start | bytes 61448 | tf_op jit(solution)/shard_map/ppermute | solution.py:24
  17.4 22.3 %collective-permute-start.1 = (s32[4,1280]{1,0:T(4,128)S(1)}, s32[4,1280]{1,0:T(4,128)S(1)}, u32[]{:S(2)}, u32[]{:S(2)}) collective-permute-start(s32[4,1280]{1,0:T(4,128)S(1)} %get-tuple-element.33), channel_id=1, source_target_pairs={{0,2},{1,3},{2,0},{3,1},{4,6},{5,7},{6,4},{7,5},{8,10},{9,11},{10,... | collective-permute-start | bytes 61448 | tf_op jit(solution)/shard_map/ppermute | solution.py:24
  32.4 6.2 %collective-permute-start.11 = (bf16[3,128,128]{2,1,0:T(8,128)(2,1)S(1)}, bf16[3,128,128]{2,1,0:T(8,128)(2,1)S(1)}, u32[]{:S(2)}, u32[]{:S(2)}) collective-permute-start(bf16[3,128,128]{2,1,0:T(8,128)(2,1)S(1)} %pad_maximum_fusion.3.refs_5_), channel_id=1, source_target_pairs={{0,24},{4,28},{8,16},{12,20},{16,8},{20,12},{24,0},{28,4},{1,25},{... | collective-permute-start | bytes 294920 | tf_op jit(solution)/shard_map/ppermute | solution.py:19
  34.9 4.7 %collective-permute-start.9 = (bf16[3,128,128]{2,1,0:T(8,128)(2,1)S(1)}, bf16[3,128,128]{2,1,0:T(8,128)(2,1)S(1)}, u32[]{:S(2)}, u32[]{:S(2)}) collective-permute-start(bf16[3,128,128]{2,1,0:T(8,128)(2,1)S(1)} %pad_maximum_fusion.3.refs_5_), channel_id=1, source_target_pairs={{0,16},{4,20},{8,24},{12,28},{16,0},{20,4},{24,8},{28,12},{1,17},{... | collective-permute-start | bytes 294920 | tf_op jit(solution)/shard_map/ppermute | solution.py:19
  35.5 5.0 %collective-permute-start.7 = (bf16[3,128,128]{2,1,0:T(8,128)(2,1)S(1)}, bf16[3,128,128]{2,1,0:T(8,128)(2,1)S(1)}, u32[]{:S(2)}, u32[]{:S(2)}) collective-permute-start(bf16[3,128,128]{2,1,0:T(8,128)(2,1)S(1)} %pad_maximum_fusion.3.refs_5_), channel_id=1, source_target_pairs={{0,8},{4,12},{8,0},{12,4},{16,24},{20,28},{24,16},{28,20},{1,9},{5... | collective-permute-start | bytes 294920 | tf_op jit(solution)/shard_map/ppermute | solution.py:19
  36.1 5.5 %collective-permute-start.6 = (bf16[3,128,128]{2,1,0:T(8,128)(2,1)S(1)}, bf16[3,128,128]{2,1,0:T(8,128)(2,1)S(1)}, u32[]{:S(2)}, u32[]{:S(2)}) collective-permute-start(bf16[3,128,128]{2,1,0:T(8,128)(2,1)S(1)} %pad_maximum_fusion.3.refs_5_), channel_id=1, source_target_pairs={{0,4},{4,0},{8,12},{12,8},{16,20},{20,16},{24,28},{28,24},{1,5},{5... | collective-permute-start | bytes 294920 | tf_op jit(solution)/shard_map/ppermute | solution.py:19
  38.6 3.1 %collective-permute-start.12 = (bf16[3,128,128]{2,1,0:T(8,128)(2,1)S(1)}, bf16[3,128,128]{2,1,0:T(8,128)(2,1)S(1)}, u32[]{:S(2)}, u32[]{:S(2)}) collective-permute-start(bf16[3,128,128]{2,1,0:T(8,128)(2,1)S(1)} %collective-permute-done.11.refs_11_), channel_id=1, source_target_pairs={{0,4},{4,0},{8,12},{12,8},{16,20},{20,16},{24,28},{28,24},{1,5},{5... | collective-permute-start | bytes 294920 | tf_op jit(solution)/shard_map/ppermute | solution.py:19
  39.6 3.0 %collective-permute-start.10 = (bf16[3,128,128]{2,1,0:T(8,128)(2,1)S(1)}, bf16[3,128,128]{2,1,0:T(8,128)(2,1)S(1)}, u32[]{:S(2)}, u32[]{:S(2)}) collective-permute-start(bf16[3,128,128]{2,1,0:T(8,128)(2,1)S(1)} %collective-permute-done.9.refs_9_), channel_id=1, source_target_pairs={{0,4},{4,0},{8,12},{12,8},{16,20},{20,16},{24,28},{28,24},{1,5},{5... | collective-permute-start | bytes 294920 | tf_op jit(solution)/shard_map/ppermute | solution.py:19
  39.6 10.6 %collective-permute-start.19 = (bf16[3,432,128]{2,1,0:T(8,128)(2,1)S(1)}, bf16[3,432,128]{2,1,0:T(8,128)(2,1)S(1)}, u32[]{:S(2)}, u32[]{:S(2)}) collective-permute-start(bf16[3,432,128]{2,1,0:T(8,128)(2,1)S(1)} %pad_maximum_fusion.refs_9_), channel_id=1, source_target_pairs={{0,16},{4,20},{8,24},{12,28},{16,0},{20,4},{24,8},{28,12},{1,17},{... | collective-permute-start | bytes 995336 | tf_op jit(solution)/shard_map/ppermute | solution.py:19
  40.5 10.6 %collective-permute-start.17 = (bf16[3,432,128]{2,1,0:T(8,128)(2,1)S(1)}, bf16[3,432,128]{2,1,0:T(8,128)(2,1)S(1)}, u32[]{:S(2)}, u32[]{:S(2)}) collective-permute-start(bf16[3,432,128]{2,1,0:T(8,128)(2,1)S(1)} %pad_maximum_fusion.refs_9_), channel_id=1, source_target_pairs={{0,8},{4,12},{8,0},{12,4},{16,24},{20,28},{24,16},{28,20},{1,9},{5... | collective-permute-start | bytes 995336 | tf_op jit(solution)/shard_map/ppermute | solution.py:19
  41.7 9.5 %collective-permute-start.16 = (bf16[3,432,128]{2,1,0:T(8,128)(2,1)S(1)}, bf16[3,432,128]{2,1,0:T(8,128)(2,1)S(1)}, u32[]{:S(2)}, u32[]{:S(2)}) collective-permute-start(bf16[3,432,128]{2,1,0:T(8,128)(2,1)S(1)} %pad_maximum_fusion.refs_9_), channel_id=1, source_target_pairs={{0,4},{4,0},{8,12},{12,8},{16,20},{20,16},{24,28},{28,24},{1,5},{5... | collective-permute-start | bytes 995336 | tf_op jit(solution)/shard_map/ppermute | solution.py:19
  41.7 15.6 %collective-permute-start.26 = (bf16[3,432,128]{2,1,0:T(8,128)(2,1)S(1)}, bf16[3,432,128]{2,1,0:T(8,128)(2,1)S(1)}, u32[]{:S(2)}, u32[]{:S(2)}) collective-permute-start(bf16[3,432,128]{2,1,0:T(8,128)(2,1)S(1)} %pad_maximum_fusion.1.refs_17_), channel_id=1, source_target_pairs={{0,16},{4,20},{8,24},{12,28},{16,0},{20,4},{24,8},{28,12},{1,17},{... | collective-permute-start | bytes 995336 | tf_op jit(solution)/shard_map/ppermute | solution.py:19
  42.6 1.4 collective-permute-start.8
  44.0 17.2 %collective-permute-start.24 = (bf16[3,432,128]{2,1,0:T(8,128)(2,1)S(1)}, bf16[3,432,128]{2,1,0:T(8,128)(2,1)}, u32[]{:S(2)}, u32[]{:S(2)}) collective-permute-start(bf16[3,432,128]{2,1,0:T(8,128)(2,1)S(1)} %pad_maximum_fusion.1.refs_17_), channel_id=1, source_target_pairs={{0,8},{4,12},{8,0},{12,4},{16,24},{20,28},{24,16},{28,20},{1,9},{5... | collective-permute-start | bytes 995336 | tf_op jit(solution)/shard_map/ppermute | solution.py:19
  50.2 11.0 %collective-permute-start.23 = (bf16[3,432,128]{2,1,0:T(8,128)(2,1)S(1)}, bf16[3,432,128]{2,1,0:T(8,128)(2,1)}, u32[]{:S(2)}, u32[]{:S(2)}) collective-permute-start(bf16[3,432,128]{2,1,0:T(8,128)(2,1)S(1)} %pad_maximum_fusion.1.refs_17_), channel_id=1, source_target_pairs={{0,4},{4,0},{8,12},{12,8},{16,20},{20,16},{24,28},{28,24},{1,5},{5... | collective-permute-start | bytes 995336 | tf_op jit(solution)/shard_map/ppermute | solution.py:19
  51.1 10.6 %collective-permute-start.20 = (bf16[3,432,128]{2,1,0:T(8,128)(2,1)S(1)}, bf16[3,432,128]{2,1,0:T(8,128)(2,1)}, u32[]{:S(2)}, u32[]{:S(2)}) collective-permute-start(bf16[3,432,128]{2,1,0:T(8,128)(2,1)S(1)} %collective-permute-done.19.refs_13_), channel_id=1, source_target_pairs={{0,4},{4,0},{8,12},{12,8},{16,20},{20,16},{24,28},{28,24},{1,5},{5... | collective-permute-start | bytes 995336 | tf_op jit(solution)/shard_map/ppermute | solution.py:19
  51.2 13.0 %collective-permute-start.21 = (bf16[3,432,128]{2,1,0:T(8,128)(2,1)S(1)}, bf16[3,432,128]{2,1,0:T(8,128)(2,1)}, u32[]{:S(2)}, u32[]{:S(2)}) collective-permute-start(bf16[3,432,128]{2,1,0:T(8,128)(2,1)S(1)} %collective-permute-done.17.refs_11_), channel_id=1, source_target_pairs={{0,16},{4,20},{8,24},{12,28},{16,0},{20,4},{24,8},{28,12},{1,17},{... | collective-permute-start | bytes 995336 | tf_op jit(solution)/shard_map/ppermute | solution.py:19
  57.3 9.3 %collective-permute-start.28 = (bf16[3,432,128]{2,1,0:T(8,128)(2,1)S(1)}, bf16[3,432,128]{2,1,0:T(8,128)(2,1)}, u32[]{:S(2)}, u32[]{:S(2)}) collective-permute-start(bf16[3,432,128]{2,1,0:T(8,128)(2,1)S(1)} %collective-permute-done.26.refs_21_), channel_id=1, source_target_pairs={{0,8},{4,12},{8,0},{12,4},{16,24},{20,28},{24,16},{28,20},{1,9},{5... | collective-permute-start | bytes 995336 | tf_op jit(solution)/shard_map/ppermute | solution.py:19
  58.2 8.5 %copy-start.1 = (f32[1024,128]{1,0:T(8,128)S(1)}, f32[1024,128]{1,0:T(8,128)}, u32[]{:S(2)}) copy-start(f32[1024,128]{1,0:T(8,128)} %refs_4_.2) | copy-start | bytes 1572868
  61.2 29.9 %collective-permute-start.18 = (bf16[3,432,128]{2,1,0:T(8,128)(2,1)S(1)}, bf16[3,432,128]{2,1,0:T(8,128)(2,1)S(1)}, u32[]{:S(2)}, u32[]{:S(2)}) collective-permute-start(bf16[3,432,128]{2,1,0:T(8,128)(2,1)S(1)} %collective-permute-done.17.refs_11_), channel_id=1, source_target_pairs={{0,4},{4,0},{8,12},{12,8},{16,20},{20,16},{24,28},{28,24},{1,5},{5... | collective-permute-start | bytes 995336 | tf_op jit(solution)/shard_map/ppermute | solution.py:19
  61.3 29.8 %collective-permute-start.27 = (bf16[3,432,128]{2,1,0:T(8,128)(2,1)S(1)}, bf16[3,432,128]{2,1,0:T(8,128)(2,1)S(1)}, u32[]{:S(2)}, u32[]{:S(2)}) collective-permute-start(bf16[3,432,128]{2,1,0:T(8,128)(2,1)S(1)} %collective-permute-done.26.refs_21_), channel_id=1, source_target_pairs={{0,4},{4,0},{8,12},{12,8},{16,20},{20,16},{24,28},{28,24},{1,5},{5... | collective-permute-start | bytes 995336 | tf_op jit(solution)/shard_map/ppermute | solution.py:19
  61.7 29.4 %collective-permute-start.25 = (bf16[3,432,128]{2,1,0:T(8,128)(2,1)}, bf16[3,432,128]{2,1,0:T(8,128)(2,1)S(1)}, u32[]{:S(2)}, u32[]{:S(2)}) collective-permute-start(bf16[3,432,128]{2,1,0:T(8,128)(2,1)} %collective-permute-done.24.refs_19_), channel_id=1, source_target_pairs={{0,4},{4,0},{8,12},{12,8},{16,20},{20,16},{24,28},{28,24},{1,5},{5... | collective-permute-start | bytes 995336 | tf_op jit(solution)/shard_map/ppermute | solution.py:19
  64.2 26.9 %collective-permute-start.22 = (bf16[3,432,128]{2,1,0:T(8,128)(2,1)}, bf16[3,432,128]{2,1,0:T(8,128)(2,1)S(1)}, u32[]{:S(2)}, u32[]{:S(2)}) collective-permute-start(bf16[3,432,128]{2,1,0:T(8,128)(2,1)} %collective-permute-done.21.refs_15_), channel_id=1, source_target_pairs={{0,4},{4,0},{8,12},{12,8},{16,20},{20,16},{24,28},{28,24},{1,5},{5... | collective-permute-start | bytes 995336 | tf_op jit(solution)/shard_map/ppermute | solution.py:19
  66.6 24.5 %collective-permute-start.29 = (bf16[3,432,128]{2,1,0:T(8,128)(2,1)}, bf16[3,432,128]{2,1,0:T(8,128)(2,1)S(1)}, u32[]{:S(2)}, u32[]{:S(2)}) collective-permute-start(bf16[3,432,128]{2,1,0:T(8,128)(2,1)} %collective-permute-done.28.refs_23_), channel_id=1, source_target_pairs={{0,4},{4,0},{8,12},{12,8},{16,20},{20,16},{24,28},{28,24},{1,5},{5... | collective-permute-start | bytes 995336 | tf_op jit(solution)/shard_map/ppermute | solution.py:19
  66.7 24.4 %copy-start.2 = (bf16[128,128]{1,0:T(8,128)(2,1)S(1)}, bf16[128,128]{1,0:T(8,128)(2,1)}, u32[]{:S(2)}) copy-start(bf16[128,128]{1,0:T(8,128)(2,1)} %refs_4_.3) | copy-start | bytes 98308
  111.4 2.3 %collective-permute-start.30 = (bf16[4,4,128,128]{3,2,1,0:T(8,128)(2,1)}, bf16[4,4,128,128]{3,2,1,0:T(8,128)(2,1)S(1)}, u32[]{:S(2)}, u32[]{:S(2)}) collective-permute-start(bf16[4,4,128,128]{3,2,1,0:T(8,128)(2,1)} %get-tuple-element.10), channel_id=1, source_target_pairs={{0,4},{4,0},{8,12},{12,8},{16,20},{20,16},{24,28},{28,24},{1,5},{5... | collective-permute-start | bytes 1572872 | tf_op jit(solution)/shard_map/ppermute | solution.py:19
  113.9 6.4 %collective-permute-start.31 = (bf16[1,4,128,128]{3,2,1,0:T(8,128)(2,1)S(1)}, bf16[1,4,128,128]{3,2,1,0:T(8,128)(2,1)S(1)}, u32[]{:S(2)}, u32[]{:S(2)}) collective-permute-start(bf16[1,4,128,128]{3,2,1,0:T(8,128)(2,1)S(1)} %get-tuple-element.19), channel_id=1, source_target_pairs={{0,8},{4,12},{8,0},{12,4},{16,24},{20,28},{24,16},{28,20},{1,9},{5... | collective-permute-start | bytes 393224 | tf_op jit(solution)/shard_map/ppermute | solution.py:19
  115.2 7.7 %collective-permute-start.33 = (bf16[1,4,128,128]{3,2,1,0:T(8,128)(2,1)S(1)}, bf16[1,4,128,128]{3,2,1,0:T(8,128)(2,1)S(1)}, u32[]{:S(2)}, u32[]{:S(2)}) collective-permute-start(bf16[1,4,128,128]{3,2,1,0:T(8,128)(2,1)S(1)} %get-tuple-element.20), channel_id=1, source_target_pairs={{0,24},{4,28},{8,16},{12,20},{16,8},{20,12},{24,0},{28,4},{1,25},{... | collective-permute-start | bytes 393224 | tf_op jit(solution)/shard_map/ppermute | solution.py:19
  116.3 8.0 %collective-permute-start.32 = (bf16[1,4,128,128]{3,2,1,0:T(8,128)(2,1)S(1)}, bf16[1,4,128,128]{3,2,1,0:T(8,128)(2,1)S(1)}, u32[]{:S(2)}, u32[]{:S(2)}) collective-permute-start(bf16[1,4,128,128]{3,2,1,0:T(8,128)(2,1)S(1)} %get-tuple-element.21), channel_id=1, source_target_pairs={{0,16},{4,20},{8,24},{12,28},{16,0},{20,4},{24,8},{28,12},{1,17},{... | collective-permute-start | bytes 393224 | tf_op jit(solution)/shard_map/ppermute | solution.py:19
  124.4 5.5 %collective-permute-start.34 = (f32[128,128]{1,0:T(8,128)S(1)}, f32[128,128]{1,0:T(8,128)S(1)}, u32[]{:S(2)}, u32[]{:S(2)}) collective-permute-start(f32[128,128]{1,0:T(8,128)S(1)} %get-tuple-element.22), channel_id=1, source_target_pairs={{0,3},{1,0},{2,1},{3,2},{4,7},{5,4},{6,5},{7,6},{8,11},{9,8},{10,9... | collective-permute-start | bytes 196616 | tf_op jit(solution)/shard_map/ppermute | solution.py:24
  124.4 6.4 %collective-permute-start.36 = (f32[128,128]{1,0:T(8,128)S(1)}, f32[128,128]{1,0:T(8,128)S(1)}, u32[]{:S(2)}, u32[]{:S(2)}) collective-permute-start(f32[128,128]{1,0:T(8,128)S(1)} %get-tuple-element.23), channel_id=1, source_target_pairs={{0,1},{1,2},{2,3},{3,0},{4,5},{5,6},{6,7},{7,4},{8,9},{9,10},{10,1... | collective-permute-start | bytes 196616 | tf_op jit(solution)/shard_map/ppermute | solution.py:24
  126.5 6.0 %collective-permute-start.35 = (f32[128,128]{1,0:T(8,128)S(1)}, f32[128,128]{1,0:T(8,128)S(1)}, u32[]{:S(2)}, u32[]{:S(2)}) collective-permute-start(f32[128,128]{1,0:T(8,128)S(1)} %get-tuple-element.24), channel_id=1, source_target_pairs={{0,2},{1,3},{2,0},{3,1},{4,6},{5,7},{6,4},{7,5},{8,10},{9,11},{10,... | collective-permute-start | bytes 196616 | tf_op jit(solution)/shard_map/ppermute | solution.py:24
  132.5 8.3 %copy-start.4 = (f32[128,128]{1,0:T(8,128)}, f32[128,128]{1,0:T(8,128)S(1)}, u32[]{:S(2)}) copy-start(f32[128,128]{1,0:T(8,128)S(1)} %fusion.5.refs_0_) | copy-start | bytes 196612
  132.5 5.4 %collective-permute-start.42 = (f32[128,128]{1,0:T(8,128)S(1)}, f32[128,128]{1,0:T(8,128)S(1)}, u32[]{:S(2)}, u32[]{:S(2)}) collective-permute-start(f32[128,128]{1,0:T(8,128)S(1)} %fusion.5.refs_0_), channel_id=1, source_target_pairs={{0,24},{4,28},{8,16},{12,20},{16,8},{20,12},{24,0},{28,4},{1,25},{... | collective-permute-start | bytes 196616 | tf_op jit(solution)/shard_map/ppermute | solution.py:19
  134.3 4.3 %collective-permute-start.40 = (f32[128,128]{1,0:T(8,128)S(1)}, f32[128,128]{1,0:T(8,128)S(1)}, u32[]{:S(2)}, u32[]{:S(2)}) collective-permute-start(f32[128,128]{1,0:T(8,128)S(1)} %fusion.5.refs_0_), channel_id=1, source_target_pairs={{0,16},{4,20},{8,24},{12,28},{16,0},{20,4},{24,8},{28,12},{1,17},{... | collective-permute-start | bytes 196616 | tf_op jit(solution)/shard_map/ppermute | solution.py:19
  135.2 4.3 %collective-permute-start.38 = (f32[128,128]{1,0:T(8,128)S(1)}, f32[128,128]{1,0:T(8,128)S(1)}, u32[]{:S(2)}, u32[]{:S(2)}) collective-permute-start(f32[128,128]{1,0:T(8,128)S(1)} %fusion.5.refs_0_), channel_id=1, source_target_pairs={{0,8},{4,12},{8,0},{12,4},{16,24},{20,28},{24,16},{28,20},{1,9},{5... | collective-permute-start | bytes 196616 | tf_op jit(solution)/shard_map/ppermute | solution.py:19
  136.1 3.5 %collective-permute-start.37 = (f32[128,128]{1,0:T(8,128)S(1)}, f32[128,128]{1,0:T(8,128)S(1)}, u32[]{:S(2)}, u32[]{:S(2)}) collective-permute-start(f32[128,128]{1,0:T(8,128)S(1)} %fusion.5.refs_0_), channel_id=1, source_target_pairs={{0,4},{4,0},{8,12},{12,8},{16,20},{20,16},{24,28},{28,24},{1,5},{5... | collective-permute-start | bytes 196616 | tf_op jit(solution)/shard_map/ppermute | solution.py:19
  137.9 1.6 %collective-permute-start.43 = (f32[128,128]{1,0:T(8,128)S(1)}, f32[128,128]{1,0:T(8,128)S(1)}, u32[]{:S(2)}, u32[]{:S(2)}) collective-permute-start(f32[128,128]{1,0:T(8,128)S(1)} %collective-permute-done.42.refs_6_), channel_id=1, source_target_pairs={{0,4},{4,0},{8,12},{12,8},{16,20},{20,16},{24,28},{28,24},{1,5},{5... | collective-permute-start | bytes 196616 | tf_op jit(solution)/shard_map/ppermute | solution.py:19
  138.6 1.3 collective-permute-start.41
  139.5 1.3 collective-permute-start.39
  (13 other events, 14.8 us)

commit v2 on v1

--- a/solution.py
+++ b/solution.py
@@ -11,6 +11,9 @@
 F32, BF16 = jnp.float32, jnp.bfloat16
 LOW = 32
 UNROLL = 8
+HOT = 4
+CHUNK = 256
+ID_BITS = 10
 VMEM_LIMIT = 48 * 1024 * 1024
 
 
@@ -49,32 +52,43 @@
     return pl.BlockSpec(memory_space=space)
 
 
-def pool_kernel(shards, replicas, scal, dest, *refs):
-    ids, (own, *pieces), (out, table, pooled) = refs[:shards], refs[shards:-3], refs[-3:]
-    hot = ids[0].shape[0]
+def pool_kernel(shards, scal, first, second, *refs):
+    (own, *pieces), (out, table, pooled) = refs[:-3], refs[-3:]
+    rows_dev = own.shape[0]
     block = pieces[0].shape[1]
     mine = scal[2 * shards]
-    table[0] = own[...]
+    table[:rows_dev, :] = own[...]
     for m, piece in enumerate(pieces):
-        rows = pl.ds(pl.multiple_of((mine ^ m) * block, block), block)
         for k in range(1, shards):
-            table[k, rows, :] = piece[k - 1].astype(F32)
-    for k in range(shards):
-        start, live = scal[k], scal[shards + k]
-
-        def one(c, k=k, start=start):
-            total = table[k, pl.ds(ids[k][0, c], 1), :]
-            for h in range(1, hot):
-                total = total + table[k, pl.ds(ids[k][h, c], 1), :]
-            pooled[pl.ds(dest[start + c], 1), :] = total
-
-        def group(i, _, one=one):
-            for u in range(UNROLL):
-                one(i * UNROLL + u)
+            rows = pl.ds(pl.multiple_of((mine ^ m) * block + k * rows_dev, block), block)
+            table[rows, :] = piece[k - 1]
+    field = (1 << ID_BITS) - 1
+    for j in range(shards):
+        start, live = scal[j], scal[shards + j]
+        base = j * rows_dev
+
+        def several(k0, count, base=base):
+            sums, places = [], []
+            for u in range(count):
+                one, two = first[k0 + u], second[k0 + u]
+                spots = (
+                    one & field,
+                    lax.shift_right_logical(one, ID_BITS) & field,
+                    two & field,
+                    lax.shift_right_logical(two, ID_BITS),
+                )
+                read = [table[pl.ds(spot + base, 1), :] for spot in spots]
+                sums.append((read[0] + read[1]) + (read[2] + read[3]))
+                places.append(lax.shift_right_logical(one, 2 * ID_BITS))
+            for total, place in zip(sums, places):
+                pooled[pl.ds(place, 1), :] = total
+
+        def group(i, _, start=start, several=several):
+            several(start + i * UNROLL, UNROLL)
             return 0
 
-        def single(c, _, one=one):
-            one(c)
+        def single(i, _, start=start, several=several):
+            several(start + i, 1)
             return 0
 
         full = live // UNROLL
@@ -83,20 +97,71 @@
     out[...] = pooled[...].astype(BF16)
 
 
-def pool(scal, dest, ids, own, pieces, bags):
-    shards, replicas = len(ids), len(pieces)
+def pool(scal, first, second, own, pieces, bags):
     rows, width = own.shape
+    shards = pieces[0].shape[0] + 1
     smem = whole(pltpu.SMEM)
     return pl.pallas_call(
-        functools.partial(pool_kernel, shards, replicas),
+        functools.partial(pool_kernel, shards),
         out_shape=jax.ShapeDtypeStruct((bags, width), BF16),
-        in_specs=[smem, smem] + [smem] * shards + [whole()] * (1 + replicas),
+        in_specs=[smem, smem, smem] + [whole()] * (1 + len(pieces)),
         out_specs=whole(),
-        scratch_shapes=[pltpu.VMEM((shards, rows, width), F32), pltpu.VMEM((bags, width), F32)],
+        scratch_shapes=[pltpu.VMEM((shards * rows, width), F32), pltpu.VMEM((bags, width), F32)],
         compiler_params=pltpu.CompilerParams(vmem_limit_bytes=VMEM_LIMIT),
         cost_estimate=pl.CostEstimate(flops=10**6, bytes_accessed=30 * 10**6, transcendentals=0),
         name="pool",
-    )(scal, dest, *ids, own, *pieces)
+    )(scal, first, second, own, *pieces)
+
+
+def pair_range(scal, shards, j):
+    start, live = scal[j], scal[shards + j]
+    source = lax.rem(scal[2 * shards + 1] - j + shards, shards)
+    return start, live, source, start // CHUNK, (start + live + CHUNK - 1) // CHUNK
+
+
+def count_kernel(shards, replicas, scal, words, out):
+    rows = out.shape[1]
+    block = rows // replicas
+    flip = scal[2 * shards] * block
+    low = lax.broadcasted_iota(jnp.int32, (LOW, CHUNK), 0)
+    field = (1 << ID_BITS) - 1
+    for j in range(shards):
+        start, live, source, begin, end = pair_range(scal, shards, j)
+
+        def pair(q, _, start=start, live=live, source=source):
+            at = pl.ds(pl.multiple_of(q * CHUNK, CHUNK), CHUNK)
+            place = q * CHUNK + lax.broadcasted_iota(jnp.int32, (1, CHUNK), 1) - start
+            inside = (place >= 0) & (place < live)
+            lows, highs = [], []
+            for h in range(HOT):
+                word = words[h // 2 : h // 2 + 1, at]
+                row = (lax.shift_right_logical(word, (h % 2) * ID_BITS) & field) ^ flip
+                row = jnp.where(inside, row, -1)
+                highs.append(lax.shift_right_arithmetic(row, LOW.bit_length() - 1))
+                lows.append((low == (row & (LOW - 1))).astype(F32).astype(BF16))
+            for b in range(rows // LOW):
+                count = None
+                for h in range(HOT):
+                    hit = (highs[h] == b).astype(F32).astype(BF16)
+                    term = lows[h] * hit
+                    count = term if count is None else count + term
+                out[q + source, b * LOW : (b + 1) * LOW, :] = count
+            return 0
+
+        lax.fori_loop(begin, end, pair, 0)
+
+
+def count_rows(scal, words, shards, replicas, rows):
+    pairs = words.shape[1] // CHUNK + shards - 1
+    return pl.pallas_call(
+        functools.partial(count_kernel, shards, replicas),
+        out_shape=jax.ShapeDtypeStruct((pairs, rows, CHUNK), BF16),
+        in_specs=[whole(pltpu.SMEM), whole()],
+        out_specs=whole(),
+        compiler_params=pltpu.CompilerParams(vmem_limit_bytes=VMEM_LIMIT),
+        cost_estimate=pl.CostEstimate(flops=10**6, bytes_accessed=10 * 10**6, transcendentals=0),
+        name="count_rows",
+    )(scal, words)
 
 
 def column_of(row, size):
@@ -115,22 +180,21 @@
     )
 
 
-def dense_kernel(shards, replicas, spots, chunk, scal, dest, *refs):
-    ids = refs[:shards]
-    dense, rows_in, bias, head, labels = refs[shards : shards + 5]
-    weights = refs[shards + 5 : shards + 5 + len(spots)]
-    logits, even, odd = refs[shards + 5 + len(spots) : shards + 8 + len(spots)]
-    full_in, full_out, cross, scaled, grads, slots, counts, total = refs[shards + 8 + len(spots) :]
-    factor = (full_in, full_out)
+def dense_kernel(shards, replicas, spots, scal, places, *refs):
+    dense, rows_in, bias, head, labels, counted = refs[:6]
+    weights = refs[6 : 6 + len(spots)]
+    logits, even, odd = refs[6 + len(spots) : 9 + len(spots)]
+    full_in, full_out, cross, scaled, grads, slots, narrow, counts, total, done = refs[9 + len(spots) :]
     batch, width = dense.shape
     features = full_in.shape[0]
-    hot, capacity = ids[0].shape
+    bags = grads.shape[0]
     table_rows = total.shape[0]
-    mine = scal[2 * shards]
     across = (((1,), (1,)), ((), ()))
 
-    for ref, placing in zip(weights, spots):
-        placing(ref, factor, scal)
+    fetch = pltpu.make_async_copy(counted, counts, done)
+    fetch.start()
+    for ref, spot in zip(weights, spots):
+        spot.copy(ref, (full_in, full_out)[spot.which], scal)
 
     cross[:, :width] = dense[...]
     for f in range(1, features // width):
@@ -162,94 +226,76 @@
         at = slice(f * batch, (f + 1) * batch)
         grads[at, :] = (grads[at, :] * lean).astype(BF16).astype(F32)
 
-    slots[...] = jnp.zeros_like(slots)
-    low = lax.broadcasted_iota(jnp.int32, (LOW, chunk), 0)
+    middle = bags // 2
+
+    def group(i, _):
+        for u in range(UNROLL):
+            k = i * UNROLL + u
+            word = places[k]
+            slots[pl.ds(k, 1), :] = grads[pl.ds(word & 0xFFFF, 1), :]
+            slots[pl.ds(k + middle, 1), :] = grads[pl.ds(lax.shift_right_logical(word, 16), 1), :]
+        return 0
+
+    lax.fori_loop(0, middle // UNROLL, group, 0)
+    narrow[...] = slots[...].astype(BF16)
+    fetch.wait()
     block = table_rows // replicas
-    for k in range(shards):
-        start, live = scal[k], scal[shards + k]
-
-        def group(i, _, start=start):
-            for u in range(UNROLL):
-                c = i * UNROLL + u
-                slots[pl.ds(c, 1), :] = grads[pl.ds(dest[start + c], 1), :]
-            return 0
-
-        lax.fori_loop(0, (live + UNROLL - 1) // UNROLL, group, 0)
+    for j in range(shards):
+        start, live, source, begin, end = pair_range(scal, shards, j)
         total[...] = jnp.zeros_like(total)
 
-        def piece(q, _, k=k, live=live):
-            at = pl.ds(pl.multiple_of(q * chunk, chunk), chunk)
-            place = q * chunk + lax.broadcasted_iota(jnp.int32, (1, chunk), 1)
-            lows, highs = [], []
-            for h in range(hot):
-                row = ids[k][h : h + 1, at] ^ (mine * block)
-                row = jnp.where(place < live, row, -1)
-                high = lax.shift_right_arithmetic(row, LOW.bit_length() - 1)
-                lows.append((low == (row & (LOW - 1))).astype(F32).astype(BF16))
-                highs.append(high)
-            for b in range(table_rows // LOW):
-                count = None
-                for h in range(hot):
-                    hit = (highs[h] == b).astype(F32).astype(BF16)
-                    term = lows[h] * hit
-                    count = term if count is None else count + term
-                counts[b * LOW : (b + 1) * LOW, :] = count
+        def pair(q, _, source=source):
+            at = pl.ds(pl.multiple_of(q * CHUNK, CHUNK), CHUNK)
             total[...] += jnp.dot(
-                counts[...], slots[at, :].astype(BF16), preferred_element_type=F32
+                counts[q + source], narrow[at, :], preferred_element_type=F32
             )
             return 0
 
-        lax.fori_loop(0, (live + chunk - 1) // chunk, piece, 0)
+        lax.fori_loop(begin, end, pair, 0)
         for m in range(replicas):
             half = even if m % 2 == 0 else odd
-            half[m // 2, k] = total[m * block : (m + 1) * block, :].astype(BF16)
-
-
-def dense_step(scal, dest, ids, dense, rows_in, bias, head, labels, weights, spots, replicas, rows):
-    shards = len(ids)
+            half[m // 2, j] = total[m * block : (m + 1) * block, :].astype(BF16)
+
+
+def dense_step(scal, places, dense, rows_in, bias, head, labels, counted, weights, spots, shards, replicas):
     batch, width = dense.shape
     features = bias.shape[1]
-    rank = sum_columns(weights, spots)
-    capacity = ids[0].shape[1]
-    chunk = 256 if capacity % 256 == 0 else 128
+    bags = rows_in.shape[0]
+    rows = counted.shape[1]
+    rank = spots[0].rank
     half = jax.ShapeDtypeStruct((replicas // 2, shards, rows // replicas, width), BF16)
     smem = whole(pltpu.SMEM)
     return pl.pallas_call(
-        functools.partial(dense_kernel, shards, replicas, spots, chunk),
+        functools.partial(dense_kernel, shards, replicas, spots),
         out_shape=(jax.ShapeDtypeStruct((1, batch), F32), half, half),
-        in_specs=[smem, smem] + [whole()] * (shards + 5 + len(weights)),
+        in_specs=[smem, smem] + [whole()] * 5 + [whole(pl.ANY)] + [whole()] * len(weights),
         out_specs=(whole(), whole(), whole()),
         scratch_shapes=[
             pltpu.VMEM((features, rank), BF16),
             pltpu.VMEM((features, rank), BF16),
             pltpu.VMEM((batch, features), BF16),
             pltpu.VMEM((batch, features), BF16),
-            pltpu.VMEM((features // width * batch - batch, width), F32),
-            pltpu.VMEM((capacity, width), F32),
-            pltpu.VMEM((rows, chunk), BF16),
+            pltpu.VMEM((bags, width), F32),
+            pltpu.VMEM((bags, width), F32),
+            pltpu.VMEM((bags, width), BF16),
+            pltpu.VMEM(counted.shape, BF16),
             pltpu.VMEM((rows, width), F32),
+            pltpu.SemaphoreType.DMA(()),
         ],
         compiler_params=pltpu.CompilerParams(vmem_limit_bytes=VMEM_LIMIT),
         cost_estimate=pl.CostEstimate(
             flops=4 * 10**9, bytes_accessed=30 * 10**6, transcendentals=0
         ),
         name="dense",
-    )(scal, dest, *ids, dense, rows_in, bias, head, labels, *weights)
-
-
-def sum_columns(weights, spots):
-    return max(spot.rank for spot in spots)
+    )(scal, places, dense, rows_in, bias, head, labels, counted, *weights)
 
 
 class Spot:
     def __init__(self, which, rank, copy):
         self.which, self.rank, self.copy = which, rank, copy
 
-    def __call__(self, ref, factor, scal):
-        self.copy(ref, factor[self.which], scal)
-
-
-def gather_weights(cross_in, cross_out):
+
+def gather_weights(cross_in, cross_out, after):
     shards, replicas = lax.axis_size("table"), lax.axis_size("replica")
     shard_rows, rank = cross_in.shape
     mine = lax.axis_index("replica")
@@ -260,16 +306,17 @@
         def whole_copy(ref, full, scal):
             full[...] = ref[...]
 
-        return both, [Spot(i, rank, whole_copy) for i in range(2)]
+        return both, [Spot(i, rank, whole_copy) for i in range(2)], after
 
     start = ((mine & 1) * half, (mine >> 1) * lanes)
-    piece = jnp.stack([lax.dynamic_slice(w, start, (half, lanes)) for w in (cross_in, cross_out)])
-    far = [shift(piece, k) for k in range(1, shards)]
-    top = jnp.stack([f[0] for f in far])
-    bottom = jnp.stack([f[1] for f in far])
+    top, bottom = (
+        jnp.stack([shift(lax.dynamic_slice(w, start, (half, lanes)), k) for k in range(1, shards)])
+        for w in (cross_in, cross_out)
+    )
     tops, bottoms = {0: top}, {0: bottom}
     tops[2], bottoms[2], tops[4], bottoms[4] = swap(top, 2), swap(bottom, 2), swap(top, 4), swap(bottom, 4)
-    tops[6], bottoms[6] = swap(tops[2], 4), swap(bottoms[4], 2)
+    (near_top, near_bottom), after = lax.optimization_barrier(((tops[2], bottoms[4]), after))
+    tops[6], bottoms[6] = swap(near_top, 4), swap(near_bottom, 2)
     arrays, spots = [], []
     for which, held in enumerate((tops, bottoms)):
         for m in (0, 2, 4, 6):
@@ -296,7 +343,7 @@
 
         arrays.append(own_rows)
         spots.append(Spot(which, rank, copy_own))
-    return arrays, spots
+    return arrays, spots, after
 
 
 def reduce_rows(even, odd):
@@ -339,6 +386,7 @@
         ),
         in_specs=[whole(pltpu.SMEM)] + [whole()] * (1 + replicas),
         out_specs=(whole(), whole()),
+        compiler_params=pltpu.CompilerParams(vmem_limit_bytes=VMEM_LIMIT),
         name="finish",
     )(mine, accum, *pieces)
 
@@ -363,42 +411,56 @@
     bags = bag_order.shape[2]
     per_sample = bags // batch
     capacity = look_rows.shape[4]
-    padded = -(-capacity // 128) * 128
-
-    sent = jnp.pad(look_rows[0, 0], ((0, 0), (0, 0), (0, padded - capacity)))
-    around = [lax.rem(here + k, shards) for k in range(shards)]
-    ids = [lax.dynamic_index_in_dim(sent, around[k], 0, keepdims=False) for k in range(shards)]
-    ids = [ids[0]] + [shift(ids[k], k) for k in range(1, shards)]
-
+    padded = -(-capacity // width) * width
     block = rows // replicas
-    piece = lax.dynamic_slice_in_dim(emb_table, mine * block, block, 0).astype(BF16)
-    near = jnp.stack([shift(piece, k) for k in range(1, shards)])
-    pieces = replica_gather(near)
-
-    weights, spots = gather_weights(cross_in, cross_out)
 
     live = lax.dynamic_index_in_dim(live_counts[0], here, 0, keepdims=False)
     starts = jnp.cumsum(live) - live
-    back = lax.rem(here - jnp.arange(shards, dtype=jnp.int32) + shards, shards)
-    scal = jnp.concatenate([starts[back], live[back], jnp.stack([mine, here])]).astype(jnp.int32)
+    back = [lax.rem(here - k + shards, shards) for k in range(shards)]
+    starts = [lax.dynamic_index_in_dim(starts, b, 0, keepdims=False) for b in back]
+    lives = [lax.dynamic_index_in_dim(live, b, 0, keepdims=False) for b in back]
+    scal = jnp.stack(starts + lives + [mine, here]).astype(jnp.int32)
     order = bag_order[0, 0]
     dest = (order % per_sample) * batch + order // per_sample
-    dest = jnp.pad(dest, (0, 128))
-
-    rows_in = pool(scal, dest, ids, emb_table, pieces, bags)
+    places = dest[: bags // 2] | (dest[bags // 2 :] << 16)
+
+    piece = lax.dynamic_slice_in_dim(emb_table, mine * block, block, 0)
+    sent = jnp.pad(look_rows[0, 0], ((0, 0), (0, 0), (0, padded - capacity))).astype(F32)
+    sent = sent.reshape(shards, -1, width)
+    parcels = []
+    for k in range(shards):
+        to = lax.rem(here + k, shards)
+        parcel = jnp.concatenate([piece, lax.dynamic_index_in_dim(sent, to, 0, keepdims=False)])
+        parcels.append(parcel if k == 0 else shift(parcel, k))
+
+    slot = jnp.arange(bags, dtype=jnp.int32)
+    words = jnp.zeros((2, bags), jnp.int32)
+    for k in range(shards):
+        ids = parcels[k][block:].reshape(HOT, padded).astype(jnp.int32)
+        word = ids[0::2] | (ids[1::2] << ID_BITS)
+        word = jnp.pad(word, ((0, 0), (bags, bags)))
+        moved = lax.dynamic_slice_in_dim(word, bags - starts[k], bags, 1)
+        words = jnp.where((slot >= starts[k]) & (slot < starts[k] + lives[k]), moved, words)
+    counted = count_rows(scal, words, shards, replicas, rows)
+
+    near = jnp.stack([parcels[k][:block] for k in range(1, shards)])
+    pieces = replica_gather(near)
+    scal, counted = lax.optimization_barrier((scal, counted))
+    rows_in = pool(scal, words[0] | (dest << (2 * ID_BITS)), words[1], emb_table, pieces, bags)
+    weights, spots, rows_in = gather_weights(cross_in, cross_out, rows_in)
     logits, even, odd = dense_step(
         scal,
-        dest,
-        ids,
+        places,
         dense_emb,
         rows_in,
         cross_bias.reshape(1, -1),
         head_weight.reshape(1, -1),
         labels.reshape(1, -1),
+        counted,
         weights,
         spots,
+        shards,
         replicas,
-        rows,
     )
     grad = reduce_rows(even, odd)
     update, accum = finish(

time: 144 us -> 153 us (1.062)
  starting transfers between devices: 46.1 us -> 34.5 us
  between operations: 0.97 us -> 11.2 us
  other arithmetic: 0.83 us -> 6.7 us
  local copies, waits for them, and re-layouts: 7.51 us -> 12.1 us
  Pallas kernels: 45.6 us -> 43.5 us
    ppermute x12, starting transfers between devices: 27.6 us -> 15.2 us  [shift(): lax.ppermute(array, 'table', [(i, (i + step) % size) for i in range(size)])]
    ppermute x12, waiting for transfers between devices: 9.46 us -> 20.6 us  [shift(): lax.ppermute(array, 'table', [(i, (i + step) % size) for i in range(size)])]
    ppermute x32, waiting for transfers between devices: 33.5 us -> 23.8 us  [swap(): return lax.ppermute(array, 'replica', [(i, i ^ mask) for i in range(size)])]
    dynamic_slice x0 -> x5, local copies, waits for them, and re-layouts: none -> 4.87 us  [the longest x2 1.86 us: gather_weights(): lax.dynamic_slice(w, start, (half, lanes))]
    another operation x2 -> x5, local copies, waits for them, and re-layouts: 0.97 us -> 5.82 us  [the longest x1 5.11 us: local(): scal = jnp.stack(starts + lives + [mine, here]).astype(jnp.int32)]
    unnamed x34 -> x14, local copies, waits for them, and re-layouts: 4.28 us -> 0.93 us
    and x0 -> x2, other arithmetic: none -> 2.58 us  [local(): (slot >= starts[k]) & (slot < starts[k] + lives[k])]
    pallas_call x2 -> x3, Pallas kernels: 43.1 us -> 42.1 us  [the longest x1 16.6 us: pool(): pl.pallas_call(functools.partial(pool_kernel, shards), out_shape=jax.Shap...]
  transfers between devices with their start and end apart: 44 -> 44, of which waited for: 22 -> 21; matrix products, arithmetic and copies ran while one was open for 2% -> 11% of each run, Pallas kernels for 16% -> 17%
where the time goes in v2:
time: 153 us; the launch traced here: 152 us
  waiting for transfers between devices  44.4 us (29%)
  Pallas kernels  43.5 us (28%)
  starting transfers between devices  34.5 us (23%)
  local copies, waits for them, and re-layouts  12.1 us (8%)
  between operations  11.2 us (7%)
  other arithmetic  6.7 us (4%)
    ppermute x32, waiting for transfers between devices, swap(): return lax.ppermute(array, 'replica', [(i, i ^ mask) for i in range(size)])  23.8 us
    ppermute x12, waiting for transfers between devices, shift(): lax.ppermute(array, 'table', [(i, (i + step) % size) for i in range(size)])  20.6 us
    ppermute x32, starting transfers between devices, swap(): return lax.ppermute(array, 'replica', [(i, i ^ mask) for i in range(size)])  19.3 us
    pallas_call x1, Pallas kernels, pool(): pl.pallas_call(functools.partial(pool_kernel, shards), out_shape=jax.Shap...  16.6 us
    pallas_call x1, Pallas kernels, dense_step(): pl.pallas_call(functools.partial(dense_kernel, shards, replicas, spots),...  16.3 us
    ppermute x12, starting transfers between devices, shift(): lax.ppermute(array, 'table', [(i, (i + step) % size) for i in range(size)])  15.2 us
    pallas_call x1, Pallas kernels, count_rows(): pl.pallas_call(functools.partial(count_kernel, shards, replicas), out_sha...  9.13 us
    another operation x1, local copies, waits for them, and re-layouts, local(): scal = jnp.stack(starts + lives + [mine, here]).astype(jnp.int32)  5.11 us
  transfers between devices with their start and end apart: 44, of which 21 were waited for; matrix products, arithmetic and copies ran while one was open for 11% of the time, Pallas kernels for 17%

profile of v2, /device:TPU:0, one launch (start us, length us, event | category | flops | bytes accessed | tf_op | source)
XLA Modules:
  0.0 152.3 jit_solution(4520121251652334055)
XLA Ops:
  0.7 1.0 dynamic_slice.98
  1.7 5.0 %collective-permute-start.9 = (bf16[432,128]{1,0:T(8,128)(2,1)S(1)}, bf16[432,128]{1,0:T(8,128)(2,1)S(1)}, u32[]{:S(2)}, u32[]{:S(2)}) collective-permute-start(bf16[432,128]{1,0:T(8,128)(2,1)S(1)} %dynamic_slice.98), channel_id=1, source_target_pairs={{0,3},{1,0},{2,1},{3,2},{4,7},{5,4},{6,5},{7,6},{8,11},{9,8},{10,9... | collective-permute-start | bytes 331784 | tf_op jit(solution)/shard_map/ppermute | solution.py:27
  6.7 0.9 dynamic_slice.97
  8.1 2.5 %collective-permute-start.4 = (bf16[432,128]{1,0:T(8,128)(2,1)S(1)}, bf16[432,128]{1,0:T(8,128)(2,1)S(1)}, u32[]{:S(2)}, u32[]{:S(2)}) collective-permute-start(bf16[432,128]{1,0:T(8,128)(2,1)S(1)} %dynamic_slice.97), channel_id=1, source_target_pairs={{0,2},{1,3},{2,0},{3,1},{4,6},{5,7},{6,4},{7,5},{8,10},{9,11},{10,... | collective-permute-start | bytes 331784 | tf_op jit(solution)/shard_map/ppermute | solution.py:27
  10.6 0.9 pad_convert_fusion
  11.6 0.9 constant_dynamic-slice_fusion
  12.5 2.0 %collective-permute-start.2 = (f32[168,128]{1,0:T(8,128)S(1)}, f32[168,128]{1,0:T(8,128)S(1)}, u32[]{:S(2)}, u32[]{:S(2)}) collective-permute-start(f32[168,128]{1,0:T(8,128)S(1)} %get-tuple-element.41), channel_id=1, source_target_pairs={{0,1},{1,2},{2,3},{3,0},{4,5},{5,6},{6,7},{7,4},{8,9},{9,10},{10,1... | collective-permute-start | bytes 258056 | tf_op jit(solution)/shard_map/ppermute | solution.py:27
  14.5 0.7 fusion.17
  15.3 0.7 bitcast_subtract_fusion
  16.0 0.7 fusion.20
  21.8 0.8 compare_reduce_fusion
  22.6 0.8 divide_reduce_fusion
  23.5 1.5 constant_dynamic-slice_fusion.1
  30.0 1.3 fusion.12
  31.4 5.1 %stack.56.scal = s32[10]{0:T(128)S(1)} concatenate(s32[1]{0:T(128)} %get-tuple-element.51, s32[1]{0:T(128)} %get-tuple-element.50, s32[1]{0:T(128)} %get-tuple-element.49, s32[1]{0:T(128)} %get-tuple-element.48, s32[1]{0:T(128)} %bitcast.3, s32[1]{0:T(128)} %bitcast.4, s32[1]{0:T(128)} %bitcast.5, s32[1]{0:T(128)} %bitcast.6, s32[1]{0:T(128)} %bitcast.7.scal, s32[1]{0:T(128)} %bitcast.8), dimensions={0} | concatenate | bytes 80 | tf_op jit(solution)/shard_map/stack | solution.py:422
  36.5 1.3 fusion.14
  37.9 6.5 %collective-permute-done.1 = f32[168,128]{1,0:T(8,128)S(1)} collective-permute-done((f32[168,128]{1,0:T(8,128)S(1)}, f32[168,128]{1,0:T(8,128)S(1)}, u32[]{:S(2)}, u32[]{:S(2)}) %collective-permute-start.1) | collective-permute-done | bytes 86048 | tf_op jit(solution)/shard_map/ppermute | solution.py:27
  44.3 0.8 collective-permute-start
  45.2 3.6 %collective-permute-done = f32[168,128]{1,0:T(8,128)S(1)} collective-permute-done((f32[168,128]{1,0:T(8,128)S(1)}, f32[168,128]{1,0:T(8,128)S(1)}, u32[]{:S(2)}, u32[]{:S(2)}) %collective-permute-start) | collective-permute-done | bytes 86048 | tf_op jit(solution)/shard_map/ppermute | solution.py:27
  49.0 2.5 %collective-permute-start.16 = (f32[3,128,128]{2,1,0:T(8,128)S(1)}, f32[3,128,128]{2,1,0:T(8,128)S(1)}, u32[]{:S(2)}, u32[]{:S(2)}) collective-permute-start(f32[3,128,128]{2,1,0:T(8,128)S(1)} %pad_maximum_fusion.2.refs_1_), channel_id=1, source_target_pairs={{0,24},{4,28},{8,16},{12,20},{16,8},{20,12},{24,0},{28,4},{1,25},{... | collective-permute-start | bytes 589832 | tf_op jit(solution)/shard_map/ppermute | solution.py:22
  52.3 9.1 %count_rows.1.refs_5_ = bf16[16,1024,256]{2,1,0:T(8,128)(2,1)} custom-call(s32[10]{0:T(128)S(1)} %stack.56.scal, s32[2,3328]{1,0:T(2,128)S(1)} %fusion.6.words), custom_call_target="tpu_custom_call" | custom-call | flops 1000000 | bytes 10000000 | tf_op jit(solution)/shard_map/count_rows/pallas_call | solution.py:156
  62.7 5.3 %collective-permute-done.7 = bf16[432,128]{1,0:T(8,128)(2,1)S(1)} collective-permute-done((bf16[432,128]{1,0:T(8,128)(2,1)S(1)}, bf16[432,128]{1,0:T(8,128)(2,1)S(1)}, u32[]{:S(2)}, u32[]{:S(2)}) %collective-permute-start.7) | collective-permute-done | bytes 110624 | tf_op jit(solution)/shard_map/ppermute | solution.py:27
  68.0 1.5 collective-permute-start.20
  71.4 1.4 collective-permute-done.13.refs_4_
  72.8 1.5 collective-permute-start.25
  74.3 16.6 %pool.1.refs_1_ = bf16[3328,128]{1,0:T(8,128)(2,1)S(1)} custom-call(s32[10]{0:T(128)S(1)} %stack.56.scal, s32[3328]{0:T(1024)S(1)} %get-tuple-element.27.first, s32[3328]{0:T(1024)S(1)} %get-tuple-element.23.second, f32[1024,128]{1,0:T(8,128)S(1)} %copy-done.1, f32[3,128,128]{2,1,0:T(8,128)S(1)} %pad_maximum_fusion.2.refs_1_, ...), custom_call_target="tpu_custom_call" | custom-call | flops 1000000 | bytes 30000000 | tf_op jit(solution)/shard_map/pool/pallas_call | solution.py:104
  90.9 0.9 copy-done
  92.4 1.5 collective-permute-start.22
  95.0 7.1 %collective-permute-done.22.refs_12_ = bf16[3,432,128]{2,1,0:T(8,128)(2,1)S(1)} collective-permute-done((bf16[3,432,128]{2,1,0:T(8,128)(2,1)S(1)}, bf16[3,432,128]{2,1,0:T(8,128)(2,1)S(1)}, u32[]{:S(2)}, u32[]{:S(2)}) %collective-permute-start.22) | collective-permute-done | bytes 331808 | tf_op jit(solution)/shard_map/ppermute | solution.py:22
  102.1 1.2 collective-permute-done.28.refs_20_
  103.8 1.2 collective-permute-done.29.refs_21_
  105.0 16.3 %dense.1 = (f32[1,128]{1,0:T(1,128)}, bf16[4,4,128,128]{3,2,1,0:T(8,128)(2,1)S(1)}, bf16[4,4,128,128]{3,2,1,0:T(8,128)(2,1)}) custom-call(s32[10]{0:T(128)S(1)} %stack.56.scal, s32[1664]{0:T(1024)S(1)} %fusion.16.places, bf16[128,128]{1,0:T(8,128)(2,1)S(1)} %copy-done.2, bf16[3328,128]{1,0:T(8,128)(2,1)} %copy-done, f32[1,3456]{1,0:T(1,128)S(1)} %reshape.133.refs_2_, ...), custom_call_target="tpu_custom_call" | custom-call | flops 4000000000 | bytes 30000000 | tf_op jit(solution)/shard_map/dense/pallas_call | solution.py:268
  121.5 2.0 %collective-permute-done.30 = bf16[4,4,128,128]{3,2,1,0:T(8,128)(2,1)S(1)} collective-permute-done((bf16[4,4,128,128]{3,2,1,0:T(8,128)(2,1)}, bf16[4,4,128,128]{3,2,1,0:T(8,128)(2,1)S(1)}, u32[]{:S(2)}, u32[]{:S(2)}) %collective-permute-start.30) | collective-permute-done | bytes 524320 | tf_op jit(solution)/shard_map/ppermute | solution.py:22
  124.1 1.9 %collective-permute-start.33 = (bf16[1,4,128,128]{3,2,1,0:T(8,128)(2,1)S(1)}, bf16[1,4,128,128]{3,2,1,0:T(8,128)(2,1)S(1)}, u32[]{:S(2)}, u32[]{:S(2)}) collective-permute-start(bf16[1,4,128,128]{3,2,1,0:T(8,128)(2,1)S(1)} %get-tuple-element.32), channel_id=1, source_target_pairs={{0,24},{4,28},{8,16},{12,20},{16,8},{20,12},{24,0},{28,4},{1,25},{... | collective-permute-start | bytes 393224 | tf_op jit(solution)/shard_map/ppermute | solution.py:22
  126.0 1.3 collective-permute-start.32
  127.3 2.9 %collective-permute-done.31 = bf16[1,4,128,128]{3,2,1,0:T(8,128)(2,1)S(1)} collective-permute-done((bf16[1,4,128,128]{3,2,1,0:T(8,128)(2,1)S(1)}, bf16[1,4,128,128]{3,2,1,0:T(8,128)(2,1)S(1)}, u32[]{:S(2)}, u32[]{:S(2)}) %collective-permute-start.31) | collective-permute-done | bytes 131104 | tf_op jit(solution)/shard_map/ppermute | solution.py:22
  130.2 2.3 %collective-permute-done.33 = bf16[1,4,128,128]{3,2,1,0:T(8,128)(2,1)S(1)} collective-permute-done((bf16[1,4,128,128]{3,2,1,0:T(8,128)(2,1)S(1)}, bf16[1,4,128,128]{3,2,1,0:T(8,128)(2,1)S(1)}, u32[]{:S(2)}, u32[]{:S(2)}) %collective-permute-start.33) | collective-permute-done | bytes 131104 | tf_op jit(solution)/shard_map/ppermute | solution.py:22
  132.5 1.4 collective-permute-done.32
  133.9 2.0 %collective-permute-start.34 = (f32[128,128]{1,0:T(8,128)S(1)}, f32[128,128]{1,0:T(8,128)S(1)}, u32[]{:S(2)}, u32[]{:S(2)}) collective-permute-start(f32[128,128]{1,0:T(8,128)S(1)} %get-tuple-element.34), channel_id=1, source_target_pairs={{0,3},{1,0},{2,1},{3,2},{4,7},{5,4},{6,5},{7,6},{8,11},{9,8},{10,9... | collective-permute-start | bytes 196616 | tf_op jit(solution)/shard_map/ppermute | solution.py:27
  136.0 2.1 %collective-permute-start.35 = (f32[128,128]{1,0:T(8,128)S(1)}, f32[128,128]{1,0:T(8,128)S(1)}, u32[]{:S(2)}, u32[]{:S(2)}) collective-permute-start(f32[128,128]{1,0:T(8,128)S(1)} %get-tuple-element.36), channel_id=1, source_target_pairs={{0,2},{1,3},{2,0},{3,1},{4,6},{5,7},{6,4},{7,5},{8,10},{9,11},{10,... | collective-permute-start | bytes 196616 | tf_op jit(solution)/shard_map/ppermute | solution.py:27
  138.2 3.8 %collective-permute-done.36 = f32[128,128]{1,0:T(8,128)S(1)} collective-permute-done((f32[128,128]{1,0:T(8,128)S(1)}, f32[128,128]{1,0:T(8,128)S(1)}, u32[]{:S(2)}, u32[]{:S(2)}) %collective-permute-start.36) | collective-permute-done | bytes 65568 | tf_op jit(solution)/shard_map/ppermute | solution.py:27
  142.0 1.2 collective-permute-done.35
  143.3 1.1 collective-permute-start.42
  144.4 1.0 collective-permute-start.40
  145.4 1.5 collective-permute-start.38
  146.8 1.7 %collective-permute-done.42.refs_6_ = f32[128,128]{1,0:T(8,128)S(1)} collective-permute-done((f32[128,128]{1,0:T(8,128)S(1)}, f32[128,128]{1,0:T(8,128)S(1)}, u32[]{:S(2)}, u32[]{:S(2)}) %collective-permute-start.42) | collective-permute-done | bytes 65568 | tf_op jit(solution)/shard_map/ppermute | solution.py:22
  149.8 0.6 collective-permute-done.41.refs_5_
  150.9 1.4 finish.1
  (109 shorter events, 9.8 us)
Async XLA Ops:
  0.6 102.7 %copy-start.5 = (f32[3456]{0:T(1024)S(1)}, f32[3456]{0:T(1024)}, u32[]{:S(2)}) copy-start(f32[3456]{0:T(1024)} %param.20) | copy-start | bytes 41476
  0.7 102.7 %copy-start.6 = (f32[3456]{0:T(1024)S(1)}, f32[3456]{0:T(1024)}, u32[]{:S(2)}) copy-start(f32[3456]{0:T(1024)} %param.21) | copy-start | bytes 41476
  0.7 104.3 %copy-start.4 = (s32[128]{0:T(128)S(1)}, s32[128]{0:T(128)}, u32[]{:S(2)}) copy-start(s32[128]{0:T(128)} %param.17) | copy-start | bytes 1540
  0.7 104.3 %copy-start.2 = (bf16[128,128]{1,0:T(8,128)(2,1)S(1)}, bf16[128,128]{1,0:T(8,128)(2,1)}, u32[]{:S(2)}) copy-start(bf16[128,128]{1,0:T(8,128)(2,1)} %refs_0_.3) | copy-start | bytes 98308
  1.7 47.4 %collective-permute-start.9 = (bf16[432,128]{1,0:T(8,128)(2,1)S(1)}, bf16[432,128]{1,0:T(8,128)(2,1)S(1)}, u32[]{:S(2)}, u32[]{:S(2)}) collective-permute-start(bf16[432,128]{1,0:T(8,128)(2,1)S(1)} %dynamic_slice.98), channel_id=1, source_target_pairs={{0,3},{1,0},{2,1},{3,2},{4,7},{5,4},{6,5},{7,6},{8,11},{9,8},{10,9... | collective-permute-start | bytes 331784 | tf_op jit(solution)/shard_map/ppermute | solution.py:27
  6.7 44.8 %collective-permute-start.8 = (bf16[432,128]{1,0:T(8,128)(2,1)S(1)}, bf16[432,128]{1,0:T(8,128)(2,1)S(1)}, u32[]{:S(2)}, u32[]{:S(2)}) collective-permute-start(bf16[432,128]{1,0:T(8,128)(2,1)S(1)} %dynamic_slice.98), channel_id=1, source_target_pairs={{0,2},{1,3},{2,0},{3,1},{4,6},{5,7},{6,4},{7,5},{8,10},{9,11},{10,... | collective-permute-start | bytes 331784 | tf_op jit(solution)/shard_map/ppermute | solution.py:27
  7.6 53.9 %collective-permute-start.5 = (bf16[432,128]{1,0:T(8,128)(2,1)S(1)}, bf16[432,128]{1,0:T(8,128)(2,1)S(1)}, u32[]{:S(2)}, u32[]{:S(2)}) collective-permute-start(bf16[432,128]{1,0:T(8,128)(2,1)S(1)} %dynamic_slice.97), channel_id=1, source_target_pairs={{0,3},{1,0},{2,1},{3,2},{4,7},{5,4},{6,5},{7,6},{8,11},{9,8},{10,9... | collective-permute-start | bytes 331784 | tf_op jit(solution)/shard_map/ppermute | solution.py:27
  8.1 53.5 %collective-permute-start.4 = (bf16[432,128]{1,0:T(8,128)(2,1)S(1)}, bf16[432,128]{1,0:T(8,128)(2,1)S(1)}, u32[]{:S(2)}, u32[]{:S(2)}) collective-permute-start(bf16[432,128]{1,0:T(8,128)(2,1)S(1)} %dynamic_slice.97), channel_id=1, source_target_pairs={{0,2},{1,3},{2,0},{3,1},{4,6},{5,7},{6,4},{7,5},{8,10},{9,11},{10,... | collective-permute-start | bytes 331784 | tf_op jit(solution)/shard_map/ppermute | solution.py:27
  12.5 25.3 %collective-permute-start.2 = (f32[168,128]{1,0:T(8,128)S(1)}, f32[168,128]{1,0:T(8,128)S(1)}, u32[]{:S(2)}, u32[]{:S(2)}) collective-permute-start(f32[168,128]{1,0:T(8,128)S(1)} %get-tuple-element.41), channel_id=1, source_target_pairs={{0,1},{1,2},{2,3},{3,0},{4,5},{5,6},{6,7},{7,4},{8,9},{9,10},{10,1... | collective-permute-start | bytes 258056 | tf_op jit(solution)/shard_map/ppermute | solution.py:27
  37.8 6.5 %collective-permute-start.1 = (f32[168,128]{1,0:T(8,128)S(1)}, f32[168,128]{1,0:T(8,128)S(1)}, u32[]{:S(2)}, u32[]{:S(2)}) collective-permute-start(f32[168,128]{1,0:T(8,128)S(1)} %get-tuple-element.42), channel_id=1, source_target_pairs={{0,2},{1,3},{2,0},{3,1},{4,6},{5,7},{6,4},{7,5},{8,10},{9,11},{10,... | collective-permute-start | bytes 258056 | tf_op jit(solution)/shard_map/ppermute | solution.py:27
  44.3 4.5 %collective-permute-start = (f32[168,128]{1,0:T(8,128)S(1)}, f32[168,128]{1,0:T(8,128)S(1)}, u32[]{:S(2)}, u32[]{:S(2)}) collective-permute-start(f32[168,128]{1,0:T(8,128)S(1)} %get-tuple-element.43), channel_id=1, source_target_pairs={{0,3},{1,0},{2,1},{3,2},{4,7},{5,4},{6,5},{7,6},{8,11},{9,8},{10,9... | collective-permute-start | bytes 258056 | tf_op jit(solution)/shard_map/ppermute | solution.py:27
  48.8 13.3 %collective-permute-start.3 = (bf16[432,128]{1,0:T(8,128)(2,1)S(1)}, bf16[432,128]{1,0:T(8,128)(2,1)S(1)}, u32[]{:S(2)}, u32[]{:S(2)}) collective-permute-start(bf16[432,128]{1,0:T(8,128)(2,1)S(1)} %dynamic_slice.97), channel_id=1, source_target_pairs={{0,1},{1,2},{2,3},{3,0},{4,5},{5,6},{6,7},{7,4},{8,9},{9,10},{10,1... | collective-permute-start | bytes 331784 | tf_op jit(solution)/shard_map/ppermute | solution.py:27
  49.0 13.1 %collective-permute-start.16 = (f32[3,128,128]{2,1,0:T(8,128)S(1)}, f32[3,128,128]{2,1,0:T(8,128)S(1)}, u32[]{:S(2)}, u32[]{:S(2)}) collective-permute-start(f32[3,128,128]{2,1,0:T(8,128)S(1)} %pad_maximum_fusion.2.refs_1_), channel_id=1, source_target_pairs={{0,24},{4,28},{8,16},{12,20},{16,8},{20,12},{24,0},{28,4},{1,25},{... | collective-permute-start | bytes 589832 | tf_op jit(solution)/shard_map/ppermute | solution.py:22
  51.5 18.0 %collective-permute-start.14 = (f32[3,128,128]{2,1,0:T(8,128)S(1)}, f32[3,128,128]{2,1,0:T(8,128)S(1)}, u32[]{:S(2)}, u32[]{:S(2)}) collective-permute-start(f32[3,128,128]{2,1,0:T(8,128)S(1)} %pad_maximum_fusion.2.refs_1_), channel_id=1, source_target_pairs={{0,16},{4,20},{8,24},{12,28},{16,0},{20,4},{24,8},{28,12},{1,17},{... | collective-permute-start | bytes 589832 | tf_op jit(solution)/shard_map/ppermute | solution.py:22
  61.5 6.5 %collective-permute-start.7 = (bf16[432,128]{1,0:T(8,128)(2,1)S(1)}, bf16[432,128]{1,0:T(8,128)(2,1)S(1)}, u32[]{:S(2)}, u32[]{:S(2)}) collective-permute-start(bf16[432,128]{1,0:T(8,128)(2,1)S(1)} %dynamic_slice.98), channel_id=1, source_target_pairs={{0,1},{1,2},{2,3},{3,0},{4,5},{5,6},{6,7},{7,4},{8,9},{9,10},{10,1... | collective-permute-start | bytes 331784 | tf_op jit(solution)/shard_map/ppermute | solution.py:27
  61.6 8.0 %collective-permute-start.12 = (f32[3,128,128]{2,1,0:T(8,128)S(1)}, f32[3,128,128]{2,1,0:T(8,128)S(1)}, u32[]{:S(2)}, u32[]{:S(2)}) collective-permute-start(f32[3,128,128]{2,1,0:T(8,128)S(1)} %pad_maximum_fusion.2.refs_1_), channel_id=1, source_target_pairs={{0,8},{4,12},{8,0},{12,4},{16,24},{20,28},{24,16},{28,20},{1,9},{5... | collective-permute-start | bytes 589832 | tf_op jit(solution)/shard_map/ppermute | solution.py:22
  62.1 8.1 %collective-permute-start.11 = (f32[3,128,128]{2,1,0:T(8,128)S(1)}, f32[3,128,128]{2,1,0:T(8,128)S(1)}, u32[]{:S(2)}, u32[]{:S(2)}) collective-permute-start(f32[3,128,128]{2,1,0:T(8,128)S(1)} %pad_maximum_fusion.2.refs_1_), channel_id=1, source_target_pairs={{0,4},{4,0},{8,12},{12,8},{16,20},{20,16},{24,28},{28,24},{1,5},{5... | collective-permute-start | bytes 589832 | tf_op jit(solution)/shard_map/ppermute | solution.py:22
  62.1 8.6 %collective-permute-start.17 = (f32[3,128,128]{2,1,0:T(8,128)S(1)}, f32[3,128,128]{2,1,0:T(8,128)S(1)}, u32[]{:S(2)}, u32[]{:S(2)}) collective-permute-start(f32[3,128,128]{2,1,0:T(8,128)S(1)} %collective-permute-done.16.refs_7_), channel_id=1, source_target_pairs={{0,4},{4,0},{8,12},{12,8},{16,20},{20,16},{24,28},{28,24},{1,5},{5... | collective-permute-start | bytes 589832 | tf_op jit(solution)/shard_map/ppermute | solution.py:22
  68.0 23.8 %collective-permute-start.20 = (bf16[3,432,128]{2,1,0:T(8,128)(2,1)S(1)}, bf16[3,432,128]{2,1,0:T(8,128)(2,1)S(1)}, u32[]{:S(2)}, u32[]{:S(2)}) collective-permute-start(bf16[3,432,128]{2,1,0:T(8,128)(2,1)S(1)} %pad_maximum_fusion.refs_6_), channel_id=1, source_target_pairs={{0,16},{4,20},{8,24},{12,28},{16,0},{20,4},{24,8},{28,12},{1,17},{... | collective-permute-start | bytes 995336 | tf_op jit(solution)/shard_map/ppermute | solution.py:22
  69.5 1.7 %collective-permute-start.15 = (f32[3,128,128]{2,1,0:T(8,128)S(1)}, f32[3,128,128]{2,1,0:T(8,128)S(1)}, u32[]{:S(2)}, u32[]{:S(2)}) collective-permute-start(f32[3,128,128]{2,1,0:T(8,128)S(1)} %collective-permute-done.14.refs_5_), channel_id=1, source_target_pairs={{0,4},{4,0},{8,12},{12,8},{16,20},{20,16},{24,28},{28,24},{1,5},{5... | collective-permute-start | bytes 589832 | tf_op jit(solution)/shard_map/ppermute | solution.py:22
  69.6 24.3 %collective-permute-start.18 = (bf16[3,432,128]{2,1,0:T(8,128)(2,1)S(1)}, bf16[3,432,128]{2,1,0:T(8,128)(2,1)S(1)}, u32[]{:S(2)}, u32[]{:S(2)}) collective-permute-start(bf16[3,432,128]{2,1,0:T(8,128)(2,1)S(1)} %pad_maximum_fusion.refs_6_), channel_id=1, source_target_pairs={{0,4},{4,0},{8,12},{12,8},{16,20},{20,16},{24,28},{28,24},{1,5},{5... | collective-permute-start | bytes 995336 | tf_op jit(solution)/shard_map/ppermute | solution.py:22
  70.2 21.7 %collective-permute-start.6 = (bf16[3,432,128]{2,1,0:T(8,128)(2,1)S(1)}, bf16[3,432,128]{2,1,0:T(8,128)(2,1)S(1)}, u32[]{:S(2)}, u32[]{:S(2)}) collective-permute-start(bf16[3,432,128]{2,1,0:T(8,128)(2,1)S(1)} %pad_maximum_fusion.refs_6_), channel_id=1, source_target_pairs={{0,8},{4,12},{8,0},{12,4},{16,24},{20,28},{24,16},{28,20},{1,9},{5... | collective-permute-start | bytes 995336 | tf_op jit(solution)/shard_map/ppermute | solution.py:22
  70.7 21.6 %collective-permute-start.10 = (bf16[3,432,128]{2,1,0:T(8,128)(2,1)S(1)}, bf16[3,432,128]{2,1,0:T(8,128)(2,1)S(1)}, u32[]{:S(2)}, u32[]{:S(2)}) collective-permute-start(bf16[3,432,128]{2,1,0:T(8,128)(2,1)S(1)} %pad_maximum_fusion.1.refs_14_), channel_id=1, source_target_pairs={{0,16},{4,20},{8,24},{12,28},{16,0},{20,4},{24,8},{28,12},{1,17},{... | collective-permute-start | bytes 995336 | tf_op jit(solution)/shard_map/ppermute | solution.py:22
  71.3 1.5 collective-permute-start.13
  72.8 21.6 %collective-permute-start.25 = (bf16[3,432,128]{2,1,0:T(8,128)(2,1)S(1)}, bf16[3,432,128]{2,1,0:T(8,128)(2,1)S(1)}, u32[]{:S(2)}, u32[]{:S(2)}) collective-permute-start(bf16[3,432,128]{2,1,0:T(8,128)(2,1)S(1)} %pad_maximum_fusion.1.refs_14_), channel_id=1, source_target_pairs={{0,8},{4,12},{8,0},{12,4},{16,24},{20,28},{24,16},{28,20},{1,9},{5... | collective-permute-start | bytes 995336 | tf_op jit(solution)/shard_map/ppermute | solution.py:22
  91.8 2.6 %collective-permute-start.24 = (bf16[3,432,128]{2,1,0:T(8,128)(2,1)S(1)}, bf16[3,432,128]{2,1,0:T(8,128)(2,1)S(1)}, u32[]{:S(2)}, u32[]{:S(2)}) collective-permute-start(bf16[3,432,128]{2,1,0:T(8,128)(2,1)S(1)} %pad_maximum_fusion.1.refs_14_), channel_id=1, source_target_pairs={{0,4},{4,0},{8,12},{12,8},{16,20},{20,16},{24,28},{28,24},{1,5},{5... | collective-permute-start | bytes 995336 | tf_op jit(solution)/shard_map/ppermute | solution.py:22
  91.8 3.1 %collective-permute-start.21 = (bf16[3,432,128]{2,1,0:T(8,128)(2,1)S(1)}, bf16[3,432,128]{2,1,0:T(8,128)(2,1)S(1)}, u32[]{:S(2)}, u32[]{:S(2)}) collective-permute-start(bf16[3,432,128]{2,1,0:T(8,128)(2,1)S(1)} %collective-permute-done.20.refs_10_), channel_id=1, source_target_pairs={{0,4},{4,0},{8,12},{12,8},{16,20},{20,16},{24,28},{28,24},{1,5},{5... | collective-permute-start | bytes 995336 | tf_op jit(solution)/shard_map/ppermute | solution.py:22
  92.4 9.8 %collective-permute-start.22 = (bf16[3,432,128]{2,1,0:T(8,128)(2,1)S(1)}, bf16[3,432,128]{2,1,0:T(8,128)(2,1)S(1)}, u32[]{:S(2)}, u32[]{:S(2)}) collective-permute-start(bf16[3,432,128]{2,1,0:T(8,128)(2,1)S(1)} %collective-permute-done.6.refs_8_), channel_id=1, source_target_pairs={{0,16},{4,20},{8,24},{12,28},{16,0},{20,4},{24,8},{28,12},{1,17},{... | collective-permute-start | bytes 995336 | tf_op jit(solution)/shard_map/ppermute | solution.py:22
  93.9 9.5 %collective-permute-start.28 = (bf16[3,432,128]{2,1,0:T(8,128)(2,1)S(1)}, bf16[3,432,128]{2,1,0:T(8,128)(2,1)S(1)}, u32[]{:S(2)}, u32[]{:S(2)}) collective-permute-start(bf16[3,432,128]{2,1,0:T(8,128)(2,1)S(1)} %collective-permute-done.10.refs_18_), channel_id=1, source_target_pairs={{0,8},{4,12},{8,0},{12,4},{16,24},{20,28},{24,16},{28,20},{1,9},{5... | collective-permute-start | bytes 995336 | tf_op jit(solution)/shard_map/ppermute | solution.py:22
  94.4 9.0 %collective-permute-start.19 = (bf16[3,432,128]{2,1,0:T(8,128)(2,1)S(1)}, bf16[3,432,128]{2,1,0:T(8,128)(2,1)S(1)}, u32[]{:S(2)}, u32[]{:S(2)}) collective-permute-start(bf16[3,432,128]{2,1,0:T(8,128)(2,1)S(1)} %collective-permute-done.6.refs_8_), channel_id=1, source_target_pairs={{0,4},{4,0},{8,12},{12,8},{16,20},{20,16},{24,28},{28,24},{1,5},{5... | collective-permute-start | bytes 995336 | tf_op jit(solution)/shard_map/ppermute | solution.py:22
  94.4 9.0 %collective-permute-start.27 = (bf16[3,432,128]{2,1,0:T(8,128)(2,1)S(1)}, bf16[3,432,128]{2,1,0:T(8,128)(2,1)S(1)}, u32[]{:S(2)}, u32[]{:S(2)}) collective-permute-start(bf16[3,432,128]{2,1,0:T(8,128)(2,1)S(1)} %collective-permute-done.10.refs_18_), channel_id=1, source_target_pairs={{0,4},{4,0},{8,12},{12,8},{16,20},{20,16},{24,28},{28,24},{1,5},{5... | collective-permute-start | bytes 995336 | tf_op jit(solution)/shard_map/ppermute | solution.py:22
  94.9 8.5 %collective-permute-start.26 = (bf16[3,432,128]{2,1,0:T(8,128)(2,1)S(1)}, bf16[3,432,128]{2,1,0:T(8,128)(2,1)S(1)}, u32[]{:S(2)}, u32[]{:S(2)}) collective-permute-start(bf16[3,432,128]{2,1,0:T(8,128)(2,1)S(1)} %collective-permute-done.25.refs_16_), channel_id=1, source_target_pairs={{0,4},{4,0},{8,12},{12,8},{16,20},{20,16},{24,28},{28,24},{1,5},{5... | collective-permute-start | bytes 995336 | tf_op jit(solution)/shard_map/ppermute | solution.py:22
  102.1 1.6 %collective-permute-start.23 = (bf16[3,432,128]{2,1,0:T(8,128)(2,1)S(1)}, bf16[3,432,128]{2,1,0:T(8,128)(2,1)S(1)}, u32[]{:S(2)}, u32[]{:S(2)}) collective-permute-start(bf16[3,432,128]{2,1,0:T(8,128)(2,1)S(1)} %collective-permute-done.22.refs_12_), channel_id=1, source_target_pairs={{0,4},{4,0},{8,12},{12,8},{16,20},{20,16},{24,28},{28,24},{1,5},{5... | collective-permute-start | bytes 995336 | tf_op jit(solution)/shard_map/ppermute | solution.py:22
  103.4 1.6 %collective-permute-start.29 = (bf16[3,432,128]{2,1,0:T(8,128)(2,1)S(1)}, bf16[3,432,128]{2,1,0:T(8,128)(2,1)S(1)}, u32[]{:S(2)}, u32[]{:S(2)}) collective-permute-start(bf16[3,432,128]{2,1,0:T(8,128)(2,1)S(1)} %collective-permute-done.28.refs_20_), channel_id=1, source_target_pairs={{0,4},{4,0},{8,12},{12,8},{16,20},{20,16},{24,28},{28,24},{1,5},{5... | collective-permute-start | bytes 995336 | tf_op jit(solution)/shard_map/ppermute | solution.py:22
  121.3 2.2 %collective-permute-start.30 = (bf16[4,4,128,128]{3,2,1,0:T(8,128)(2,1)}, bf16[4,4,128,128]{3,2,1,0:T(8,128)(2,1)S(1)}, u32[]{:S(2)}, u32[]{:S(2)}) collective-permute-start(bf16[4,4,128,128]{3,2,1,0:T(8,128)(2,1)} %get-tuple-element.20), channel_id=1, source_target_pairs={{0,4},{4,0},{8,12},{12,8},{16,20},{20,16},{24,28},{28,24},{1,5},{5... | collective-permute-start | bytes 1572872 | tf_op jit(solution)/shard_map/ppermute | solution.py:22
  123.7 6.4 %collective-permute-start.31 = (bf16[1,4,128,128]{3,2,1,0:T(8,128)(2,1)S(1)}, bf16[1,4,128,128]{3,2,1,0:T(8,128)(2,1)S(1)}, u32[]{:S(2)}, u32[]{:S(2)}) collective-permute-start(bf16[1,4,128,128]{3,2,1,0:T(8,128)(2,1)S(1)} %get-tuple-element.31), channel_id=1, source_target_pairs={{0,8},{4,12},{8,0},{12,4},{16,24},{20,28},{24,16},{28,20},{1,9},{5... | collective-permute-start | bytes 393224 | tf_op jit(solution)/shard_map/ppermute | solution.py:22
  124.1 8.3 %collective-permute-start.33 = (bf16[1,4,128,128]{3,2,1,0:T(8,128)(2,1)S(1)}, bf16[1,4,128,128]{3,2,1,0:T(8,128)(2,1)S(1)}, u32[]{:S(2)}, u32[]{:S(2)}) collective-permute-start(bf16[1,4,128,128]{3,2,1,0:T(8,128)(2,1)S(1)} %get-tuple-element.32), channel_id=1, source_target_pairs={{0,24},{4,28},{8,16},{12,20},{16,8},{20,12},{24,0},{28,4},{1,25},{... | collective-permute-start | bytes 393224 | tf_op jit(solution)/shard_map/ppermute | solution.py:22
  126.0 7.8 %collective-permute-start.32 = (bf16[1,4,128,128]{3,2,1,0:T(8,128)(2,1)S(1)}, bf16[1,4,128,128]{3,2,1,0:T(8,128)(2,1)S(1)}, u32[]{:S(2)}, u32[]{:S(2)}) collective-permute-start(bf16[1,4,128,128]{3,2,1,0:T(8,128)(2,1)S(1)} %get-tuple-element.33), channel_id=1, source_target_pairs={{0,16},{4,20},{8,24},{12,28},{16,0},{20,4},{24,8},{28,12},{1,17},{... | collective-permute-start | bytes 393224 | tf_op jit(solution)/shard_map/ppermute | solution.py:22
  133.9 4.3 %collective-permute-start.34 = (f32[128,128]{1,0:T(8,128)S(1)}, f32[128,128]{1,0:T(8,128)S(1)}, u32[]{:S(2)}, u32[]{:S(2)}) collective-permute-start(f32[128,128]{1,0:T(8,128)S(1)} %get-tuple-element.34), channel_id=1, source_target_pairs={{0,3},{1,0},{2,1},{3,2},{4,7},{5,4},{6,5},{7,6},{8,11},{9,8},{10,9... | collective-permute-start | bytes 196616 | tf_op jit(solution)/shard_map/ppermute | solution.py:27
  136.0 6.1 %collective-permute-start.36 = (f32[128,128]{1,0:T(8,128)S(1)}, f32[128,128]{1,0:T(8,128)S(1)}, u32[]{:S(2)}, u32[]{:S(2)}) collective-permute-start(f32[128,128]{1,0:T(8,128)S(1)} %get-tuple-element.35), channel_id=1, source_target_pairs={{0,1},{1,2},{2,3},{3,0},{4,5},{5,6},{6,7},{7,4},{8,9},{9,10},{10,1... | collective-permute-start | bytes 196616 | tf_op jit(solution)/shard_map/ppermute | solution.py:27
  136.0 7.3 %collective-permute-start.35 = (f32[128,128]{1,0:T(8,128)S(1)}, f32[128,128]{1,0:T(8,128)S(1)}, u32[]{:S(2)}, u32[]{:S(2)}) collective-permute-start(f32[128,128]{1,0:T(8,128)S(1)} %get-tuple-element.36), channel_id=1, source_target_pairs={{0,2},{1,3},{2,0},{3,1},{4,6},{5,7},{6,4},{7,5},{8,10},{9,11},{10,... | collective-permute-start | bytes 196616 | tf_op jit(solution)/shard_map/ppermute | solution.py:27
  143.3 5.3 %collective-permute-start.42 = (f32[128,128]{1,0:T(8,128)S(1)}, f32[128,128]{1,0:T(8,128)S(1)}, u32[]{:S(2)}, u32[]{:S(2)}) collective-permute-start(f32[128,128]{1,0:T(8,128)S(1)} %fusion.5.refs_0_), channel_id=1, source_target_pairs={{0,24},{4,28},{8,16},{12,20},{16,8},{20,12},{24,0},{28,4},{1,25},{... | collective-permute-start | bytes 196616 | tf_op jit(solution)/shard_map/ppermute | solution.py:22
  144.4 4.8 %collective-permute-start.40 = (f32[128,128]{1,0:T(8,128)S(1)}, f32[128,128]{1,0:T(8,128)S(1)}, u32[]{:S(2)}, u32[]{:S(2)}) collective-permute-start(f32[128,128]{1,0:T(8,128)S(1)} %fusion.5.refs_0_), channel_id=1, source_target_pairs={{0,16},{4,20},{8,24},{12,28},{16,0},{20,4},{24,8},{28,12},{1,17},{... | collective-permute-start | bytes 196616 | tf_op jit(solution)/shard_map/ppermute | solution.py:22
  145.4 4.3 %collective-permute-start.38 = (f32[128,128]{1,0:T(8,128)S(1)}, f32[128,128]{1,0:T(8,128)S(1)}, u32[]{:S(2)}, u32[]{:S(2)}) collective-permute-start(f32[128,128]{1,0:T(8,128)S(1)} %fusion.5.refs_0_), channel_id=1, source_target_pairs={{0,8},{4,12},{8,0},{12,4},{16,24},{20,28},{24,16},{28,20},{1,9},{5... | collective-permute-start | bytes 196616 | tf_op jit(solution)/shard_map/ppermute | solution.py:22
  146.8 2.9 %collective-permute-start.37 = (f32[128,128]{1,0:T(8,128)S(1)}, f32[128,128]{1,0:T(8,128)S(1)}, u32[]{:S(2)}, u32[]{:S(2)}) collective-permute-start(f32[128,128]{1,0:T(8,128)S(1)} %fusion.5.refs_0_), channel_id=1, source_target_pairs={{0,4},{4,0},{8,12},{12,8},{16,20},{20,16},{24,28},{28,24},{1,5},{5... | collective-permute-start | bytes 196616 | tf_op jit(solution)/shard_map/ppermute | solution.py:22
  148.6 1.3 collective-permute-start.43
  149.2 1.3 collective-permute-start.41
  149.6 1.3 collective-permute-start.39
  (3 other events, 120.5 us)

commit v3 on v2

v3 whole, which is shorter than its diff:
```python
import functools

import jax
import jax.numpy as jnp
from jax import lax
from jax.experimental import pallas as pl
from jax.experimental.pallas import tpu as pltpu
from jax.sharding import PartitionSpec as P

EPSILON = 1e-08
F32, BF16 = jnp.float32, jnp.bfloat16
LOW = 32
UNROLL = 8
HOT = 4
CHUNK = 256
ID_BITS = 10
VMEM_LIMIT = 28 * 1024 * 1024
PACK_LIMIT = 60 * 1024 * 1024


def swap(array, mask):
    size = lax.axis_size("replica")
    return lax.ppermute(array, "replica", [(i, i ^ mask) for i in range(size)])


def shift(array, step):
    size = lax.axis_size("table")
    return lax.ppermute(array, "table", [(i, (i + step) % size) for i in range(size)])


def mask_stages(size):
    stages, bit = [(1,)], 1
    while (1 << bit) < size:
        if (2 << bit) < size:
            stages.append((1 << bit, 2 << bit, 3 << bit))
            bit += 2
        else:
            stages.append((1 << bit,))
            bit += 1
    return stages


def replica_gather(piece, *beside):
    held = [piece]
    for masks in reversed(mask_stages(lax.axis_size("replica"))[1:]):
        held = [held] + [[swap(h, mask) for h in held] for mask in masks]
        held = [h for group in held for h in group]
    order = sorted(range(len(held)), key=lambda i: gather_masks(lax.axis_size("replica"))[i])
    even = jnp.stack([held[i] for i in order])
    even, *beside = lax.optimization_barrier((even, *beside))
    return (even, swap(even, 1)), *beside


def gather_masks(size):
    masks = [0]
    for group in reversed(mask_stages(size)[1:]):
        masks = masks + [m ^ mask for mask in group for m in masks]
    return masks


def whole(space=pltpu.VMEM):
    return pl.BlockSpec(memory_space=space)


def slot_range(live_counts, shards, j):
    here = lax.axis_index("table")
    source = lax.rem(here - j + shards, shards)
    start = jnp.int32(0)
    for s in range(shards):
        start = start + jnp.where(s < source, live_counts[0, here, s], 0)
    return source, start, live_counts[0, here, source]


def pack_kernel(shards, wanted, look_rows, table, *refs):
    factors, refs = refs[: len(wanted)], refs[len(wanted) :]
    parcels, blocks, done = refs[: shards - 1], refs[shards - 1 : -1], refs[-1]
    width = table.shape[1]
    capacity = look_rows.shape[4]
    lines = -(-capacity // width)
    block = parcels[0].shape[0] - HOT * lines
    mine, here = lax.axis_index("replica"), lax.axis_index("table")
    rows = table.at[pl.ds(pl.multiple_of(mine * block, block), block), :]
    copies = [
        pltpu.make_async_copy(rows, parcel.at[:block, :], done.at[i])
        for i, parcel in enumerate(parcels)
    ]
    for i, factor in enumerate(factors):
        both = blocks[0]
        half, lanes = both.shape[0] // 2, both.shape[1]
        at = (
            pl.ds(pl.multiple_of((mine & 1) * half, 16), half),
            pl.ds(pl.multiple_of((mine >> 1) * lanes, lanes), lanes),
        )
        into = both.at[i * half : (i + 1) * half, :]
        copies.append(pltpu.make_async_copy(factor.at[at], into, done.at[shards - 1 + i]))
    for copy in copies:
        copy.start()
    for i, parcel in enumerate(parcels):
        owner = lax.rem(here + i + 1, shards)
        for h in range(HOT):
            for q in range(lines):
                line = block + h * lines + q
                size = min(width, capacity - q * width)
                if size < width:
                    parcel[line : line + 1, :] = jnp.zeros((1, width), F32)
                parcel[line : line + 1, :size] = look_rows[
                    0, 0, owner, h : h + 1, q * width : q * width + size
                ].astype(F32)
    for copy in copies:
        copy.wait()


def pack(look_rows, table, factors, shards, replicas):
    rows, width = table.shape
    capacity = look_rows.shape[4]
    lines = -(-capacity // width)
    parcel = jax.ShapeDtypeStruct((rows // replicas + HOT * lines, width), F32)
    blocks = [jax.ShapeDtypeStruct((f.shape[0], width), BF16) for f in factors[:1]]
    count = shards - 1 + len(factors)
    return pl.pallas_call(
        functools.partial(pack_kernel, shards, factors),
        out_shape=[parcel] * (shards - 1) + blocks,
        in_specs=[whole()] + [whole(pltpu.HBM)] * (1 + len(factors)),
        out_specs=[whole()] * (shards - 1 + len(blocks)),
        scratch_shapes=[pltpu.SemaphoreType.DMA((count,))],
        compiler_params=pltpu.CompilerParams(vmem_limit_bytes=PACK_LIMIT),
        name="pack",
    )(look_rows, table, *factors)


def quotient(value, divisor, below):
    shift = 19
    factor = (1 << shift) // divisor + 1
    assert below * factor < 1 << 31
    assert all((v * factor) >> shift == v // divisor for v in range(below))
    return lax.shift_right_logical(value * factor, shift)


def slots_kernel(shards, replicas, batch, live_counts, look_rows, bag_order, *refs):
    parcels, (places, counted, shifted, words) = refs[: shards - 1], refs[shards - 1 :]
    width = parcels[0].shape[1]
    capacity = look_rows.shape[4]
    lines = -(-capacity // width)
    bags = bag_order.shape[2]
    rows = counted.shape[1]
    block = rows // replicas
    field = (1 << ID_BITS) - 1
    slot = lax.broadcasted_iota(jnp.int32, (8, bags), 1)
    ranges = [slot_range(live_counts, shards, j) for j in range(shards)]
    here = lax.axis_index("table")
    shifted[...] = jnp.zeros_like(shifted)
    for j, (source, start, live) in enumerate(ranges):
        for pair in range(HOT // 2):
            for q in range(lines):
                size = min(width, capacity - q * width)

                def line(h, j=j, q=q, size=size):
                    if j == 0:
                        return look_rows[0, 0, here, h : h + 1, q * width : q * width + size]
                    at = block + h * lines + q
                    return parcels[j - 1][at : at + 1, :size].astype(jnp.int32)

                shifted[pair : pair + 1, q * width : q * width + size] = line(2 * pair) | (
                    line(2 * pair + 1) << ID_BITS
                )
        moved = pltpu.roll(shifted[...], start, 1)[:, :bags]
        inside = (slot >= start) & (slot < start + live)
        words[...] = jnp.where(inside, moved, words[...] if j else 0)
    order = bag_order[0]
    sample = quotient(order, bags // batch, bags)
    dest = (order - sample * (bags // batch)) * batch + sample
    places[...] = dest[:, : bags // 2] | (dest[:, bags // 2 :] << 16)

    flip = lax.axis_index("replica") * block
    low = lax.broadcasted_iota(jnp.int32, (LOW, CHUNK), 0)
    for source, start, live in ranges:

        def pair(q, _, start=start, live=live, source=source):
            at = pl.ds(pl.multiple_of(q * CHUNK, CHUNK), CHUNK)
            place = q * CHUNK + lax.broadcasted_iota(jnp.int32, (1, CHUNK), 1) - start
            inside = (place >= 0) & (place < live)
            lows, highs = [], []
            for h in range(HOT):
                word = words[h // 2 : h // 2 + 1, at]
                row = (lax.shift_right_logical(word, (h % 2) * ID_BITS) & field) ^ flip
                row = jnp.where(inside, row, -1)
                highs.append(lax.shift_right_arithmetic(row, LOW.bit_length() - 1))
                lows.append((low == (row & (LOW - 1))).astype(F32).astype(BF16))
            for b in range(rows // LOW):
                count = None
                for h in range(HOT):
                    hit = (highs[h] == b).astype(F32).astype(BF16)
                    term = lows[h] * hit
                    count = term if count is None else count + term
                counted[q + source, b * LOW : (b + 1) * LOW, :] = count
            return 0

        lax.fori_loop(start // CHUNK, (start + live + CHUNK - 1) // CHUNK, pair, 0)


def slots(live_counts, look_rows, bag_order, parcels, rows, shards, replicas, batch):
    bags = bag_order.shape[2]
    capacity = -(-look_rows.shape[4] // 128) * 128
    pairs = bags // CHUNK + shards - 1
    return pl.pallas_call(
        functools.partial(slots_kernel, shards, replicas, batch),
        out_shape=[
            jax.ShapeDtypeStruct((1, bags // 2), jnp.int32),
            jax.ShapeDtypeStruct((pairs, rows, CHUNK), BF16),
        ],
        in_specs=[whole(pltpu.SMEM)] + [whole()] * (2 + len(parcels)),
        out_specs=[whole()] * 2,
        scratch_shapes=[
            pltpu.VMEM((8, bags + capacity), jnp.int32),
            pltpu.VMEM((8, bags), jnp.int32),
        ],
        compiler_params=pltpu.CompilerParams(vmem_limit_bytes=VMEM_LIMIT),
        cost_estimate=pl.CostEstimate(flops=1000, bytes_accessed=1000, transcendentals=0),
        name="slots",
    )(live_counts, look_rows, bag_order, *parcels)


def pool_kernel(shards, live_counts, places, counted, own, even, odd, out, table, sums, pooled):
    rows_dev, width = own.shape
    block = even.shape[2]
    middle = sums.shape[0] // 2
    mine = lax.axis_index("replica")

    def put(shard, rows, value):
        high = value.astype(BF16)
        table[shard, rows, :width] = high
        table[shard, rows, width:] = (value - high.astype(F32)).astype(BF16)

    for m in range(2 * even.shape[0]):
        there = pl.ds(pl.multiple_of((mine ^ m) * block, block), block)
        rows = slice(m * block, (m + 1) * block)
        put(0, rows, own[there, :])
        for k in range(1, shards):
            put(k, rows, (odd if m % 2 else even)[m // 2, k - 1])
    sums[...] = jnp.zeros_like(sums)
    for j in range(shards):
        source, start, live = slot_range(live_counts, shards, j)

        def pair(q, _, j=j, source=source):
            at = pl.ds(pl.multiple_of(q * CHUNK, CHUNK), CHUNK)
            found = lax.dot_general(
                counted[q + source], table[j], (((0,), (0,)), ((), ())), preferred_element_type=F32
            )
            sums[at, :] += found[:, :width] + found[:, width:]
            return 0

        lax.fori_loop(start // CHUNK, (start + live + CHUNK - 1) // CHUNK, pair, 0)

    def group(i, _):
        for u in range(UNROLL):
            k = i * UNROLL + u
            word = places[0, k]
            pooled[pl.ds(word & 0xFFFF, 1), :] = sums[pl.ds(k, 1), :]
            pooled[pl.ds(lax.shift_right_logical(word, 16), 1), :] = sums[pl.ds(k + middle, 1), :]
        return 0

    lax.fori_loop(0, middle // UNROLL, group, 0)
    out[...] = pooled[...].astype(BF16)


def pool(live_counts, places, counted, own, pieces):
    rows, width = own.shape
    bags = 2 * places.shape[1]
    shards = pieces[0].shape[1] + 1
    smem = whole(pltpu.SMEM)
    return pl.pallas_call(
        functools.partial(pool_kernel, shards),
        out_shape=jax.ShapeDtypeStruct((bags, width), BF16),
        in_specs=[smem, smem] + [whole()] * 4,
        out_specs=whole(),
        scratch_shapes=[
            pltpu.VMEM((shards, rows, 2 * width), BF16),
            pltpu.VMEM((bags, width), F32),
            pltpu.VMEM((bags, width), F32),
        ],
        compiler_params=pltpu.CompilerParams(vmem_limit_bytes=VMEM_LIMIT),
        cost_estimate=pl.CostEstimate(flops=1000, bytes_accessed=1000, transcendentals=0),
        name="pool",
    )(live_counts, places, counted, own, *pieces)


def column_of(row, size):
    eye = lax.broadcasted_iota(jnp.int32, (size, size), 0) == lax.broadcasted_iota(
        jnp.int32, (size, size), 1
    )
    return jnp.sum(jnp.where(eye, jnp.broadcast_to(row, (size, size)), 0.0), axis=1, keepdims=True)


def row_of(column, size):
    eye = lax.broadcasted_iota(jnp.int32, (size, size), 0) == lax.broadcasted_iota(
        jnp.int32, (size, size), 1
    )
    return jnp.sum(
        jnp.where(eye, jnp.broadcast_to(column, (size, size)), 0.0), axis=0, keepdims=True
    )


def dense_kernel(shards, replicas, copies, live_counts, places, *refs):
    dense, rows_in, bias, head, labels, counted = refs[:6]
    weights = refs[6 : 6 + len(copies)]
    logits, even, odd = refs[6 + len(copies) : 9 + len(copies)]
    full_in, full_out, cross, scaled, grads, slots, narrow, total = refs[9 + len(copies) :]
    batch, width = dense.shape
    features = full_in.shape[0]
    bags = grads.shape[0]
    table_rows = total.shape[0]
    across = (((1,), (1,)), ((), ()))

    factor = (full_in, full_out)
    for ref, copy in zip(weights, copies):
        copy(ref, factor)

    cross[:, :width] = dense[...]
    for f in range(1, features // width):
        cross[:, f * width : (f + 1) * width] = rows_in[(f - 1) * batch : f * batch, :]
    for f in range(features // width):
        at = slice(f * width, (f + 1) * width)
        scaled[:, at] = (cross[:, at].astype(F32) * head[:, at]).astype(BF16)
    hidden = jnp.dot(cross[...], full_in[...], preferred_element_type=F32).astype(BF16)
    back = jnp.dot(scaled[...], full_out[...], preferred_element_type=F32).astype(BF16)

    step = 3 * width if (features // width) % 3 == 0 else width
    logit = jnp.zeros((batch, width), F32)
    for n in range(features // step):
        at = slice(n * step, (n + 1) * step)
        mixed = lax.dot_general(hidden, full_out[at, :], across, preferred_element_type=F32)
        gain = head[:, at] * (mixed + bias[:, at] + 1.0)
        term = cross[:, at].astype(F32) * gain
        grad = gain + lax.dot_general(back, full_in[at, :], across, preferred_element_type=F32)
        for p in range(step // width):
            part = slice(p * width, (p + 1) * width)
            logit = logit + term[:, part]
            f = n * (step // width) + p
            if f > 0:
                grads[(f - 1) * batch : f * batch, :] = grad[:, part]
    logit = jnp.sum(logit, axis=1, keepdims=True)
    logits[...] = row_of(logit, batch)
    lean = jax.nn.sigmoid(logit) - column_of(labels[...].astype(F32), batch)
    for f in range(features // width - 1):
        at = slice(f * batch, (f + 1) * batch)
        grads[at, :] = (grads[at, :] * lean).astype(BF16).astype(F32)

    middle = bags // 2

    def group(i, _):
        for u in range(UNROLL):
            k = i * UNROLL + u
            word = places[0, k]
            slots[pl.ds(k, 1), :] = grads[pl.ds(word & 0xFFFF, 1), :]
            slots[pl.ds(k + middle, 1), :] = grads[pl.ds(lax.shift_right_logical(word, 16), 1), :]
        return 0

    lax.fori_loop(0, middle // UNROLL, group, 0)
    narrow[...] = slots[...].astype(BF16)
    block = table_rows // replicas
    for j in range(shards):
        source, start, live = slot_range(live_counts, shards, j)
        total[...] = jnp.zeros_like(total)

        def pair(q, _, source=source):
            at = pl.ds(pl.multiple_of(q * CHUNK, CHUNK), CHUNK)
            total[...] += jnp.dot(
                counted[q + source], narrow[at, :], preferred_element_type=F32
            )
            return 0

        lax.fori_loop(start // CHUNK, (start + live + CHUNK - 1) // CHUNK, pair, 0)
        for m in range(replicas):
            half = even if m % 2 == 0 else odd
            half[m // 2, j] = total[m * block : (m + 1) * block, :].astype(BF16)


def dense_step(live_counts, places, dense, rows_in, bias, head, labels, counted, weights, copies, rank, shards, replicas):
    batch, width = dense.shape
    features = bias.shape[1]
    bags = rows_in.shape[0]
    rows = counted.shape[1]
    half = jax.ShapeDtypeStruct((replicas // 2, shards, rows // replicas, width), BF16)
    smem = whole(pltpu.SMEM)
    return pl.pallas_call(
        functools.partial(dense_kernel, shards, replicas, copies),
        out_shape=(jax.ShapeDtypeStruct((1, batch), F32), half, half),
        in_specs=[smem, smem] + [whole()] * 6 + [whole()] * len(weights),
        out_specs=(whole(), whole(), whole()),
        scratch_shapes=[
            pltpu.VMEM((features, rank), BF16),
            pltpu.VMEM((features, rank), BF16),
            pltpu.VMEM((batch, features), BF16),
            pltpu.VMEM((batch, features), BF16),
            pltpu.VMEM((bags, width), F32),
            pltpu.VMEM((bags, width), F32),
            pltpu.VMEM((bags, width), BF16),
            pltpu.VMEM((rows, width), F32),
        ],
        compiler_params=pltpu.CompilerParams(vmem_limit_bytes=VMEM_LIMIT),
        cost_estimate=pl.CostEstimate(
            flops=4 * 10**9, bytes_accessed=30 * 10**6, transcendentals=0
        ),
        name="dense",
    )(live_counts, places, dense, rows_in, bias, head, labels, counted, *weights)


def splits_evenly(factor, replicas):
    return replicas == 8 and factor.shape[1] == 4 * 128 and factor.shape[0] % 32 == 0


def gather_whole(factors):
    def spot(which):
        def copy(ref, full):
            full[which][...] = ref[...]

        return copy

    return [lax.all_gather(w, "table", axis=0, tiled=True) for w in factors], [spot(0), spot(1)]


def gather_blocks(factors, near, after):
    shards = lax.axis_size("table")
    shard_rows = factors[0].shape[0]
    half, lanes = shard_rows // 2, near.shape[2]
    first, second = swap(near, 2), swap(near, 4)
    first, second, after = lax.optimization_barrier((first, second, after))
    blocks = [(0, near, 0, 2), (2, first, 0, 2), (4, second, 0, 2)]
    blocks += [(6, swap(first[:, :half], 4), 0, 1), (6, swap(second[:, half:], 2), 1, 2)]
    arrays, copies = [], []
    for m, block, begin, end in blocks:
        for core in (0, 1):
            arrays.append(block if core == 0 else swap(block, 1))

            def copy(ref, full, m=m, core=core, begin=begin, end=end):
                own, here = lax.axis_index("replica"), lax.axis_index("table")
                for k in range(1, shards):
                    source = lax.rem(here - k + shards, shards)
                    first = source * shard_rows + ((own & 1) ^ core) * half
                    at = pl.ds(pl.multiple_of(first, 16), half)
                    for which in range(begin, end):
                        full[which][at, (m // 2) * lanes : (m // 2 + 1) * lanes] = ref[
                            k - 1, (which - begin) * half : (which - begin + 1) * half, :
                        ]

            copies.append(copy)
    for which, own_rows in enumerate(factors):

        def copy_own(ref, full, which=which):
            own, here = lax.axis_index("replica"), lax.axis_index("table")
            at = pl.ds(pl.multiple_of(here * shard_rows, 16), shard_rows)
            for m in range(4):
                columns = pl.ds(pl.multiple_of(((own >> 1) ^ m) * lanes, lanes), lanes)
                full[which][at, m * lanes : (m + 1) * lanes] = ref[:, columns]

        arrays.append(own_rows)
        copies.append(copy_own)
    return arrays, copies, after


def reduce_rows(even, odd):
    shards, replicas = lax.axis_size("table"), lax.axis_size("replica")
    kept = even.astype(F32) + swap(odd, 1).astype(F32)
    for masks in mask_stages(replicas)[1:]:
        split = kept.reshape((-1, len(masks) + 1) + kept.shape[1:])
        kept = split[:, 0]
        for i, mask in enumerate(masks):
            kept = kept + swap(split[:, i + 1].astype(BF16), mask).astype(F32)
    kept = kept[0]
    total = kept[0]
    for k in range(1, shards):
        total = total + shift(kept[k], -k)
    return total


def finish_kernel(accum, even, odd, update, fresh):
    count, block, width = even.shape
    mine = lax.axis_index("replica")
    for m in range(2 * count):
        own = mine ^ m
        grad = (odd if m % 2 else even)[m // 2]
        square = jnp.sum(grad * grad, axis=1, keepdims=True) * (1.0 / width)
        row = accum[pl.ds(own, 1), :] + row_of(square, block)
        fresh[pl.ds(own, 1), :] = row
        rows = pl.ds(pl.multiple_of(own * block, block), block)
        update[rows, :] = -grad / (jnp.sqrt(column_of(row, block)) + EPSILON)


def finish(accum, even, odd):
    replicas, block = accum.shape
    width = even.shape[2]
    return pl.pallas_call(
        finish_kernel,
        out_shape=(
            jax.ShapeDtypeStruct((replicas * block, width), F32),
            jax.ShapeDtypeStruct((replicas, block), F32),
        ),
        in_specs=[whole()] * 3,
        out_specs=(whole(), whole()),
        compiler_params=pltpu.CompilerParams(vmem_limit_bytes=VMEM_LIMIT),
        name="finish",
    )(accum, even, odd)


def local(
    emb_table,
    row_accum,
    look_rows,
    live_counts,
    bag_order,
    dense_emb,
    labels,
    cross_in,
    cross_out,
    cross_bias,
    head_weight,
):
    shards, replicas = lax.axis_size("table"), lax.axis_size("replica")
    rows = emb_table.shape[0]
    block = rows // replicas
    batch = dense_emb.shape[0]
    factors = (cross_in, cross_out)
    even_split = splits_evenly(cross_in, replicas)

    packed = pack(look_rows, emb_table, factors if even_split else (), shards, replicas)
    parcels = [shift(p, k + 1) for k, p in enumerate(packed[: shards - 1])]
    far = [shift(packed[shards - 1], k) for k in range(1, shards)] if even_split else []
    places, counted = slots(
        live_counts, look_rows, bag_order, parcels, rows, shards, replicas, batch
    )
    pieces, far, counted = replica_gather(
        jnp.stack([p[:block] for p in parcels]), far, counted
    )
    rows_in = pool(live_counts, places, counted, emb_table, pieces)
    if even_split:
        near = jnp.stack(far)
    if even_split:
        weights, copies, rows_in = gather_blocks(factors, near, rows_in)
    else:
        weights, copies = gather_whole(factors)
    logits, even, odd = dense_step(
        live_counts,
        places,
        dense_emb,
        rows_in,
        cross_bias.reshape(1, -1),
        head_weight.reshape(1, -1),
        labels.reshape(1, -1),
        counted,
        weights,
        copies,
        cross_in.shape[1],
        shards,
        replicas,
    )
    grad = reduce_rows(even, odd)
    update, accum = finish(row_accum.reshape(replicas, block), *replica_gather(grad)[0])
    return (logits.reshape(-1), update, accum.reshape(-1))


def solution(mesh):
    placed = (
        P("table", None),
        P("table"),
        P("replica", "table", None, None, None),
        P("replica", None, None),
        P("replica", "table", None),
        P(("replica", "table"), None),
        P(("replica", "table")),
        P("table", None),
        P("table", None),
        P(),
        P(),
    )
    return jax.shard_map(
        local,
        mesh=mesh,
        in_specs=placed,
        out_specs=(P(("replica", "table")), P("table", None), P("table")),
        check_vma=False,
    )
```

time: 153 us -> 117 us (0.76)
  between operations: 11.2 us -> 0.88 us
  local copies, waits for them, and re-layouts: 12.1 us -> 4.16 us
  Pallas kernels: 43.5 us -> 36.3 us
  other arithmetic: 6.7 us -> 0.43 us
  starting transfers between devices: 34.5 us -> 32 us
    pallas_call x1, Pallas kernels: 16.6 us -> 10.6 us  [pool(): pl.pallas_call(functools.partial(pool_kernel, shards), out_shape=jax.Shap...]
    another operation x5 -> x3, local copies, waits for them, and re-layouts: 5.82 us -> 0.02 us  [local(): jnp.stack([p[:block] for p in parcels])]
    dynamic_slice x5 -> x0, local copies, waits for them, and re-layouts: 4.87 us -> none  [the longest x2 1.86 us: gather_weights(): lax.dynamic_slice(w, start, (half, lanes))]
    unnamed x14 -> x24, local copies, waits for them, and re-layouts: 0.93 us -> 4.03 us
    ppermute x32 -> x21, starting transfers between devices: 19.3 us -> 16.5 us  [swap(): return lax.ppermute(array, 'replica', [(i, i ^ mask) for i in range(size)])]
    and x2 -> x0, other arithmetic: 2.58 us -> none  [local(): (slot >= starts[k]) & (slot < starts[k] + lives[k])]
    ppermute x12 -> x9, waiting for transfers between devices: 20.6 us -> 18 us  [shift(): lax.ppermute(array, 'table', [(i, (i + step) % size) for i in range(size)])]
    ppermute x32 -> x21, waiting for transfers between devices: 23.8 us -> 25.2 us  [swap(): return lax.ppermute(array, 'replica', [(i, i ^ mask) for i in range(size)])]
  transfers between devices with their start and end apart: 44 -> 30, of which waited for: 21 -> 21; matrix products, arithmetic and copies ran while one was open for 11% -> 0% of each run, Pallas kernels for 17% -> 14%
where the time goes in v3:
time: 117 us
  waiting for transfers between devices  43.2 us (37%)
  Pallas kernels  36.3 us (31%)
  starting transfers between devices  32 us (27%)
  local copies, waits for them, and re-layouts  4.16 us (4%)
    ppermute x21, waiting for transfers between devices, swap(): return lax.ppermute(array, 'replica', [(i, i ^ mask) for i in range(size)])  25.2 us
    ppermute x9, waiting for transfers between devices, shift(): lax.ppermute(array, 'table', [(i, (i + step) % size) for i in range(size)])  18 us
    ppermute x21, starting transfers between devices, swap(): return lax.ppermute(array, 'replica', [(i, i ^ mask) for i in range(size)])  16.5 us
    ppermute x9, starting transfers between devices, shift(): lax.ppermute(array, 'table', [(i, (i + step) % size) for i in range(size)])  15.5 us
    pallas_call x1, Pallas kernels, dense_step(): pl.pallas_call(functools.partial(dense_kernel, shards, replicas, copies),...  15.3 us
    pallas_call x1, Pallas kernels, pool(): pl.pallas_call(functools.partial(pool_kernel, shards), out_shape=jax.Shap...  10.6 us
    pallas_call x1, Pallas kernels, slots(): pl.pallas_call(functools.partial(slots_kernel, shards, replicas, batch),...  6.27 us
    unnamed x24, local copies, waits for them, and re-layouts  4.03 us
  transfers between devices with their start and end apart: 30, of which 21 were waited for; matrix products, arithmetic and copies ran while one was open for 0% of the time, Pallas kernels for 14%

profile of v3, /device:TPU:0, one launch (start us, length us, event | category | flops | bytes accessed | tf_op | source)
XLA Modules:
  0.0 117.0 jit_solution(13352026035147768253)
XLA Ops:
  0.6 2.8 %pack.1 = (f32[168,128]{1,0:T(8,128)}, f32[168,128]{1,0:T(8,128)}, f32[168,128]{1,0:T(8,128)}, bf16[864,128]{1,0:T(8,128)(2,1)}) custom-call(s32[1,1,4,4,1248]{4,3,2,1,0:T(4,128)} %look_rows.3, f32[1024,128]{1,0:T(8,128)} %own.1, bf16[864,512]{1,0:T(8,128)(2,1)} %refs_16_.1, bf16[864,512]{1,0:T(8,128)(2,1)} %refs_17_.1), custom_call_target="tpu_custom_call" | custom-call | tf_op jit(solution)/shard_map/pack/pallas_call | solution.py:120
  3.4 3.1 %collective-permute-start = (f32[168,128]{1,0:T(8,128)}, f32[168,128]{1,0:T(8,128)S(1)}, u32[]{:S(2)}, u32[]{:S(2)}) collective-permute-start(f32[168,128]{1,0:T(8,128)} %get-tuple-element.22), channel_id=1, source_target_pairs={{0,1},{1,2},{2,3},{3,0},{4,5},{5,6},{6,7},{7,4},{8,9},{9,10},{10,1... | collective-permute-start | bytes 258056 | tf_op jit(solution)/shard_map/ppermute | solution.py:28
  6.5 2.6 %collective-permute-start.1 = (f32[168,128]{1,0:T(8,128)}, f32[168,128]{1,0:T(8,128)S(1)}, u32[]{:S(2)}, u32[]{:S(2)}) collective-permute-start(f32[168,128]{1,0:T(8,128)} %get-tuple-element.23), channel_id=1, source_target_pairs={{0,2},{1,3},{2,0},{3,1},{4,6},{5,7},{6,4},{7,5},{8,10},{9,11},{10,... | collective-permute-start | bytes 258056 | tf_op jit(solution)/shard_map/ppermute | solution.py:28
  9.1 1.3 %collective-permute-start.2 = (f32[168,128]{1,0:T(8,128)}, f32[168,128]{1,0:T(8,128)S(1)}, u32[]{:S(2)}, u32[]{:S(2)}) collective-permute-start(f32[168,128]{1,0:T(8,128)} %get-tuple-element.24), channel_id=1, source_target_pairs={{0,3},{1,0},{2,1},{3,2},{4,7},{5,4},{6,5},{7,6},{8,11},{9,8},{10,9... | collective-permute-start | bytes 258056 | tf_op jit(solution)/shard_map/ppermute | solution.py:28
  10.4 1.5 %collective-permute-done.refs_0_ = f32[168,128]{1,0:T(8,128)S(1)} collective-permute-done((f32[168,128]{1,0:T(8,128)}, f32[168,128]{1,0:T(8,128)S(1)}, u32[]{:S(2)}, u32[]{:S(2)}) %collective-permute-start) | collective-permute-done | bytes 86048 | tf_op jit(solution)/shard_map/ppermute | solution.py:28
  11.9 3.1 %collective-permute-done.1.refs_1_ = f32[168,128]{1,0:T(8,128)S(1)} collective-permute-done((f32[168,128]{1,0:T(8,128)}, f32[168,128]{1,0:T(8,128)S(1)}, u32[]{:S(2)}, u32[]{:S(2)}) %collective-permute-start.1) | collective-permute-done | bytes 86048 | tf_op jit(solution)/shard_map/ppermute | solution.py:28
  15.3 1.6 %collective-permute-start.4 = (f32[3,128,128]{2,1,0:T(8,128)S(1)}, f32[3,128,128]{2,1,0:T(8,128)S(1)}, u32[]{:S(2)}, u32[]{:S(2)}) collective-permute-start(f32[3,128,128]{2,1,0:T(8,128)S(1)} %get-tuple-element.50), channel_id=1, source_target_pairs={{0,16},{4,20},{8,24},{12,28},{16,0},{20,4},{24,8},{28,12},{1,17},{... | collective-permute-start | bytes 589832 | tf_op jit(solution)/shard_map/ppermute | solution.py:23
  16.9 1.5 %collective-permute-start.3 = (f32[3,128,128]{2,1,0:T(8,128)S(1)}, f32[3,128,128]{2,1,0:T(8,128)S(1)}, u32[]{:S(2)}, u32[]{:S(2)}) collective-permute-start(f32[3,128,128]{2,1,0:T(8,128)S(1)} %get-tuple-element.50), channel_id=1, source_target_pairs={{0,8},{4,12},{8,0},{12,4},{16,24},{20,28},{24,16},{28,20},{1,9},{5... | collective-permute-start | bytes 589832 | tf_op jit(solution)/shard_map/ppermute | solution.py:23
  18.8 3.4 %collective-permute-start.8 = (bf16[864,128]{1,0:T(8,128)(2,1)}, bf16[864,128]{1,0:T(8,128)(2,1)S(1)}, u32[]{:S(2)}, u32[]{:S(2)}) collective-permute-start(bf16[864,128]{1,0:T(8,128)(2,1)} %get-tuple-element.26), channel_id=1, source_target_pairs={{0,3},{1,0},{2,1},{3,2},{4,7},{5,4},{6,5},{7,6},{8,11},{9,8},{10,9... | collective-permute-start | bytes 663560 | tf_op jit(solution)/shard_map/ppermute | solution.py:28
  22.4 1.9 %collective-permute-start.6 = (bf16[864,128]{1,0:T(8,128)(2,1)}, bf16[864,128]{1,0:T(8,128)(2,1)S(1)}, u32[]{:S(2)}, u32[]{:S(2)}) collective-permute-start(bf16[864,128]{1,0:T(8,128)(2,1)} %get-tuple-element.26), channel_id=1, source_target_pairs={{0,1},{1,2},{2,3},{3,0},{4,5},{5,6},{6,7},{7,4},{8,9},{9,10},{10,1... | collective-permute-start | bytes 663560 | tf_op jit(solution)/shard_map/ppermute | solution.py:28
  24.3 0.9 copy-done.3
  25.2 0.7 copy-done.5
  25.9 0.7 copy-done.7
  26.6 6.3 %slots.1 = (s32[1,1664]{1,0:T(1,128)S(1)}, bf16[16,1024,256]{2,1,0:T(8,128)(2,1)S(1)}) custom-call(s32[1,4,4]{2,1,0:T(4,128)S(1)} %copy-done.5, s32[1,1,4,4,1248]{4,3,2,1,0:T(4,128)S(1)} %copy-done.3, s32[1,1,3328]{2,1,0:T(1,128)S(1)} %copy-done.7, f32[168,128]{1,0:T(8,128)S(1)} %collective-permute-done.refs_0_, ...), custom_call_target="tpu_custom_call" | custom-call | flops 1000 | bytes 1000 | tf_op jit(solution)/shard_map/slots/pallas_call | solution.py:205
  33.0 8.3 %collective-permute-done.7 = bf16[864,128]{1,0:T(8,128)(2,1)S(1)} collective-permute-done((bf16[864,128]{1,0:T(8,128)(2,1)}, bf16[864,128]{1,0:T(8,128)(2,1)S(1)}, u32[]{:S(2)}, u32[]{:S(2)}) %collective-permute-start.7) | collective-permute-done | bytes 221216 | tf_op jit(solution)/shard_map/ppermute | solution.py:28
  41.4 1.5 %collective-permute-start.10 = (bf16[3,864,128]{2,1,0:T(8,128)(2,1)S(1)}, bf16[3,864,128]{2,1,0:T(8,128)(2,1)S(1)}, u32[]{:S(2)}, u32[]{:S(2)}) collective-permute-start(bf16[3,864,128]{2,1,0:T(8,128)(2,1)S(1)} %pad_maximum_fusion.1.refs_6_), channel_id=1, source_target_pairs={{0,16},{4,20},{8,24},{12,28},{16,0},{20,4},{24,8},{28,12},{1,17},{... | collective-permute-start | bytes 1990664 | tf_op jit(solution)/shard_map/ppermute | solution.py:23
  42.9 1.5 %collective-permute-start.9 = (bf16[3,864,128]{2,1,0:T(8,128)(2,1)S(1)}, bf16[3,864,128]{2,1,0:T(8,128)(2,1)S(1)}, u32[]{:S(2)}, u32[]{:S(2)}) collective-permute-start(bf16[3,864,128]{2,1,0:T(8,128)(2,1)S(1)} %pad_maximum_fusion.1.refs_6_), channel_id=1, source_target_pairs={{0,8},{4,12},{8,0},{12,4},{16,24},{20,28},{24,16},{28,20},{1,9},{5... | collective-permute-start | bytes 1990664 | tf_op jit(solution)/shard_map/ppermute | solution.py:23
  44.4 1.0 copy-done.2
  45.5 0.7 copy-done.6
  46.1 10.6 %pool.1.refs_1_ = bf16[3328,128]{1,0:T(8,128)(2,1)S(1)} custom-call(s32[1,4,4]{2,1,0:T(4,128)S(1)} %copy-done.6, s32[1,1664]{1,0:T(1,128)S(1)} %get-tuple-element.25.places, bf16[16,1024,256]{2,1,0:T(8,128)(2,1)S(1)} %get-tuple-element.31.counted.refs_5_, f32[1024,128]{1,0:T(8,128)S(1)} %copy-done.2, f32[4,3,128,128]{3,2,1,0:T(8,128)S(1)} %pad_maximum_fusion.even, ...), custom_call_target="tpu_custom_call" | custom-call | flops 1000 | bytes 1000 | tf_op jit(solution)/shard_map/pool/pallas_call | solution.py:271
  56.7 2.0 %collective-permute-done.10.refs_10_ = bf16[3,864,128]{2,1,0:T(8,128)(2,1)S(1)} collective-permute-done((bf16[3,864,128]{2,1,0:T(8,128)(2,1)S(1)}, bf16[3,864,128]{2,1,0:T(8,128)(2,1)S(1)}, u32[]{:S(2)}, u32[]{:S(2)}) %collective-permute-start.10) | collective-permute-done | bytes 663584 | tf_op jit(solution)/shard_map/ppermute | solution.py:23
  58.8 1.2 %collective-permute-done.9.refs_8_ = bf16[3,864,128]{2,1,0:T(8,128)(2,1)S(1)} collective-permute-done((bf16[3,864,128]{2,1,0:T(8,128)(2,1)S(1)}, bf16[3,864,128]{2,1,0:T(8,128)(2,1)S(1)}, u32[]{:S(2)}, u32[]{:S(2)}) %collective-permute-start.9) | collective-permute-done | bytes 663584 | tf_op jit(solution)/shard_map/ppermute | solution.py:23
  60.0 1.6 %collective-permute-start.17 = (bf16[3,432,128]{2,1,0:T(8,128)(2,1)S(1)}, bf16[3,432,128]{2,1,0:T(8,128)(2,1)S(1)}, u32[]{:S(2)}, u32[]{:S(2)}) collective-permute-start(bf16[3,432,128]{2,1,0:T(8,128)(2,1)S(1)} %slice.50), channel_id=1, source_target_pairs={{0,8},{4,12},{8,0},{12,4},{16,24},{20,28},{24,16},{28,20},{1,9},{5... | collective-permute-start | bytes 995336 | tf_op jit(solution)/shard_map/ppermute | solution.py:23
  61.6 0.6 collective-permute-start.15
  62.1 0.5 collective-permute-start.14
  62.6 6.5 %collective-permute-done.17.refs_14_ = bf16[3,432,128]{2,1,0:T(8,128)(2,1)S(1)} collective-permute-done((bf16[3,432,128]{2,1,0:T(8,128)(2,1)S(1)}, bf16[3,432,128]{2,1,0:T(8,128)(2,1)S(1)}, u32[]{:S(2)}, u32[]{:S(2)}) %collective-permute-start.17) | collective-permute-done | bytes 331808 | tf_op jit(solution)/shard_map/ppermute | solution.py:23
  69.2 1.3 %collective-permute-done.15.refs_12_ = bf16[3,432,128]{2,1,0:T(8,128)(2,1)S(1)} collective-permute-done((bf16[3,432,128]{2,1,0:T(8,128)(2,1)S(1)}, bf16[3,432,128]{2,1,0:T(8,128)(2,1)S(1)}, u32[]{:S(2)}, u32[]{:S(2)}) %collective-permute-start.15) | collective-permute-done | bytes 331808 | tf_op jit(solution)/shard_map/ppermute | solution.py:23
  70.8 1.3 %collective-permute-done.16.refs_13_ = bf16[3,432,128]{2,1,0:T(8,128)(2,1)S(1)} collective-permute-done((bf16[3,432,128]{2,1,0:T(8,128)(2,1)S(1)}, bf16[3,432,128]{2,1,0:T(8,128)(2,1)S(1)}, u32[]{:S(2)}, u32[]{:S(2)}) %collective-permute-start.16) | collective-permute-done | bytes 331808 | tf_op jit(solution)/shard_map/ppermute | solution.py:23
  72.2 15.3 %dense.1 = (f32[1,128]{1,0:T(1,128)}, bf16[4,4,128,128]{3,2,1,0:T(8,128)(2,1)S(1)}, bf16[4,4,128,128]{3,2,1,0:T(8,128)(2,1)S(1)}) custom-call(s32[1,4,4]{2,1,0:T(4,128)S(1)} %copy-done.6, s32[1,1664]{1,0:T(1,128)S(1)} %get-tuple-element.25.places, bf16[128,128]{1,0:T(8,128)(2,1)S(1)} %copy-done.4, bf16[3328,128]{1,0:T(8,128)(2,1)S(1)} %pool.1.refs_1_, ...), custom_call_target="tpu_custom_call" | custom-call | flops 4000000000 | bytes 30000000 | tf_op jit(solution)/shard_map/dense/pallas_call | solution.py:385
  87.5 1.8 %collective-permute-done.19 = bf16[4,4,128,128]{3,2,1,0:T(8,128)(2,1)S(1)} collective-permute-done((bf16[4,4,128,128]{3,2,1,0:T(8,128)(2,1)S(1)}, bf16[4,4,128,128]{3,2,1,0:T(8,128)(2,1)S(1)}, u32[]{:S(2)}, u32[]{:S(2)}) %collective-permute-start.19) | collective-permute-done | bytes 524320 | tf_op jit(solution)/shard_map/ppermute | solution.py:23
  89.6 0.7 collective-permute-start.20
  90.3 1.4 %collective-permute-start.22 = (bf16[1,4,128,128]{3,2,1,0:T(8,128)(2,1)S(1)}, bf16[1,4,128,128]{3,2,1,0:T(8,128)(2,1)S(1)}, u32[]{:S(2)}, u32[]{:S(2)}) collective-permute-start(bf16[1,4,128,128]{3,2,1,0:T(8,128)(2,1)S(1)} %get-tuple-element.44), channel_id=1, source_target_pairs={{0,24},{4,28},{8,16},{12,20},{16,8},{20,12},{24,0},{28,4},{1,25},{... | collective-permute-start | bytes 393224 | tf_op jit(solution)/shard_map/ppermute | solution.py:23
  91.7 1.5 %collective-permute-start.21 = (bf16[1,4,128,128]{3,2,1,0:T(8,128)(2,1)S(1)}, bf16[1,4,128,128]{3,2,1,0:T(8,128)(2,1)S(1)}, u32[]{:S(2)}, u32[]{:S(2)}) collective-permute-start(bf16[1,4,128,128]{3,2,1,0:T(8,128)(2,1)S(1)} %get-tuple-element.45), channel_id=1, source_target_pairs={{0,16},{4,20},{8,24},{12,28},{16,0},{20,4},{24,8},{28,12},{1,17},{... | collective-permute-start | bytes 393224 | tf_op jit(solution)/shard_map/ppermute | solution.py:23
  93.1 2.9 %collective-permute-done.20 = bf16[1,4,128,128]{3,2,1,0:T(8,128)(2,1)S(1)} collective-permute-done((bf16[1,4,128,128]{3,2,1,0:T(8,128)(2,1)S(1)}, bf16[1,4,128,128]{3,2,1,0:T(8,128)(2,1)S(1)}, u32[]{:S(2)}, u32[]{:S(2)}) %collective-permute-start.20) | collective-permute-done | bytes 131104 | tf_op jit(solution)/shard_map/ppermute | solution.py:23
  96.0 2.2 %collective-permute-done.22 = bf16[1,4,128,128]{3,2,1,0:T(8,128)(2,1)S(1)} collective-permute-done((bf16[1,4,128,128]{3,2,1,0:T(8,128)(2,1)S(1)}, bf16[1,4,128,128]{3,2,1,0:T(8,128)(2,1)S(1)}, u32[]{:S(2)}, u32[]{:S(2)}) %collective-permute-start.22) | collective-permute-done | bytes 131104 | tf_op jit(solution)/shard_map/ppermute | solution.py:23
  98.2 1.4 %collective-permute-done.21 = bf16[1,4,128,128]{3,2,1,0:T(8,128)(2,1)S(1)} collective-permute-done((bf16[1,4,128,128]{3,2,1,0:T(8,128)(2,1)S(1)}, bf16[1,4,128,128]{3,2,1,0:T(8,128)(2,1)S(1)}, u32[]{:S(2)}, u32[]{:S(2)}) %collective-permute-start.21) | collective-permute-done | bytes 131104 | tf_op jit(solution)/shard_map/ppermute | solution.py:23
  99.7 2.0 %collective-permute-start.25 = (f32[128,128]{1,0:T(8,128)S(1)}, f32[128,128]{1,0:T(8,128)S(1)}, u32[]{:S(2)}, u32[]{:S(2)}) collective-permute-start(f32[128,128]{1,0:T(8,128)S(1)} %get-tuple-element.47), channel_id=1, source_target_pairs={{0,1},{1,2},{2,3},{3,0},{4,5},{5,6},{6,7},{7,4},{8,9},{9,10},{10,1... | collective-permute-start | bytes 196616 | tf_op jit(solution)/shard_map/ppermute | solution.py:28
  101.7 0.9 collective-permute-start.24
  102.6 2.8 %collective-permute-done.23 = f32[128,128]{1,0:T(8,128)S(1)} collective-permute-done((f32[128,128]{1,0:T(8,128)S(1)}, f32[128,128]{1,0:T(8,128)S(1)}, u32[]{:S(2)}, u32[]{:S(2)}) %collective-permute-start.23) | collective-permute-done | bytes 65568 | tf_op jit(solution)/shard_map/ppermute | solution.py:28
  105.4 0.7 collective-permute-done.25
  106.1 1.4 %collective-permute-done.24 = f32[128,128]{1,0:T(8,128)S(1)} collective-permute-done((f32[128,128]{1,0:T(8,128)S(1)}, f32[128,128]{1,0:T(8,128)S(1)}, u32[]{:S(2)}, u32[]{:S(2)}) %collective-permute-start.24) | collective-permute-done | bytes 65568 | tf_op jit(solution)/shard_map/ppermute | solution.py:28
  107.5 1.6 %collective-permute-start.28 = (f32[128,128]{1,0:T(8,128)S(1)}, f32[128,128]{1,0:T(8,128)S(1)}, u32[]{:S(2)}, u32[]{:S(2)}) collective-permute-start(f32[128,128]{1,0:T(8,128)S(1)} %fusion.5), channel_id=1, source_target_pairs={{0,24},{4,28},{8,16},{12,20},{16,8},{20,12},{24,0},{28,4},{1,25},{... | collective-permute-start | bytes 196616 | tf_op jit(solution)/shard_map/ppermute | solution.py:23
  109.1 0.6 collective-permute-start.27
  109.7 1.4 %collective-permute-start.26 = (f32[128,128]{1,0:T(8,128)S(1)}, f32[128,128]{1,0:T(8,128)S(1)}, u32[]{:S(2)}, u32[]{:S(2)}) collective-permute-start(f32[128,128]{1,0:T(8,128)S(1)} %fusion.5), channel_id=1, source_target_pairs={{0,8},{4,12},{8,0},{12,4},{16,24},{20,28},{24,16},{28,20},{1,9},{5... | collective-permute-start | bytes 196616 | tf_op jit(solution)/shard_map/ppermute | solution.py:23
  111.1 2.1 %collective-permute-done.28 = f32[128,128]{1,0:T(8,128)S(1)} collective-permute-done((f32[128,128]{1,0:T(8,128)S(1)}, f32[128,128]{1,0:T(8,128)S(1)}, u32[]{:S(2)}, u32[]{:S(2)}) %collective-permute-start.28) | collective-permute-done | bytes 65568 | tf_op jit(solution)/shard_map/ppermute | solution.py:23
  113.2 0.5 collective-permute-done.27
  114.0 1.5 %collective-permute-done.29.odd = f32[4,128,128]{2,1,0:T(8,128)S(1)} collective-permute-done((f32[4,128,128]{2,1,0:T(8,128)S(1)}, f32[4,128,128]{2,1,0:T(8,128)S(1)}, u32[]{:S(2)}, u32[]{:S(2)}) %collective-permute-start.29) | collective-permute-done | bytes 262176 | tf_op jit(solution)/shard_map/ppermute | solution.py:23
  115.6 1.4 %finish.1 = (f32[1024,128]{1,0:T(8,128)}, f32[8,128]{1,0:T(8,128)}) custom-call(f32[8,128]{1,0:T(8,128)S(1)} %bitcast.54, f32[4,128,128]{2,1,0:T(8,128)S(1)} %pad_maximum_fusion.2.even, f32[4,128,128]{2,1,0:T(8,128)S(1)} %collective-permute-done.29.odd), custom_call_target="tpu_custom_call" | custom-call | tf_op jit(solution)/shard_map/finish/pallas_call | solution.py:492
  (57 shorter events, 2.1 us)
Async XLA Ops:
  3.4 8.5 %collective-permute-start = (f32[168,128]{1,0:T(8,128)}, f32[168,128]{1,0:T(8,128)S(1)}, u32[]{:S(2)}, u32[]{:S(2)}) collective-permute-start(f32[168,128]{1,0:T(8,128)} %get-tuple-element.22), channel_id=1, source_target_pairs={{0,1},{1,2},{2,3},{3,0},{4,5},{5,6},{6,7},{7,4},{8,9},{9,10},{10,1... | collective-permute-start | bytes 258056 | tf_op jit(solution)/shard_map/ppermute | solution.py:28
  6.5 8.6 %collective-permute-start.1 = (f32[168,128]{1,0:T(8,128)}, f32[168,128]{1,0:T(8,128)S(1)}, u32[]{:S(2)}, u32[]{:S(2)}) collective-permute-start(f32[168,128]{1,0:T(8,128)} %get-tuple-element.23), channel_id=1, source_target_pairs={{0,2},{1,3},{2,0},{3,1},{4,6},{5,7},{6,4},{7,5},{8,10},{9,11},{10,... | collective-permute-start | bytes 258056 | tf_op jit(solution)/shard_map/ppermute | solution.py:28
  9.1 6.2 %collective-permute-start.2 = (f32[168,128]{1,0:T(8,128)}, f32[168,128]{1,0:T(8,128)S(1)}, u32[]{:S(2)}, u32[]{:S(2)}) collective-permute-start(f32[168,128]{1,0:T(8,128)} %get-tuple-element.24), channel_id=1, source_target_pairs={{0,3},{1,0},{2,1},{3,2},{4,7},{5,4},{6,5},{7,6},{8,11},{9,8},{10,9... | collective-permute-start | bytes 258056 | tf_op jit(solution)/shard_map/ppermute | solution.py:28
  11.9 58.6 %copy-start.10 = (f32[3456]{0:T(1024)S(1)}, f32[3456]{0:T(1024)}, u32[]{:S(2)}) copy-start(f32[3456]{0:T(1024)} %param.20) | copy-start | bytes 41476
  11.9 58.6 %copy-start.11 = (f32[3456]{0:T(1024)S(1)}, f32[3456]{0:T(1024)}, u32[]{:S(2)}) copy-start(f32[3456]{0:T(1024)} %param.21) | copy-start | bytes 41476
  15.0 57.1 %copy-start.4 = (bf16[128,128]{1,0:T(8,128)(2,1)S(1)}, bf16[128,128]{1,0:T(8,128)(2,1)}, u32[]{:S(2)}) copy-start(bf16[128,128]{1,0:T(8,128)(2,1)} %refs_0_.3) | copy-start | bytes 98308
  15.0 57.1 %copy-start.9 = (s32[128]{0:T(128)S(1)}, s32[128]{0:T(128)}, u32[]{:S(2)}) copy-start(s32[128]{0:T(128)} %param.17) | copy-start | bytes 1540
  15.0 57.1 %copy-start = (bf16[864,512]{1,0:T(8,128)(2,1)S(1)}, bf16[864,512]{1,0:T(8,128)(2,1)}, u32[]{:S(2)}) copy-start(bf16[864,512]{1,0:T(8,128)(2,1)} %refs_16_.1) | copy-start | bytes 2654212
  15.1 57.1 %copy-start.1 = (bf16[864,512]{1,0:T(8,128)(2,1)S(1)}, bf16[864,512]{1,0:T(8,128)(2,1)}, u32[]{:S(2)}) copy-start(bf16[864,512]{1,0:T(8,128)(2,1)} %refs_17_.1) | copy-start | bytes 2654212
  15.3 7.1 %collective-permute-start.4 = (f32[3,128,128]{2,1,0:T(8,128)S(1)}, f32[3,128,128]{2,1,0:T(8,128)S(1)}, u32[]{:S(2)}, u32[]{:S(2)}) collective-permute-start(f32[3,128,128]{2,1,0:T(8,128)S(1)} %get-tuple-element.50), channel_id=1, source_target_pairs={{0,16},{4,20},{8,24},{12,28},{16,0},{20,4},{24,8},{28,12},{1,17},{... | collective-permute-start | bytes 589832 | tf_op jit(solution)/shard_map/ppermute | solution.py:23
  16.9 16.0 %collective-permute-start.3 = (f32[3,128,128]{2,1,0:T(8,128)S(1)}, f32[3,128,128]{2,1,0:T(8,128)S(1)}, u32[]{:S(2)}, u32[]{:S(2)}) collective-permute-start(f32[3,128,128]{2,1,0:T(8,128)S(1)} %get-tuple-element.50), channel_id=1, source_target_pairs={{0,8},{4,12},{8,0},{12,4},{16,24},{20,28},{24,16},{28,20},{1,9},{5... | collective-permute-start | bytes 589832 | tf_op jit(solution)/shard_map/ppermute | solution.py:23
  18.3 14.6 %collective-permute-start.5 = (f32[3,128,128]{2,1,0:T(8,128)S(1)}, f32[3,128,128]{2,1,0:T(8,128)S(1)}, u32[]{:S(2)}, u32[]{:S(2)}) collective-permute-start(f32[3,128,128]{2,1,0:T(8,128)S(1)} %get-tuple-element.50), channel_id=1, source_target_pairs={{0,24},{4,28},{8,16},{12,20},{16,8},{20,12},{24,0},{28,4},{1,25},{... | collective-permute-start | bytes 589832 | tf_op jit(solution)/shard_map/ppermute | solution.py:23
  18.8 14.1 %collective-permute-start.8 = (bf16[864,128]{1,0:T(8,128)(2,1)}, bf16[864,128]{1,0:T(8,128)(2,1)S(1)}, u32[]{:S(2)}, u32[]{:S(2)}) collective-permute-start(bf16[864,128]{1,0:T(8,128)(2,1)} %get-tuple-element.26), channel_id=1, source_target_pairs={{0,3},{1,0},{2,1},{3,2},{4,7},{5,4},{6,5},{7,6},{8,11},{9,8},{10,9... | collective-permute-start | bytes 663560 | tf_op jit(solution)/shard_map/ppermute | solution.py:28
  22.2 19.1 %collective-permute-start.7 = (bf16[864,128]{1,0:T(8,128)(2,1)}, bf16[864,128]{1,0:T(8,128)(2,1)S(1)}, u32[]{:S(2)}, u32[]{:S(2)}) collective-permute-start(bf16[864,128]{1,0:T(8,128)(2,1)} %get-tuple-element.26), channel_id=1, source_target_pairs={{0,2},{1,3},{2,0},{3,1},{4,6},{5,7},{6,4},{7,5},{8,10},{9,11},{10,... | collective-permute-start | bytes 663560 | tf_op jit(solution)/shard_map/ppermute | solution.py:28
  22.4 18.9 %collective-permute-start.6 = (bf16[864,128]{1,0:T(8,128)(2,1)}, bf16[864,128]{1,0:T(8,128)(2,1)S(1)}, u32[]{:S(2)}, u32[]{:S(2)}) collective-permute-start(bf16[864,128]{1,0:T(8,128)(2,1)} %get-tuple-element.26), channel_id=1, source_target_pairs={{0,1},{1,2},{2,3},{3,0},{4,5},{5,6},{6,7},{7,4},{8,9},{9,10},{10,1... | collective-permute-start | bytes 663560 | tf_op jit(solution)/shard_map/ppermute | solution.py:28
  24.3 0.9 copy-start.3
  25.2 0.7 copy-start.5
  25.9 0.7 copy-start.7
  41.3 3.1 %collective-permute-start.11 = (f32[4,3,128,128]{3,2,1,0:T(8,128)S(1)}, f32[4,3,128,128]{3,2,1,0:T(8,128)S(1)}, u32[]{:S(2)}, u32[]{:S(2)}) collective-permute-start(f32[4,3,128,128]{3,2,1,0:T(8,128)S(1)} %pad_maximum_fusion.even), channel_id=1, source_target_pairs={{0,4},{4,0},{8,12},{12,8},{16,20},{20,16},{24,28},{28,24},{1,5},{5... | collective-permute-start | bytes 2359304 | tf_op jit(solution)/shard_map/ppermute | solution.py:23
  41.4 17.4 %collective-permute-start.10 = (bf16[3,864,128]{2,1,0:T(8,128)(2,1)S(1)}, bf16[3,864,128]{2,1,0:T(8,128)(2,1)S(1)}, u32[]{:S(2)}, u32[]{:S(2)}) collective-permute-start(bf16[3,864,128]{2,1,0:T(8,128)(2,1)S(1)} %pad_maximum_fusion.1.refs_6_), channel_id=1, source_target_pairs={{0,16},{4,20},{8,24},{12,28},{16,0},{20,4},{24,8},{28,12},{1,17},{... | collective-permute-start | bytes 1990664 | tf_op jit(solution)/shard_map/ppermute | solution.py:23
  42.9 17.0 %collective-permute-start.9 = (bf16[3,864,128]{2,1,0:T(8,128)(2,1)S(1)}, bf16[3,864,128]{2,1,0:T(8,128)(2,1)S(1)}, u32[]{:S(2)}, u32[]{:S(2)}) collective-permute-start(bf16[3,864,128]{2,1,0:T(8,128)(2,1)S(1)} %pad_maximum_fusion.1.refs_6_), channel_id=1, source_target_pairs={{0,8},{4,12},{8,0},{12,4},{16,24},{20,28},{24,16},{28,20},{1,9},{5... | collective-permute-start | bytes 1990664 | tf_op jit(solution)/shard_map/ppermute | solution.py:23
  44.4 26.1 %collective-permute-start.12 = (bf16[3,864,128]{2,1,0:T(8,128)(2,1)S(1)}, bf16[3,864,128]{2,1,0:T(8,128)(2,1)S(1)}, u32[]{:S(2)}, u32[]{:S(2)}) collective-permute-start(bf16[3,864,128]{2,1,0:T(8,128)(2,1)S(1)} %pad_maximum_fusion.1.refs_6_), channel_id=1, source_target_pairs={{0,4},{4,0},{8,12},{12,8},{16,20},{20,16},{24,28},{28,24},{1,5},{5... | collective-permute-start | bytes 1990664 | tf_op jit(solution)/shard_map/ppermute | solution.py:23
  44.4 1.0 copy-start.2
  45.5 0.7 copy-start.6
  60.0 9.2 %collective-permute-start.17 = (bf16[3,432,128]{2,1,0:T(8,128)(2,1)S(1)}, bf16[3,432,128]{2,1,0:T(8,128)(2,1)S(1)}, u32[]{:S(2)}, u32[]{:S(2)}) collective-permute-start(bf16[3,432,128]{2,1,0:T(8,128)(2,1)S(1)} %slice.50), channel_id=1, source_target_pairs={{0,8},{4,12},{8,0},{12,4},{16,24},{20,28},{24,16},{28,20},{1,9},{5... | collective-permute-start | bytes 995336 | tf_op jit(solution)/shard_map/ppermute | solution.py:23
  61.6 8.9 %collective-permute-start.15 = (bf16[3,432,128]{2,1,0:T(8,128)(2,1)S(1)}, bf16[3,432,128]{2,1,0:T(8,128)(2,1)S(1)}, u32[]{:S(2)}, u32[]{:S(2)}) collective-permute-start(bf16[3,432,128]{2,1,0:T(8,128)(2,1)S(1)} %slice.49), channel_id=1, source_target_pairs={{0,16},{4,20},{8,24},{12,28},{16,0},{20,4},{24,8},{28,12},{1,17},{... | collective-permute-start | bytes 995336 | tf_op jit(solution)/shard_map/ppermute | solution.py:23
  62.1 10.0 %collective-permute-start.13 = (bf16[3,864,128]{2,1,0:T(8,128)(2,1)S(1)}, bf16[3,864,128]{2,1,0:T(8,128)(2,1)S(1)}, u32[]{:S(2)}, u32[]{:S(2)}) collective-permute-start(bf16[3,864,128]{2,1,0:T(8,128)(2,1)S(1)} %collective-permute-done.9.refs_8_), channel_id=1, source_target_pairs={{0,4},{4,0},{8,12},{12,8},{16,20},{20,16},{24,28},{28,24},{1,5},{5... | collective-permute-start | bytes 1990664 | tf_op jit(solution)/shard_map/ppermute | solution.py:23
  62.1 10.0 %collective-permute-start.14 = (bf16[3,864,128]{2,1,0:T(8,128)(2,1)S(1)}, bf16[3,864,128]{2,1,0:T(8,128)(2,1)S(1)}, u32[]{:S(2)}, u32[]{:S(2)}) collective-permute-start(bf16[3,864,128]{2,1,0:T(8,128)(2,1)S(1)} %collective-permute-done.10.refs_10_), channel_id=1, source_target_pairs={{0,4},{4,0},{8,12},{12,8},{16,20},{20,16},{24,28},{28,24},{1,5},{5... | collective-permute-start | bytes 1990664 | tf_op jit(solution)/shard_map/ppermute | solution.py:23
  69.2 1.6 %collective-permute-start.18 = (bf16[3,432,128]{2,1,0:T(8,128)(2,1)S(1)}, bf16[3,432,128]{2,1,0:T(8,128)(2,1)S(1)}, u32[]{:S(2)}, u32[]{:S(2)}) collective-permute-start(bf16[3,432,128]{2,1,0:T(8,128)(2,1)S(1)} %collective-permute-done.17.refs_14_), channel_id=1, source_target_pairs={{0,4},{4,0},{8,12},{12,8},{16,20},{20,16},{24,28},{28,24},{1,5},{5... | collective-permute-start | bytes 995336 | tf_op jit(solution)/shard_map/ppermute | solution.py:23
  70.5 1.6 %collective-permute-start.16 = (bf16[3,432,128]{2,1,0:T(8,128)(2,1)S(1)}, bf16[3,432,128]{2,1,0:T(8,128)(2,1)S(1)}, u32[]{:S(2)}, u32[]{:S(2)}) collective-permute-start(bf16[3,432,128]{2,1,0:T(8,128)(2,1)S(1)} %collective-permute-done.15.refs_12_), channel_id=1, source_target_pairs={{0,4},{4,0},{8,12},{12,8},{16,20},{20,16},{24,28},{28,24},{1,5},{5... | collective-permute-start | bytes 995336 | tf_op jit(solution)/shard_map/ppermute | solution.py:23
  72.1 43.4 %copy-start.8 = (f32[1024]{0:T(1024)S(1)}, f32[1024]{0:T(1024)}, u32[]{:S(2)}) copy-start(f32[1024]{0:T(1024)} %param.12) | copy-start | bytes 12292
  87.5 1.9 %collective-permute-start.19 = (bf16[4,4,128,128]{3,2,1,0:T(8,128)(2,1)S(1)}, bf16[4,4,128,128]{3,2,1,0:T(8,128)(2,1)S(1)}, u32[]{:S(2)}, u32[]{:S(2)}) collective-permute-start(bf16[4,4,128,128]{3,2,1,0:T(8,128)(2,1)S(1)} %get-tuple-element.38), channel_id=1, source_target_pairs={{0,4},{4,0},{8,12},{12,8},{16,20},{20,16},{24,28},{28,24},{1,5},{5... | collective-permute-start | bytes 1572872 | tf_op jit(solution)/shard_map/ppermute | solution.py:23
  89.6 6.4 %collective-permute-start.20 = (bf16[1,4,128,128]{3,2,1,0:T(8,128)(2,1)S(1)}, bf16[1,4,128,128]{3,2,1,0:T(8,128)(2,1)S(1)}, u32[]{:S(2)}, u32[]{:S(2)}) collective-permute-start(bf16[1,4,128,128]{3,2,1,0:T(8,128)(2,1)S(1)} %get-tuple-element.43), channel_id=1, source_target_pairs={{0,8},{4,12},{8,0},{12,4},{16,24},{20,28},{24,16},{28,20},{1,9},{5... | collective-permute-start | bytes 393224 | tf_op jit(solution)/shard_map/ppermute | solution.py:23
  90.3 7.9 %collective-permute-start.22 = (bf16[1,4,128,128]{3,2,1,0:T(8,128)(2,1)S(1)}, bf16[1,4,128,128]{3,2,1,0:T(8,128)(2,1)S(1)}, u32[]{:S(2)}, u32[]{:S(2)}) collective-permute-start(bf16[1,4,128,128]{3,2,1,0:T(8,128)(2,1)S(1)} %get-tuple-element.44), channel_id=1, source_target_pairs={{0,24},{4,28},{8,16},{12,20},{16,8},{20,12},{24,0},{28,4},{1,25},{... | collective-permute-start | bytes 393224 | tf_op jit(solution)/shard_map/ppermute | solution.py:23
  91.7 7.8 %collective-permute-start.21 = (bf16[1,4,128,128]{3,2,1,0:T(8,128)(2,1)S(1)}, bf16[1,4,128,128]{3,2,1,0:T(8,128)(2,1)S(1)}, u32[]{:S(2)}, u32[]{:S(2)}) collective-permute-start(bf16[1,4,128,128]{3,2,1,0:T(8,128)(2,1)S(1)} %get-tuple-element.45), channel_id=1, source_target_pairs={{0,16},{4,20},{8,24},{12,28},{16,0},{20,4},{24,8},{28,12},{1,17},{... | collective-permute-start | bytes 393224 | tf_op jit(solution)/shard_map/ppermute | solution.py:23
  99.6 5.8 %collective-permute-start.23 = (f32[128,128]{1,0:T(8,128)S(1)}, f32[128,128]{1,0:T(8,128)S(1)}, u32[]{:S(2)}, u32[]{:S(2)}) collective-permute-start(f32[128,128]{1,0:T(8,128)S(1)} %get-tuple-element.46), channel_id=1, source_target_pairs={{0,3},{1,0},{2,1},{3,2},{4,7},{5,4},{6,5},{7,6},{8,11},{9,8},{10,9... | collective-permute-start | bytes 196616 | tf_op jit(solution)/shard_map/ppermute | solution.py:28
  99.7 6.4 %collective-permute-start.25 = (f32[128,128]{1,0:T(8,128)S(1)}, f32[128,128]{1,0:T(8,128)S(1)}, u32[]{:S(2)}, u32[]{:S(2)}) collective-permute-start(f32[128,128]{1,0:T(8,128)S(1)} %get-tuple-element.47), channel_id=1, source_target_pairs={{0,1},{1,2},{2,3},{3,0},{4,5},{5,6},{6,7},{7,4},{8,9},{9,10},{10,1... | collective-permute-start | bytes 196616 | tf_op jit(solution)/shard_map/ppermute | solution.py:28
  101.7 5.8 %collective-permute-start.24 = (f32[128,128]{1,0:T(8,128)S(1)}, f32[128,128]{1,0:T(8,128)S(1)}, u32[]{:S(2)}, u32[]{:S(2)}) collective-permute-start(f32[128,128]{1,0:T(8,128)S(1)} %get-tuple-element.48), channel_id=1, source_target_pairs={{0,2},{1,3},{2,0},{3,1},{4,6},{5,7},{6,4},{7,5},{8,10},{9,11},{10,... | collective-permute-start | bytes 196616 | tf_op jit(solution)/shard_map/ppermute | solution.py:28
  107.5 5.7 %collective-permute-start.28 = (f32[128,128]{1,0:T(8,128)S(1)}, f32[128,128]{1,0:T(8,128)S(1)}, u32[]{:S(2)}, u32[]{:S(2)}) collective-permute-start(f32[128,128]{1,0:T(8,128)S(1)} %fusion.5), channel_id=1, source_target_pairs={{0,24},{4,28},{8,16},{12,20},{16,8},{20,12},{24,0},{28,4},{1,25},{... | collective-permute-start | bytes 196616 | tf_op jit(solution)/shard_map/ppermute | solution.py:23
  109.1 4.7 %collective-permute-start.27 = (f32[128,128]{1,0:T(8,128)S(1)}, f32[128,128]{1,0:T(8,128)S(1)}, u32[]{:S(2)}, u32[]{:S(2)}) collective-permute-start(f32[128,128]{1,0:T(8,128)S(1)} %fusion.5), channel_id=1, source_target_pairs={{0,16},{4,20},{8,24},{12,28},{16,0},{20,4},{24,8},{28,12},{1,17},{... | collective-permute-start | bytes 196616 | tf_op jit(solution)/shard_map/ppermute | solution.py:23
  109.7 4.3 %collective-permute-start.26 = (f32[128,128]{1,0:T(8,128)S(1)}, f32[128,128]{1,0:T(8,128)S(1)}, u32[]{:S(2)}, u32[]{:S(2)}) collective-permute-start(f32[128,128]{1,0:T(8,128)S(1)} %fusion.5), channel_id=1, source_target_pairs={{0,8},{4,12},{8,0},{12,4},{16,24},{20,28},{24,16},{28,20},{1,9},{5... | collective-permute-start | bytes 196616 | tf_op jit(solution)/shard_map/ppermute | solution.py:23
  114.0 1.6 %collective-permute-start.29 = (f32[4,128,128]{2,1,0:T(8,128)S(1)}, f32[4,128,128]{2,1,0:T(8,128)S(1)}, u32[]{:S(2)}, u32[]{:S(2)}) collective-permute-start(f32[4,128,128]{2,1,0:T(8,128)S(1)} %pad_maximum_fusion.2.even), channel_id=1, source_target_pairs={{0,4},{4,0},{8,12},{12,8},{16,20},{20,16},{24,28},{28,24},{1,5},{5... | collective-permute-start | bytes 786440 | tf_op jit(solution)/shard_map/ppermute | solution.py:23

commit v4 on v3

--- a/solution.py
+++ b/solution.py
@@ -23,9 +23,9 @@
     return lax.ppermute(array, "replica", [(i, i ^ mask) for i in range(size)])
 
 
-def shift(array, step):
+def cross_over(array, mask):
     size = lax.axis_size("table")
-    return lax.ppermute(array, "table", [(i, (i + step) % size) for i in range(size)])
+    return lax.ppermute(array, "table", [(i, i ^ mask) for i in range(size)])
 
 
 def mask_stages(size):
@@ -64,7 +64,7 @@
 
 def slot_range(live_counts, shards, j):
     here = lax.axis_index("table")
-    source = lax.rem(here - j + shards, shards)
+    source = here ^ j
     start = jnp.int32(0)
     for s in range(shards):
         start = start + jnp.where(s < source, live_counts[0, here, s], 0)
@@ -77,7 +77,8 @@
     width = table.shape[1]
     capacity = look_rows.shape[4]
     lines = -(-capacity // width)
-    block = parcels[0].shape[0] - HOT * lines
+    paired = HOT // 2 * lines
+    block = parcels[0].shape[0] - paired
     mine, here = lax.axis_index("replica"), lax.axis_index("table")
     rows = table.at[pl.ds(pl.multiple_of(mine * block, block), block), :]
     copies = [
@@ -96,16 +97,18 @@
     for copy in copies:
         copy.start()
     for i, parcel in enumerate(parcels):
-        owner = lax.rem(here + i + 1, shards)
-        for h in range(HOT):
+        owner = here ^ (i + 1)
+        for pair in range(HOT // 2):
             for q in range(lines):
-                line = block + h * lines + q
+                line = block + pair * lines + q
                 size = min(width, capacity - q * width)
                 if size < width:
                     parcel[line : line + 1, :] = jnp.zeros((1, width), F32)
-                parcel[line : line + 1, :size] = look_rows[
-                    0, 0, owner, h : h + 1, q * width : q * width + size
-                ].astype(F32)
+                at = slice(q * width, q * width + size)
+                value = (look_rows[0, 0, owner, 2 * pair : 2 * pair + 1, at] << ID_BITS) | (
+                    look_rows[0, 0, owner, 2 * pair + 1 : 2 * pair + 2, at]
+                )
+                parcel[line : line + 1, :size] = value.astype(F32)
     for copy in copies:
         copy.wait()
 
@@ -113,16 +116,15 @@
 def pack(look_rows, table, factors, shards, replicas):
     rows, width = table.shape
     capacity = look_rows.shape[4]
-    lines = -(-capacity // width)
-    parcel = jax.ShapeDtypeStruct((rows // replicas + HOT * lines, width), F32)
+    lines = HOT // 2 * -(-capacity // width)
+    parcel = jax.ShapeDtypeStruct((rows // replicas + lines, width), F32)
     blocks = [jax.ShapeDtypeStruct((f.shape[0], width), BF16) for f in factors[:1]]
-    count = shards - 1 + len(factors)
     return pl.pallas_call(
         functools.partial(pack_kernel, shards, factors),
         out_shape=[parcel] * (shards - 1) + blocks,
         in_specs=[whole()] + [whole(pltpu.HBM)] * (1 + len(factors)),
         out_specs=[whole()] * (shards - 1 + len(blocks)),
-        scratch_shapes=[pltpu.SemaphoreType.DMA((count,))],
+        scratch_shapes=[pltpu.SemaphoreType.DMA((shards - 1 + len(factors),))],
         compiler_params=pltpu.CompilerParams(vmem_limit_bytes=PACK_LIMIT),
         name="pack",
     )(look_rows, table, *factors)
@@ -154,22 +156,24 @@
             for q in range(lines):
                 size = min(width, capacity - q * width)
 
-                def line(h, j=j, q=q, size=size):
-                    if j == 0:
-                        return look_rows[0, 0, here, h : h + 1, q * width : q * width + size]
-                    at = block + h * lines + q
-                    return parcels[j - 1][at : at + 1, :size].astype(jnp.int32)
-
-                shifted[pair : pair + 1, q * width : q * width + size] = line(2 * pair) | (
-                    line(2 * pair + 1) << ID_BITS
-                )
+                at = slice(q * width, q * width + size)
+                if j == 0:
+                    own = [look_rows[0, 0, here, 2 * pair + h : 2 * pair + h + 1, at] for h in (0, 1)]
+                    value = (own[0] << ID_BITS) | own[1]
+                else:
+                    line = block + pair * lines + q
+                    value = parcels[j - 1][line : line + 1, :size].astype(jnp.int32)
+                shifted[pair : pair + 1, at] = value
         moved = pltpu.roll(shifted[...], start, 1)[:, :bags]
         inside = (slot >= start) & (slot < start + live)
         words[...] = jnp.where(inside, moved, words[...] if j else 0)
     order = bag_order[0]
     sample = quotient(order, bags // batch, bags)
     dest = (order - sample * (bags // batch)) * batch + sample
-    places[...] = dest[:, : bags // 2] | (dest[:, bags // 2 :] << 16)
+    for q in range(bags // CHUNK):
+        one = dest[:, q * CHUNK : q * CHUNK + CHUNK // 2]
+        two = dest[:, q * CHUNK + CHUNK // 2 : (q + 1) * CHUNK]
+        places[:, q * CHUNK // 2 : (q + 1) * CHUNK // 2] = one | (two << 16)
 
     flip = lax.axis_index("replica") * block
     low = lax.broadcasted_iota(jnp.int32, (LOW, CHUNK), 0)
@@ -220,10 +224,13 @@
     )(live_counts, look_rows, bag_order, *parcels)
 
 
-def pool_kernel(shards, live_counts, places, counted, own, even, odd, out, table, sums, pooled):
+def pool_kernel(
+    shards, live_counts, places, counted, own, even, odd, dense, head, cross, scaled, table, sums, pooled
+):
     rows_dev, width = own.shape
     block = even.shape[2]
-    middle = sums.shape[0] // 2
+    batch = dense.shape[0]
+    half = CHUNK // 2
     mine = lax.axis_index("replica")
 
     def put(shard, rows, value):
@@ -252,27 +259,32 @@
         lax.fori_loop(start // CHUNK, (start + live + CHUNK - 1) // CHUNK, pair, 0)
 
     def group(i, _):
+        k0 = i * UNROLL
+        k0 = k0 + lax.div(k0, half) * half
         for u in range(UNROLL):
-            k = i * UNROLL + u
-            word = places[0, k]
-            pooled[pl.ds(word & 0xFFFF, 1), :] = sums[pl.ds(k, 1), :]
-            pooled[pl.ds(lax.shift_right_logical(word, 16), 1), :] = sums[pl.ds(k + middle, 1), :]
+            word = places[0, i * UNROLL + u]
+            pooled[pl.ds(word & 0xFFFF, 1), :] = sums[pl.ds(k0 + u, 1), :]
+            pooled[pl.ds(lax.shift_right_logical(word, 16), 1), :] = sums[pl.ds(k0 + u + half, 1), :]
         return 0
 
-    lax.fori_loop(0, middle // UNROLL, group, 0)
-    out[...] = pooled[...].astype(BF16)
-
-
-def pool(live_counts, places, counted, own, pieces):
+    lax.fori_loop(0, sums.shape[0] // (2 * UNROLL), group, 0)
+    for f in range(cross.shape[1] // width):
+        at = slice(f * width, (f + 1) * width)
+        block = dense[...] if f == 0 else pooled[(f - 1) * batch : f * batch, :].astype(BF16)
+        cross[:, at] = block
+        scaled[:, at] = (block.astype(F32) * head[:, at]).astype(BF16)
+
+
+def pool(live_counts, places, counted, own, pieces, dense, head):
     rows, width = own.shape
     bags = 2 * places.shape[1]
     shards = pieces[0].shape[1] + 1
     smem = whole(pltpu.SMEM)
     return pl.pallas_call(
         functools.partial(pool_kernel, shards),
-        out_shape=jax.ShapeDtypeStruct((bags, width), BF16),
-        in_specs=[smem, smem] + [whole()] * 4,
-        out_specs=whole(),
+        out_shape=[jax.ShapeDtypeStruct((dense.shape[0], head.shape[1]), BF16)] * 2,
+        in_specs=[smem, smem] + [whole()] * 6,
+        out_specs=[whole()] * 2,
         scratch_shapes=[
             pltpu.VMEM((shards, rows, 2 * width), BF16),
             pltpu.VMEM((bags, width), F32),
@@ -281,7 +293,7 @@
         compiler_params=pltpu.CompilerParams(vmem_limit_bytes=VMEM_LIMIT),
         cost_estimate=pl.CostEstimate(flops=1000, bytes_accessed=1000, transcendentals=0),
         name="pool",
-    )(live_counts, places, counted, own, *pieces)
+    )(live_counts, places, counted, own, *pieces, dense, head)
 
 
 def column_of(row, size):
@@ -300,109 +312,166 @@
     )
 
 
-def dense_kernel(shards, replicas, copies, live_counts, places, *refs):
-    dense, rows_in, bias, head, labels, counted = refs[:6]
-    weights = refs[6 : 6 + len(copies)]
-    logits, even, odd = refs[6 + len(copies) : 9 + len(copies)]
-    full_in, full_out, cross, scaled, grads, slots, narrow, total = refs[9 + len(copies) :]
-    batch, width = dense.shape
-    features = full_in.shape[0]
-    bags = grads.shape[0]
-    table_rows = total.shape[0]
+def first_kernel(copies, cross, scaled, bias, head, *refs):
+    weights, (grads, logit, full_in, full_out) = refs[: len(copies)], refs[len(copies) :]
+    for ref, copy in zip(weights, copies):
+        copy(ref, (full_in, full_out))
+    add_rank(cross, scaled, head, full_in, full_out, bias, None, grads, logit)
+
+
+def add_rank(cross, scaled, head, full_in, full_out, bias, before, grads, logit):
+    batch, features = cross.shape
+    width = logit.shape[1]
     across = (((1,), (1,)), ((), ()))
-
-    factor = (full_in, full_out)
-    for ref, copy in zip(weights, copies):
-        copy(ref, factor)
-
-    cross[:, :width] = dense[...]
-    for f in range(1, features // width):
-        cross[:, f * width : (f + 1) * width] = rows_in[(f - 1) * batch : f * batch, :]
-    for f in range(features // width):
-        at = slice(f * width, (f + 1) * width)
-        scaled[:, at] = (cross[:, at].astype(F32) * head[:, at]).astype(BF16)
     hidden = jnp.dot(cross[...], full_in[...], preferred_element_type=F32).astype(BF16)
     back = jnp.dot(scaled[...], full_out[...], preferred_element_type=F32).astype(BF16)
-
     step = 3 * width if (features // width) % 3 == 0 else width
-    logit = jnp.zeros((batch, width), F32)
+    total = jnp.zeros((batch, width), F32) if before is None else before[1][...]
     for n in range(features // step):
         at = slice(n * step, (n + 1) * step)
         mixed = lax.dot_general(hidden, full_out[at, :], across, preferred_element_type=F32)
-        gain = head[:, at] * (mixed + bias[:, at] + 1.0)
+        if bias is not None:
+            mixed = mixed + bias[:, at] + 1.0
+        gain = head[:, at] * mixed
         term = cross[:, at].astype(F32) * gain
         grad = gain + lax.dot_general(back, full_in[at, :], across, preferred_element_type=F32)
         for p in range(step // width):
             part = slice(p * width, (p + 1) * width)
-            logit = logit + term[:, part]
+            total = total + term[:, part]
             f = n * (step // width) + p
             if f > 0:
-                grads[(f - 1) * batch : f * batch, :] = grad[:, part]
-    logit = jnp.sum(logit, axis=1, keepdims=True)
-    logits[...] = row_of(logit, batch)
-    lean = jax.nn.sigmoid(logit) - column_of(labels[...].astype(F32), batch)
-    for f in range(features // width - 1):
+                rows = slice((f - 1) * batch, f * batch)
+                grads[rows, :] = grad[:, part] + (0.0 if before is None else before[0][rows, :])
+    logit[...] = total
+
+
+def first_step(cross, scaled, bias, head, weights, copies, rank):
+    batch, features = cross.shape
+    width = 128
+    return pl.pallas_call(
+        functools.partial(first_kernel, copies),
+        out_shape=(
+            jax.ShapeDtypeStruct((features // width * batch - batch, width), F32),
+            jax.ShapeDtypeStruct((batch, width), F32),
+        ),
+        in_specs=[whole()] * (4 + len(weights)),
+        out_specs=(whole(), whole()),
+        scratch_shapes=[pltpu.VMEM((features, rank), BF16)] * 2,
+        compiler_params=pltpu.CompilerParams(vmem_limit_bytes=VMEM_LIMIT),
+        cost_estimate=pl.CostEstimate(
+            flops=2 * 10**9, bytes_accessed=20 * 10**6, transcendentals=0
+        ),
+        name="first",
+    )(cross, scaled, bias, head, *weights)
+
+
+def dense_kernel(shards, replicas, copies, live_counts, places, cross, scaled, head, labels, counted, *refs):
+    begun, partial = refs[:2]
+    weights = refs[2 : 2 + len(copies)]
+    logits, even, odd, full_in, full_out, grads, logit, slots, narrow, total, spots, done = refs[
+        2 + len(copies) :
+    ]
+    batch = cross.shape[0]
+    width = slots.shape[1]
+    bags = grads.shape[0]
+    rows = total.shape[2]
+    here = lax.axis_index("table")
+    fetch = pltpu.make_async_copy(places, spots, done)
+    fetch.start()
+
+    if copies:
+        for ref, copy in zip(weights, copies):
+            copy(ref, (full_in, full_out))
+        add_rank(cross, scaled, head, full_in, full_out, None, (begun, partial), grads, logit)
+    else:
+        grads[...] = begun[...]
+        logit[...] = partial[...]
+    sums = jnp.sum(logit[...], axis=1, keepdims=True)
+    logits[...] = row_of(sums, batch)
+    lean = jax.nn.sigmoid(sums) - column_of(labels[...].astype(F32), batch)
+    for f in range(bags // batch):
         at = slice(f * batch, (f + 1) * batch)
         grads[at, :] = (grads[at, :] * lean).astype(BF16).astype(F32)
 
-    middle = bags // 2
-
-    def group(i, _):
-        for u in range(UNROLL):
-            k = i * UNROLL + u
-            word = places[0, k]
-            slots[pl.ds(k, 1), :] = grads[pl.ds(word & 0xFFFF, 1), :]
-            slots[pl.ds(k + middle, 1), :] = grads[pl.ds(lax.shift_right_logical(word, 16), 1), :]
+    half = CHUNK // 2
+    chunks = bags // CHUNK
+    total[...] = jnp.zeros_like(total)
+
+    def gather(q):
+        for i in range(half):
+            word = spots[0, q * half + i]
+            slots[i : i + 1, :] = grads[pl.ds(word & 0xFFFF, 1), :]
+            slots[i + half : i + half + 1, :] = grads[pl.ds(lax.shift_right_logical(word, 16), 1), :]
+
+    def shard_of(k):
+        end, shard = jnp.int32(0), jnp.int32(0)
+        for s in range(shards - 1):
+            end = end + live_counts[0, here, s]
+            shard = shard + jnp.where(k >= end, 1, 0)
+        return shard
+
+    def add(q, shard):
+        place = here ^ shard
+        total[place] += lax.dot_general(
+            narrow[...], counted[q + shard], (((0,), (1,)), ((), ())), preferred_element_type=F32
+        )
+
+    fetch.wait()
+    gather(0)
+
+    def chunk(q, _):
+        narrow[...] = slots[...].astype(BF16)
+        shard = shard_of(q * CHUNK)
+        add(q, shard)
+        gather(jnp.minimum(q + 1, chunks - 1))
+
+        def more(s, _):
+            add(q, s)
+            return 0
+
+        lax.fori_loop(shard + 1, shard_of((q + 1) * CHUNK - 1) + 1, more, 0)
         return 0
 
-    lax.fori_loop(0, middle // UNROLL, group, 0)
-    narrow[...] = slots[...].astype(BF16)
-    block = table_rows // replicas
+    lax.fori_loop(0, chunks, chunk, 0)
+    block = rows // replicas
     for j in range(shards):
-        source, start, live = slot_range(live_counts, shards, j)
-        total[...] = jnp.zeros_like(total)
-
-        def pair(q, _, source=source):
-            at = pl.ds(pl.multiple_of(q * CHUNK, CHUNK), CHUNK)
-            total[...] += jnp.dot(
-                counted[q + source], narrow[at, :], preferred_element_type=F32
-            )
-            return 0
-
-        lax.fori_loop(start // CHUNK, (start + live + CHUNK - 1) // CHUNK, pair, 0)
         for m in range(replicas):
-            half = even if m % 2 == 0 else odd
-            half[m // 2, j] = total[m * block : (m + 1) * block, :].astype(BF16)
-
-
-def dense_step(live_counts, places, dense, rows_in, bias, head, labels, counted, weights, copies, rank, shards, replicas):
-    batch, width = dense.shape
-    features = bias.shape[1]
-    bags = rows_in.shape[0]
+            sums = total[j, :, m * block : (m + 1) * block].T
+            (odd if m % 2 else even)[m // 2, j] = sums.astype(BF16)
+
+
+def dense_step(
+    live_counts, places, cross, scaled, head, labels, counted, begun, weights, copies, shards, replicas
+):
+    batch, features = cross.shape
+    width = 128
+    bags = begun[0].shape[0]
     rows = counted.shape[1]
     half = jax.ShapeDtypeStruct((replicas // 2, shards, rows // replicas, width), BF16)
     smem = whole(pltpu.SMEM)
+    part = pltpu.VMEM((features, width) if copies else (16, width), BF16)
     return pl.pallas_call(
         functools.partial(dense_kernel, shards, replicas, copies),
         out_shape=(jax.ShapeDtypeStruct((1, batch), F32), half, half),
-        in_specs=[smem, smem] + [whole()] * 6 + [whole()] * len(weights),
+        in_specs=[smem] + [whole()] * (8 + len(weights)),
         out_specs=(whole(), whole(), whole()),
         scratch_shapes=[
-            pltpu.VMEM((features, rank), BF16),
-            pltpu.VMEM((features, rank), BF16),
-            pltpu.VMEM((batch, features), BF16),
-            pltpu.VMEM((batch, features), BF16),
+            part,
+            part,
             pltpu.VMEM((bags, width), F32),
-            pltpu.VMEM((bags, width), F32),
-            pltpu.VMEM((bags, width), BF16),
-            pltpu.VMEM((rows, width), F32),
+            pltpu.VMEM((batch, width), F32),
+            pltpu.VMEM((CHUNK, width), F32),
+            pltpu.VMEM((CHUNK, width), BF16),
+            pltpu.VMEM((shards, width, rows), F32),
+            pltpu.SMEM(places.shape, jnp.int32),
+            pltpu.SemaphoreType.DMA(()),
         ],
         compiler_params=pltpu.CompilerParams(vmem_limit_bytes=VMEM_LIMIT),
         cost_estimate=pl.CostEstimate(
-            flops=4 * 10**9, bytes_accessed=30 * 10**6, transcendentals=0
+            flops=2 * 10**9, bytes_accessed=20 * 10**6, transcendentals=0
         ),
         name="dense",
-    )(live_counts, places, dense, rows_in, bias, head, labels, counted, *weights)
+    )(live_counts, places, cross, scaled, head, labels, counted, *begun, *weights)
 
 
 def splits_evenly(factor, replicas):
@@ -416,7 +485,9 @@
 
         return copy
 
-    return [lax.all_gather(w, "table", axis=0, tiled=True) for w in factors], [spot(0), spot(1)]
+    return [
+        (lax.all_gather(w, "table", axis=0, tiled=True), spot(i)) for i, w in enumerate(factors)
+    ]
 
 
 def gather_blocks(factors, near, after):
@@ -425,37 +496,44 @@
     half, lanes = shard_rows // 2, near.shape[2]
     first, second = swap(near, 2), swap(near, 4)
     first, second, after = lax.optimization_barrier((first, second, after))
-    blocks = [(0, near, 0, 2), (2, first, 0, 2), (4, second, 0, 2)]
-    blocks += [(6, swap(first[:, :half], 4), 0, 1), (6, swap(second[:, half:], 2), 1, 2)]
-    arrays, copies = [], []
-    for m, block, begin, end in blocks:
-        for core in (0, 1):
-            arrays.append(block if core == 0 else swap(block, 1))
-
-            def copy(ref, full, m=m, core=core, begin=begin, end=end):
-                own, here = lax.axis_index("replica"), lax.axis_index("table")
-                for k in range(1, shards):
-                    source = lax.rem(here - k + shards, shards)
-                    first = source * shard_rows + ((own & 1) ^ core) * half
-                    at = pl.ds(pl.multiple_of(first, 16), half)
-                    for which in range(begin, end):
-                        full[which][at, (m // 2) * lanes : (m // 2 + 1) * lanes] = ref[
-                            k - 1, (which - begin) * half : (which - begin + 1) * half, :
-                        ]
-
-            copies.append(copy)
-    for which, own_rows in enumerate(factors):
-
-        def copy_own(ref, full, which=which):
+    corners = [(swap(first[:, :half], 4), 0), (swap(second[:, half:], 2), 1)]
+
+    def put(block, core, column, begin, end):
+        def copy(ref, full):
+            own, here = lax.axis_index("replica"), lax.axis_index("table")
+            for k in range(1, shards):
+                source = here ^ k
+                start = source * shard_rows + ((own & 1) ^ core) * half
+                at = pl.ds(pl.multiple_of(start, 16), half)
+                for which in range(begin, end):
+                    full[which][at, column * lanes : (column + 1) * lanes] = ref[
+                        k - 1, (which - begin) * half : (which - begin + 1) * half, :
+                    ]
+
+        return block, copy
+
+    def put_own(which, masks):
+        def copy(ref, full):
             own, here = lax.axis_index("replica"), lax.axis_index("table")
             at = pl.ds(pl.multiple_of(here * shard_rows, 16), shard_rows)
-            for m in range(4):
-                columns = pl.ds(pl.multiple_of(((own >> 1) ^ m) * lanes, lanes), lanes)
-                full[which][at, m * lanes : (m + 1) * lanes] = ref[:, columns]
-
-        arrays.append(own_rows)
-        copies.append(copy_own)
-    return arrays, copies, after
+            for column, mask in enumerate(masks):
+                columns = pl.ds(pl.multiple_of(((own >> 1) ^ mask) * lanes, lanes), lanes)
+                full[which][at, column * lanes : (column + 1) * lanes] = ref[:, columns]
+
+        return factors[which], copy
+
+    early = [put_own(which, (0, 1, 2)) for which in range(2)]
+    for column, block in enumerate((near, first, second)):
+        early += [put(block, 0, column, 0, 2), put(swap(block, 1), 1, column, 0, 2)]
+
+    def late(after):
+        blocks, after = lax.optimization_barrier(([c[0] for c in corners], after))
+        out = [put_own(which, (3,)) for which in range(2)]
+        for block, (_, which) in zip(blocks, corners):
+            out += [put(block, 0, 0, which, which + 1), put(swap(block, 1), 1, 0, which, which + 1)]
+        return out, after
+
+    return early, late, after
 
 
 def reduce_rows(even, odd):
@@ -469,7 +547,7 @@
     kept = kept[0]
     total = kept[0]
     for k in range(1, shards):
-        total = total + shift(kept[k], -k)
+        total = total + cross_over(kept[k].astype(BF16), k).astype(F32)
     return total
 
 
@@ -523,33 +601,36 @@
     even_split = splits_evenly(cross_in, replicas)
 
     packed = pack(look_rows, emb_table, factors if even_split else (), shards, replicas)
-    parcels = [shift(p, k + 1) for k, p in enumerate(packed[: shards - 1])]
-    far = [shift(packed[shards - 1], k) for k in range(1, shards)] if even_split else []
+    parcels = [cross_over(p, k + 1) for k, p in enumerate(packed[: shards - 1])]
+    far = [cross_over(packed[shards - 1], k) for k in range(1, shards)] if even_split else []
     places, counted = slots(
         live_counts, look_rows, bag_order, parcels, rows, shards, replicas, batch
     )
     pieces, far, counted = replica_gather(
         jnp.stack([p[:block] for p in parcels]), far, counted
     )
-    rows_in = pool(live_counts, places, counted, emb_table, pieces)
+    bias, head = cross_bias.reshape(1, -1), head_weight.reshape(1, -1)
+    crossed = pool(live_counts, places, counted, emb_table, pieces, dense_emb, head)
+    rank = cross_in.shape[1]
     if even_split:
-        near = jnp.stack(far)
-    if even_split:
-        weights, copies, rows_in = gather_blocks(factors, near, rows_in)
+        early, late, crossed = gather_blocks(factors, jnp.stack(far), crossed)
+        rank = rank - 128
     else:
-        weights, copies = gather_whole(factors)
+        early, late = gather_whole(factors), None
+    begun = first_step(*crossed, bias, head, *zip(*early), rank)
+    last = []
+    if late:
+        last, begun = late(begun)
     logits, even, odd = dense_step(
         live_counts,
         places,
-        dense_emb,
-        rows_in,
-        cross_bias.reshape(1, -1),
-        head_weight.reshape(1, -1),
+        *crossed,
+        head,
         labels.reshape(1, -1),
         counted,
-        weights,
-        copies,
-        cross_in.shape[1],
+        begun,
+        [block for block, _ in last],
+        [copy for _, copy in last],
         shards,
         replicas,
     )

time: 117 us -> 110 us (0.940)
  waiting for transfers between devices: 43.2 us -> 33.7 us
  starting transfers between devices: 32 us -> 34.7 us
  Pallas kernels: 36.3 us -> 33.8 us
  local copies, waits for them, and re-layouts: 4.16 us -> 5.61 us
    pallas_call x1, Pallas kernels: 15.3 us -> 8.53 us  [dense_step(): pl.pallas_call(functools.partial(dense_kernel, shards, replicas, copies),...]
    ppermute x9, waiting for transfers between devices: 18 us -> 12.8 us  [cross_over(): return lax.ppermute(array, 'table', [(i, i ^ mask) for i in range(size)])]
    pallas_call x1 -> x2, Pallas kernels: 10.6 us -> 14.9 us  [the longest x1 11.3 us: pool(): pl.pallas_call(functools.partial(pool_kernel, shards), out_shape=[jax.Sha...]
    ppermute x21, waiting for transfers between devices: 25.2 us -> 21 us  [swap(): return lax.ppermute(array, 'replica', [(i, i ^ mask) for i in range(size)])]
    ppermute x9, starting transfers between devices: 15.5 us -> 17.5 us  [cross_over(): return lax.ppermute(array, 'table', [(i, i ^ mask) for i in range(size)])]
    unnamed x24 -> x22, local copies, waits for them, and re-layouts: 4.03 us -> 4.78 us
  transfers between devices with their start and end apart: 30 -> 30, of which waited for: 21 -> 19; matrix products, arithmetic and copies ran while one was open for 0% -> 1% of each run, Pallas kernels for 14% -> 19%
where the time goes in v4:
time: 110 us; the launch traced here: 109 us
  starting transfers between devices  34.7 us (32%)
  Pallas kernels  33.8 us (31%)
  waiting for transfers between devices  33.7 us (31%)
  local copies, waits for them, and re-layouts  5.61 us (5%)
    ppermute x21, waiting for transfers between devices, swap(): return lax.ppermute(array, 'replica', [(i, i ^ mask) for i in range(size)])  21 us
    ppermute x9, starting transfers between devices, cross_over(): return lax.ppermute(array, 'table', [(i, i ^ mask) for i in range(size)])  17.5 us
    ppermute x21, starting transfers between devices, swap(): return lax.ppermute(array, 'replica', [(i, i ^ mask) for i in range(size)])  17.2 us
    ppermute x9, waiting for transfers between devices, cross_over(): return lax.ppermute(array, 'table', [(i, i ^ mask) for i in range(size)])  12.8 us
    pallas_call x1, Pallas kernels, pool(): pl.pallas_call(functools.partial(pool_kernel, shards), out_shape=[jax.Sha...  11.3 us
    pallas_call x1, Pallas kernels, dense_step(): pl.pallas_call(functools.partial(dense_kernel, shards, replicas, copies),...  8.53 us
    pallas_call x1, Pallas kernels, slots(): pl.pallas_call(functools.partial(slots_kernel, shards, replicas, batch),...  6.27 us
    unnamed x22, local copies, waits for them, and re-layouts  4.78 us
  transfers between devices with their start and end apart: 30, of which 19 were waited for; matrix products, arithmetic and copies ran while one was open for 1% of the time, Pallas kernels for 19%

profile of v4, /device:TPU:0, one launch (start us, length us, event | category | flops | bytes accessed | tf_op | source)
XLA Modules:
  0.0 109.2 jit_solution(13309475376323437916)
XLA Ops:
  0.6 2.8 %pack.1 = (f32[148,128]{1,0:T(8,128)}, f32[148,128]{1,0:T(8,128)}, f32[148,128]{1,0:T(8,128)}, bf16[864,128]{1,0:T(8,128)(2,1)}) custom-call(s32[1,1,4,4,1248]{4,3,2,1,0:T(4,128)} %look_rows.3, f32[1024,128]{1,0:T(8,128)} %own.1, bf16[864,512]{1,0:T(8,128)(2,1)} %refs_2_.1, bf16[864,512]{1,0:T(8,128)(2,1)} %refs_3_.1), custom_call_target="tpu_custom_call" | custom-call | tf_op jit(solution)/shard_map/pack/pallas_call | solution.py:122
  3.4 5.1 %collective-permute-start.2 = (f32[148,128]{1,0:T(8,128)}, f32[148,128]{1,0:T(8,128)S(1)}, u32[]{:S(2)}, u32[]{:S(2)}) collective-permute-start(f32[148,128]{1,0:T(8,128)} %get-tuple-element.33), channel_id=1, source_target_pairs={{0,3},{1,2},{2,1},{3,0},{4,7},{5,6},{6,5},{7,4},{8,11},{9,10},{10,... | collective-permute-start | bytes 227336 | tf_op jit(solution)/shard_map/ppermute | solution.py:28
  8.5 0.6 collective-permute-start
  9.2 2.4 %collective-permute-done.2.refs_2_ = f32[148,128]{1,0:T(8,128)S(1)} collective-permute-done((f32[148,128]{1,0:T(8,128)}, f32[148,128]{1,0:T(8,128)S(1)}, u32[]{:S(2)}, u32[]{:S(2)}) %collective-permute-start.2) | collective-permute-done | bytes 75808 | tf_op jit(solution)/shard_map/ppermute | solution.py:28
  11.6 3.6 %collective-permute-done.1.refs_1_ = f32[148,128]{1,0:T(8,128)S(1)} collective-permute-done((f32[148,128]{1,0:T(8,128)}, f32[148,128]{1,0:T(8,128)S(1)}, u32[]{:S(2)}, u32[]{:S(2)}) %collective-permute-start.1) | collective-permute-done | bytes 75808 | tf_op jit(solution)/shard_map/ppermute | solution.py:28
  15.3 1.6 %collective-permute-start.3 = (f32[3,128,128]{2,1,0:T(8,128)S(1)}, f32[3,128,128]{2,1,0:T(8,128)S(1)}, u32[]{:S(2)}, u32[]{:S(2)}) collective-permute-start(f32[3,128,128]{2,1,0:T(8,128)S(1)} %get-tuple-element.67), channel_id=1, source_target_pairs={{0,8},{4,12},{8,0},{12,4},{16,24},{20,28},{24,16},{28,20},{1,9},{5... | collective-permute-start | bytes 589832 | tf_op jit(solution)/shard_map/ppermute | solution.py:23
  16.9 1.5 %collective-permute-start.4 = (f32[3,128,128]{2,1,0:T(8,128)S(1)}, f32[3,128,128]{2,1,0:T(8,128)S(1)}, u32[]{:S(2)}, u32[]{:S(2)}) collective-permute-start(f32[3,128,128]{2,1,0:T(8,128)S(1)} %get-tuple-element.67), channel_id=1, source_target_pairs={{0,16},{4,20},{8,24},{12,28},{16,0},{20,4},{24,8},{28,12},{1,17},{... | collective-permute-start | bytes 589832 | tf_op jit(solution)/shard_map/ppermute | solution.py:23
  18.9 0.9 collective-permute-start.6
  19.8 2.4 %collective-permute-start.7 = (bf16[864,128]{1,0:T(8,128)(2,1)}, bf16[864,128]{1,0:T(8,128)(2,1)S(1)}, u32[]{:S(2)}, u32[]{:S(2)}) collective-permute-start(bf16[864,128]{1,0:T(8,128)(2,1)} %get-tuple-element.35), channel_id=1, source_target_pairs={{0,2},{1,3},{2,0},{3,1},{4,6},{5,7},{6,4},{7,5},{8,10},{9,11},{10,... | collective-permute-start | bytes 663560 | tf_op jit(solution)/shard_map/ppermute | solution.py:28
  22.2 1.0 collective-permute-done.3
  23.2 2.7 %collective-permute-start.8 = (bf16[864,128]{1,0:T(8,128)(2,1)}, bf16[864,128]{1,0:T(8,128)(2,1)S(1)}, u32[]{:S(2)}, u32[]{:S(2)}) collective-permute-start(bf16[864,128]{1,0:T(8,128)(2,1)} %get-tuple-element.35), channel_id=1, source_target_pairs={{0,3},{1,2},{2,1},{3,0},{4,7},{5,6},{6,5},{7,4},{8,11},{9,10},{10,... | collective-permute-start | bytes 663560 | tf_op jit(solution)/shard_map/ppermute | solution.py:28
  25.9 0.9 copy-done.3
  26.8 0.7 copy-done.5
  27.5 0.7 copy-done.7
  28.2 6.3 %slots.1 = (s32[1,1664]{1,0:T(1,128)S(1)}, bf16[16,1024,256]{2,1,0:T(8,128)(2,1)S(1)}) custom-call(s32[1,4,4]{2,1,0:T(4,128)S(1)} %copy-done.5, s32[1,1,4,4,1248]{4,3,2,1,0:T(4,128)S(1)} %copy-done.3, s32[1,1,3328]{2,1,0:T(1,128)S(1)} %copy-done.7, f32[148,128]{1,0:T(8,128)S(1)} %collective-permute-done.refs_0_, ...), custom_call_target="tpu_custom_call" | custom-call | flops 1000 | bytes 1000 | tf_op jit(solution)/shard_map/slots/pallas_call | solution.py:209
  34.5 3.1 %collective-permute-done.7 = bf16[864,128]{1,0:T(8,128)(2,1)S(1)} collective-permute-done((bf16[864,128]{1,0:T(8,128)(2,1)}, bf16[864,128]{1,0:T(8,128)(2,1)S(1)}, u32[]{:S(2)}, u32[]{:S(2)}) %collective-permute-start.7) | collective-permute-done | bytes 221216 | tf_op jit(solution)/shard_map/ppermute | solution.py:28
  37.7 1.6 %collective-permute-start.10 = (bf16[3,864,128]{2,1,0:T(8,128)(2,1)S(1)}, bf16[3,864,128]{2,1,0:T(8,128)(2,1)S(1)}, u32[]{:S(2)}, u32[]{:S(2)}) collective-permute-start(bf16[3,864,128]{2,1,0:T(8,128)(2,1)S(1)} %pad_maximum_fusion.1.refs_2_), channel_id=1, source_target_pairs={{0,16},{4,20},{8,24},{12,28},{16,0},{20,4},{24,8},{28,12},{1,17},{... | collective-permute-start | bytes 1990664 | tf_op jit(solution)/shard_map/ppermute | solution.py:23
  39.3 1.5 %collective-permute-start.9 = (bf16[3,864,128]{2,1,0:T(8,128)(2,1)S(1)}, bf16[3,864,128]{2,1,0:T(8,128)(2,1)S(1)}, u32[]{:S(2)}, u32[]{:S(2)}) collective-permute-start(bf16[3,864,128]{2,1,0:T(8,128)(2,1)S(1)} %pad_maximum_fusion.1.refs_2_), channel_id=1, source_target_pairs={{0,8},{4,12},{8,0},{12,4},{16,24},{20,28},{24,16},{28,20},{1,9},{5... | collective-permute-start | bytes 1990664 | tf_op jit(solution)/shard_map/ppermute | solution.py:23
  40.8 0.7 reshape.77.head
  41.6 1.0 copy-done.2
  42.6 0.8 copy-done.4
  43.4 0.7 copy-done.6
  44.1 11.3 %pool.1 = (bf16[128,3456]{1,0:T(8,128)(2,1)S(1)}, bf16[128,3456]{1,0:T(8,128)(2,1)S(1)}) custom-call(s32[1,4,4]{2,1,0:T(4,128)S(1)} %copy-done.6, s32[1,1664]{1,0:T(1,128)S(1)} %get-tuple-element.34.places, bf16[16,1024,256]{2,1,0:T(8,128)(2,1)S(1)} %get-tuple-element.40.counted, f32[1024,128]{1,0:T(8,128)S(1)} %copy-done.2, ...), custom_call_target="tpu_custom_call" | custom-call | flops 1000 | bytes 1000 | tf_op jit(solution)/shard_map/pool/pallas_call | solution.py:283
  55.4 0.9 collective-permute-done.9.refs_4_
  56.3 0.5 collective-permute-start.16
  56.9 0.6 collective-permute-start.12
  57.5 1.5 %collective-permute-start.13 = (bf16[3,432,128]{2,1,0:T(8,128)(2,1)S(1)}, bf16[3,432,128]{2,1,0:T(8,128)(2,1)S(1)}, u32[]{:S(2)}, u32[]{:S(2)}) collective-permute-start(bf16[3,432,128]{2,1,0:T(8,128)(2,1)S(1)} %slice.53), channel_id=1, source_target_pairs={{0,8},{4,12},{8,0},{12,4},{16,24},{20,28},{24,16},{28,20},{1,9},{5... | collective-permute-start | bytes 995336 | tf_op jit(solution)/shard_map/ppermute | solution.py:23
  59.4 3.6 %first.1 = (f32[3328,128]{1,0:T(8,128)S(1)}, f32[128,128]{1,0:T(8,128)S(1)}) custom-call(bf16[128,3456]{1,0:T(8,128)(2,1)S(1)} %get-tuple-element.44.cross, bf16[128,3456]{1,0:T(8,128)(2,1)S(1)} %get-tuple-element.45.scaled, f32[1,3456]{1,0:T(1,128)S(1)} %reshape.79.bias, f32[1,3456]{1,0:T(1,128)S(1)} %reshape.77.head, bf16[864,512]{1,0:T(8,128)(2,1)S(1)} %copy-done, ...), custom_call_target="tpu_custom_call" | custom-call | flops 2000000000 | bytes 20000000 | tf_op jit(solution)/shard_map/first/pallas_call | solution.py:351
  63.0 3.7 %collective-permute-done.12.refs_4_ = bf16[3,432,128]{2,1,0:T(8,128)(2,1)S(1)} collective-permute-done((bf16[3,432,128]{2,1,0:T(8,128)(2,1)S(1)}, bf16[3,432,128]{2,1,0:T(8,128)(2,1)S(1)}, u32[]{:S(2)}, u32[]{:S(2)}) %collective-permute-start.12) | collective-permute-done | bytes 331808 | tf_op jit(solution)/shard_map/ppermute | solution.py:23
  67.4 1.1 %collective-permute-done.17.refs_5_ = bf16[3,432,128]{2,1,0:T(8,128)(2,1)S(1)} collective-permute-done((bf16[3,432,128]{2,1,0:T(8,128)(2,1)S(1)}, bf16[3,432,128]{2,1,0:T(8,128)(2,1)S(1)}, u32[]{:S(2)}, u32[]{:S(2)}) %collective-permute-start.17) | collective-permute-done | bytes 331808 | tf_op jit(solution)/shard_map/ppermute | solution.py:23
  69.0 8.5 %dense.3 = (f32[1,128]{1,0:T(1,128)}, bf16[4,4,128,128]{3,2,1,0:T(8,128)(2,1)S(1)}, bf16[4,4,128,128]{3,2,1,0:T(8,128)(2,1)S(1)}) custom-call(s32[1,4,4]{2,1,0:T(4,128)S(1)} %copy-done.6, s32[1,1664]{1,0:T(1,128)S(1)} %get-tuple-element.34.places, bf16[128,3456]{1,0:T(8,128)(2,1)S(1)} %get-tuple-element.44.cross, ...), custom_call_target="tpu_custom_call" | custom-call | flops 2000000000 | bytes 20000000 | tf_op jit(solution)/shard_map/dense/pallas_call | solution.py:453
  77.7 1.8 %collective-permute-done.19 = bf16[4,4,128,128]{3,2,1,0:T(8,128)(2,1)S(1)} collective-permute-done((bf16[4,4,128,128]{3,2,1,0:T(8,128)(2,1)S(1)}, bf16[4,4,128,128]{3,2,1,0:T(8,128)(2,1)S(1)}, u32[]{:S(2)}, u32[]{:S(2)}) %collective-permute-start.19) | collective-permute-done | bytes 524320 | tf_op jit(solution)/shard_map/ppermute | solution.py:23
  79.7 1.6 %collective-permute-start.20 = (bf16[1,4,128,128]{3,2,1,0:T(8,128)(2,1)S(1)}, bf16[1,4,128,128]{3,2,1,0:T(8,128)(2,1)S(1)}, u32[]{:S(2)}, u32[]{:S(2)}) collective-permute-start(bf16[1,4,128,128]{3,2,1,0:T(8,128)(2,1)S(1)} %get-tuple-element.63), channel_id=1, source_target_pairs={{0,8},{4,12},{8,0},{12,4},{16,24},{20,28},{24,16},{28,20},{1,9},{5... | collective-permute-start | bytes 393224 | tf_op jit(solution)/shard_map/ppermute | solution.py:23
  81.3 1.5 %collective-permute-start.21 = (bf16[1,4,128,128]{3,2,1,0:T(8,128)(2,1)S(1)}, bf16[1,4,128,128]{3,2,1,0:T(8,128)(2,1)S(1)}, u32[]{:S(2)}, u32[]{:S(2)}) collective-permute-start(bf16[1,4,128,128]{3,2,1,0:T(8,128)(2,1)S(1)} %get-tuple-element.65), channel_id=1, source_target_pairs={{0,16},{4,20},{8,24},{12,28},{16,0},{20,4},{24,8},{28,12},{1,17},{... | collective-permute-start | bytes 393224 | tf_op jit(solution)/shard_map/ppermute | solution.py:23
  83.3 2.4 %collective-permute-done.20 = bf16[1,4,128,128]{3,2,1,0:T(8,128)(2,1)S(1)} collective-permute-done((bf16[1,4,128,128]{3,2,1,0:T(8,128)(2,1)S(1)}, bf16[1,4,128,128]{3,2,1,0:T(8,128)(2,1)S(1)}, u32[]{:S(2)}, u32[]{:S(2)}) %collective-permute-start.20) | collective-permute-done | bytes 131104 | tf_op jit(solution)/shard_map/ppermute | solution.py:23
  85.7 3.7 %collective-permute-done.21 = bf16[1,4,128,128]{3,2,1,0:T(8,128)(2,1)S(1)} collective-permute-done((bf16[1,4,128,128]{3,2,1,0:T(8,128)(2,1)S(1)}, bf16[1,4,128,128]{3,2,1,0:T(8,128)(2,1)S(1)}, u32[]{:S(2)}, u32[]{:S(2)}) %collective-permute-start.21) | collective-permute-done | bytes 131104 | tf_op jit(solution)/shard_map/ppermute | solution.py:23
  89.5 3.4 %collective-permute-start.23 = (bf16[128,128]{1,0:T(8,128)(2,1)S(1)}, bf16[128,128]{1,0:T(8,128)(2,1)S(1)}, u32[]{:S(2)}, u32[]{:S(2)}) collective-permute-start(bf16[128,128]{1,0:T(8,128)(2,1)S(1)} %get-tuple-element.68), channel_id=1, source_target_pairs={{0,1},{1,0},{2,3},{3,2},{4,5},{5,4},{6,7},{7,6},{8,9},{9,8},{10,11... | collective-permute-start | bytes 98312 | tf_op jit(solution)/shard_map/ppermute | solution.py:28
  93.2 2.1 %collective-permute-start.25 = (bf16[128,128]{1,0:T(8,128)(2,1)S(1)}, bf16[128,128]{1,0:T(8,128)(2,1)S(1)}, u32[]{:S(2)}, u32[]{:S(2)}) collective-permute-start(bf16[128,128]{1,0:T(8,128)(2,1)S(1)} %get-tuple-element.69), channel_id=1, source_target_pairs={{0,3},{1,2},{2,1},{3,0},{4,7},{5,6},{6,5},{7,4},{8,11},{9,10},{10,... | collective-permute-start | bytes 98312 | tf_op jit(solution)/shard_map/ppermute | solution.py:28
  95.3 2.4 %collective-permute-done.24 = bf16[128,128]{1,0:T(8,128)(2,1)S(1)} collective-permute-done((bf16[128,128]{1,0:T(8,128)(2,1)S(1)}, bf16[128,128]{1,0:T(8,128)(2,1)S(1)}, u32[]{:S(2)}, u32[]{:S(2)}) %collective-permute-start.24) | collective-permute-done | bytes 32800 | tf_op jit(solution)/shard_map/ppermute | solution.py:28
  97.6 1.2 %collective-permute-done.25 = bf16[128,128]{1,0:T(8,128)(2,1)S(1)} collective-permute-done((bf16[128,128]{1,0:T(8,128)(2,1)S(1)}, bf16[128,128]{1,0:T(8,128)(2,1)S(1)}, u32[]{:S(2)}, u32[]{:S(2)}) %collective-permute-start.25) | collective-permute-done | bytes 32800 | tf_op jit(solution)/shard_map/ppermute | solution.py:28
  98.9 1.3 %collective-permute-start.26 = (f32[128,128]{1,0:T(8,128)S(1)}, f32[128,128]{1,0:T(8,128)S(1)}, u32[]{:S(2)}, u32[]{:S(2)}) collective-permute-start(f32[128,128]{1,0:T(8,128)S(1)} %fusion.5), channel_id=1, source_target_pairs={{0,8},{4,12},{8,0},{12,4},{16,24},{20,28},{24,16},{28,20},{1,9},{5... | collective-permute-start | bytes 196616 | tf_op jit(solution)/shard_map/ppermute | solution.py:23
  100.2 0.8 collective-permute-start.27
  101.0 1.4 %collective-permute-start.28 = (f32[128,128]{1,0:T(8,128)S(1)}, f32[128,128]{1,0:T(8,128)S(1)}, u32[]{:S(2)}, u32[]{:S(2)}) collective-permute-start(f32[128,128]{1,0:T(8,128)S(1)} %fusion.5), channel_id=1, source_target_pairs={{0,24},{4,28},{8,16},{12,20},{16,8},{20,12},{24,0},{28,4},{1,25},{... | collective-permute-start | bytes 196616 | tf_op jit(solution)/shard_map/ppermute | solution.py:23
  102.5 0.8 collective-permute-done.26
  103.2 1.2 %collective-permute-done.27 = f32[128,128]{1,0:T(8,128)S(1)} collective-permute-done((f32[128,128]{1,0:T(8,128)S(1)}, f32[128,128]{1,0:T(8,128)S(1)}, u32[]{:S(2)}, u32[]{:S(2)}) %collective-permute-start.27) | collective-permute-done | bytes 65568 | tf_op jit(solution)/shard_map/ppermute | solution.py:23
  104.5 1.7 %collective-permute-done.28 = f32[128,128]{1,0:T(8,128)S(1)} collective-permute-done((f32[128,128]{1,0:T(8,128)S(1)}, f32[128,128]{1,0:T(8,128)S(1)}, u32[]{:S(2)}, u32[]{:S(2)}) %collective-permute-start.28) | collective-permute-done | bytes 65568 | tf_op jit(solution)/shard_map/ppermute | solution.py:23
  106.3 1.5 %collective-permute-done.29.odd = f32[4,128,128]{2,1,0:T(8,128)S(1)} collective-permute-done((f32[4,128,128]{2,1,0:T(8,128)S(1)}, f32[4,128,128]{2,1,0:T(8,128)S(1)}, u32[]{:S(2)}, u32[]{:S(2)}) %collective-permute-start.29) | collective-permute-done | bytes 262176 | tf_op jit(solution)/shard_map/ppermute | solution.py:23
  107.8 1.4 %finish.1 = (f32[1024,128]{1,0:T(8,128)}, f32[8,128]{1,0:T(8,128)}) custom-call(f32[8,128]{1,0:T(8,128)S(1)} %bitcast.55, f32[4,128,128]{2,1,0:T(8,128)S(1)} %pad_maximum_fusion.2.even, f32[4,128,128]{2,1,0:T(8,128)S(1)} %collective-permute-done.29.odd), custom_call_target="tpu_custom_call" | custom-call | tf_op jit(solution)/shard_map/finish/pallas_call | solution.py:570
  (56 shorter events, 3.9 us)
Async XLA Ops:
  0.6 58.3 %copy-start.10 = (f32[3456]{0:T(1024)S(1)}, f32[3456]{0:T(1024)}, u32[]{:S(2)}) copy-start(f32[3456]{0:T(1024)} %param.20) | copy-start | bytes 41476
  3.4 56.0 %copy-start = (bf16[864,512]{1,0:T(8,128)(2,1)S(1)}, bf16[864,512]{1,0:T(8,128)(2,1)}, u32[]{:S(2)}) copy-start(bf16[864,512]{1,0:T(8,128)(2,1)} %refs_2_.1) | copy-start | bytes 2654212
  3.4 56.0 %copy-start.1 = (bf16[864,512]{1,0:T(8,128)(2,1)S(1)}, bf16[864,512]{1,0:T(8,128)(2,1)}, u32[]{:S(2)}) copy-start(bf16[864,512]{1,0:T(8,128)(2,1)} %refs_3_.1) | copy-start | bytes 2654212
  3.4 8.2 %collective-permute-start.2 = (f32[148,128]{1,0:T(8,128)}, f32[148,128]{1,0:T(8,128)S(1)}, u32[]{:S(2)}, u32[]{:S(2)}) collective-permute-start(f32[148,128]{1,0:T(8,128)} %get-tuple-element.33), channel_id=1, source_target_pairs={{0,3},{1,2},{2,1},{3,0},{4,7},{5,6},{6,5},{7,4},{8,11},{9,10},{10,... | collective-permute-start | bytes 227336 | tf_op jit(solution)/shard_map/ppermute | solution.py:28
  8.5 6.7 %collective-permute-start.1 = (f32[148,128]{1,0:T(8,128)}, f32[148,128]{1,0:T(8,128)S(1)}, u32[]{:S(2)}, u32[]{:S(2)}) collective-permute-start(f32[148,128]{1,0:T(8,128)} %get-tuple-element.32), channel_id=1, source_target_pairs={{0,2},{1,3},{2,0},{3,1},{4,6},{5,7},{6,4},{7,5},{8,10},{9,11},{10,... | collective-permute-start | bytes 227336 | tf_op jit(solution)/shard_map/ppermute | solution.py:28
  8.5 6.7 %collective-permute-start = (f32[148,128]{1,0:T(8,128)}, f32[148,128]{1,0:T(8,128)S(1)}, u32[]{:S(2)}, u32[]{:S(2)}) collective-permute-start(f32[148,128]{1,0:T(8,128)} %get-tuple-element.31), channel_id=1, source_target_pairs={{0,1},{1,0},{2,3},{3,2},{4,5},{5,4},{6,7},{7,6},{8,9},{9,8},{10,11... | collective-permute-start | bytes 227336 | tf_op jit(solution)/shard_map/ppermute | solution.py:28
  15.3 7.9 %collective-permute-start.3 = (f32[3,128,128]{2,1,0:T(8,128)S(1)}, f32[3,128,128]{2,1,0:T(8,128)S(1)}, u32[]{:S(2)}, u32[]{:S(2)}) collective-permute-start(f32[3,128,128]{2,1,0:T(8,128)S(1)} %get-tuple-element.67), channel_id=1, source_target_pairs={{0,8},{4,12},{8,0},{12,4},{16,24},{20,28},{24,16},{28,20},{1,9},{5... | collective-permute-start | bytes 589832 | tf_op jit(solution)/shard_map/ppermute | solution.py:23
  16.9 17.6 %collective-permute-start.4 = (f32[3,128,128]{2,1,0:T(8,128)S(1)}, f32[3,128,128]{2,1,0:T(8,128)S(1)}, u32[]{:S(2)}, u32[]{:S(2)}) collective-permute-start(f32[3,128,128]{2,1,0:T(8,128)S(1)} %get-tuple-element.67), channel_id=1, source_target_pairs={{0,16},{4,20},{8,24},{12,28},{16,0},{20,4},{24,8},{28,12},{1,17},{... | collective-permute-start | bytes 589832 | tf_op jit(solution)/shard_map/ppermute | solution.py:23
  18.4 16.1 %collective-permute-start.5 = (f32[3,128,128]{2,1,0:T(8,128)S(1)}, f32[3,128,128]{2,1,0:T(8,128)S(1)}, u32[]{:S(2)}, u32[]{:S(2)}) collective-permute-start(f32[3,128,128]{2,1,0:T(8,128)S(1)} %get-tuple-element.67), channel_id=1, source_target_pairs={{0,24},{4,28},{8,16},{12,20},{16,8},{20,12},{24,0},{28,4},{1,25},{... | collective-permute-start | bytes 589832 | tf_op jit(solution)/shard_map/ppermute | solution.py:23
  18.9 15.6 %collective-permute-start.6 = (bf16[864,128]{1,0:T(8,128)(2,1)}, bf16[864,128]{1,0:T(8,128)(2,1)S(1)}, u32[]{:S(2)}, u32[]{:S(2)}) collective-permute-start(bf16[864,128]{1,0:T(8,128)(2,1)} %get-tuple-element.35), channel_id=1, source_target_pairs={{0,1},{1,0},{2,3},{3,2},{4,5},{5,4},{6,7},{7,6},{8,9},{9,8},{10,11... | collective-permute-start | bytes 663560 | tf_op jit(solution)/shard_map/ppermute | solution.py:28
  19.8 17.8 %collective-permute-start.7 = (bf16[864,128]{1,0:T(8,128)(2,1)}, bf16[864,128]{1,0:T(8,128)(2,1)S(1)}, u32[]{:S(2)}, u32[]{:S(2)}) collective-permute-start(bf16[864,128]{1,0:T(8,128)(2,1)} %get-tuple-element.35), channel_id=1, source_target_pairs={{0,2},{1,3},{2,0},{3,1},{4,6},{5,7},{6,4},{7,5},{8,10},{9,11},{10,... | collective-permute-start | bytes 663560 | tf_op jit(solution)/shard_map/ppermute | solution.py:28
  23.2 14.4 %collective-permute-start.8 = (bf16[864,128]{1,0:T(8,128)(2,1)}, bf16[864,128]{1,0:T(8,128)(2,1)S(1)}, u32[]{:S(2)}, u32[]{:S(2)}) collective-permute-start(bf16[864,128]{1,0:T(8,128)(2,1)} %get-tuple-element.35), channel_id=1, source_target_pairs={{0,3},{1,2},{2,1},{3,0},{4,7},{5,6},{6,5},{7,4},{8,11},{9,10},{10,... | collective-permute-start | bytes 663560 | tf_op jit(solution)/shard_map/ppermute | solution.py:28
  25.9 0.9 copy-start.3
  26.8 0.7 copy-start.5
  27.5 0.7 copy-start.7
  37.6 4.0 %collective-permute-start.11 = (f32[4,3,128,128]{3,2,1,0:T(8,128)S(1)}, f32[4,3,128,128]{3,2,1,0:T(8,128)S(1)}, u32[]{:S(2)}, u32[]{:S(2)}) collective-permute-start(f32[4,3,128,128]{3,2,1,0:T(8,128)S(1)} %pad_maximum_fusion.even), channel_id=1, source_target_pairs={{0,4},{4,0},{8,12},{12,8},{16,20},{20,16},{24,28},{28,24},{1,5},{5... | collective-permute-start | bytes 2359304 | tf_op jit(solution)/shard_map/ppermute | solution.py:23
  37.7 17.7 %collective-permute-start.10 = (bf16[3,864,128]{2,1,0:T(8,128)(2,1)S(1)}, bf16[3,864,128]{2,1,0:T(8,128)(2,1)S(1)}, u32[]{:S(2)}, u32[]{:S(2)}) collective-permute-start(bf16[3,864,128]{2,1,0:T(8,128)(2,1)S(1)} %pad_maximum_fusion.1.refs_2_), channel_id=1, source_target_pairs={{0,16},{4,20},{8,24},{12,28},{16,0},{20,4},{24,8},{28,12},{1,17},{... | collective-permute-start | bytes 1990664 | tf_op jit(solution)/shard_map/ppermute | solution.py:23
  39.3 17.0 %collective-permute-start.9 = (bf16[3,864,128]{2,1,0:T(8,128)(2,1)S(1)}, bf16[3,864,128]{2,1,0:T(8,128)(2,1)S(1)}, u32[]{:S(2)}, u32[]{:S(2)}) collective-permute-start(bf16[3,864,128]{2,1,0:T(8,128)(2,1)S(1)} %pad_maximum_fusion.1.refs_2_), channel_id=1, source_target_pairs={{0,8},{4,12},{8,0},{12,4},{16,24},{20,28},{24,16},{28,20},{1,9},{5... | collective-permute-start | bytes 1990664 | tf_op jit(solution)/shard_map/ppermute | solution.py:23
  41.5 17.5 %collective-permute-start.14 = (bf16[3,864,128]{2,1,0:T(8,128)(2,1)S(1)}, bf16[3,864,128]{2,1,0:T(8,128)(2,1)S(1)}, u32[]{:S(2)}, u32[]{:S(2)}) collective-permute-start(bf16[3,864,128]{2,1,0:T(8,128)(2,1)S(1)} %pad_maximum_fusion.1.refs_2_), channel_id=1, source_target_pairs={{0,4},{4,0},{8,12},{12,8},{16,20},{20,16},{24,28},{28,24},{1,5},{5... | collective-permute-start | bytes 1990664 | tf_op jit(solution)/shard_map/ppermute | solution.py:23
  41.6 1.0 copy-start.2
  42.6 0.8 copy-start.4
  43.4 0.7 copy-start.6
  44.1 24.9 %copy-start.9 = (s32[128]{0:T(128)S(1)}, s32[128]{0:T(128)}, u32[]{:S(2)}) copy-start(s32[128]{0:T(128)} %param.17) | copy-start | bytes 1540
  56.3 2.7 %collective-permute-start.15 = (bf16[3,864,128]{2,1,0:T(8,128)(2,1)S(1)}, bf16[3,864,128]{2,1,0:T(8,128)(2,1)S(1)}, u32[]{:S(2)}, u32[]{:S(2)}) collective-permute-start(bf16[3,864,128]{2,1,0:T(8,128)(2,1)S(1)} %collective-permute-done.9.refs_4_), channel_id=1, source_target_pairs={{0,4},{4,0},{8,12},{12,8},{16,20},{20,16},{24,28},{28,24},{1,5},{5... | collective-permute-start | bytes 1990664 | tf_op jit(solution)/shard_map/ppermute | solution.py:23
  56.3 3.1 %collective-permute-start.16 = (bf16[3,864,128]{2,1,0:T(8,128)(2,1)S(1)}, bf16[3,864,128]{2,1,0:T(8,128)(2,1)S(1)}, u32[]{:S(2)}, u32[]{:S(2)}) collective-permute-start(bf16[3,864,128]{2,1,0:T(8,128)(2,1)S(1)} %collective-permute-done.10.refs_6_), channel_id=1, source_target_pairs={{0,4},{4,0},{8,12},{12,8},{16,20},{20,16},{24,28},{28,24},{1,5},{5... | collective-permute-start | bytes 1990664 | tf_op jit(solution)/shard_map/ppermute | solution.py:23
  56.9 9.8 %collective-permute-start.12 = (bf16[3,432,128]{2,1,0:T(8,128)(2,1)S(1)}, bf16[3,432,128]{2,1,0:T(8,128)(2,1)S(1)}, u32[]{:S(2)}, u32[]{:S(2)}) collective-permute-start(bf16[3,432,128]{2,1,0:T(8,128)(2,1)S(1)} %slice.52), channel_id=1, source_target_pairs={{0,16},{4,20},{8,24},{12,28},{16,0},{20,4},{24,8},{28,12},{1,17},{... | collective-permute-start | bytes 995336 | tf_op jit(solution)/shard_map/ppermute | solution.py:23
  57.5 9.4 %collective-permute-start.13 = (bf16[3,432,128]{2,1,0:T(8,128)(2,1)S(1)}, bf16[3,432,128]{2,1,0:T(8,128)(2,1)S(1)}, u32[]{:S(2)}, u32[]{:S(2)}) collective-permute-start(bf16[3,432,128]{2,1,0:T(8,128)(2,1)S(1)} %slice.53), channel_id=1, source_target_pairs={{0,8},{4,12},{8,0},{12,4},{16,24},{20,28},{24,16},{28,20},{1,9},{5... | collective-permute-start | bytes 995336 | tf_op jit(solution)/shard_map/ppermute | solution.py:23
  66.9 1.6 %collective-permute-start.17 = (bf16[3,432,128]{2,1,0:T(8,128)(2,1)S(1)}, bf16[3,432,128]{2,1,0:T(8,128)(2,1)S(1)}, u32[]{:S(2)}, u32[]{:S(2)}) collective-permute-start(bf16[3,432,128]{2,1,0:T(8,128)(2,1)S(1)} %collective-permute-done.12.refs_4_), channel_id=1, source_target_pairs={{0,4},{4,0},{8,12},{12,8},{16,20},{20,16},{24,28},{28,24},{1,5},{5... | collective-permute-start | bytes 995336 | tf_op jit(solution)/shard_map/ppermute | solution.py:23
  66.9 2.1 %collective-permute-start.18 = (bf16[3,432,128]{2,1,0:T(8,128)(2,1)S(1)}, bf16[3,432,128]{2,1,0:T(8,128)(2,1)S(1)}, u32[]{:S(2)}, u32[]{:S(2)}) collective-permute-start(bf16[3,432,128]{2,1,0:T(8,128)(2,1)S(1)} %collective-permute-done.13.refs_6_), channel_id=1, source_target_pairs={{0,4},{4,0},{8,12},{12,8},{16,20},{20,16},{24,28},{28,24},{1,5},{5... | collective-permute-start | bytes 995336 | tf_op jit(solution)/shard_map/ppermute | solution.py:23
  69.0 38.8 %copy-start.8 = (f32[1024]{0:T(1024)S(1)}, f32[1024]{0:T(1024)}, u32[]{:S(2)}) copy-start(f32[1024]{0:T(1024)} %param.12) | copy-start | bytes 12292
  77.5 2.0 %collective-permute-start.19 = (bf16[4,4,128,128]{3,2,1,0:T(8,128)(2,1)S(1)}, bf16[4,4,128,128]{3,2,1,0:T(8,128)(2,1)S(1)}, u32[]{:S(2)}, u32[]{:S(2)}) collective-permute-start(bf16[4,4,128,128]{3,2,1,0:T(8,128)(2,1)S(1)} %get-tuple-element.56), channel_id=1, source_target_pairs={{0,4},{4,0},{8,12},{12,8},{16,20},{20,16},{24,28},{28,24},{1,5},{5... | collective-permute-start | bytes 1572872 | tf_op jit(solution)/shard_map/ppermute | solution.py:23
  79.7 6.0 %collective-permute-start.20 = (bf16[1,4,128,128]{3,2,1,0:T(8,128)(2,1)S(1)}, bf16[1,4,128,128]{3,2,1,0:T(8,128)(2,1)S(1)}, u32[]{:S(2)}, u32[]{:S(2)}) collective-permute-start(bf16[1,4,128,128]{3,2,1,0:T(8,128)(2,1)S(1)} %get-tuple-element.63), channel_id=1, source_target_pairs={{0,8},{4,12},{8,0},{12,4},{16,24},{20,28},{24,16},{28,20},{1,9},{5... | collective-permute-start | bytes 393224 | tf_op jit(solution)/shard_map/ppermute | solution.py:23
  81.3 8.1 %collective-permute-start.21 = (bf16[1,4,128,128]{3,2,1,0:T(8,128)(2,1)S(1)}, bf16[1,4,128,128]{3,2,1,0:T(8,128)(2,1)S(1)}, u32[]{:S(2)}, u32[]{:S(2)}) collective-permute-start(bf16[1,4,128,128]{3,2,1,0:T(8,128)(2,1)S(1)} %get-tuple-element.65), channel_id=1, source_target_pairs={{0,16},{4,20},{8,24},{12,28},{16,0},{20,4},{24,8},{28,12},{1,17},{... | collective-permute-start | bytes 393224 | tf_op jit(solution)/shard_map/ppermute | solution.py:23
  82.8 6.6 %collective-permute-start.22 = (bf16[1,4,128,128]{3,2,1,0:T(8,128)(2,1)S(1)}, bf16[1,4,128,128]{3,2,1,0:T(8,128)(2,1)S(1)}, u32[]{:S(2)}, u32[]{:S(2)}) collective-permute-start(bf16[1,4,128,128]{3,2,1,0:T(8,128)(2,1)S(1)} %get-tuple-element.64), channel_id=1, source_target_pairs={{0,24},{4,28},{8,16},{12,20},{16,8},{20,12},{24,0},{28,4},{1,25},{... | collective-permute-start | bytes 393224 | tf_op jit(solution)/shard_map/ppermute | solution.py:23
  89.5 5.8 %collective-permute-start.23 = (bf16[128,128]{1,0:T(8,128)(2,1)S(1)}, bf16[128,128]{1,0:T(8,128)(2,1)S(1)}, u32[]{:S(2)}, u32[]{:S(2)}) collective-permute-start(bf16[128,128]{1,0:T(8,128)(2,1)S(1)} %get-tuple-element.68), channel_id=1, source_target_pairs={{0,1},{1,0},{2,3},{3,2},{4,5},{5,4},{6,7},{7,6},{8,9},{9,8},{10,11... | collective-permute-start | bytes 98312 | tf_op jit(solution)/shard_map/ppermute | solution.py:28
  92.8 4.8 %collective-permute-start.24 = (bf16[128,128]{1,0:T(8,128)(2,1)S(1)}, bf16[128,128]{1,0:T(8,128)(2,1)S(1)}, u32[]{:S(2)}, u32[]{:S(2)}) collective-permute-start(bf16[128,128]{1,0:T(8,128)(2,1)S(1)} %get-tuple-element.70), channel_id=1, source_target_pairs={{0,2},{1,3},{2,0},{3,1},{4,6},{5,7},{6,4},{7,5},{8,10},{9,11},{10,... | collective-permute-start | bytes 98312 | tf_op jit(solution)/shard_map/ppermute | solution.py:28
  93.2 5.7 %collective-permute-start.25 = (bf16[128,128]{1,0:T(8,128)(2,1)S(1)}, bf16[128,128]{1,0:T(8,128)(2,1)S(1)}, u32[]{:S(2)}, u32[]{:S(2)}) collective-permute-start(bf16[128,128]{1,0:T(8,128)(2,1)S(1)} %get-tuple-element.69), channel_id=1, source_target_pairs={{0,3},{1,2},{2,1},{3,0},{4,7},{5,6},{6,5},{7,4},{8,11},{9,10},{10,... | collective-permute-start | bytes 98312 | tf_op jit(solution)/shard_map/ppermute | solution.py:28
  98.9 4.3 %collective-permute-start.26 = (f32[128,128]{1,0:T(8,128)S(1)}, f32[128,128]{1,0:T(8,128)S(1)}, u32[]{:S(2)}, u32[]{:S(2)}) collective-permute-start(f32[128,128]{1,0:T(8,128)S(1)} %fusion.5), channel_id=1, source_target_pairs={{0,8},{4,12},{8,0},{12,4},{16,24},{20,28},{24,16},{28,20},{1,9},{5... | collective-permute-start | bytes 196616 | tf_op jit(solution)/shard_map/ppermute | solution.py:23
  100.2 4.3 %collective-permute-start.27 = (f32[128,128]{1,0:T(8,128)S(1)}, f32[128,128]{1,0:T(8,128)S(1)}, u32[]{:S(2)}, u32[]{:S(2)}) collective-permute-start(f32[128,128]{1,0:T(8,128)S(1)} %fusion.5), channel_id=1, source_target_pairs={{0,16},{4,20},{8,24},{12,28},{16,0},{20,4},{24,8},{28,12},{1,17},{... | collective-permute-start | bytes 196616 | tf_op jit(solution)/shard_map/ppermute | solution.py:23
  101.0 5.2 %collective-permute-start.28 = (f32[128,128]{1,0:T(8,128)S(1)}, f32[128,128]{1,0:T(8,128)S(1)}, u32[]{:S(2)}, u32[]{:S(2)}) collective-permute-start(f32[128,128]{1,0:T(8,128)S(1)} %fusion.5), channel_id=1, source_target_pairs={{0,24},{4,28},{8,16},{12,20},{16,8},{20,12},{24,0},{28,4},{1,25},{... | collective-permute-start | bytes 196616 | tf_op jit(solution)/shard_map/ppermute | solution.py:23
  106.2 1.6 %collective-permute-start.29 = (f32[4,128,128]{2,1,0:T(8,128)S(1)}, f32[4,128,128]{2,1,0:T(8,128)S(1)}, u32[]{:S(2)}, u32[]{:S(2)}) collective-permute-start(f32[4,128,128]{2,1,0:T(8,128)S(1)} %pad_maximum_fusion.2.even), channel_id=1, source_target_pairs={{0,4},{4,0},{8,12},{12,8},{16,20},{20,16},{24,28},{28,24},{1,5},{5... | collective-permute-start | bytes 786440 | tf_op jit(solution)/shard_map/ppermute | solution.py:23

commit v5 on v4

--- a/solution.py
+++ b/solution.py
@@ -45,9 +45,9 @@
     for masks in reversed(mask_stages(lax.axis_size("replica"))[1:]):
         held = [held] + [[swap(h, mask) for h in held] for mask in masks]
         held = [h for group in held for h in group]
+    held, *beside = lax.optimization_barrier((held, *beside))
     order = sorted(range(len(held)), key=lambda i: gather_masks(lax.axis_size("replica"))[i])
     even = jnp.stack([held[i] for i in order])
-    even, *beside = lax.optimization_barrier((even, *beside))
     return (even, swap(even, 1)), *beside
 
 
@@ -71,29 +71,18 @@
     return source, start, live_counts[0, here, source]
 
 
-def pack_kernel(shards, wanted, look_rows, table, *refs):
-    factors, refs = refs[: len(wanted)], refs[len(wanted) :]
-    parcels, blocks, done = refs[: shards - 1], refs[shards - 1 : -1], refs[-1]
+def pack_kernel(shards, look_rows, table, *refs):
+    parcels, done = refs[:-1], refs[-1]
     width = table.shape[1]
     capacity = look_rows.shape[4]
     lines = -(-capacity // width)
-    paired = HOT // 2 * lines
-    block = parcels[0].shape[0] - paired
+    block = parcels[0].shape[0] - HOT // 2 * lines
     mine, here = lax.axis_index("replica"), lax.axis_index("table")
     rows = table.at[pl.ds(pl.multiple_of(mine * block, block), block), :]
     copies = [
         pltpu.make_async_copy(rows, parcel.at[:block, :], done.at[i])
         for i, parcel in enumerate(parcels)
     ]
-    for i, factor in enumerate(factors):
-        both = blocks[0]
-        half, lanes = both.shape[0] // 2, both.shape[1]
-        at = (
-            pl.ds(pl.multiple_of((mine & 1) * half, 16), half),
-            pl.ds(pl.multiple_of((mine >> 1) * lanes, lanes), lanes),
-        )
-        into = both.at[i * half : (i + 1) * half, :]
-        copies.append(pltpu.make_async_copy(factor.at[at], into, done.at[shards - 1 + i]))
     for copy in copies:
         copy.start()
     for i, parcel in enumerate(parcels):
@@ -113,21 +102,51 @@
         copy.wait()
 
 
-def pack(look_rows, table, factors, shards, replicas):
+def pack(look_rows, table, shards, replicas):
     rows, width = table.shape
     capacity = look_rows.shape[4]
     lines = HOT // 2 * -(-capacity // width)
     parcel = jax.ShapeDtypeStruct((rows // replicas + lines, width), F32)
-    blocks = [jax.ShapeDtypeStruct((f.shape[0], width), BF16) for f in factors[:1]]
     return pl.pallas_call(
-        functools.partial(pack_kernel, shards, factors),
-        out_shape=[parcel] * (shards - 1) + blocks,
-        in_specs=[whole()] + [whole(pltpu.HBM)] * (1 + len(factors)),
-        out_specs=[whole()] * (shards - 1 + len(blocks)),
-        scratch_shapes=[pltpu.SemaphoreType.DMA((shards - 1 + len(factors),))],
+        functools.partial(pack_kernel, shards),
+        out_shape=[parcel] * (shards - 1),
+        in_specs=[whole(), whole(pltpu.HBM)],
+        out_specs=[whole()] * (shards - 1),
+        scratch_shapes=[pltpu.SemaphoreType.DMA((shards - 1,))],
         compiler_params=pltpu.CompilerParams(vmem_limit_bytes=PACK_LIMIT),
         name="pack",
-    )(look_rows, table, *factors)
+    )(look_rows, table)
+
+
+def cut_kernel(first, second, near, corner, done):
+    half, lanes = near.shape[0] // 2, near.shape[1]
+    mine = lax.axis_index("replica")
+    copies = []
+    for out, mask in ((near, 0), (corner, 3)):
+        for i, factor in enumerate((first, second)):
+            at = (
+                pl.ds(pl.multiple_of((mine & 1) * half, 16), half),
+                pl.ds(pl.multiple_of(((mine >> 1) ^ mask) * lanes, lanes), lanes),
+            )
+            into = out.at[i * half : (i + 1) * half, :]
+            copies.append(pltpu.make_async_copy(factor.at[at], into, done.at[len(copies)]))
+    for copy in copies:
+        copy.start()
+    for copy in copies:
+        copy.wait()
+
+
+def cut(factors):
+    rows = factors[0].shape[0]
+    return pl.pallas_call(
+        cut_kernel,
+        out_shape=[jax.ShapeDtypeStruct((r, 128), BF16) for r in (rows, rows)],
+        in_specs=[whole(pltpu.HBM)] * 2,
+        out_specs=[whole()] * 2,
+        scratch_shapes=[pltpu.SemaphoreType.DMA((4,))],
+        compiler_params=pltpu.CompilerParams(vmem_limit_bytes=PACK_LIMIT),
+        name="cut",
+    )(*factors)
 
 
 def quotient(value, divisor, below):
@@ -490,24 +509,24 @@
     ]
 
 
-def gather_blocks(factors, near, after):
+def gather_blocks(factors, near, corner, after):
     shards = lax.axis_size("table")
     shard_rows = factors[0].shape[0]
     half, lanes = shard_rows // 2, near.shape[2]
     first, second = swap(near, 2), swap(near, 4)
-    first, second, after = lax.optimization_barrier((first, second, after))
-    corners = [(swap(first[:, :half], 4), 0), (swap(second[:, half:], 2), 1)]
-
-    def put(block, core, column, begin, end):
+    first, second, corner, after = lax.optimization_barrier((first, second, corner, after))
+    corners = [(swap(first[1:, :half], 4), 0), (swap(second[1:, half:], 2), 1)]
+    every = tuple(range(1, shards))
+
+    def put(masks, block, core, column, begin, end):
         def copy(ref, full):
             own, here = lax.axis_index("replica"), lax.axis_index("table")
-            for k in range(1, shards):
-                source = here ^ k
-                start = source * shard_rows + ((own & 1) ^ core) * half
+            for i, mask in enumerate(masks):
+                start = (here ^ mask) * shard_rows + ((own & 1) ^ core) * half
                 at = pl.ds(pl.multiple_of(start, 16), half)
                 for which in range(begin, end):
                     full[which][at, column * lanes : (column + 1) * lanes] = ref[
-                        k - 1, (which - begin) * half : (which - begin + 1) * half, :
+                        i, (which - begin) * half : (which - begin + 1) * half, :
                     ]
 
         return block, copy
@@ -524,13 +543,15 @@
 
     early = [put_own(which, (0, 1, 2)) for which in range(2)]
     for column, block in enumerate((near, first, second)):
-        early += [put(block, 0, column, 0, 2), put(swap(block, 1), 1, column, 0, 2)]
+        early += [put(every, block, 0, column, 0, 2), put(every, swap(block, 1), 1, column, 0, 2)]
 
     def late(after):
         blocks, after = lax.optimization_barrier(([c[0] for c in corners], after))
         out = [put_own(which, (3,)) for which in range(2)]
+        out += [put((1,), corner, 0, 0, 0, 2), put((1,), swap(corner, 1), 1, 0, 0, 2)]
         for block, (_, which) in zip(blocks, corners):
-            out += [put(block, 0, 0, which, which + 1), put(swap(block, 1), 1, 0, which, which + 1)]
+            out.append(put(every[1:], block, 0, 0, which, which + 1))
+            out.append(put(every[1:], swap(block, 1), 1, 0, which, which + 1))
         return out, after
 
     return early, late, after
@@ -600,9 +621,13 @@
     factors = (cross_in, cross_out)
     even_split = splits_evenly(cross_in, replicas)
 
-    packed = pack(look_rows, emb_table, factors if even_split else (), shards, replicas)
-    parcels = [cross_over(p, k + 1) for k, p in enumerate(packed[: shards - 1])]
-    far = [cross_over(packed[shards - 1], k) for k in range(1, shards)] if even_split else []
+    packed = pack(look_rows, emb_table, shards, replicas)
+    parcels = [cross_over(p, k + 1) for k, p in enumerate(packed)]
+    far = []
+    if even_split:
+        parcels, blocks = lax.optimization_barrier((parcels, cut(factors)))
+        far = jnp.stack([cross_over(blocks[0], k) for k in range(1, shards)])
+        corner = cross_over(blocks[1], 1)[None]
     places, counted = slots(
         live_counts, look_rows, bag_order, parcels, rows, shards, replicas, batch
     )
@@ -613,7 +638,7 @@
     crossed = pool(live_counts, places, counted, emb_table, pieces, dense_emb, head)
     rank = cross_in.shape[1]
     if even_split:
-        early, late, crossed = gather_blocks(factors, jnp.stack(far), crossed)
+        early, late, crossed = gather_blocks(factors, far, corner, crossed)
         rank = rank - 128
     else:
         early, late = gather_whole(factors), None

time: 110 us -> 107 us (0.973)
  waiting for transfers between devices: 33.7 us -> 28 us
  Pallas kernels: 33.8 us -> 35.8 us
  starting transfers between devices: 34.7 us -> 36 us
    ppermute x21 -> x22, waiting for transfers between devices: 21 us -> 17.6 us  [swap(): return lax.ppermute(array, 'replica', [(i, i ^ mask) for i in range(size)])]
    ppermute x9 -> x10, waiting for transfers between devices: 12.8 us -> 10.4 us  [cross_over(): return lax.ppermute(array, 'table', [(i, i ^ mask) for i in range(size)])]
    pallas_call x1 -> x2, Pallas kernels: 2.75 us -> 4.56 us  [the longest x1 2.55 us: pack(): pl.pallas_call(functools.partial(pack_kernel, shards), out_shape=[parcel]...]
    ppermute x21 -> x22, starting transfers between devices: 17.2 us -> 18.5 us  [swap(): return lax.ppermute(array, 'replica', [(i, i ^ mask) for i in range(size)])]
    ppermute x9 -> x10, starting transfers between devices: 17.5 us -> 17.4 us  [cross_over(): return lax.ppermute(array, 'table', [(i, i ^ mask) for i in range(size)])]
    unnamed x22 -> x24, local copies, waits for them, and re-layouts: 4.78 us -> 4.77 us
  transfers between devices with their start and end apart: 30 -> 32, of which waited for: 19 -> 20; matrix products, arithmetic and copies ran while one was open for 1% -> 1% of each run, Pallas kernels for 19% -> 22%
where the time goes in v5:
time: 107 us
  starting transfers between devices  36 us (34%)
  Pallas kernels  35.8 us (33%)
  waiting for transfers between devices  28 us (26%)
  local copies, waits for them, and re-layouts  5.6 us (5%)
    ppermute x22, starting transfers between devices, swap(): return lax.ppermute(array, 'replica', [(i, i ^ mask) for i in range(size)])  18.5 us
    ppermute x22, waiting for transfers between devices, swap(): return lax.ppermute(array, 'replica', [(i, i ^ mask) for i in range(size)])  17.6 us
    ppermute x10, starting transfers between devices, cross_over(): return lax.ppermute(array, 'table', [(i, i ^ mask) for i in range(size)])  17.4 us
    pallas_call x1, Pallas kernels, pool(): pl.pallas_call(functools.partial(pool_kernel, shards), out_shape=[jax.Sha...  11.3 us
    ppermute x10, waiting for transfers between devices, cross_over(): return lax.ppermute(array, 'table', [(i, i ^ mask) for i in range(size)])  10.4 us
    pallas_call x1, Pallas kernels, dense_step(): pl.pallas_call(functools.partial(dense_kernel, shards, replicas, copies),...  8.64 us
    pallas_call x1, Pallas kernels, slots(): pl.pallas_call(functools.partial(slots_kernel, shards, replicas, batch),...  6.27 us
    unnamed x24, local copies, waits for them, and re-layouts  4.77 us
  transfers between devices with their start and end apart: 32, of which 20 were waited for; matrix products, arithmetic and copies ran while one was open for 1% of the time, Pallas kernels for 22%

profile of v5, /device:TPU:0, one launch (start us, length us, event | category | flops | bytes accessed | tf_op | source)
XLA Modules:
  0.0 106.7 jit_solution(643000253744625482)
XLA Ops:
  0.6 2.6 %pack.1 = (f32[148,128]{1,0:T(8,128)}, f32[148,128]{1,0:T(8,128)}, f32[148,128]{1,0:T(8,128)}) custom-call(s32[1,1,4,4,1248]{4,3,2,1,0:T(4,128)} %look_rows.3, f32[1024,128]{1,0:T(8,128)} %own.1), custom_call_target="tpu_custom_call" | custom-call | tf_op jit(solution)/shard_map/pack/pallas_call | solution.py:110
  3.2 3.1 %collective-permute-start = (f32[148,128]{1,0:T(8,128)}, f32[148,128]{1,0:T(8,128)S(1)}, u32[]{:S(2)}, u32[]{:S(2)}) collective-permute-start(f32[148,128]{1,0:T(8,128)} %get-tuple-element.43), channel_id=1, source_target_pairs={{0,1},{1,0},{2,3},{3,2},{4,5},{5,4},{6,7},{7,6},{8,9},{9,8},{10,11... | collective-permute-start | bytes 227336 | tf_op jit(solution)/shard_map/ppermute | solution.py:28
  6.3 2.6 %collective-permute-start.1 = (f32[148,128]{1,0:T(8,128)}, f32[148,128]{1,0:T(8,128)S(1)}, u32[]{:S(2)}, u32[]{:S(2)}) collective-permute-start(f32[148,128]{1,0:T(8,128)} %get-tuple-element.44), channel_id=1, source_target_pairs={{0,2},{1,3},{2,0},{3,1},{4,6},{5,7},{6,4},{7,5},{8,10},{9,11},{10,... | collective-permute-start | bytes 227336 | tf_op jit(solution)/shard_map/ppermute | solution.py:28
  8.9 2.0 %cut.1 = (bf16[864,128]{1,0:T(8,128)(2,1)}, bf16[864,128]{1,0:T(8,128)(2,1)}) custom-call(bf16[864,512]{1,0:T(8,128)(2,1)} %refs_2_.1, bf16[864,512]{1,0:T(8,128)(2,1)} %refs_3_.1), custom_call_target="tpu_custom_call" | custom-call | tf_op jit(solution)/shard_map/cut/pallas_call | solution.py:141
  10.9 3.6 %collective-permute-done.1.refs_1_ = f32[148,128]{1,0:T(8,128)S(1)} collective-permute-done((f32[148,128]{1,0:T(8,128)}, f32[148,128]{1,0:T(8,128)S(1)}, u32[]{:S(2)}, u32[]{:S(2)}) %collective-permute-start.1) | collective-permute-done | bytes 75808 | tf_op jit(solution)/shard_map/ppermute | solution.py:28
  14.6 0.8 collective-permute-done.2.refs_2_
  15.4 1.4 %collective-permute-start.6 = (bf16[864,128]{1,0:T(8,128)(2,1)}, bf16[864,128]{1,0:T(8,128)(2,1)S(1)}, u32[]{:S(2)}, u32[]{:S(2)}) collective-permute-start(bf16[864,128]{1,0:T(8,128)(2,1)} %get-tuple-element.52), channel_id=1, source_target_pairs={{0,1},{1,0},{2,3},{3,2},{4,5},{5,4},{6,7},{7,6},{8,9},{9,8},{10,11... | collective-permute-start | bytes 663560 | tf_op jit(solution)/shard_map/ppermute | solution.py:28
  16.8 1.6 %collective-permute-start.7 = (bf16[864,128]{1,0:T(8,128)(2,1)}, bf16[864,128]{1,0:T(8,128)(2,1)S(1)}, u32[]{:S(2)}, u32[]{:S(2)}) collective-permute-start(bf16[864,128]{1,0:T(8,128)(2,1)} %get-tuple-element.52), channel_id=1, source_target_pairs={{0,2},{1,3},{2,0},{3,1},{4,6},{5,7},{6,4},{7,5},{8,10},{9,11},{10,... | collective-permute-start | bytes 663560 | tf_op jit(solution)/shard_map/ppermute | solution.py:28
  18.4 1.4 %collective-permute-start.8 = (bf16[864,128]{1,0:T(8,128)(2,1)}, bf16[864,128]{1,0:T(8,128)(2,1)S(1)}, u32[]{:S(2)}, u32[]{:S(2)}) collective-permute-start(bf16[864,128]{1,0:T(8,128)(2,1)} %get-tuple-element.52), channel_id=1, source_target_pairs={{0,3},{1,2},{2,1},{3,0},{4,7},{5,6},{6,5},{7,4},{8,11},{9,10},{10,... | collective-permute-start | bytes 663560 | tf_op jit(solution)/shard_map/ppermute | solution.py:28
  19.8 1.6 %collective-permute-start.3 = (f32[3,128,128]{2,1,0:T(8,128)S(1)}, f32[3,128,128]{2,1,0:T(8,128)S(1)}, u32[]{:S(2)}, u32[]{:S(2)}) collective-permute-start(f32[3,128,128]{2,1,0:T(8,128)S(1)} %pad_maximum_fusion.3), channel_id=1, source_target_pairs={{0,8},{4,12},{8,0},{12,4},{16,24},{20,28},{24,16},{28,20},{1,9},{5... | collective-permute-start | bytes 589832 | tf_op jit(solution)/shard_map/ppermute | solution.py:23
  21.4 1.5 %collective-permute-start.4 = (f32[3,128,128]{2,1,0:T(8,128)S(1)}, f32[3,128,128]{2,1,0:T(8,128)S(1)}, u32[]{:S(2)}, u32[]{:S(2)}) collective-permute-start(f32[3,128,128]{2,1,0:T(8,128)S(1)} %pad_maximum_fusion.3), channel_id=1, source_target_pairs={{0,16},{4,20},{8,24},{12,28},{16,0},{20,4},{24,8},{28,12},{1,17},{... | collective-permute-start | bytes 589832 | tf_op jit(solution)/shard_map/ppermute | solution.py:23
  22.9 1.0 collective-permute-done.6
  23.9 2.4 %collective-permute-start.5 = (f32[3,128,128]{2,1,0:T(8,128)S(1)}, f32[3,128,128]{2,1,0:T(8,128)S(1)}, u32[]{:S(2)}, u32[]{:S(2)}) collective-permute-start(f32[3,128,128]{2,1,0:T(8,128)S(1)} %pad_maximum_fusion.3), channel_id=1, source_target_pairs={{0,24},{4,28},{8,16},{12,20},{16,8},{20,12},{24,0},{28,4},{1,25},{... | collective-permute-start | bytes 589832 | tf_op jit(solution)/shard_map/ppermute | solution.py:23
  26.4 0.9 copy-done.3
  27.2 0.7 copy-done.5
  27.9 0.7 copy-done.8
  28.6 6.3 %slots.1 = (s32[1,1664]{1,0:T(1,128)S(1)}, bf16[16,1024,256]{2,1,0:T(8,128)(2,1)S(1)}) custom-call(s32[1,4,4]{2,1,0:T(4,128)S(1)} %copy-done.5, s32[1,1,4,4,1248]{4,3,2,1,0:T(4,128)S(1)} %copy-done.3, s32[1,1,3328]{2,1,0:T(1,128)S(1)} %copy-done.8, f32[148,128]{1,0:T(8,128)S(1)} %collective-permute-done.refs_0_, ...), custom_call_target="tpu_custom_call" | custom-call | flops 1000 | bytes 1000 | tf_op jit(solution)/shard_map/slots/pallas_call | solution.py:228
  35.2 1.6 %collective-permute-start.10 = (bf16[3,864,128]{2,1,0:T(8,128)(2,1)S(1)}, bf16[3,864,128]{2,1,0:T(8,128)(2,1)S(1)}, u32[]{:S(2)}, u32[]{:S(2)}) collective-permute-start(bf16[3,864,128]{2,1,0:T(8,128)(2,1)S(1)} %pad_maximum_fusion.1.refs_2_), channel_id=1, source_target_pairs={{0,16},{4,20},{8,24},{12,28},{16,0},{20,4},{24,8},{28,12},{1,17},{... | collective-permute-start | bytes 1990664 | tf_op jit(solution)/shard_map/ppermute | solution.py:23
  36.8 1.5 %collective-permute-start.9 = (bf16[3,864,128]{2,1,0:T(8,128)(2,1)S(1)}, bf16[3,864,128]{2,1,0:T(8,128)(2,1)S(1)}, u32[]{:S(2)}, u32[]{:S(2)}) collective-permute-start(bf16[3,864,128]{2,1,0:T(8,128)(2,1)S(1)} %pad_maximum_fusion.1.refs_2_), channel_id=1, source_target_pairs={{0,8},{4,12},{8,0},{12,4},{16,24},{20,28},{24,16},{28,20},{1,9},{5... | collective-permute-start | bytes 1990664 | tf_op jit(solution)/shard_map/ppermute | solution.py:23
  38.3 2.9 %collective-permute-start.11 = (bf16[864,128]{1,0:T(8,128)(2,1)}, bf16[864,128]{1,0:T(8,128)(2,1)S(1)}, u32[]{:S(2)}, u32[]{:S(2)}) collective-permute-start(bf16[864,128]{1,0:T(8,128)(2,1)} %get-tuple-element.55), channel_id=1, source_target_pairs={{0,1},{1,0},{2,3},{3,2},{4,5},{5,4},{6,7},{7,6},{8,9},{9,8},{10,11... | collective-permute-start | bytes 663560 | tf_op jit(solution)/shard_map/ppermute | solution.py:28
  41.2 0.7 reshape.77.head
  42.1 1.0 copy-done.2
  43.1 0.8 copy-done.4
  43.9 0.7 copy-done.6
  44.6 11.3 %pool.1 = (bf16[128,3456]{1,0:T(8,128)(2,1)S(1)}, bf16[128,3456]{1,0:T(8,128)(2,1)S(1)}) custom-call(s32[1,4,4]{2,1,0:T(4,128)S(1)} %copy-done.6, s32[1,1664]{1,0:T(1,128)S(1)} %get-tuple-element.51.places, bf16[16,1024,256]{2,1,0:T(8,128)(2,1)S(1)} %get-tuple-element.56.counted, f32[1024,128]{1,0:T(8,128)S(1)} %copy-done.2, ...), custom_call_target="tpu_custom_call" | custom-call | flops 1000 | bytes 1000 | tf_op jit(solution)/shard_map/pool/pallas_call | solution.py:302
  58.2 0.9 collective-permute-done.17.refs_7_
  59.1 3.6 %first.3 = (f32[3328,128]{1,0:T(8,128)S(1)}, f32[128,128]{1,0:T(8,128)S(1)}) custom-call(bf16[128,3456]{1,0:T(8,128)(2,1)S(1)} %get-tuple-element.63.cross, bf16[128,3456]{1,0:T(8,128)(2,1)S(1)} %get-tuple-element.64.scaled, f32[1,3456]{1,0:T(1,128)S(1)} %reshape.79.bias, f32[1,3456]{1,0:T(1,128)S(1)} %reshape.77.head, bf16[864,512]{1,0:T(8,128)(2,1)S(1)} %copy-done, ...), custom_call_target="tpu_custom_call" | custom-call | flops 2000000000 | bytes 20000000 | tf_op jit(solution)/shard_map/first/pallas_call | solution.py:370
  62.8 1.6 %collective-permute-done.13.refs_6_ = bf16[2,432,128]{2,1,0:T(8,128)(2,1)S(1)} collective-permute-done((bf16[2,432,128]{2,1,0:T(8,128)(2,1)S(1)}, bf16[2,432,128]{2,1,0:T(8,128)(2,1)S(1)}, u32[]{:S(2)}, u32[]{:S(2)}) %collective-permute-start.13) | collective-permute-done | bytes 221216 | tf_op jit(solution)/shard_map/ppermute | solution.py:23
  65.1 1.0 collective-permute-done.19.refs_7_
  66.4 8.6 %dense.3 = (f32[1,128]{1,0:T(1,128)}, bf16[4,4,128,128]{3,2,1,0:T(8,128)(2,1)S(1)}, bf16[4,4,128,128]{3,2,1,0:T(8,128)(2,1)S(1)}) custom-call(s32[1,4,4]{2,1,0:T(4,128)S(1)} %copy-done.7, s32[1,1664]{1,0:T(1,128)S(1)} %get-tuple-element.51.places, bf16[128,3456]{1,0:T(8,128)(2,1)S(1)} %get-tuple-element.63.cross, ...), custom_call_target="tpu_custom_call" | custom-call | flops 2000000000 | bytes 20000000 | tf_op jit(solution)/shard_map/dense/pallas_call | solution.py:472
  75.3 1.7 %collective-permute-done.21 = bf16[4,4,128,128]{3,2,1,0:T(8,128)(2,1)S(1)} collective-permute-done((bf16[4,4,128,128]{3,2,1,0:T(8,128)(2,1)S(1)}, bf16[4,4,128,128]{3,2,1,0:T(8,128)(2,1)S(1)}, u32[]{:S(2)}, u32[]{:S(2)}) %collective-permute-start.21) | collective-permute-done | bytes 524320 | tf_op jit(solution)/shard_map/ppermute | solution.py:23
  77.9 1.5 %collective-permute-start.23 = (bf16[1,4,128,128]{3,2,1,0:T(8,128)(2,1)S(1)}, bf16[1,4,128,128]{3,2,1,0:T(8,128)(2,1)S(1)}, u32[]{:S(2)}, u32[]{:S(2)}) collective-permute-start(bf16[1,4,128,128]{3,2,1,0:T(8,128)(2,1)S(1)} %get-tuple-element.89), channel_id=1, source_target_pairs={{0,16},{4,20},{8,24},{12,28},{16,0},{20,4},{24,8},{28,12},{1,17},{... | collective-permute-start | bytes 393224 | tf_op jit(solution)/shard_map/ppermute | solution.py:23
  79.4 1.4 %collective-permute-start.24 = (bf16[1,4,128,128]{3,2,1,0:T(8,128)(2,1)S(1)}, bf16[1,4,128,128]{3,2,1,0:T(8,128)(2,1)S(1)}, u32[]{:S(2)}, u32[]{:S(2)}) collective-permute-start(bf16[1,4,128,128]{3,2,1,0:T(8,128)(2,1)S(1)} %get-tuple-element.88), channel_id=1, source_target_pairs={{0,24},{4,28},{8,16},{12,20},{16,8},{20,12},{24,0},{28,4},{1,25},{... | collective-permute-start | bytes 393224 | tf_op jit(solution)/shard_map/ppermute | solution.py:23
  80.8 2.8 %collective-permute-done.22 = bf16[1,4,128,128]{3,2,1,0:T(8,128)(2,1)S(1)} collective-permute-done((bf16[1,4,128,128]{3,2,1,0:T(8,128)(2,1)S(1)}, bf16[1,4,128,128]{3,2,1,0:T(8,128)(2,1)S(1)}, u32[]{:S(2)}, u32[]{:S(2)}) %collective-permute-start.22) | collective-permute-done | bytes 131104 | tf_op jit(solution)/shard_map/ppermute | solution.py:23
  83.7 1.4 %collective-permute-done.23 = bf16[1,4,128,128]{3,2,1,0:T(8,128)(2,1)S(1)} collective-permute-done((bf16[1,4,128,128]{3,2,1,0:T(8,128)(2,1)S(1)}, bf16[1,4,128,128]{3,2,1,0:T(8,128)(2,1)S(1)}, u32[]{:S(2)}, u32[]{:S(2)}) %collective-permute-start.23) | collective-permute-done | bytes 131104 | tf_op jit(solution)/shard_map/ppermute | solution.py:23
  85.1 1.6 %collective-permute-done.24 = bf16[1,4,128,128]{3,2,1,0:T(8,128)(2,1)S(1)} collective-permute-done((bf16[1,4,128,128]{3,2,1,0:T(8,128)(2,1)S(1)}, bf16[1,4,128,128]{3,2,1,0:T(8,128)(2,1)S(1)}, u32[]{:S(2)}, u32[]{:S(2)}) %collective-permute-start.24) | collective-permute-done | bytes 131104 | tf_op jit(solution)/shard_map/ppermute | solution.py:23
  87.4 2.9 %collective-permute-start.26 = (bf16[128,128]{1,0:T(8,128)(2,1)S(1)}, bf16[128,128]{1,0:T(8,128)(2,1)S(1)}, u32[]{:S(2)}, u32[]{:S(2)}) collective-permute-start(bf16[128,128]{1,0:T(8,128)(2,1)S(1)} %get-tuple-element.92), channel_id=1, source_target_pairs={{0,2},{1,3},{2,0},{3,1},{4,6},{5,7},{6,4},{7,5},{8,10},{9,11},{10,... | collective-permute-start | bytes 98312 | tf_op jit(solution)/shard_map/ppermute | solution.py:28
  90.4 0.9 collective-permute-start.27
  91.2 1.0 collective-permute-done.26
  92.3 3.8 %collective-permute-done.27 = bf16[128,128]{1,0:T(8,128)(2,1)S(1)} collective-permute-done((bf16[128,128]{1,0:T(8,128)(2,1)S(1)}, bf16[128,128]{1,0:T(8,128)(2,1)S(1)}, u32[]{:S(2)}, u32[]{:S(2)}) %collective-permute-start.27) | collective-permute-done | bytes 32800 | tf_op jit(solution)/shard_map/ppermute | solution.py:28
  96.1 0.8 collective-permute-start.28
  96.9 1.5 %collective-permute-start.29 = (f32[128,128]{1,0:T(8,128)S(1)}, f32[128,128]{1,0:T(8,128)S(1)}, u32[]{:S(2)}, u32[]{:S(2)}) collective-permute-start(f32[128,128]{1,0:T(8,128)S(1)} %fusion.5), channel_id=1, source_target_pairs={{0,16},{4,20},{8,24},{12,28},{16,0},{20,4},{24,8},{28,12},{1,17},{... | collective-permute-start | bytes 196616 | tf_op jit(solution)/shard_map/ppermute | solution.py:23
  98.5 1.2 %collective-permute-start.30 = (f32[128,128]{1,0:T(8,128)S(1)}, f32[128,128]{1,0:T(8,128)S(1)}, u32[]{:S(2)}, u32[]{:S(2)}) collective-permute-start(f32[128,128]{1,0:T(8,128)S(1)} %fusion.5), channel_id=1, source_target_pairs={{0,24},{4,28},{8,16},{12,20},{16,8},{20,12},{24,0},{28,4},{1,25},{... | collective-permute-start | bytes 196616 | tf_op jit(solution)/shard_map/ppermute | solution.py:23
  99.6 0.8 collective-permute-done.28
  100.4 0.8 collective-permute-done.29
  101.2 2.4 %collective-permute-done.30 = f32[128,128]{1,0:T(8,128)S(1)} collective-permute-done((f32[128,128]{1,0:T(8,128)S(1)}, f32[128,128]{1,0:T(8,128)S(1)}, u32[]{:S(2)}, u32[]{:S(2)}) %collective-permute-start.30) | collective-permute-done | bytes 65568 | tf_op jit(solution)/shard_map/ppermute | solution.py:23
  103.7 1.5 %collective-permute-done.31.odd = f32[4,128,128]{2,1,0:T(8,128)S(1)} collective-permute-done((f32[4,128,128]{2,1,0:T(8,128)S(1)}, f32[4,128,128]{2,1,0:T(8,128)S(1)}, u32[]{:S(2)}, u32[]{:S(2)}) %collective-permute-start.31) | collective-permute-done | bytes 262176 | tf_op jit(solution)/shard_map/ppermute | solution.py:23
  105.3 1.4 %finish.1 = (f32[1024,128]{1,0:T(8,128)}, f32[8,128]{1,0:T(8,128)}) custom-call(f32[8,128]{1,0:T(8,128)S(1)} %bitcast.57, f32[4,128,128]{2,1,0:T(8,128)S(1)} %pad_maximum_fusion.2.even, f32[4,128,128]{2,1,0:T(8,128)S(1)} %collective-permute-done.31.odd), custom_call_target="tpu_custom_call" | custom-call | tf_op jit(solution)/shard_map/finish/pallas_call | solution.py:591
  (62 shorter events, 5.7 us)
Async XLA Ops:
  3.2 7.7 %collective-permute-start = (f32[148,128]{1,0:T(8,128)}, f32[148,128]{1,0:T(8,128)S(1)}, u32[]{:S(2)}, u32[]{:S(2)}) collective-permute-start(f32[148,128]{1,0:T(8,128)} %get-tuple-element.43), channel_id=1, source_target_pairs={{0,1},{1,0},{2,3},{3,2},{4,5},{5,4},{6,7},{7,6},{8,9},{9,8},{10,11... | collective-permute-start | bytes 227336 | tf_op jit(solution)/shard_map/ppermute | solution.py:28
  6.3 8.3 %collective-permute-start.1 = (f32[148,128]{1,0:T(8,128)}, f32[148,128]{1,0:T(8,128)S(1)}, u32[]{:S(2)}, u32[]{:S(2)}) collective-permute-start(f32[148,128]{1,0:T(8,128)} %get-tuple-element.44), channel_id=1, source_target_pairs={{0,2},{1,3},{2,0},{3,1},{4,6},{5,7},{6,4},{7,5},{8,10},{9,11},{10,... | collective-permute-start | bytes 227336 | tf_op jit(solution)/shard_map/ppermute | solution.py:28
  8.9 48.8 %copy-start.11 = (f32[3456]{0:T(1024)S(1)}, f32[3456]{0:T(1024)}, u32[]{:S(2)}) copy-start(f32[3456]{0:T(1024)} %param.20) | copy-start | bytes 41476
  8.9 50.2 %copy-start = (bf16[864,512]{1,0:T(8,128)(2,1)S(1)}, bf16[864,512]{1,0:T(8,128)(2,1)}, u32[]{:S(2)}) copy-start(bf16[864,512]{1,0:T(8,128)(2,1)} %refs_2_.1) | copy-start | bytes 2654212
  8.9 50.2 %copy-start.1 = (bf16[864,512]{1,0:T(8,128)(2,1)S(1)}, bf16[864,512]{1,0:T(8,128)(2,1)}, u32[]{:S(2)}) copy-start(bf16[864,512]{1,0:T(8,128)(2,1)} %refs_3_.1) | copy-start | bytes 2654212
  8.9 6.5 %collective-permute-start.2 = (f32[148,128]{1,0:T(8,128)}, f32[148,128]{1,0:T(8,128)S(1)}, u32[]{:S(2)}, u32[]{:S(2)}) collective-permute-start(f32[148,128]{1,0:T(8,128)} %get-tuple-element.45), channel_id=1, source_target_pairs={{0,3},{1,2},{2,1},{3,0},{4,7},{5,6},{6,5},{7,4},{8,11},{9,10},{10,... | collective-permute-start | bytes 227336 | tf_op jit(solution)/shard_map/ppermute | solution.py:28
  15.4 8.5 %collective-permute-start.6 = (bf16[864,128]{1,0:T(8,128)(2,1)}, bf16[864,128]{1,0:T(8,128)(2,1)S(1)}, u32[]{:S(2)}, u32[]{:S(2)}) collective-permute-start(bf16[864,128]{1,0:T(8,128)(2,1)} %get-tuple-element.52), channel_id=1, source_target_pairs={{0,1},{1,0},{2,3},{3,2},{4,5},{5,4},{6,7},{7,6},{8,9},{9,8},{10,11... | collective-permute-start | bytes 663560 | tf_op jit(solution)/shard_map/ppermute | solution.py:28
  16.8 18.2 %collective-permute-start.7 = (bf16[864,128]{1,0:T(8,128)(2,1)}, bf16[864,128]{1,0:T(8,128)(2,1)S(1)}, u32[]{:S(2)}, u32[]{:S(2)}) collective-permute-start(bf16[864,128]{1,0:T(8,128)(2,1)} %get-tuple-element.52), channel_id=1, source_target_pairs={{0,2},{1,3},{2,0},{3,1},{4,6},{5,7},{6,4},{7,5},{8,10},{9,11},{10,... | collective-permute-start | bytes 663560 | tf_op jit(solution)/shard_map/ppermute | solution.py:28
  18.4 16.6 %collective-permute-start.8 = (bf16[864,128]{1,0:T(8,128)(2,1)}, bf16[864,128]{1,0:T(8,128)(2,1)S(1)}, u32[]{:S(2)}, u32[]{:S(2)}) collective-permute-start(bf16[864,128]{1,0:T(8,128)(2,1)} %get-tuple-element.52), channel_id=1, source_target_pairs={{0,3},{1,2},{2,1},{3,0},{4,7},{5,6},{6,5},{7,4},{8,11},{9,10},{10,... | collective-permute-start | bytes 663560 | tf_op jit(solution)/shard_map/ppermute | solution.py:28
  19.8 15.2 %collective-permute-start.3 = (f32[3,128,128]{2,1,0:T(8,128)S(1)}, f32[3,128,128]{2,1,0:T(8,128)S(1)}, u32[]{:S(2)}, u32[]{:S(2)}) collective-permute-start(f32[3,128,128]{2,1,0:T(8,128)S(1)} %pad_maximum_fusion.3), channel_id=1, source_target_pairs={{0,8},{4,12},{8,0},{12,4},{16,24},{20,28},{24,16},{28,20},{1,9},{5... | collective-permute-start | bytes 589832 | tf_op jit(solution)/shard_map/ppermute | solution.py:23
  21.4 13.7 %collective-permute-start.4 = (f32[3,128,128]{2,1,0:T(8,128)S(1)}, f32[3,128,128]{2,1,0:T(8,128)S(1)}, u32[]{:S(2)}, u32[]{:S(2)}) collective-permute-start(f32[3,128,128]{2,1,0:T(8,128)S(1)} %pad_maximum_fusion.3), channel_id=1, source_target_pairs={{0,16},{4,20},{8,24},{12,28},{16,0},{20,4},{24,8},{28,12},{1,17},{... | collective-permute-start | bytes 589832 | tf_op jit(solution)/shard_map/ppermute | solution.py:23
  23.9 11.2 %collective-permute-start.5 = (f32[3,128,128]{2,1,0:T(8,128)S(1)}, f32[3,128,128]{2,1,0:T(8,128)S(1)}, u32[]{:S(2)}, u32[]{:S(2)}) collective-permute-start(f32[3,128,128]{2,1,0:T(8,128)S(1)} %pad_maximum_fusion.3), channel_id=1, source_target_pairs={{0,24},{4,28},{8,16},{12,20},{16,8},{20,12},{24,0},{28,4},{1,25},{... | collective-permute-start | bytes 589832 | tf_op jit(solution)/shard_map/ppermute | solution.py:23
  26.4 0.9 copy-start.3
  27.2 0.7 copy-start.5
  27.9 0.7 copy-start.8
  35.2 6.9 %collective-permute-start.12 = (f32[4,3,128,128]{3,2,1,0:T(8,128)S(1)}, f32[4,3,128,128]{3,2,1,0:T(8,128)S(1)}, u32[]{:S(2)}, u32[]{:S(2)}) collective-permute-start(f32[4,3,128,128]{3,2,1,0:T(8,128)S(1)} %pad_maximum_fusion.even), channel_id=1, source_target_pairs={{0,4},{4,0},{8,12},{12,8},{16,20},{20,16},{24,28},{28,24},{1,5},{5... | collective-permute-start | bytes 2359304 | tf_op jit(solution)/shard_map/ppermute | solution.py:23
  35.2 20.6 %collective-permute-start.10 = (bf16[3,864,128]{2,1,0:T(8,128)(2,1)S(1)}, bf16[3,864,128]{2,1,0:T(8,128)(2,1)S(1)}, u32[]{:S(2)}, u32[]{:S(2)}) collective-permute-start(bf16[3,864,128]{2,1,0:T(8,128)(2,1)S(1)} %pad_maximum_fusion.1.refs_2_), channel_id=1, source_target_pairs={{0,16},{4,20},{8,24},{12,28},{16,0},{20,4},{24,8},{28,12},{1,17},{... | collective-permute-start | bytes 1990664 | tf_op jit(solution)/shard_map/ppermute | solution.py:23
  36.8 19.0 %collective-permute-start.9 = (bf16[3,864,128]{2,1,0:T(8,128)(2,1)S(1)}, bf16[3,864,128]{2,1,0:T(8,128)(2,1)S(1)}, u32[]{:S(2)}, u32[]{:S(2)}) collective-permute-start(bf16[3,864,128]{2,1,0:T(8,128)(2,1)S(1)} %pad_maximum_fusion.1.refs_2_), channel_id=1, source_target_pairs={{0,8},{4,12},{8,0},{12,4},{16,24},{20,28},{24,16},{28,20},{1,9},{5... | collective-permute-start | bytes 1990664 | tf_op jit(solution)/shard_map/ppermute | solution.py:23
  38.3 17.5 %collective-permute-start.11 = (bf16[864,128]{1,0:T(8,128)(2,1)}, bf16[864,128]{1,0:T(8,128)(2,1)S(1)}, u32[]{:S(2)}, u32[]{:S(2)}) collective-permute-start(bf16[864,128]{1,0:T(8,128)(2,1)} %get-tuple-element.55), channel_id=1, source_target_pairs={{0,1},{1,0},{2,3},{3,2},{4,5},{5,4},{6,7},{7,6},{8,9},{9,8},{10,11... | collective-permute-start | bytes 663560 | tf_op jit(solution)/shard_map/ppermute | solution.py:28
  42.0 15.7 %collective-permute-start.15 = (bf16[3,864,128]{2,1,0:T(8,128)(2,1)S(1)}, bf16[3,864,128]{2,1,0:T(8,128)(2,1)S(1)}, u32[]{:S(2)}, u32[]{:S(2)}) collective-permute-start(bf16[3,864,128]{2,1,0:T(8,128)(2,1)S(1)} %pad_maximum_fusion.1.refs_2_), channel_id=1, source_target_pairs={{0,4},{4,0},{8,12},{12,8},{16,20},{20,16},{24,28},{28,24},{1,5},{5... | collective-permute-start | bytes 1990664 | tf_op jit(solution)/shard_map/ppermute | solution.py:23
  42.1 1.0 copy-start.2
  43.1 0.8 copy-start.4
  43.9 0.7 copy-start.6
  44.5 21.9 %copy-start.7 = (s32[1,4,4]{2,1,0:T(4,128)S(1)}, s32[1,4,4]{2,1,0:T(4,128)}, u32[]{:S(2)}) copy-start(s32[1,4,4]{2,1,0:T(4,128)} %live_counts.5) | copy-start | bytes 196
  44.5 21.9 %copy-start.10 = (s32[128]{0:T(128)S(1)}, s32[128]{0:T(128)}, u32[]{:S(2)}) copy-start(s32[128]{0:T(128)} %param.17) | copy-start | bytes 1540
  55.9 2.3 %collective-permute-start.16 = (bf16[3,864,128]{2,1,0:T(8,128)(2,1)S(1)}, bf16[3,864,128]{2,1,0:T(8,128)(2,1)S(1)}, u32[]{:S(2)}, u32[]{:S(2)}) collective-permute-start(bf16[3,864,128]{2,1,0:T(8,128)(2,1)S(1)} %collective-permute-done.9.refs_4_), channel_id=1, source_target_pairs={{0,4},{4,0},{8,12},{12,8},{16,20},{20,16},{24,28},{28,24},{1,5},{5... | collective-permute-start | bytes 1990664 | tf_op jit(solution)/shard_map/ppermute | solution.py:23
  56.4 2.7 %collective-permute-start.17 = (bf16[3,864,128]{2,1,0:T(8,128)(2,1)S(1)}, bf16[3,864,128]{2,1,0:T(8,128)(2,1)S(1)}, u32[]{:S(2)}, u32[]{:S(2)}) collective-permute-start(bf16[3,864,128]{2,1,0:T(8,128)(2,1)S(1)} %collective-permute-done.10.refs_6_), channel_id=1, source_target_pairs={{0,4},{4,0},{8,12},{12,8},{16,20},{20,16},{24,28},{28,24},{1,5},{5... | collective-permute-start | bytes 1990664 | tf_op jit(solution)/shard_map/ppermute | solution.py:23
  56.5 7.8 %collective-permute-start.13 = (bf16[2,432,128]{2,1,0:T(8,128)(2,1)S(1)}, bf16[2,432,128]{2,1,0:T(8,128)(2,1)S(1)}, u32[]{:S(2)}, u32[]{:S(2)}) collective-permute-start(bf16[2,432,128]{2,1,0:T(8,128)(2,1)S(1)} %slice.52), channel_id=1, source_target_pairs={{0,16},{4,20},{8,24},{12,28},{16,0},{20,4},{24,8},{28,12},{1,17},{... | collective-permute-start | bytes 663560 | tf_op jit(solution)/shard_map/ppermute | solution.py:23
  57.1 7.5 %collective-permute-start.14 = (bf16[2,432,128]{2,1,0:T(8,128)(2,1)S(1)}, bf16[2,432,128]{2,1,0:T(8,128)(2,1)S(1)}, u32[]{:S(2)}, u32[]{:S(2)}) collective-permute-start(bf16[2,432,128]{2,1,0:T(8,128)(2,1)S(1)} %slice.53), channel_id=1, source_target_pairs={{0,8},{4,12},{8,0},{12,4},{16,24},{20,28},{24,16},{28,20},{1,9},{5... | collective-permute-start | bytes 663560 | tf_op jit(solution)/shard_map/ppermute | solution.py:23
  57.7 7.4 %collective-permute-start.18 = (bf16[1,864,128]{2,1,0:T(8,128)(2,1)S(1)}, bf16[1,864,128]{2,1,0:T(8,128)(2,1)S(1)}, u32[]{:S(2)}, u32[]{:S(2)}) collective-permute-start(bf16[1,864,128]{2,1,0:T(8,128)(2,1)S(1)} %bitcast.55), channel_id=1, source_target_pairs={{0,4},{4,0},{8,12},{12,8},{16,20},{20,16},{24,28},{28,24},{1,5},{5... | collective-permute-start | bytes 663560 | tf_op jit(solution)/shard_map/ppermute | solution.py:23
  64.6 1.5 %collective-permute-start.19 = (bf16[2,432,128]{2,1,0:T(8,128)(2,1)S(1)}, bf16[2,432,128]{2,1,0:T(8,128)(2,1)S(1)}, u32[]{:S(2)}, u32[]{:S(2)}) collective-permute-start(bf16[2,432,128]{2,1,0:T(8,128)(2,1)S(1)} %collective-permute-done.13.refs_6_), channel_id=1, source_target_pairs={{0,4},{4,0},{8,12},{12,8},{16,20},{20,16},{24,28},{28,24},{1,5},{5... | collective-permute-start | bytes 663560 | tf_op jit(solution)/shard_map/ppermute | solution.py:23
  64.6 1.8 %collective-permute-start.20 = (bf16[2,432,128]{2,1,0:T(8,128)(2,1)S(1)}, bf16[2,432,128]{2,1,0:T(8,128)(2,1)S(1)}, u32[]{:S(2)}, u32[]{:S(2)}) collective-permute-start(bf16[2,432,128]{2,1,0:T(8,128)(2,1)S(1)} %collective-permute-done.14.refs_8_), channel_id=1, source_target_pairs={{0,4},{4,0},{8,12},{12,8},{16,20},{20,16},{24,28},{28,24},{1,5},{5... | collective-permute-start | bytes 663560 | tf_op jit(solution)/shard_map/ppermute | solution.py:23
  66.4 38.9 %copy-start.9 = (f32[1024]{0:T(1024)S(1)}, f32[1024]{0:T(1024)}, u32[]{:S(2)}) copy-start(f32[1024]{0:T(1024)} %param.12) | copy-start | bytes 12292
  75.1 2.0 %collective-permute-start.21 = (bf16[4,4,128,128]{3,2,1,0:T(8,128)(2,1)S(1)}, bf16[4,4,128,128]{3,2,1,0:T(8,128)(2,1)S(1)}, u32[]{:S(2)}, u32[]{:S(2)}) collective-permute-start(bf16[4,4,128,128]{3,2,1,0:T(8,128)(2,1)S(1)} %get-tuple-element.76), channel_id=1, source_target_pairs={{0,4},{4,0},{8,12},{12,8},{16,20},{20,16},{24,28},{28,24},{1,5},{5... | collective-permute-start | bytes 1572872 | tf_op jit(solution)/shard_map/ppermute | solution.py:23
  77.3 6.4 %collective-permute-start.22 = (bf16[1,4,128,128]{3,2,1,0:T(8,128)(2,1)S(1)}, bf16[1,4,128,128]{3,2,1,0:T(8,128)(2,1)S(1)}, u32[]{:S(2)}, u32[]{:S(2)}) collective-permute-start(bf16[1,4,128,128]{3,2,1,0:T(8,128)(2,1)S(1)} %get-tuple-element.87), channel_id=1, source_target_pairs={{0,8},{4,12},{8,0},{12,4},{16,24},{20,28},{24,16},{28,20},{1,9},{5... | collective-permute-start | bytes 393224 | tf_op jit(solution)/shard_map/ppermute | solution.py:23
  77.9 7.2 %collective-permute-start.23 = (bf16[1,4,128,128]{3,2,1,0:T(8,128)(2,1)S(1)}, bf16[1,4,128,128]{3,2,1,0:T(8,128)(2,1)S(1)}, u32[]{:S(2)}, u32[]{:S(2)}) collective-permute-start(bf16[1,4,128,128]{3,2,1,0:T(8,128)(2,1)S(1)} %get-tuple-element.89), channel_id=1, source_target_pairs={{0,16},{4,20},{8,24},{12,28},{16,0},{20,4},{24,8},{28,12},{1,17},{... | collective-permute-start | bytes 393224 | tf_op jit(solution)/shard_map/ppermute | solution.py:23
  79.4 7.3 %collective-permute-start.24 = (bf16[1,4,128,128]{3,2,1,0:T(8,128)(2,1)S(1)}, bf16[1,4,128,128]{3,2,1,0:T(8,128)(2,1)S(1)}, u32[]{:S(2)}, u32[]{:S(2)}) collective-permute-start(bf16[1,4,128,128]{3,2,1,0:T(8,128)(2,1)S(1)} %get-tuple-element.88), channel_id=1, source_target_pairs={{0,24},{4,28},{8,16},{12,20},{16,8},{20,12},{24,0},{28,4},{1,25},{... | collective-permute-start | bytes 393224 | tf_op jit(solution)/shard_map/ppermute | solution.py:23
  86.8 4.5 %collective-permute-start.25 = (bf16[128,128]{1,0:T(8,128)(2,1)S(1)}, bf16[128,128]{1,0:T(8,128)(2,1)S(1)}, u32[]{:S(2)}, u32[]{:S(2)}) collective-permute-start(bf16[128,128]{1,0:T(8,128)(2,1)S(1)} %get-tuple-element.90), channel_id=1, source_target_pairs={{0,1},{1,0},{2,3},{3,2},{4,5},{5,4},{6,7},{7,6},{8,9},{9,8},{10,11... | collective-permute-start | bytes 98312 | tf_op jit(solution)/shard_map/ppermute | solution.py:28
  87.4 4.8 %collective-permute-start.26 = (bf16[128,128]{1,0:T(8,128)(2,1)S(1)}, bf16[128,128]{1,0:T(8,128)(2,1)S(1)}, u32[]{:S(2)}, u32[]{:S(2)}) collective-permute-start(bf16[128,128]{1,0:T(8,128)(2,1)S(1)} %get-tuple-element.92), channel_id=1, source_target_pairs={{0,2},{1,3},{2,0},{3,1},{4,6},{5,7},{6,4},{7,5},{8,10},{9,11},{10,... | collective-permute-start | bytes 98312 | tf_op jit(solution)/shard_map/ppermute | solution.py:28
  90.4 5.7 %collective-permute-start.27 = (bf16[128,128]{1,0:T(8,128)(2,1)S(1)}, bf16[128,128]{1,0:T(8,128)(2,1)S(1)}, u32[]{:S(2)}, u32[]{:S(2)}) collective-permute-start(bf16[128,128]{1,0:T(8,128)(2,1)S(1)} %get-tuple-element.91), channel_id=1, source_target_pairs={{0,3},{1,2},{2,1},{3,0},{4,7},{5,6},{6,5},{7,4},{8,11},{9,10},{10,... | collective-permute-start | bytes 98312 | tf_op jit(solution)/shard_map/ppermute | solution.py:28
  96.1 4.3 %collective-permute-start.28 = (f32[128,128]{1,0:T(8,128)S(1)}, f32[128,128]{1,0:T(8,128)S(1)}, u32[]{:S(2)}, u32[]{:S(2)}) collective-permute-start(f32[128,128]{1,0:T(8,128)S(1)} %fusion.5), channel_id=1, source_target_pairs={{0,8},{4,12},{8,0},{12,4},{16,24},{20,28},{24,16},{28,20},{1,9},{5... | collective-permute-start | bytes 196616 | tf_op jit(solution)/shard_map/ppermute | solution.py:23
  96.9 4.3 %collective-permute-start.29 = (f32[128,128]{1,0:T(8,128)S(1)}, f32[128,128]{1,0:T(8,128)S(1)}, u32[]{:S(2)}, u32[]{:S(2)}) collective-permute-start(f32[128,128]{1,0:T(8,128)S(1)} %fusion.5), channel_id=1, source_target_pairs={{0,16},{4,20},{8,24},{12,28},{16,0},{20,4},{24,8},{28,12},{1,17},{... | collective-permute-start | bytes 196616 | tf_op jit(solution)/shard_map/ppermute | solution.py:23
  98.5 5.2 %collective-permute-start.30 = (f32[128,128]{1,0:T(8,128)S(1)}, f32[128,128]{1,0:T(8,128)S(1)}, u32[]{:S(2)}, u32[]{:S(2)}) collective-permute-start(f32[128,128]{1,0:T(8,128)S(1)} %fusion.5), channel_id=1, source_target_pairs={{0,24},{4,28},{8,16},{12,20},{16,8},{20,12},{24,0},{28,4},{1,25},{... | collective-permute-start | bytes 196616 | tf_op jit(solution)/shard_map/ppermute | solution.py:23
  103.7 1.6 %collective-permute-start.31 = (f32[4,128,128]{2,1,0:T(8,128)S(1)}, f32[4,128,128]{2,1,0:T(8,128)S(1)}, u32[]{:S(2)}, u32[]{:S(2)}) collective-permute-start(f32[4,128,128]{2,1,0:T(8,128)S(1)} %pad_maximum_fusion.2.even), channel_id=1, source_target_pairs={{0,4},{4,0},{8,12},{12,8},{16,20},{20,16},{24,28},{28,24},{1,5},{5... | collective-permute-start | bytes 786440 | tf_op jit(solution)/shard_map/ppermute | solution.py:23

commit v6 on v5

--- a/solution.py
+++ b/solution.py
@@ -62,13 +62,12 @@
     return pl.BlockSpec(memory_space=space)
 
 
-def slot_range(live_counts, shards, j):
-    here = lax.axis_index("table")
-    source = here ^ j
+def slot_range(info, shards, j):
+    source = lax.axis_index("table") ^ j
     start = jnp.int32(0)
     for s in range(shards):
-        start = start + jnp.where(s < source, live_counts[0, here, s], 0)
-    return source, start, live_counts[0, here, source]
+        start = start + jnp.where(s < source, info[0, s], 0)
+    return source, start, info[0, source]
 
 
 def pack_kernel(shards, look_rows, table, *refs):
@@ -157,35 +156,18 @@
     return lax.shift_right_logical(value * factor, shift)
 
 
-def slots_kernel(shards, replicas, batch, live_counts, look_rows, bag_order, *refs):
-    parcels, (places, counted, shifted, words) = refs[: shards - 1], refs[shards - 1 :]
-    width = parcels[0].shape[1]
+def split_rows(value):
+    high = value.astype(BF16)
+    return high, (value - high.astype(F32)).astype(BF16)
+
+
+def ready_kernel(
+    shards, live_counts, look_rows, bag_order, dense, head, places, info, words, lead
+):
+    batch, width = dense.shape
     capacity = look_rows.shape[4]
-    lines = -(-capacity // width)
     bags = bag_order.shape[2]
-    rows = counted.shape[1]
-    block = rows // replicas
-    field = (1 << ID_BITS) - 1
-    slot = lax.broadcasted_iota(jnp.int32, (8, bags), 1)
-    ranges = [slot_range(live_counts, shards, j) for j in range(shards)]
     here = lax.axis_index("table")
-    shifted[...] = jnp.zeros_like(shifted)
-    for j, (source, start, live) in enumerate(ranges):
-        for pair in range(HOT // 2):
-            for q in range(lines):
-                size = min(width, capacity - q * width)
-
-                at = slice(q * width, q * width + size)
-                if j == 0:
-                    own = [look_rows[0, 0, here, 2 * pair + h : 2 * pair + h + 1, at] for h in (0, 1)]
-                    value = (own[0] << ID_BITS) | own[1]
-                else:
-                    line = block + pair * lines + q
-                    value = parcels[j - 1][line : line + 1, :size].astype(jnp.int32)
-                shifted[pair : pair + 1, at] = value
-        moved = pltpu.roll(shifted[...], start, 1)[:, :bags]
-        inside = (slot >= start) & (slot < start + live)
-        words[...] = jnp.where(inside, moved, words[...] if j else 0)
     order = bag_order[0]
     sample = quotient(order, bags // batch, bags)
     dest = (order - sample * (bags // batch)) * batch + sample
@@ -193,6 +175,86 @@
         one = dest[:, q * CHUNK : q * CHUNK + CHUNK // 2]
         two = dest[:, q * CHUNK + CHUNK // 2 : (q + 1) * CHUNK]
         places[:, q * CHUNK // 2 : (q + 1) * CHUNK // 2] = one | (two << 16)
+    lane = lax.broadcasted_iota(jnp.int32, info.shape, 1)
+    counts = jnp.zeros(info.shape, jnp.int32)
+    for s in range(shards):
+        counts = jnp.where(lane == s, live_counts[0, here, s], counts)
+    info[...] = counts
+    words[...] = jnp.zeros_like(words)
+    for pair in range(HOT // 2):
+        words[pair : pair + 1, :capacity] = (
+            look_rows[0, 0, here, 2 * pair : 2 * pair + 1, :] << ID_BITS
+        ) | look_rows[0, 0, here, 2 * pair + 1 : 2 * pair + 2, :]
+    lead[:, :width] = dense[...]
+    lead[:, width:] = (dense[...].astype(F32) * head[:, :width]).astype(BF16)
+
+
+def ready(live_counts, look_rows, bag_order, dense, head, shards):
+    batch, width = dense.shape
+    bags = bag_order.shape[2]
+    padded = -(-look_rows.shape[4] // width) * width
+    return pl.pallas_call(
+        functools.partial(ready_kernel, shards),
+        out_shape=[
+            jax.ShapeDtypeStruct((1, bags // 2), jnp.int32),
+            jax.ShapeDtypeStruct((1, 128), jnp.int32),
+            jax.ShapeDtypeStruct((8, padded), jnp.int32),
+            jax.ShapeDtypeStruct((batch, 2 * width), BF16),
+        ],
+        in_specs=[whole(pltpu.SMEM)] + [whole()] * 4,
+        out_specs=[whole()] * 4,
+        compiler_params=pltpu.CompilerParams(vmem_limit_bytes=VMEM_LIMIT),
+        cost_estimate=pl.CostEstimate(flops=1000, bytes_accessed=1000, transcendentals=0),
+        name="ready",
+    )(live_counts, look_rows, bag_order, dense, head)
+
+
+def own_kernel(replicas, table, own):
+    rows, width = table.shape
+    block = rows // replicas
+    mine = lax.axis_index("replica")
+    for m in range(replicas):
+        there = pl.ds(pl.multiple_of((mine ^ m) * block, block), block)
+        at = slice(m * block, (m + 1) * block)
+        own[at, :width], own[at, width:] = split_rows(table[there, :])
+
+
+def split_own(table, replicas):
+    rows, width = table.shape
+    return pl.pallas_call(
+        functools.partial(own_kernel, replicas),
+        out_shape=jax.ShapeDtypeStruct((rows, 2 * width), BF16),
+        in_specs=[whole()],
+        out_specs=whole(),
+        compiler_params=pltpu.CompilerParams(vmem_limit_bytes=VMEM_LIMIT),
+        cost_estimate=pl.CostEstimate(flops=1000, bytes_accessed=1000, transcendentals=0),
+        name="split_own",
+    )(table)
+
+
+def slots_kernel(shards, replicas, bags, info, own, *refs):
+    parcels, (counted, shifted, words) = refs[: shards - 1], refs[shards - 1 :]
+    width = parcels[0].shape[1]
+    padded = own.shape[1]
+    rows = counted.shape[1]
+    block = rows // replicas
+    field = (1 << ID_BITS) - 1
+    slot = lax.broadcasted_iota(jnp.int32, (8, bags), 1)
+    ranges = [slot_range(info, shards, j) for j in range(shards)]
+    shifted[...] = jnp.zeros_like(shifted)
+    for j, (source, start, live) in enumerate(ranges):
+        if j == 0:
+            shifted[:, :padded] = own[...]
+        else:
+            for pair in range(HOT // 2):
+                for q in range(padded // width):
+                    line = block + pair * (padded // width) + q
+                    shifted[pair : pair + 1, q * width : (q + 1) * width] = parcels[j - 1][
+                        line : line + 1, :
+                    ].astype(jnp.int32)
+        moved = pltpu.roll(shifted[...], start, 1)[:, :bags]
+        inside = (slot >= start) & (slot < start + live)
+        words[...] = jnp.where(inside, moved, words[...] if j else 0)
 
     flip = lax.axis_index("replica") * block
     low = lax.broadcasted_iota(jnp.int32, (LOW, CHUNK), 0)
@@ -221,56 +283,44 @@
         lax.fori_loop(start // CHUNK, (start + live + CHUNK - 1) // CHUNK, pair, 0)
 
 
-def slots(live_counts, look_rows, bag_order, parcels, rows, shards, replicas, batch):
-    bags = bag_order.shape[2]
-    capacity = -(-look_rows.shape[4] // 128) * 128
+def slots(info, own, parcels, bags, rows, shards, replicas):
     pairs = bags // CHUNK + shards - 1
     return pl.pallas_call(
-        functools.partial(slots_kernel, shards, replicas, batch),
-        out_shape=[
-            jax.ShapeDtypeStruct((1, bags // 2), jnp.int32),
-            jax.ShapeDtypeStruct((pairs, rows, CHUNK), BF16),
-        ],
-        in_specs=[whole(pltpu.SMEM)] + [whole()] * (2 + len(parcels)),
-        out_specs=[whole()] * 2,
+        functools.partial(slots_kernel, shards, replicas, bags),
+        out_shape=jax.ShapeDtypeStruct((pairs, rows, CHUNK), BF16),
+        in_specs=[whole(pltpu.SMEM)] + [whole()] * (1 + len(parcels)),
+        out_specs=whole(),
         scratch_shapes=[
-            pltpu.VMEM((8, bags + capacity), jnp.int32),
+            pltpu.VMEM((8, bags + own.shape[1]), jnp.int32),
             pltpu.VMEM((8, bags), jnp.int32),
         ],
         compiler_params=pltpu.CompilerParams(vmem_limit_bytes=VMEM_LIMIT),
         cost_estimate=pl.CostEstimate(flops=1000, bytes_accessed=1000, transcendentals=0),
         name="slots",
-    )(live_counts, look_rows, bag_order, *parcels)
+    )(info, own, *parcels)
 
 
 def pool_kernel(
-    shards, live_counts, places, counted, own, even, odd, dense, head, cross, scaled, table, sums, pooled
+    shards, info, places, counted, own, even, odd, lead, head, cross, scaled, table, sums, pooled
 ):
-    rows_dev, width = own.shape
+    width = lead.shape[1] // 2
     block = even.shape[2]
-    batch = dense.shape[0]
+    batch = lead.shape[0]
     half = CHUNK // 2
-    mine = lax.axis_index("replica")
-
-    def put(shard, rows, value):
-        high = value.astype(BF16)
-        table[shard, rows, :width] = high
-        table[shard, rows, width:] = (value - high.astype(F32)).astype(BF16)
-
     for m in range(2 * even.shape[0]):
-        there = pl.ds(pl.multiple_of((mine ^ m) * block, block), block)
-        rows = slice(m * block, (m + 1) * block)
-        put(0, rows, own[there, :])
+        at = slice(m * block, (m + 1) * block)
         for k in range(1, shards):
-            put(k, rows, (odd if m % 2 else even)[m // 2, k - 1])
+            value = (odd if m % 2 else even)[m // 2, k - 1]
+            table[k - 1, at, :width], table[k - 1, at, width:] = split_rows(value)
     sums[...] = jnp.zeros_like(sums)
     for j in range(shards):
-        source, start, live = slot_range(live_counts, shards, j)
-
-        def pair(q, _, j=j, source=source):
+        source, start, live = slot_range(info, shards, j)
+        found_in = own if j == 0 else table.at[j - 1]
+
+        def pair(q, _, found_in=found_in, source=source):
             at = pl.ds(pl.multiple_of(q * CHUNK, CHUNK), CHUNK)
             found = lax.dot_general(
-                counted[q + source], table[j], (((0,), (0,)), ((), ())), preferred_element_type=F32
+                counted[q + source], found_in[...], (((0,), (0,)), ((), ())), preferred_element_type=F32
             )
             sums[at, :] += found[:, :width] + found[:, width:]
             return 0
@@ -287,32 +337,34 @@
         return 0
 
     lax.fori_loop(0, sums.shape[0] // (2 * UNROLL), group, 0)
-    for f in range(cross.shape[1] // width):
+    cross[:, :width] = lead[:, :width]
+    scaled[:, :width] = lead[:, width:]
+    for f in range(1, cross.shape[1] // width):
         at = slice(f * width, (f + 1) * width)
-        block = dense[...] if f == 0 else pooled[(f - 1) * batch : f * batch, :].astype(BF16)
-        cross[:, at] = block
-        scaled[:, at] = (block.astype(F32) * head[:, at]).astype(BF16)
-
-
-def pool(live_counts, places, counted, own, pieces, dense, head):
-    rows, width = own.shape
+        value = pooled[(f - 1) * batch : f * batch, :].astype(BF16)
+        cross[:, at] = value
+        scaled[:, at] = (value.astype(F32) * head[:, at]).astype(BF16)
+
+
+def pool(info, places, counted, own, pieces, lead, head):
+    rows, width = own.shape[0], own.shape[1] // 2
     bags = 2 * places.shape[1]
     shards = pieces[0].shape[1] + 1
     smem = whole(pltpu.SMEM)
     return pl.pallas_call(
         functools.partial(pool_kernel, shards),
-        out_shape=[jax.ShapeDtypeStruct((dense.shape[0], head.shape[1]), BF16)] * 2,
+        out_shape=[jax.ShapeDtypeStruct((lead.shape[0], head.shape[1]), BF16)] * 2,
         in_specs=[smem, smem] + [whole()] * 6,
         out_specs=[whole()] * 2,
         scratch_shapes=[
-            pltpu.VMEM((shards, rows, 2 * width), BF16),
+            pltpu.VMEM((shards - 1, rows, 2 * width), BF16),
             pltpu.VMEM((bags, width), F32),
             pltpu.VMEM((bags, width), F32),
         ],
         compiler_params=pltpu.CompilerParams(vmem_limit_bytes=VMEM_LIMIT),
         cost_estimate=pl.CostEstimate(flops=1000, bytes_accessed=1000, transcendentals=0),
         name="pool",
-    )(live_counts, places, counted, own, *pieces, dense, head)
+    )(info, places, counted, own, *pieces, lead, head)
 
 
 def column_of(row, size):
@@ -384,7 +436,7 @@
     )(cross, scaled, bias, head, *weights)
 
 
-def dense_kernel(shards, replicas, copies, live_counts, places, cross, scaled, head, labels, counted, *refs):
+def dense_kernel(shards, replicas, copies, info, places, cross, scaled, head, labels, counted, *refs):
     begun, partial = refs[:2]
     weights = refs[2 : 2 + len(copies)]
     logits, even, odd, full_in, full_out, grads, logit, slots, narrow, total, spots, done = refs[
@@ -425,7 +477,7 @@
     def shard_of(k):
         end, shard = jnp.int32(0), jnp.int32(0)
         for s in range(shards - 1):
-            end = end + live_counts[0, here, s]
+            end = end + info[0, s]
             shard = shard + jnp.where(k >= end, 1, 0)
         return shard
 
@@ -460,7 +512,7 @@
 
 
 def dense_step(
-    live_counts, places, cross, scaled, head, labels, counted, begun, weights, copies, shards, replicas
+    info, places, cross, scaled, head, labels, counted, begun, weights, copies, shards, replicas
 ):
     batch, features = cross.shape
     width = 128
@@ -490,7 +542,7 @@
             flops=2 * 10**9, bytes_accessed=20 * 10**6, transcendentals=0
         ),
         name="dense",
-    )(live_counts, places, cross, scaled, head, labels, counted, *begun, *weights)
+    )(info, places, cross, scaled, head, labels, counted, *begun, *weights)
 
 
 def splits_evenly(factor, replicas):
@@ -623,19 +675,21 @@
 
     packed = pack(look_rows, emb_table, shards, replicas)
     parcels = [cross_over(p, k + 1) for k, p in enumerate(packed)]
-    far = []
+    bias, head, label_row = (x.reshape(1, -1) for x in (cross_bias, head_weight, labels))
+    prepared = ready(live_counts, look_rows, bag_order, dense_emb, head, shards)
+    parcels, prepared, blocks = lax.optimization_barrier(
+        (parcels, prepared, cut(factors) if even_split else [])
+    )
+    places, info, own_words, lead = prepared
+    far, corner = [], []
     if even_split:
-        parcels, blocks = lax.optimization_barrier((parcels, cut(factors)))
         far = jnp.stack([cross_over(blocks[0], k) for k in range(1, shards)])
         corner = cross_over(blocks[1], 1)[None]
-    places, counted = slots(
-        live_counts, look_rows, bag_order, parcels, rows, shards, replicas, batch
+    counted = slots(info, own_words, parcels, bag_order.shape[2], rows, shards, replicas)
+    pieces, far, counted, own_rows = replica_gather(
+        jnp.stack([p[:block] for p in parcels]), far, counted, split_own(emb_table, replicas)
     )
-    pieces, far, counted = replica_gather(
-        jnp.stack([p[:block] for p in parcels]), far, counted
-    )
-    bias, head = cross_bias.reshape(1, -1), head_weight.reshape(1, -1)
-    crossed = pool(live_counts, places, counted, emb_table, pieces, dense_emb, head)
+    crossed = pool(info, places, counted, own_rows, pieces, lead, head)
     rank = cross_in.shape[1]
     if even_split:
         early, late, crossed = gather_blocks(factors, far, corner, crossed)
@@ -647,11 +701,11 @@
     if late:
         last, begun = late(begun)
     logits, even, odd = dense_step(
-        live_counts,
+        info,
         places,
         *crossed,
         head,
-        labels.reshape(1, -1),
+        label_row,
         counted,
         begun,
         [block for block, _ in last],

time: 107 us -> 106 us (level)
  waiting for transfers between devices: 28 us -> 24.6 us
  starting transfers between devices: 36 us -> 38.4 us
    ppermute x10, waiting for transfers between devices: 10.4 us -> 7.43 us  [cross_over(): return lax.ppermute(array, 'table', [(i, i ^ mask) for i in range(size)])]
    ppermute x10, starting transfers between devices: 17.4 us -> 19.1 us  [cross_over(): return lax.ppermute(array, 'table', [(i, i ^ mask) for i in range(size)])]
    unnamed x24 -> x22, local copies, waits for them, and re-layouts: 4.77 us -> 4.1 us
    pallas_call x1 -> x3, Pallas kernels: 6.27 us -> 6.91 us  [the longest x1 6.23 us: slots(): pl.pallas_call(functools.partial(slots_kernel, shards, replicas, bags), o...]
  transfers between devices with their start and end apart: 32 -> 32, of which waited for: 20 -> 18; matrix products, arithmetic and copies ran while one was open for 1% -> 1% of each run, Pallas kernels for 22% -> 22%
where the time goes in v6:
time: 106 us; the launch traced here: 105 us
  starting transfers between devices  38.4 us (36%)
  Pallas kernels  36.1 us (34%)
  waiting for transfers between devices  24.6 us (23%)
  local copies, waits for them, and re-layouts  4.93 us (5%)
    ppermute x22, starting transfers between devices, swap(): return lax.ppermute(array, 'replica', [(i, i ^ mask) for i in range(size)])  19.3 us
    ppermute x10, starting transfers between devices, cross_over(): return lax.ppermute(array, 'table', [(i, i ^ mask) for i in range(size)])  19.1 us
    ppermute x22, waiting for transfers between devices, swap(): return lax.ppermute(array, 'replica', [(i, i ^ mask) for i in range(size)])  17.2 us
    pallas_call x1, Pallas kernels, pool(): pl.pallas_call(functools.partial(pool_kernel, shards), out_shape=[jax.Sha...  11.2 us
    pallas_call x1, Pallas kernels, dense_step(): pl.pallas_call(functools.partial(dense_kernel, shards, replicas, copies),...  8.51 us
    ppermute x10, waiting for transfers between devices, cross_over(): return lax.ppermute(array, 'table', [(i, i ^ mask) for i in range(size)])  7.43 us
    pallas_call x1, Pallas kernels, slots(): pl.pallas_call(functools.partial(slots_kernel, shards, replicas, bags), o...  6.23 us
    unnamed x22, local copies, waits for them, and re-layouts  4.1 us
  transfers between devices with their start and end apart: 32, of which 18 were waited for; matrix products, arithmetic and copies ran while one was open for 1% of the time, Pallas kernels for 22%

profile of v6, /device:TPU:0, one launch (start us, length us, event | category | flops | bytes accessed | tf_op | source)
XLA Modules:
  0.0 105.5 jit_solution(10311853516977322631)
XLA Ops:
  0.6 2.5 %pack.1 = (f32[148,128]{1,0:T(8,128)}, f32[148,128]{1,0:T(8,128)}, f32[148,128]{1,0:T(8,128)}) custom-call(s32[1,1,4,4,1248]{4,3,2,1,0:T(4,128)} %look_rows.3, f32[1024,128]{1,0:T(8,128)} %table.3), custom_call_target="tpu_custom_call" | custom-call | tf_op jit(solution)/shard_map/pack/pallas_call | solution.py:109
  3.2 3.1 %collective-permute-start = (f32[148,128]{1,0:T(8,128)}, f32[148,128]{1,0:T(8,128)S(1)}, u32[]{:S(2)}, u32[]{:S(2)}) collective-permute-start(f32[148,128]{1,0:T(8,128)} %get-tuple-element.50), channel_id=1, source_target_pairs={{0,1},{1,0},{2,3},{3,2},{4,5},{5,4},{6,7},{7,6},{8,9},{9,8},{10,11... | collective-permute-start | bytes 227336 | tf_op jit(solution)/shard_map/ppermute | solution.py:28
  6.3 2.6 %collective-permute-start.1 = (f32[148,128]{1,0:T(8,128)}, f32[148,128]{1,0:T(8,128)S(1)}, u32[]{:S(2)}, u32[]{:S(2)}) collective-permute-start(f32[148,128]{1,0:T(8,128)} %get-tuple-element.51), channel_id=1, source_target_pairs={{0,2},{1,3},{2,0},{3,1},{4,6},{5,7},{6,4},{7,5},{8,10},{9,11},{10,... | collective-permute-start | bytes 227336 | tf_op jit(solution)/shard_map/ppermute | solution.py:28
  8.9 0.7 reshape.77.head
  9.6 0.9 copy-done.3
  10.5 0.8 copy-done.4
  11.2 0.7 copy-done.5
  12.0 0.7 copy-done.7
  12.6 0.6 ready.1
  13.2 1.9 %cut.1 = (bf16[864,128]{1,0:T(8,128)(2,1)}, bf16[864,128]{1,0:T(8,128)(2,1)}) custom-call(bf16[864,512]{1,0:T(8,128)(2,1)} %refs_2_.1, bf16[864,512]{1,0:T(8,128)(2,1)} %refs_3_.1), custom_call_target="tpu_custom_call" | custom-call | tf_op jit(solution)/shard_map/cut/pallas_call | solution.py:140
  15.4 1.4 %collective-permute-start.6 = (bf16[864,128]{1,0:T(8,128)(2,1)}, bf16[864,128]{1,0:T(8,128)(2,1)S(1)}, u32[]{:S(2)}, u32[]{:S(2)}) collective-permute-start(bf16[864,128]{1,0:T(8,128)(2,1)} %get-tuple-element.64), channel_id=1, source_target_pairs={{0,1},{1,0},{2,3},{3,2},{4,5},{5,4},{6,7},{7,6},{8,9},{9,8},{10,11... | collective-permute-start | bytes 663560 | tf_op jit(solution)/shard_map/ppermute | solution.py:28
  16.8 2.8 %collective-permute-start.7 = (bf16[864,128]{1,0:T(8,128)(2,1)}, bf16[864,128]{1,0:T(8,128)(2,1)S(1)}, u32[]{:S(2)}, u32[]{:S(2)}) collective-permute-start(bf16[864,128]{1,0:T(8,128)(2,1)} %get-tuple-element.64), channel_id=1, source_target_pairs={{0,2},{1,3},{2,0},{3,1},{4,6},{5,7},{6,4},{7,5},{8,10},{9,11},{10,... | collective-permute-start | bytes 663560 | tf_op jit(solution)/shard_map/ppermute | solution.py:28
  19.8 1.6 %collective-permute-start.3 = (f32[3,128,128]{2,1,0:T(8,128)S(1)}, f32[3,128,128]{2,1,0:T(8,128)S(1)}, u32[]{:S(2)}, u32[]{:S(2)}) collective-permute-start(f32[3,128,128]{2,1,0:T(8,128)S(1)} %pad_maximum_fusion.3), channel_id=1, source_target_pairs={{0,8},{4,12},{8,0},{12,4},{16,24},{20,28},{24,16},{28,20},{1,9},{5... | collective-permute-start | bytes 589832 | tf_op jit(solution)/shard_map/ppermute | solution.py:23
  21.4 1.5 %collective-permute-start.4 = (f32[3,128,128]{2,1,0:T(8,128)S(1)}, f32[3,128,128]{2,1,0:T(8,128)S(1)}, u32[]{:S(2)}, u32[]{:S(2)}) collective-permute-start(f32[3,128,128]{2,1,0:T(8,128)S(1)} %pad_maximum_fusion.3), channel_id=1, source_target_pairs={{0,16},{4,20},{8,24},{12,28},{16,0},{20,4},{24,8},{28,12},{1,17},{... | collective-permute-start | bytes 589832 | tf_op jit(solution)/shard_map/ppermute | solution.py:23
  23.0 2.6 %collective-permute-done.6 = bf16[864,128]{1,0:T(8,128)(2,1)S(1)} collective-permute-done((bf16[864,128]{1,0:T(8,128)(2,1)}, bf16[864,128]{1,0:T(8,128)(2,1)S(1)}, u32[]{:S(2)}, u32[]{:S(2)}) %collective-permute-start.6) | collective-permute-done | bytes 221216 | tf_op jit(solution)/shard_map/ppermute | solution.py:28
  25.5 2.4 %collective-permute-start.5 = (f32[3,128,128]{2,1,0:T(8,128)S(1)}, f32[3,128,128]{2,1,0:T(8,128)S(1)}, u32[]{:S(2)}, u32[]{:S(2)}) collective-permute-start(f32[3,128,128]{2,1,0:T(8,128)S(1)} %pad_maximum_fusion.3), channel_id=1, source_target_pairs={{0,24},{4,28},{8,16},{12,20},{16,8},{20,12},{24,0},{28,4},{1,25},{... | collective-permute-start | bytes 589832 | tf_op jit(solution)/shard_map/ppermute | solution.py:23
  28.0 1.0 copy-done.2
  29.1 6.2 %slots.1.counted = bf16[16,1024,256]{2,1,0:T(8,128)(2,1)S(1)} custom-call(s32[1,128]{1,0:T(1,128)S(1)} %get-tuple-element.59.info, s32[8,1280]{1,0:T(8,128)S(1)} %get-tuple-element.65.own, f32[148,128]{1,0:T(8,128)S(1)} %collective-permute-done.refs_0_, f32[148,128]{1,0:T(8,128)S(1)} %collective-permute-done.1.refs_1_, ...), custom_call_target="tpu_custom_call" | custom-call | flops 1000 | bytes 1000 | tf_op jit(solution)/shard_map/slots/pallas_call | solution.py:288
  36.0 1.6 %collective-permute-start.10 = (bf16[3,864,128]{2,1,0:T(8,128)(2,1)S(1)}, bf16[3,864,128]{2,1,0:T(8,128)(2,1)S(1)}, u32[]{:S(2)}, u32[]{:S(2)}) collective-permute-start(bf16[3,864,128]{2,1,0:T(8,128)(2,1)S(1)} %pad_maximum_fusion.1.refs_2_), channel_id=1, source_target_pairs={{0,16},{4,20},{8,24},{12,28},{16,0},{20,4},{24,8},{28,12},{1,17},{... | collective-permute-start | bytes 1990664 | tf_op jit(solution)/shard_map/ppermute | solution.py:23
  37.6 1.5 %collective-permute-start.9 = (bf16[3,864,128]{2,1,0:T(8,128)(2,1)S(1)}, bf16[3,864,128]{2,1,0:T(8,128)(2,1)S(1)}, u32[]{:S(2)}, u32[]{:S(2)}) collective-permute-start(bf16[3,864,128]{2,1,0:T(8,128)(2,1)S(1)} %pad_maximum_fusion.1.refs_2_), channel_id=1, source_target_pairs={{0,8},{4,12},{8,0},{12,4},{16,24},{20,28},{24,16},{28,20},{1,9},{5... | collective-permute-start | bytes 1990664 | tf_op jit(solution)/shard_map/ppermute | solution.py:23
  39.1 3.3 %collective-permute-start.11 = (bf16[864,128]{1,0:T(8,128)(2,1)S(1)}, bf16[864,128]{1,0:T(8,128)(2,1)S(1)}, u32[]{:S(2)}, u32[]{:S(2)}) collective-permute-start(bf16[864,128]{1,0:T(8,128)(2,1)S(1)} %copy-done.10), channel_id=1, source_target_pairs={{0,1},{1,0},{2,3},{3,2},{4,5},{5,4},{6,7},{7,6},{8,9},{9,8},{10,11... | collective-permute-start | bytes 663560 | tf_op jit(solution)/shard_map/ppermute | solution.py:28
  42.4 11.2 %pool.1 = (bf16[128,3456]{1,0:T(8,128)(2,1)S(1)}, bf16[128,3456]{1,0:T(8,128)(2,1)S(1)}) custom-call(s32[1,128]{1,0:T(1,128)S(1)} %get-tuple-element.59.info, s32[1,1664]{1,0:T(1,128)S(1)} %get-tuple-element.60.places, bf16[16,1024,256]{2,1,0:T(8,128)(2,1)S(1)} %slots.1.counted, bf16[1024,256]{1,0:T(8,128)(2,1)S(1)} %split_own.1.own, ...), custom_call_target="tpu_custom_call" | custom-call | flops 1000 | bytes 1000 | tf_op jit(solution)/shard_map/pool/pallas_call | solution.py:354
  53.6 1.0 collective-permute-done.9.refs_4_
  54.6 0.5 collective-permute-start.17
  55.1 0.6 collective-permute-start.13
  55.7 1.5 %collective-permute-start.14 = (bf16[2,432,128]{2,1,0:T(8,128)(2,1)S(1)}, bf16[2,432,128]{2,1,0:T(8,128)(2,1)S(1)}, u32[]{:S(2)}, u32[]{:S(2)}) collective-permute-start(bf16[2,432,128]{2,1,0:T(8,128)(2,1)S(1)} %slice.53), channel_id=1, source_target_pairs={{0,8},{4,12},{8,0},{12,4},{16,24},{20,28},{24,16},{28,20},{1,9},{5... | collective-permute-start | bytes 663560 | tf_op jit(solution)/shard_map/ppermute | solution.py:23
  57.6 3.6 %first.3 = (f32[3328,128]{1,0:T(8,128)S(1)}, f32[128,128]{1,0:T(8,128)S(1)}) custom-call(bf16[128,3456]{1,0:T(8,128)(2,1)S(1)} %get-tuple-element.77.cross, bf16[128,3456]{1,0:T(8,128)(2,1)S(1)} %get-tuple-element.78.scaled, f32[1,3456]{1,0:T(1,128)S(1)} %reshape.79.bias, f32[1,3456]{1,0:T(1,128)S(1)} %reshape.77.head, bf16[864,512]{1,0:T(8,128)(2,1)S(1)} %copy-done, ...), custom_call_target="tpu_custom_call" | custom-call | flops 2000000000 | bytes 20000000 | tf_op jit(solution)/shard_map/first/pallas_call | solution.py:422
  61.3 1.2 %collective-permute-done.13.refs_6_ = bf16[2,432,128]{2,1,0:T(8,128)(2,1)S(1)} collective-permute-done((bf16[2,432,128]{2,1,0:T(8,128)(2,1)S(1)}, bf16[2,432,128]{2,1,0:T(8,128)(2,1)S(1)}, u32[]{:S(2)}, u32[]{:S(2)}) %collective-permute-start.13) | collective-permute-done | bytes 221216 | tf_op jit(solution)/shard_map/ppermute | solution.py:23
  63.3 1.0 collective-permute-done.19.refs_7_
  64.5 8.5 %dense.3 = (f32[1,128]{1,0:T(1,128)}, bf16[4,4,128,128]{3,2,1,0:T(8,128)(2,1)S(1)}, bf16[4,4,128,128]{3,2,1,0:T(8,128)(2,1)S(1)}) custom-call(s32[1,128]{1,0:T(1,128)S(1)} %get-tuple-element.59.info, s32[1,1664]{1,0:T(1,128)S(1)} %get-tuple-element.60.places, bf16[128,3456]{1,0:T(8,128)(2,1)S(1)} %get-tuple-element.77.cross, ...), custom_call_target="tpu_custom_call" | custom-call | flops 2000000000 | bytes 20000000 | tf_op jit(solution)/shard_map/dense/pallas_call | solution.py:524
  73.3 1.7 %collective-permute-done.21 = bf16[4,4,128,128]{3,2,1,0:T(8,128)(2,1)S(1)} collective-permute-done((bf16[4,4,128,128]{3,2,1,0:T(8,128)(2,1)S(1)}, bf16[4,4,128,128]{3,2,1,0:T(8,128)(2,1)S(1)}, u32[]{:S(2)}, u32[]{:S(2)}) %collective-permute-start.21) | collective-permute-done | bytes 524320 | tf_op jit(solution)/shard_map/ppermute | solution.py:23
  75.3 1.6 %collective-permute-start.22 = (bf16[1,4,128,128]{3,2,1,0:T(8,128)(2,1)S(1)}, bf16[1,4,128,128]{3,2,1,0:T(8,128)(2,1)S(1)}, u32[]{:S(2)}, u32[]{:S(2)}) collective-permute-start(bf16[1,4,128,128]{3,2,1,0:T(8,128)(2,1)S(1)} %get-tuple-element.101), channel_id=1, source_target_pairs={{0,8},{4,12},{8,0},{12,4},{16,24},{20,28},{24,16},{28,20},{1,9},{5... | collective-permute-start | bytes 393224 | tf_op jit(solution)/shard_map/ppermute | solution.py:23
  76.8 1.5 %collective-permute-start.23 = (bf16[1,4,128,128]{3,2,1,0:T(8,128)(2,1)S(1)}, bf16[1,4,128,128]{3,2,1,0:T(8,128)(2,1)S(1)}, u32[]{:S(2)}, u32[]{:S(2)}) collective-permute-start(bf16[1,4,128,128]{3,2,1,0:T(8,128)(2,1)S(1)} %get-tuple-element.103), channel_id=1, source_target_pairs={{0,16},{4,20},{8,24},{12,28},{16,0},{20,4},{24,8},{28,12},{1,17},{... | collective-permute-start | bytes 393224 | tf_op jit(solution)/shard_map/ppermute | solution.py:23
  78.8 2.5 %collective-permute-done.22 = bf16[1,4,128,128]{3,2,1,0:T(8,128)(2,1)S(1)} collective-permute-done((bf16[1,4,128,128]{3,2,1,0:T(8,128)(2,1)S(1)}, bf16[1,4,128,128]{3,2,1,0:T(8,128)(2,1)S(1)}, u32[]{:S(2)}, u32[]{:S(2)}) %collective-permute-start.22) | collective-permute-done | bytes 131104 | tf_op jit(solution)/shard_map/ppermute | solution.py:23
  81.3 3.7 %collective-permute-done.23 = bf16[1,4,128,128]{3,2,1,0:T(8,128)(2,1)S(1)} collective-permute-done((bf16[1,4,128,128]{3,2,1,0:T(8,128)(2,1)S(1)}, bf16[1,4,128,128]{3,2,1,0:T(8,128)(2,1)S(1)}, u32[]{:S(2)}, u32[]{:S(2)}) %collective-permute-start.23) | collective-permute-done | bytes 131104 | tf_op jit(solution)/shard_map/ppermute | solution.py:23
  85.0 3.3 %collective-permute-start.25 = (bf16[128,128]{1,0:T(8,128)(2,1)S(1)}, bf16[128,128]{1,0:T(8,128)(2,1)S(1)}, u32[]{:S(2)}, u32[]{:S(2)}) collective-permute-start(bf16[128,128]{1,0:T(8,128)(2,1)S(1)} %get-tuple-element.104), channel_id=1, source_target_pairs={{0,1},{1,0},{2,3},{3,2},{4,5},{5,4},{6,7},{7,6},{8,9},{9,8},{10,11... | collective-permute-start | bytes 98312 | tf_op jit(solution)/shard_map/ppermute | solution.py:28
  88.4 1.0 collective-permute-start.26
  89.4 1.4 %collective-permute-start.27 = (bf16[128,128]{1,0:T(8,128)(2,1)S(1)}, bf16[128,128]{1,0:T(8,128)(2,1)S(1)}, u32[]{:S(2)}, u32[]{:S(2)}) collective-permute-start(bf16[128,128]{1,0:T(8,128)(2,1)S(1)} %get-tuple-element.105), channel_id=1, source_target_pairs={{0,3},{1,2},{2,1},{3,0},{4,7},{5,6},{6,5},{7,4},{8,11},{9,10},{10,... | collective-permute-start | bytes 98312 | tf_op jit(solution)/shard_map/ppermute | solution.py:28
  90.8 2.9 %collective-permute-done.26 = bf16[128,128]{1,0:T(8,128)(2,1)S(1)} collective-permute-done((bf16[128,128]{1,0:T(8,128)(2,1)S(1)}, bf16[128,128]{1,0:T(8,128)(2,1)S(1)}, u32[]{:S(2)}, u32[]{:S(2)}) %collective-permute-start.26) | collective-permute-done | bytes 32800 | tf_op jit(solution)/shard_map/ppermute | solution.py:28
  93.7 1.4 %collective-permute-done.27 = bf16[128,128]{1,0:T(8,128)(2,1)S(1)} collective-permute-done((bf16[128,128]{1,0:T(8,128)(2,1)S(1)}, bf16[128,128]{1,0:T(8,128)(2,1)S(1)}, u32[]{:S(2)}, u32[]{:S(2)}) %collective-permute-start.27) | collective-permute-done | bytes 32800 | tf_op jit(solution)/shard_map/ppermute | solution.py:28
  95.1 1.3 %collective-permute-start.28 = (f32[128,128]{1,0:T(8,128)S(1)}, f32[128,128]{1,0:T(8,128)S(1)}, u32[]{:S(2)}, u32[]{:S(2)}) collective-permute-start(f32[128,128]{1,0:T(8,128)S(1)} %fusion.5), channel_id=1, source_target_pairs={{0,8},{4,12},{8,0},{12,4},{16,24},{20,28},{24,16},{28,20},{1,9},{5... | collective-permute-start | bytes 196616 | tf_op jit(solution)/shard_map/ppermute | solution.py:23
  96.4 0.8 collective-permute-start.29
  97.3 1.4 %collective-permute-start.30 = (f32[128,128]{1,0:T(8,128)S(1)}, f32[128,128]{1,0:T(8,128)S(1)}, u32[]{:S(2)}, u32[]{:S(2)}) collective-permute-start(f32[128,128]{1,0:T(8,128)S(1)} %fusion.5), channel_id=1, source_target_pairs={{0,24},{4,28},{8,16},{12,20},{16,8},{20,12},{24,0},{28,4},{1,25},{... | collective-permute-start | bytes 196616 | tf_op jit(solution)/shard_map/ppermute | solution.py:23
  98.7 0.8 collective-permute-done.28
  99.5 1.2 %collective-permute-done.29 = f32[128,128]{1,0:T(8,128)S(1)} collective-permute-done((f32[128,128]{1,0:T(8,128)S(1)}, f32[128,128]{1,0:T(8,128)S(1)}, u32[]{:S(2)}, u32[]{:S(2)}) %collective-permute-start.29) | collective-permute-done | bytes 65568 | tf_op jit(solution)/shard_map/ppermute | solution.py:23
  100.7 1.7 %collective-permute-done.30 = f32[128,128]{1,0:T(8,128)S(1)} collective-permute-done((f32[128,128]{1,0:T(8,128)S(1)}, f32[128,128]{1,0:T(8,128)S(1)}, u32[]{:S(2)}, u32[]{:S(2)}) %collective-permute-start.30) | collective-permute-done | bytes 65568 | tf_op jit(solution)/shard_map/ppermute | solution.py:23
  102.5 1.5 %collective-permute-done.31.odd = f32[4,128,128]{2,1,0:T(8,128)S(1)} collective-permute-done((f32[4,128,128]{2,1,0:T(8,128)S(1)}, f32[4,128,128]{2,1,0:T(8,128)S(1)}, u32[]{:S(2)}, u32[]{:S(2)}) %collective-permute-start.31) | collective-permute-done | bytes 262176 | tf_op jit(solution)/shard_map/ppermute | solution.py:23
  104.0 1.4 %finish.1 = (f32[1024,128]{1,0:T(8,128)}, f32[8,128]{1,0:T(8,128)}) custom-call(f32[8,128]{1,0:T(8,128)S(1)} %bitcast.57, f32[4,128,128]{2,1,0:T(8,128)S(1)} %pad_maximum_fusion.2.even, f32[4,128,128]{2,1,0:T(8,128)S(1)} %collective-permute-done.31.odd), custom_call_target="tpu_custom_call" | custom-call | tf_op jit(solution)/shard_map/finish/pallas_call | solution.py:643
  (62 shorter events, 3.8 us)
Async XLA Ops:
  3.2 12.0 %collective-permute-start = (f32[148,128]{1,0:T(8,128)}, f32[148,128]{1,0:T(8,128)S(1)}, u32[]{:S(2)}, u32[]{:S(2)}) collective-permute-start(f32[148,128]{1,0:T(8,128)} %get-tuple-element.50), channel_id=1, source_target_pairs={{0,1},{1,0},{2,3},{3,2},{4,5},{5,4},{6,7},{7,6},{8,9},{9,8},{10,11... | collective-permute-start | bytes 227336 | tf_op jit(solution)/shard_map/ppermute | solution.py:28
  6.3 8.9 %collective-permute-start.1 = (f32[148,128]{1,0:T(8,128)}, f32[148,128]{1,0:T(8,128)S(1)}, u32[]{:S(2)}, u32[]{:S(2)}) collective-permute-start(f32[148,128]{1,0:T(8,128)} %get-tuple-element.51), channel_id=1, source_target_pairs={{0,2},{1,3},{2,0},{3,1},{4,6},{5,7},{6,4},{7,5},{8,10},{9,11},{10,... | collective-permute-start | bytes 227336 | tf_op jit(solution)/shard_map/ppermute | solution.py:28
  8.9 6.5 %collective-permute-start.2 = (f32[148,128]{1,0:T(8,128)}, f32[148,128]{1,0:T(8,128)S(1)}, u32[]{:S(2)}, u32[]{:S(2)}) collective-permute-start(f32[148,128]{1,0:T(8,128)} %get-tuple-element.52), channel_id=1, source_target_pairs={{0,3},{1,2},{2,1},{3,0},{4,7},{5,6},{6,5},{7,4},{8,11},{9,10},{10,... | collective-permute-start | bytes 227336 | tf_op jit(solution)/shard_map/ppermute | solution.py:28
  9.6 0.9 copy-start.3
  10.5 0.8 copy-start.4
  11.2 0.7 copy-start.5
  12.0 0.7 copy-start.7
  15.1 24.0 %copy-start.10 = (bf16[864,128]{1,0:T(8,128)(2,1)S(1)}, bf16[864,128]{1,0:T(8,128)(2,1)}, u32[]{:S(2)}) copy-start(bf16[864,128]{1,0:T(8,128)(2,1)} %get-tuple-element.67) | copy-start | bytes 663556
  15.4 10.1 %collective-permute-start.6 = (bf16[864,128]{1,0:T(8,128)(2,1)}, bf16[864,128]{1,0:T(8,128)(2,1)S(1)}, u32[]{:S(2)}, u32[]{:S(2)}) collective-permute-start(bf16[864,128]{1,0:T(8,128)(2,1)} %get-tuple-element.64), channel_id=1, source_target_pairs={{0,1},{1,0},{2,3},{3,2},{4,5},{5,4},{6,7},{7,6},{8,9},{9,8},{10,11... | collective-permute-start | bytes 663560 | tf_op jit(solution)/shard_map/ppermute | solution.py:28
  16.8 19.0 %collective-permute-start.7 = (bf16[864,128]{1,0:T(8,128)(2,1)}, bf16[864,128]{1,0:T(8,128)(2,1)S(1)}, u32[]{:S(2)}, u32[]{:S(2)}) collective-permute-start(bf16[864,128]{1,0:T(8,128)(2,1)} %get-tuple-element.64), channel_id=1, source_target_pairs={{0,2},{1,3},{2,0},{3,1},{4,6},{5,7},{6,4},{7,5},{8,10},{9,11},{10,... | collective-permute-start | bytes 663560 | tf_op jit(solution)/shard_map/ppermute | solution.py:28
  19.6 16.1 %collective-permute-start.8 = (bf16[864,128]{1,0:T(8,128)(2,1)}, bf16[864,128]{1,0:T(8,128)(2,1)S(1)}, u32[]{:S(2)}, u32[]{:S(2)}) collective-permute-start(bf16[864,128]{1,0:T(8,128)(2,1)} %get-tuple-element.64), channel_id=1, source_target_pairs={{0,3},{1,2},{2,1},{3,0},{4,7},{5,6},{6,5},{7,4},{8,11},{9,10},{10,... | collective-permute-start | bytes 663560 | tf_op jit(solution)/shard_map/ppermute | solution.py:28
  19.8 16.0 %collective-permute-start.3 = (f32[3,128,128]{2,1,0:T(8,128)S(1)}, f32[3,128,128]{2,1,0:T(8,128)S(1)}, u32[]{:S(2)}, u32[]{:S(2)}) collective-permute-start(f32[3,128,128]{2,1,0:T(8,128)S(1)} %pad_maximum_fusion.3), channel_id=1, source_target_pairs={{0,8},{4,12},{8,0},{12,4},{16,24},{20,28},{24,16},{28,20},{1,9},{5... | collective-permute-start | bytes 589832 | tf_op jit(solution)/shard_map/ppermute | solution.py:23
  21.4 14.4 %collective-permute-start.4 = (f32[3,128,128]{2,1,0:T(8,128)S(1)}, f32[3,128,128]{2,1,0:T(8,128)S(1)}, u32[]{:S(2)}, u32[]{:S(2)}) collective-permute-start(f32[3,128,128]{2,1,0:T(8,128)S(1)} %pad_maximum_fusion.3), channel_id=1, source_target_pairs={{0,16},{4,20},{8,24},{12,28},{16,0},{20,4},{24,8},{28,12},{1,17},{... | collective-permute-start | bytes 589832 | tf_op jit(solution)/shard_map/ppermute | solution.py:23
  25.5 10.3 %collective-permute-start.5 = (f32[3,128,128]{2,1,0:T(8,128)S(1)}, f32[3,128,128]{2,1,0:T(8,128)S(1)}, u32[]{:S(2)}, u32[]{:S(2)}) collective-permute-start(f32[3,128,128]{2,1,0:T(8,128)S(1)} %pad_maximum_fusion.3), channel_id=1, source_target_pairs={{0,24},{4,28},{8,16},{12,20},{16,8},{20,12},{24,0},{28,4},{1,25},{... | collective-permute-start | bytes 589832 | tf_op jit(solution)/shard_map/ppermute | solution.py:23
  28.0 1.0 copy-start.2
  35.3 21.8 %copy-start.9 = (f32[3456]{0:T(1024)S(1)}, f32[3456]{0:T(1024)}, u32[]{:S(2)}) copy-start(f32[3456]{0:T(1024)} %param.20) | copy-start | bytes 41476
  35.4 22.3 %copy-start = (bf16[864,512]{1,0:T(8,128)(2,1)S(1)}, bf16[864,512]{1,0:T(8,128)(2,1)}, u32[]{:S(2)}) copy-start(bf16[864,512]{1,0:T(8,128)(2,1)} %refs_2_.1) | copy-start | bytes 2654212
  35.4 22.3 %copy-start.1 = (bf16[864,512]{1,0:T(8,128)(2,1)S(1)}, bf16[864,512]{1,0:T(8,128)(2,1)}, u32[]{:S(2)}) copy-start(bf16[864,512]{1,0:T(8,128)(2,1)} %refs_3_.1) | copy-start | bytes 2654212
  35.9 28.6 %copy-start.8 = (s32[128]{0:T(128)S(1)}, s32[128]{0:T(128)}, u32[]{:S(2)}) copy-start(s32[128]{0:T(128)} %param.17) | copy-start | bytes 1540
  35.9 6.4 %collective-permute-start.12 = (f32[4,3,128,128]{3,2,1,0:T(8,128)S(1)}, f32[4,3,128,128]{3,2,1,0:T(8,128)S(1)}, u32[]{:S(2)}, u32[]{:S(2)}) collective-permute-start(f32[4,3,128,128]{3,2,1,0:T(8,128)S(1)} %pad_maximum_fusion.even), channel_id=1, source_target_pairs={{0,4},{4,0},{8,12},{12,8},{16,20},{20,16},{24,28},{28,24},{1,5},{5... | collective-permute-start | bytes 2359304 | tf_op jit(solution)/shard_map/ppermute | solution.py:23
  36.0 17.6 %collective-permute-start.10 = (bf16[3,864,128]{2,1,0:T(8,128)(2,1)S(1)}, bf16[3,864,128]{2,1,0:T(8,128)(2,1)S(1)}, u32[]{:S(2)}, u32[]{:S(2)}) collective-permute-start(bf16[3,864,128]{2,1,0:T(8,128)(2,1)S(1)} %pad_maximum_fusion.1.refs_2_), channel_id=1, source_target_pairs={{0,16},{4,20},{8,24},{12,28},{16,0},{20,4},{24,8},{28,12},{1,17},{... | collective-permute-start | bytes 1990664 | tf_op jit(solution)/shard_map/ppermute | solution.py:23
  37.6 17.0 %collective-permute-start.9 = (bf16[3,864,128]{2,1,0:T(8,128)(2,1)S(1)}, bf16[3,864,128]{2,1,0:T(8,128)(2,1)S(1)}, u32[]{:S(2)}, u32[]{:S(2)}) collective-permute-start(bf16[3,864,128]{2,1,0:T(8,128)(2,1)S(1)} %pad_maximum_fusion.1.refs_2_), channel_id=1, source_target_pairs={{0,8},{4,12},{8,0},{12,4},{16,24},{20,28},{24,16},{28,20},{1,9},{5... | collective-permute-start | bytes 1990664 | tf_op jit(solution)/shard_map/ppermute | solution.py:23
  39.1 14.5 %collective-permute-start.11 = (bf16[864,128]{1,0:T(8,128)(2,1)S(1)}, bf16[864,128]{1,0:T(8,128)(2,1)S(1)}, u32[]{:S(2)}, u32[]{:S(2)}) collective-permute-start(bf16[864,128]{1,0:T(8,128)(2,1)S(1)} %copy-done.10), channel_id=1, source_target_pairs={{0,1},{1,0},{2,3},{3,2},{4,5},{5,4},{6,7},{7,6},{8,9},{9,8},{10,11... | collective-permute-start | bytes 663560 | tf_op jit(solution)/shard_map/ppermute | solution.py:28
  42.3 14.9 %collective-permute-start.15 = (bf16[3,864,128]{2,1,0:T(8,128)(2,1)S(1)}, bf16[3,864,128]{2,1,0:T(8,128)(2,1)S(1)}, u32[]{:S(2)}, u32[]{:S(2)}) collective-permute-start(bf16[3,864,128]{2,1,0:T(8,128)(2,1)S(1)} %pad_maximum_fusion.1.refs_2_), channel_id=1, source_target_pairs={{0,4},{4,0},{8,12},{12,8},{16,20},{20,16},{24,28},{28,24},{1,5},{5... | collective-permute-start | bytes 1990664 | tf_op jit(solution)/shard_map/ppermute | solution.py:23
  54.6 2.7 %collective-permute-start.16 = (bf16[3,864,128]{2,1,0:T(8,128)(2,1)S(1)}, bf16[3,864,128]{2,1,0:T(8,128)(2,1)S(1)}, u32[]{:S(2)}, u32[]{:S(2)}) collective-permute-start(bf16[3,864,128]{2,1,0:T(8,128)(2,1)S(1)} %collective-permute-done.9.refs_4_), channel_id=1, source_target_pairs={{0,4},{4,0},{8,12},{12,8},{16,20},{20,16},{24,28},{28,24},{1,5},{5... | collective-permute-start | bytes 1990664 | tf_op jit(solution)/shard_map/ppermute | solution.py:23
  54.6 3.1 %collective-permute-start.17 = (bf16[3,864,128]{2,1,0:T(8,128)(2,1)S(1)}, bf16[3,864,128]{2,1,0:T(8,128)(2,1)S(1)}, u32[]{:S(2)}, u32[]{:S(2)}) collective-permute-start(bf16[3,864,128]{2,1,0:T(8,128)(2,1)S(1)} %collective-permute-done.10.refs_6_), channel_id=1, source_target_pairs={{0,4},{4,0},{8,12},{12,8},{16,20},{20,16},{24,28},{28,24},{1,5},{5... | collective-permute-start | bytes 1990664 | tf_op jit(solution)/shard_map/ppermute | solution.py:23
  55.1 7.4 %collective-permute-start.13 = (bf16[2,432,128]{2,1,0:T(8,128)(2,1)S(1)}, bf16[2,432,128]{2,1,0:T(8,128)(2,1)S(1)}, u32[]{:S(2)}, u32[]{:S(2)}) collective-permute-start(bf16[2,432,128]{2,1,0:T(8,128)(2,1)S(1)} %slice.52), channel_id=1, source_target_pairs={{0,16},{4,20},{8,24},{12,28},{16,0},{20,4},{24,8},{28,12},{1,17},{... | collective-permute-start | bytes 663560 | tf_op jit(solution)/shard_map/ppermute | solution.py:23
  55.7 7.1 %collective-permute-start.14 = (bf16[2,432,128]{2,1,0:T(8,128)(2,1)S(1)}, bf16[2,432,128]{2,1,0:T(8,128)(2,1)S(1)}, u32[]{:S(2)}, u32[]{:S(2)}) collective-permute-start(bf16[2,432,128]{2,1,0:T(8,128)(2,1)S(1)} %slice.53), channel_id=1, source_target_pairs={{0,8},{4,12},{8,0},{12,4},{16,24},{20,28},{24,16},{28,20},{1,9},{5... | collective-permute-start | bytes 663560 | tf_op jit(solution)/shard_map/ppermute | solution.py:23
  57.2 6.1 %collective-permute-start.18 = (bf16[1,864,128]{2,1,0:T(8,128)(2,1)S(1)}, bf16[1,864,128]{2,1,0:T(8,128)(2,1)S(1)}, u32[]{:S(2)}, u32[]{:S(2)}) collective-permute-start(bf16[1,864,128]{2,1,0:T(8,128)(2,1)S(1)} %bitcast.55), channel_id=1, source_target_pairs={{0,4},{4,0},{8,12},{12,8},{16,20},{20,16},{24,28},{28,24},{1,5},{5... | collective-permute-start | bytes 663560 | tf_op jit(solution)/shard_map/ppermute | solution.py:23
  62.7 1.5 %collective-permute-start.19 = (bf16[2,432,128]{2,1,0:T(8,128)(2,1)S(1)}, bf16[2,432,128]{2,1,0:T(8,128)(2,1)S(1)}, u32[]{:S(2)}, u32[]{:S(2)}) collective-permute-start(bf16[2,432,128]{2,1,0:T(8,128)(2,1)S(1)} %collective-permute-done.13.refs_6_), channel_id=1, source_target_pairs={{0,4},{4,0},{8,12},{12,8},{16,20},{20,16},{24,28},{28,24},{1,5},{5... | collective-permute-start | bytes 663560 | tf_op jit(solution)/shard_map/ppermute | solution.py:23
  62.8 1.8 %collective-permute-start.20 = (bf16[2,432,128]{2,1,0:T(8,128)(2,1)S(1)}, bf16[2,432,128]{2,1,0:T(8,128)(2,1)S(1)}, u32[]{:S(2)}, u32[]{:S(2)}) collective-permute-start(bf16[2,432,128]{2,1,0:T(8,128)(2,1)S(1)} %collective-permute-done.14.refs_8_), channel_id=1, source_target_pairs={{0,4},{4,0},{8,12},{12,8},{16,20},{20,16},{24,28},{28,24},{1,5},{5... | collective-permute-start | bytes 663560 | tf_op jit(solution)/shard_map/ppermute | solution.py:23
  64.5 39.5 %copy-start.6 = (f32[1024]{0:T(1024)S(1)}, f32[1024]{0:T(1024)}, u32[]{:S(2)}) copy-start(f32[1024]{0:T(1024)} %param.12) | copy-start | bytes 12292
  73.1 2.0 %collective-permute-start.21 = (bf16[4,4,128,128]{3,2,1,0:T(8,128)(2,1)S(1)}, bf16[4,4,128,128]{3,2,1,0:T(8,128)(2,1)S(1)}, u32[]{:S(2)}, u32[]{:S(2)}) collective-permute-start(bf16[4,4,128,128]{3,2,1,0:T(8,128)(2,1)S(1)} %get-tuple-element.90), channel_id=1, source_target_pairs={{0,4},{4,0},{8,12},{12,8},{16,20},{20,16},{24,28},{28,24},{1,5},{5... | collective-permute-start | bytes 1572872 | tf_op jit(solution)/shard_map/ppermute | solution.py:23
  75.3 6.0 %collective-permute-start.22 = (bf16[1,4,128,128]{3,2,1,0:T(8,128)(2,1)S(1)}, bf16[1,4,128,128]{3,2,1,0:T(8,128)(2,1)S(1)}, u32[]{:S(2)}, u32[]{:S(2)}) collective-permute-start(bf16[1,4,128,128]{3,2,1,0:T(8,128)(2,1)S(1)} %get-tuple-element.101), channel_id=1, source_target_pairs={{0,8},{4,12},{8,0},{12,4},{16,24},{20,28},{24,16},{28,20},{1,9},{5... | collective-permute-start | bytes 393224 | tf_op jit(solution)/shard_map/ppermute | solution.py:23
  76.8 8.1 %collective-permute-start.23 = (bf16[1,4,128,128]{3,2,1,0:T(8,128)(2,1)S(1)}, bf16[1,4,128,128]{3,2,1,0:T(8,128)(2,1)S(1)}, u32[]{:S(2)}, u32[]{:S(2)}) collective-permute-start(bf16[1,4,128,128]{3,2,1,0:T(8,128)(2,1)S(1)} %get-tuple-element.103), channel_id=1, source_target_pairs={{0,16},{4,20},{8,24},{12,28},{16,0},{20,4},{24,8},{28,12},{1,17},{... | collective-permute-start | bytes 393224 | tf_op jit(solution)/shard_map/ppermute | solution.py:23
  78.3 6.6 %collective-permute-start.24 = (bf16[1,4,128,128]{3,2,1,0:T(8,128)(2,1)S(1)}, bf16[1,4,128,128]{3,2,1,0:T(8,128)(2,1)S(1)}, u32[]{:S(2)}, u32[]{:S(2)}) collective-permute-start(bf16[1,4,128,128]{3,2,1,0:T(8,128)(2,1)S(1)} %get-tuple-element.102), channel_id=1, source_target_pairs={{0,24},{4,28},{8,16},{12,20},{16,8},{20,12},{24,0},{28,4},{1,25},{... | collective-permute-start | bytes 393224 | tf_op jit(solution)/shard_map/ppermute | solution.py:23
  85.0 5.8 %collective-permute-start.25 = (bf16[128,128]{1,0:T(8,128)(2,1)S(1)}, bf16[128,128]{1,0:T(8,128)(2,1)S(1)}, u32[]{:S(2)}, u32[]{:S(2)}) collective-permute-start(bf16[128,128]{1,0:T(8,128)(2,1)S(1)} %get-tuple-element.104), channel_id=1, source_target_pairs={{0,1},{1,0},{2,3},{3,2},{4,5},{5,4},{6,7},{7,6},{8,9},{9,8},{10,11... | collective-permute-start | bytes 98312 | tf_op jit(solution)/shard_map/ppermute | solution.py:28
  88.4 5.3 %collective-permute-start.26 = (bf16[128,128]{1,0:T(8,128)(2,1)S(1)}, bf16[128,128]{1,0:T(8,128)(2,1)S(1)}, u32[]{:S(2)}, u32[]{:S(2)}) collective-permute-start(bf16[128,128]{1,0:T(8,128)(2,1)S(1)} %get-tuple-element.106), channel_id=1, source_target_pairs={{0,2},{1,3},{2,0},{3,1},{4,6},{5,7},{6,4},{7,5},{8,10},{9,11},{10,... | collective-permute-start | bytes 98312 | tf_op jit(solution)/shard_map/ppermute | solution.py:28
  89.4 5.7 %collective-permute-start.27 = (bf16[128,128]{1,0:T(8,128)(2,1)S(1)}, bf16[128,128]{1,0:T(8,128)(2,1)S(1)}, u32[]{:S(2)}, u32[]{:S(2)}) collective-permute-start(bf16[128,128]{1,0:T(8,128)(2,1)S(1)} %get-tuple-element.105), channel_id=1, source_target_pairs={{0,3},{1,2},{2,1},{3,0},{4,7},{5,6},{6,5},{7,4},{8,11},{9,10},{10,... | collective-permute-start | bytes 98312 | tf_op jit(solution)/shard_map/ppermute | solution.py:28
  95.1 4.3 %collective-permute-start.28 = (f32[128,128]{1,0:T(8,128)S(1)}, f32[128,128]{1,0:T(8,128)S(1)}, u32[]{:S(2)}, u32[]{:S(2)}) collective-permute-start(f32[128,128]{1,0:T(8,128)S(1)} %fusion.5), channel_id=1, source_target_pairs={{0,8},{4,12},{8,0},{12,4},{16,24},{20,28},{24,16},{28,20},{1,9},{5... | collective-permute-start | bytes 196616 | tf_op jit(solution)/shard_map/ppermute | solution.py:23
  96.4 4.3 %collective-permute-start.29 = (f32[128,128]{1,0:T(8,128)S(1)}, f32[128,128]{1,0:T(8,128)S(1)}, u32[]{:S(2)}, u32[]{:S(2)}) collective-permute-start(f32[128,128]{1,0:T(8,128)S(1)} %fusion.5), channel_id=1, source_target_pairs={{0,16},{4,20},{8,24},{12,28},{16,0},{20,4},{24,8},{28,12},{1,17},{... | collective-permute-start | bytes 196616 | tf_op jit(solution)/shard_map/ppermute | solution.py:23
  97.3 5.2 %collective-permute-start.30 = (f32[128,128]{1,0:T(8,128)S(1)}, f32[128,128]{1,0:T(8,128)S(1)}, u32[]{:S(2)}, u32[]{:S(2)}) collective-permute-start(f32[128,128]{1,0:T(8,128)S(1)} %fusion.5), channel_id=1, source_target_pairs={{0,24},{4,28},{8,16},{12,20},{16,8},{20,12},{24,0},{28,4},{1,25},{... | collective-permute-start | bytes 196616 | tf_op jit(solution)/shard_map/ppermute | solution.py:23
  102.4 1.6 %collective-permute-start.31 = (f32[4,128,128]{2,1,0:T(8,128)S(1)}, f32[4,128,128]{2,1,0:T(8,128)S(1)}, u32[]{:S(2)}, u32[]{:S(2)}) collective-permute-start(f32[4,128,128]{2,1,0:T(8,128)S(1)} %pad_maximum_fusion.2.even), channel_id=1, source_target_pairs={{0,4},{4,0},{8,12},{12,8},{16,20},{20,16},{24,28},{28,24},{1,5},{5... | collective-permute-start | bytes 786440 | tf_op jit(solution)/shard_map/ppermute | solution.py:23

commit v7 on v6

--- a/solution.py
+++ b/solution.py
@@ -71,7 +71,7 @@
 
 
 def pack_kernel(shards, look_rows, table, *refs):
-    parcels, done = refs[:-1], refs[-1]
+    parcels, (ids, done) = refs[:-2], refs[-2:]
     width = table.shape[1]
     capacity = look_rows.shape[4]
     lines = -(-capacity // width)
@@ -82,10 +82,14 @@
         pltpu.make_async_copy(rows, parcel.at[:block, :], done.at[i])
         for i, parcel in enumerate(parcels)
     ]
-    for copy in copies:
+    reads = [
+        pltpu.make_async_copy(look_rows.at[0, 0, here ^ (i + 1)], ids.at[i], done.at[shards - 1 + i])
+        for i in range(shards - 1)
+    ]
+    for copy in reads + copies:
         copy.start()
     for i, parcel in enumerate(parcels):
-        owner = here ^ (i + 1)
+        reads[i].wait()
         for pair in range(HOT // 2):
             for q in range(lines):
                 line = block + pair * lines + q
@@ -93,8 +97,8 @@
                 if size < width:
                     parcel[line : line + 1, :] = jnp.zeros((1, width), F32)
                 at = slice(q * width, q * width + size)
-                value = (look_rows[0, 0, owner, 2 * pair : 2 * pair + 1, at] << ID_BITS) | (
-                    look_rows[0, 0, owner, 2 * pair + 1 : 2 * pair + 2, at]
+                value = (ids[i, 2 * pair : 2 * pair + 1, at] << ID_BITS) | (
+                    ids[i, 2 * pair + 1 : 2 * pair + 2, at]
                 )
                 parcel[line : line + 1, :size] = value.astype(F32)
     for copy in copies:
@@ -109,9 +113,12 @@
     return pl.pallas_call(
         functools.partial(pack_kernel, shards),
         out_shape=[parcel] * (shards - 1),
-        in_specs=[whole(), whole(pltpu.HBM)],
+        in_specs=[whole(pltpu.HBM)] * 2,
         out_specs=[whole()] * (shards - 1),
-        scratch_shapes=[pltpu.SemaphoreType.DMA((shards - 1,))],
+        scratch_shapes=[
+            pltpu.VMEM((shards - 1,) + look_rows.shape[3:], jnp.int32),
+            pltpu.SemaphoreType.DMA((2 * shards - 2,)),
+        ],
         compiler_params=pltpu.CompilerParams(vmem_limit_bytes=PACK_LIMIT),
         name="pack",
     )(look_rows, table)
@@ -466,7 +473,6 @@
 
     half = CHUNK // 2
     chunks = bags // CHUNK
-    total[...] = jnp.zeros_like(total)
 
     def gather(q):
         for i in range(half):
@@ -483,9 +489,11 @@
 
     def add(q, shard):
         place = here ^ shard
-        total[place] += lax.dot_general(
+        found = lax.dot_general(
             narrow[...], counted[q + shard], (((0,), (1,)), ((), ())), preferred_element_type=F32
         )
+        start = slot_range(info, shards, place)[1]
+        total[place] = found + jnp.where(start < q * CHUNK, total[place], 0.0)
 
     fetch.wait()
     gather(0)

time: 106 us -> 105 us (level)
  transfers between devices with their start and end apart: 32 -> 32, of which waited for: 18 -> 18; matrix products, arithmetic and copies ran while one was open for 1% -> 1% of each run, Pallas kernels for 22% -> 23%
where the time goes in v7:
time: 105 us
  starting transfers between devices  38.5 us (37%)
  Pallas kernels  35.2 us (34%)
  waiting for transfers between devices  24.6 us (23%)
  local copies, waits for them, and re-layouts  4.93 us (5%)
    ppermute x22, starting transfers between devices, swap(): return lax.ppermute(array, 'replica', [(i, i ^ mask) for i in range(size)])  19.3 us
    ppermute x10, starting transfers between devices, cross_over(): return lax.ppermute(array, 'table', [(i, i ^ mask) for i in range(size)])  19.1 us
    ppermute x22, waiting for transfers between devices, swap(): return lax.ppermute(array, 'replica', [(i, i ^ mask) for i in range(size)])  17.2 us
    pallas_call x1, Pallas kernels, pool(): pl.pallas_call(functools.partial(pool_kernel, shards), out_shape=[jax.Sha...  11.2 us
    pallas_call x1, Pallas kernels, dense_step(): pl.pallas_call(functools.partial(dense_kernel, shards, replicas, copies),...  8.43 us
    ppermute x10, waiting for transfers between devices, cross_over(): return lax.ppermute(array, 'table', [(i, i ^ mask) for i in range(size)])  7.42 us
    pallas_call x1, Pallas kernels, slots(): pl.pallas_call(functools.partial(slots_kernel, shards, replicas, bags), o...  6.23 us
    unnamed x22, local copies, waits for them, and re-layouts  4.1 us
  transfers between devices with their start and end apart: 32, of which 18 were waited for; matrix products, arithmetic and copies ran while one was open for 1% of the time, Pallas kernels for 23%

profile of v7, /device:TPU:0, one launch (start us, length us, event | category | flops | bytes accessed | tf_op | source)
XLA Modules:
  0.0 104.5 jit_solution(15855935209624449597)
XLA Ops:
  0.6 1.7 %pack.1 = (f32[148,128]{1,0:T(8,128)}, f32[148,128]{1,0:T(8,128)}, f32[148,128]{1,0:T(8,128)}) custom-call(s32[1,1,4,4,1248]{4,3,2,1,0:T(4,128)} %look_rows.3, f32[1024,128]{1,0:T(8,128)} %table.3), custom_call_target="tpu_custom_call" | custom-call | tf_op jit(solution)/shard_map/pack/pallas_call | solution.py:113
  2.3 3.1 %collective-permute-start = (f32[148,128]{1,0:T(8,128)}, f32[148,128]{1,0:T(8,128)S(1)}, u32[]{:S(2)}, u32[]{:S(2)}) collective-permute-start(f32[148,128]{1,0:T(8,128)} %get-tuple-element.50), channel_id=1, source_target_pairs={{0,1},{1,0},{2,3},{3,2},{4,5},{5,4},{6,7},{7,6},{8,9},{9,8},{10,11... | collective-permute-start | bytes 227336 | tf_op jit(solution)/shard_map/ppermute | solution.py:28
  5.4 2.6 %collective-permute-start.1 = (f32[148,128]{1,0:T(8,128)}, f32[148,128]{1,0:T(8,128)S(1)}, u32[]{:S(2)}, u32[]{:S(2)}) collective-permute-start(f32[148,128]{1,0:T(8,128)} %get-tuple-element.51), channel_id=1, source_target_pairs={{0,2},{1,3},{2,0},{3,1},{4,6},{5,7},{6,4},{7,5},{8,10},{9,11},{10,... | collective-permute-start | bytes 227336 | tf_op jit(solution)/shard_map/ppermute | solution.py:28
  8.0 0.7 reshape.77.head
  8.8 0.9 copy-done.3
  9.6 0.8 copy-done.4
  10.4 0.7 copy-done.5
  11.1 0.7 copy-done.7
  11.8 0.6 ready.1
  12.4 1.9 %cut.1 = (bf16[864,128]{1,0:T(8,128)(2,1)}, bf16[864,128]{1,0:T(8,128)(2,1)}) custom-call(bf16[864,512]{1,0:T(8,128)(2,1)} %refs_2_.1, bf16[864,512]{1,0:T(8,128)(2,1)} %refs_3_.1), custom_call_target="tpu_custom_call" | custom-call | tf_op jit(solution)/shard_map/cut/pallas_call | solution.py:147
  14.5 1.4 %collective-permute-start.6 = (bf16[864,128]{1,0:T(8,128)(2,1)}, bf16[864,128]{1,0:T(8,128)(2,1)S(1)}, u32[]{:S(2)}, u32[]{:S(2)}) collective-permute-start(bf16[864,128]{1,0:T(8,128)(2,1)} %get-tuple-element.64), channel_id=1, source_target_pairs={{0,1},{1,0},{2,3},{3,2},{4,5},{5,4},{6,7},{7,6},{8,9},{9,8},{10,11... | collective-permute-start | bytes 663560 | tf_op jit(solution)/shard_map/ppermute | solution.py:28
  15.9 2.8 %collective-permute-start.7 = (bf16[864,128]{1,0:T(8,128)(2,1)}, bf16[864,128]{1,0:T(8,128)(2,1)S(1)}, u32[]{:S(2)}, u32[]{:S(2)}) collective-permute-start(bf16[864,128]{1,0:T(8,128)(2,1)} %get-tuple-element.64), channel_id=1, source_target_pairs={{0,2},{1,3},{2,0},{3,1},{4,6},{5,7},{6,4},{7,5},{8,10},{9,11},{10,... | collective-permute-start | bytes 663560 | tf_op jit(solution)/shard_map/ppermute | solution.py:28
  19.0 1.6 %collective-permute-start.3 = (f32[3,128,128]{2,1,0:T(8,128)S(1)}, f32[3,128,128]{2,1,0:T(8,128)S(1)}, u32[]{:S(2)}, u32[]{:S(2)}) collective-permute-start(f32[3,128,128]{2,1,0:T(8,128)S(1)} %pad_maximum_fusion.3), channel_id=1, source_target_pairs={{0,8},{4,12},{8,0},{12,4},{16,24},{20,28},{24,16},{28,20},{1,9},{5... | collective-permute-start | bytes 589832 | tf_op jit(solution)/shard_map/ppermute | solution.py:23
  20.6 1.5 %collective-permute-start.4 = (f32[3,128,128]{2,1,0:T(8,128)S(1)}, f32[3,128,128]{2,1,0:T(8,128)S(1)}, u32[]{:S(2)}, u32[]{:S(2)}) collective-permute-start(f32[3,128,128]{2,1,0:T(8,128)S(1)} %pad_maximum_fusion.3), channel_id=1, source_target_pairs={{0,16},{4,20},{8,24},{12,28},{16,0},{20,4},{24,8},{28,12},{1,17},{... | collective-permute-start | bytes 589832 | tf_op jit(solution)/shard_map/ppermute | solution.py:23
  22.1 2.6 %collective-permute-done.6 = bf16[864,128]{1,0:T(8,128)(2,1)S(1)} collective-permute-done((bf16[864,128]{1,0:T(8,128)(2,1)}, bf16[864,128]{1,0:T(8,128)(2,1)S(1)}, u32[]{:S(2)}, u32[]{:S(2)}) %collective-permute-start.6) | collective-permute-done | bytes 221216 | tf_op jit(solution)/shard_map/ppermute | solution.py:28
  24.7 2.4 %collective-permute-start.5 = (f32[3,128,128]{2,1,0:T(8,128)S(1)}, f32[3,128,128]{2,1,0:T(8,128)S(1)}, u32[]{:S(2)}, u32[]{:S(2)}) collective-permute-start(f32[3,128,128]{2,1,0:T(8,128)S(1)} %pad_maximum_fusion.3), channel_id=1, source_target_pairs={{0,24},{4,28},{8,16},{12,20},{16,8},{20,12},{24,0},{28,4},{1,25},{... | collective-permute-start | bytes 589832 | tf_op jit(solution)/shard_map/ppermute | solution.py:23
  27.1 1.0 copy-done.2
  28.3 6.2 %slots.1.counted = bf16[16,1024,256]{2,1,0:T(8,128)(2,1)S(1)} custom-call(s32[1,128]{1,0:T(1,128)S(1)} %get-tuple-element.59.info, s32[8,1280]{1,0:T(8,128)S(1)} %get-tuple-element.65.own, f32[148,128]{1,0:T(8,128)S(1)} %collective-permute-done.refs_0_, f32[148,128]{1,0:T(8,128)S(1)} %collective-permute-done.1.refs_1_, ...), custom_call_target="tpu_custom_call" | custom-call | flops 1000 | bytes 1000 | tf_op jit(solution)/shard_map/slots/pallas_call | solution.py:295
  35.2 1.6 %collective-permute-start.10 = (bf16[3,864,128]{2,1,0:T(8,128)(2,1)S(1)}, bf16[3,864,128]{2,1,0:T(8,128)(2,1)S(1)}, u32[]{:S(2)}, u32[]{:S(2)}) collective-permute-start(bf16[3,864,128]{2,1,0:T(8,128)(2,1)S(1)} %pad_maximum_fusion.1.refs_2_), channel_id=1, source_target_pairs={{0,16},{4,20},{8,24},{12,28},{16,0},{20,4},{24,8},{28,12},{1,17},{... | collective-permute-start | bytes 1990664 | tf_op jit(solution)/shard_map/ppermute | solution.py:23
  36.7 1.5 %collective-permute-start.9 = (bf16[3,864,128]{2,1,0:T(8,128)(2,1)S(1)}, bf16[3,864,128]{2,1,0:T(8,128)(2,1)S(1)}, u32[]{:S(2)}, u32[]{:S(2)}) collective-permute-start(bf16[3,864,128]{2,1,0:T(8,128)(2,1)S(1)} %pad_maximum_fusion.1.refs_2_), channel_id=1, source_target_pairs={{0,8},{4,12},{8,0},{12,4},{16,24},{20,28},{24,16},{28,20},{1,9},{5... | collective-permute-start | bytes 1990664 | tf_op jit(solution)/shard_map/ppermute | solution.py:23
  38.2 3.3 %collective-permute-start.11 = (bf16[864,128]{1,0:T(8,128)(2,1)S(1)}, bf16[864,128]{1,0:T(8,128)(2,1)S(1)}, u32[]{:S(2)}, u32[]{:S(2)}) collective-permute-start(bf16[864,128]{1,0:T(8,128)(2,1)S(1)} %copy-done.10), channel_id=1, source_target_pairs={{0,1},{1,0},{2,3},{3,2},{4,5},{5,4},{6,7},{7,6},{8,9},{9,8},{10,11... | collective-permute-start | bytes 663560 | tf_op jit(solution)/shard_map/ppermute | solution.py:28
  41.5 11.2 %pool.1 = (bf16[128,3456]{1,0:T(8,128)(2,1)S(1)}, bf16[128,3456]{1,0:T(8,128)(2,1)S(1)}) custom-call(s32[1,128]{1,0:T(1,128)S(1)} %get-tuple-element.59.info, s32[1,1664]{1,0:T(1,128)S(1)} %get-tuple-element.60.places, bf16[16,1024,256]{2,1,0:T(8,128)(2,1)S(1)} %slots.1.counted, bf16[1024,256]{1,0:T(8,128)(2,1)S(1)} %split_own.1.own, ...), custom_call_target="tpu_custom_call" | custom-call | flops 1000 | bytes 1000 | tf_op jit(solution)/shard_map/pool/pallas_call | solution.py:361
  52.7 1.0 collective-permute-done.9.refs_4_
  54.3 0.6 collective-permute-start.13
  54.8 1.5 %collective-permute-start.14 = (bf16[2,432,128]{2,1,0:T(8,128)(2,1)S(1)}, bf16[2,432,128]{2,1,0:T(8,128)(2,1)S(1)}, u32[]{:S(2)}, u32[]{:S(2)}) collective-permute-start(bf16[2,432,128]{2,1,0:T(8,128)(2,1)S(1)} %slice.53), channel_id=1, source_target_pairs={{0,8},{4,12},{8,0},{12,4},{16,24},{20,28},{24,16},{28,20},{1,9},{5... | collective-permute-start | bytes 663560 | tf_op jit(solution)/shard_map/ppermute | solution.py:23
  56.8 3.6 %first.3 = (f32[3328,128]{1,0:T(8,128)S(1)}, f32[128,128]{1,0:T(8,128)S(1)}) custom-call(bf16[128,3456]{1,0:T(8,128)(2,1)S(1)} %get-tuple-element.77.cross, bf16[128,3456]{1,0:T(8,128)(2,1)S(1)} %get-tuple-element.78.scaled, f32[1,3456]{1,0:T(1,128)S(1)} %reshape.79.bias, f32[1,3456]{1,0:T(1,128)S(1)} %reshape.77.head, bf16[864,512]{1,0:T(8,128)(2,1)S(1)} %copy-done, ...), custom_call_target="tpu_custom_call" | custom-call | flops 2000000000 | bytes 20000000 | tf_op jit(solution)/shard_map/first/pallas_call | solution.py:429
  60.4 1.2 %collective-permute-done.13.refs_6_ = bf16[2,432,128]{2,1,0:T(8,128)(2,1)S(1)} collective-permute-done((bf16[2,432,128]{2,1,0:T(8,128)(2,1)S(1)}, bf16[2,432,128]{2,1,0:T(8,128)(2,1)S(1)}, u32[]{:S(2)}, u32[]{:S(2)}) %collective-permute-start.13) | collective-permute-done | bytes 221216 | tf_op jit(solution)/shard_map/ppermute | solution.py:23
  61.9 0.5 collective-permute-start.20
  62.4 1.0 collective-permute-done.19.refs_7_
  63.7 8.4 %dense.3 = (f32[1,128]{1,0:T(1,128)}, bf16[4,4,128,128]{3,2,1,0:T(8,128)(2,1)S(1)}, bf16[4,4,128,128]{3,2,1,0:T(8,128)(2,1)S(1)}) custom-call(s32[1,128]{1,0:T(1,128)S(1)} %get-tuple-element.59.info, s32[1,1664]{1,0:T(1,128)S(1)} %get-tuple-element.60.places, bf16[128,3456]{1,0:T(8,128)(2,1)S(1)} %get-tuple-element.77.cross, ...), custom_call_target="tpu_custom_call" | custom-call | flops 2000000000 | bytes 20000000 | tf_op jit(solution)/shard_map/dense/pallas_call | solution.py:532
  72.4 1.7 %collective-permute-done.21 = bf16[4,4,128,128]{3,2,1,0:T(8,128)(2,1)S(1)} collective-permute-done((bf16[4,4,128,128]{3,2,1,0:T(8,128)(2,1)S(1)}, bf16[4,4,128,128]{3,2,1,0:T(8,128)(2,1)S(1)}, u32[]{:S(2)}, u32[]{:S(2)}) %collective-permute-start.21) | collective-permute-done | bytes 524320 | tf_op jit(solution)/shard_map/ppermute | solution.py:23
  74.3 1.6 %collective-permute-start.22 = (bf16[1,4,128,128]{3,2,1,0:T(8,128)(2,1)S(1)}, bf16[1,4,128,128]{3,2,1,0:T(8,128)(2,1)S(1)}, u32[]{:S(2)}, u32[]{:S(2)}) collective-permute-start(bf16[1,4,128,128]{3,2,1,0:T(8,128)(2,1)S(1)} %get-tuple-element.101), channel_id=1, source_target_pairs={{0,8},{4,12},{8,0},{12,4},{16,24},{20,28},{24,16},{28,20},{1,9},{5... | collective-permute-start | bytes 393224 | tf_op jit(solution)/shard_map/ppermute | solution.py:23
  75.9 1.5 %collective-permute-start.23 = (bf16[1,4,128,128]{3,2,1,0:T(8,128)(2,1)S(1)}, bf16[1,4,128,128]{3,2,1,0:T(8,128)(2,1)S(1)}, u32[]{:S(2)}, u32[]{:S(2)}) collective-permute-start(bf16[1,4,128,128]{3,2,1,0:T(8,128)(2,1)S(1)} %get-tuple-element.103), channel_id=1, source_target_pairs={{0,16},{4,20},{8,24},{12,28},{16,0},{20,4},{24,8},{28,12},{1,17},{... | collective-permute-start | bytes 393224 | tf_op jit(solution)/shard_map/ppermute | solution.py:23
  77.9 2.5 %collective-permute-done.22 = bf16[1,4,128,128]{3,2,1,0:T(8,128)(2,1)S(1)} collective-permute-done((bf16[1,4,128,128]{3,2,1,0:T(8,128)(2,1)S(1)}, bf16[1,4,128,128]{3,2,1,0:T(8,128)(2,1)S(1)}, u32[]{:S(2)}, u32[]{:S(2)}) %collective-permute-start.22) | collective-permute-done | bytes 131104 | tf_op jit(solution)/shard_map/ppermute | solution.py:23
  80.4 3.7 %collective-permute-done.23 = bf16[1,4,128,128]{3,2,1,0:T(8,128)(2,1)S(1)} collective-permute-done((bf16[1,4,128,128]{3,2,1,0:T(8,128)(2,1)S(1)}, bf16[1,4,128,128]{3,2,1,0:T(8,128)(2,1)S(1)}, u32[]{:S(2)}, u32[]{:S(2)}) %collective-permute-start.23) | collective-permute-done | bytes 131104 | tf_op jit(solution)/shard_map/ppermute | solution.py:23
  84.1 3.3 %collective-permute-start.25 = (bf16[128,128]{1,0:T(8,128)(2,1)S(1)}, bf16[128,128]{1,0:T(8,128)(2,1)S(1)}, u32[]{:S(2)}, u32[]{:S(2)}) collective-permute-start(bf16[128,128]{1,0:T(8,128)(2,1)S(1)} %get-tuple-element.104), channel_id=1, source_target_pairs={{0,1},{1,0},{2,3},{3,2},{4,5},{5,4},{6,7},{7,6},{8,9},{9,8},{10,11... | collective-permute-start | bytes 98312 | tf_op jit(solution)/shard_map/ppermute | solution.py:28
  87.5 1.0 collective-permute-start.26
  88.5 1.4 %collective-permute-start.27 = (bf16[128,128]{1,0:T(8,128)(2,1)S(1)}, bf16[128,128]{1,0:T(8,128)(2,1)S(1)}, u32[]{:S(2)}, u32[]{:S(2)}) collective-permute-start(bf16[128,128]{1,0:T(8,128)(2,1)S(1)} %get-tuple-element.105), channel_id=1, source_target_pairs={{0,3},{1,2},{2,1},{3,0},{4,7},{5,6},{6,5},{7,4},{8,11},{9,10},{10,... | collective-permute-start | bytes 98312 | tf_op jit(solution)/shard_map/ppermute | solution.py:28
  89.9 2.9 %collective-permute-done.26 = bf16[128,128]{1,0:T(8,128)(2,1)S(1)} collective-permute-done((bf16[128,128]{1,0:T(8,128)(2,1)S(1)}, bf16[128,128]{1,0:T(8,128)(2,1)S(1)}, u32[]{:S(2)}, u32[]{:S(2)}) %collective-permute-start.26) | collective-permute-done | bytes 32800 | tf_op jit(solution)/shard_map/ppermute | solution.py:28
  92.8 1.4 %collective-permute-done.27 = bf16[128,128]{1,0:T(8,128)(2,1)S(1)} collective-permute-done((bf16[128,128]{1,0:T(8,128)(2,1)S(1)}, bf16[128,128]{1,0:T(8,128)(2,1)S(1)}, u32[]{:S(2)}, u32[]{:S(2)}) %collective-permute-start.27) | collective-permute-done | bytes 32800 | tf_op jit(solution)/shard_map/ppermute | solution.py:28
  94.2 1.3 %collective-permute-start.28 = (f32[128,128]{1,0:T(8,128)S(1)}, f32[128,128]{1,0:T(8,128)S(1)}, u32[]{:S(2)}, u32[]{:S(2)}) collective-permute-start(f32[128,128]{1,0:T(8,128)S(1)} %fusion.5), channel_id=1, source_target_pairs={{0,8},{4,12},{8,0},{12,4},{16,24},{20,28},{24,16},{28,20},{1,9},{5... | collective-permute-start | bytes 196616 | tf_op jit(solution)/shard_map/ppermute | solution.py:23
  95.5 0.8 collective-permute-start.29
  96.3 1.4 %collective-permute-start.30 = (f32[128,128]{1,0:T(8,128)S(1)}, f32[128,128]{1,0:T(8,128)S(1)}, u32[]{:S(2)}, u32[]{:S(2)}) collective-permute-start(f32[128,128]{1,0:T(8,128)S(1)} %fusion.5), channel_id=1, source_target_pairs={{0,24},{4,28},{8,16},{12,20},{16,8},{20,12},{24,0},{28,4},{1,25},{... | collective-permute-start | bytes 196616 | tf_op jit(solution)/shard_map/ppermute | solution.py:23
  97.8 0.8 collective-permute-done.28
  98.6 1.2 %collective-permute-done.29 = f32[128,128]{1,0:T(8,128)S(1)} collective-permute-done((f32[128,128]{1,0:T(8,128)S(1)}, f32[128,128]{1,0:T(8,128)S(1)}, u32[]{:S(2)}, u32[]{:S(2)}) %collective-permute-start.29) | collective-permute-done | bytes 65568 | tf_op jit(solution)/shard_map/ppermute | solution.py:23
  99.8 1.7 %collective-permute-done.30 = f32[128,128]{1,0:T(8,128)S(1)} collective-permute-done((f32[128,128]{1,0:T(8,128)S(1)}, f32[128,128]{1,0:T(8,128)S(1)}, u32[]{:S(2)}, u32[]{:S(2)}) %collective-permute-start.30) | collective-permute-done | bytes 65568 | tf_op jit(solution)/shard_map/ppermute | solution.py:23
  101.6 1.5 %collective-permute-done.31.odd = f32[4,128,128]{2,1,0:T(8,128)S(1)} collective-permute-done((f32[4,128,128]{2,1,0:T(8,128)S(1)}, f32[4,128,128]{2,1,0:T(8,128)S(1)}, u32[]{:S(2)}, u32[]{:S(2)}) %collective-permute-start.31) | collective-permute-done | bytes 262176 | tf_op jit(solution)/shard_map/ppermute | solution.py:23
  103.1 1.4 %finish.1 = (f32[1024,128]{1,0:T(8,128)}, f32[8,128]{1,0:T(8,128)}) custom-call(f32[8,128]{1,0:T(8,128)S(1)} %bitcast.57, f32[4,128,128]{2,1,0:T(8,128)S(1)} %pad_maximum_fusion.2.even, f32[4,128,128]{2,1,0:T(8,128)S(1)} %collective-permute-done.31.odd), custom_call_target="tpu_custom_call" | custom-call | tf_op jit(solution)/shard_map/finish/pallas_call | solution.py:651
  (62 shorter events, 3.8 us)
Async XLA Ops:
  2.3 12.0 %collective-permute-start = (f32[148,128]{1,0:T(8,128)}, f32[148,128]{1,0:T(8,128)S(1)}, u32[]{:S(2)}, u32[]{:S(2)}) collective-permute-start(f32[148,128]{1,0:T(8,128)} %get-tuple-element.50), channel_id=1, source_target_pairs={{0,1},{1,0},{2,3},{3,2},{4,5},{5,4},{6,7},{7,6},{8,9},{9,8},{10,11... | collective-permute-start | bytes 227336 | tf_op jit(solution)/shard_map/ppermute | solution.py:28
  5.4 8.9 %collective-permute-start.1 = (f32[148,128]{1,0:T(8,128)}, f32[148,128]{1,0:T(8,128)S(1)}, u32[]{:S(2)}, u32[]{:S(2)}) collective-permute-start(f32[148,128]{1,0:T(8,128)} %get-tuple-element.51), channel_id=1, source_target_pairs={{0,2},{1,3},{2,0},{3,1},{4,6},{5,7},{6,4},{7,5},{8,10},{9,11},{10,... | collective-permute-start | bytes 227336 | tf_op jit(solution)/shard_map/ppermute | solution.py:28
  8.0 6.5 %collective-permute-start.2 = (f32[148,128]{1,0:T(8,128)}, f32[148,128]{1,0:T(8,128)S(1)}, u32[]{:S(2)}, u32[]{:S(2)}) collective-permute-start(f32[148,128]{1,0:T(8,128)} %get-tuple-element.52), channel_id=1, source_target_pairs={{0,3},{1,2},{2,1},{3,0},{4,7},{5,6},{6,5},{7,4},{8,11},{9,10},{10,... | collective-permute-start | bytes 227336 | tf_op jit(solution)/shard_map/ppermute | solution.py:28
  8.8 0.9 copy-start.3
  9.6 0.8 copy-start.4
  10.4 0.7 copy-start.5
  11.1 0.7 copy-start.7
  14.3 24.0 %copy-start.10 = (bf16[864,128]{1,0:T(8,128)(2,1)S(1)}, bf16[864,128]{1,0:T(8,128)(2,1)}, u32[]{:S(2)}) copy-start(bf16[864,128]{1,0:T(8,128)(2,1)} %get-tuple-element.67) | copy-start | bytes 663556
  14.5 10.1 %collective-permute-start.6 = (bf16[864,128]{1,0:T(8,128)(2,1)}, bf16[864,128]{1,0:T(8,128)(2,1)S(1)}, u32[]{:S(2)}, u32[]{:S(2)}) collective-permute-start(bf16[864,128]{1,0:T(8,128)(2,1)} %get-tuple-element.64), channel_id=1, source_target_pairs={{0,1},{1,0},{2,3},{3,2},{4,5},{5,4},{6,7},{7,6},{8,9},{9,8},{10,11... | collective-permute-start | bytes 663560 | tf_op jit(solution)/shard_map/ppermute | solution.py:28
  15.9 19.0 %collective-permute-start.7 = (bf16[864,128]{1,0:T(8,128)(2,1)}, bf16[864,128]{1,0:T(8,128)(2,1)S(1)}, u32[]{:S(2)}, u32[]{:S(2)}) collective-permute-start(bf16[864,128]{1,0:T(8,128)(2,1)} %get-tuple-element.64), channel_id=1, source_target_pairs={{0,2},{1,3},{2,0},{3,1},{4,6},{5,7},{6,4},{7,5},{8,10},{9,11},{10,... | collective-permute-start | bytes 663560 | tf_op jit(solution)/shard_map/ppermute | solution.py:28
  18.8 16.1 %collective-permute-start.8 = (bf16[864,128]{1,0:T(8,128)(2,1)}, bf16[864,128]{1,0:T(8,128)(2,1)S(1)}, u32[]{:S(2)}, u32[]{:S(2)}) collective-permute-start(bf16[864,128]{1,0:T(8,128)(2,1)} %get-tuple-element.64), channel_id=1, source_target_pairs={{0,3},{1,2},{2,1},{3,0},{4,7},{5,6},{6,5},{7,4},{8,11},{9,10},{10,... | collective-permute-start | bytes 663560 | tf_op jit(solution)/shard_map/ppermute | solution.py:28
  19.0 16.0 %collective-permute-start.3 = (f32[3,128,128]{2,1,0:T(8,128)S(1)}, f32[3,128,128]{2,1,0:T(8,128)S(1)}, u32[]{:S(2)}, u32[]{:S(2)}) collective-permute-start(f32[3,128,128]{2,1,0:T(8,128)S(1)} %pad_maximum_fusion.3), channel_id=1, source_target_pairs={{0,8},{4,12},{8,0},{12,4},{16,24},{20,28},{24,16},{28,20},{1,9},{5... | collective-permute-start | bytes 589832 | tf_op jit(solution)/shard_map/ppermute | solution.py:23
  20.6 14.4 %collective-permute-start.4 = (f32[3,128,128]{2,1,0:T(8,128)S(1)}, f32[3,128,128]{2,1,0:T(8,128)S(1)}, u32[]{:S(2)}, u32[]{:S(2)}) collective-permute-start(f32[3,128,128]{2,1,0:T(8,128)S(1)} %pad_maximum_fusion.3), channel_id=1, source_target_pairs={{0,16},{4,20},{8,24},{12,28},{16,0},{20,4},{24,8},{28,12},{1,17},{... | collective-permute-start | bytes 589832 | tf_op jit(solution)/shard_map/ppermute | solution.py:23
  24.7 10.3 %collective-permute-start.5 = (f32[3,128,128]{2,1,0:T(8,128)S(1)}, f32[3,128,128]{2,1,0:T(8,128)S(1)}, u32[]{:S(2)}, u32[]{:S(2)}) collective-permute-start(f32[3,128,128]{2,1,0:T(8,128)S(1)} %pad_maximum_fusion.3), channel_id=1, source_target_pairs={{0,24},{4,28},{8,16},{12,20},{16,8},{20,12},{24,0},{28,4},{1,25},{... | collective-permute-start | bytes 589832 | tf_op jit(solution)/shard_map/ppermute | solution.py:23
  27.1 1.0 copy-start.2
  34.5 21.8 %copy-start.9 = (f32[3456]{0:T(1024)S(1)}, f32[3456]{0:T(1024)}, u32[]{:S(2)}) copy-start(f32[3456]{0:T(1024)} %param.20) | copy-start | bytes 41476
  34.5 22.3 %copy-start = (bf16[864,512]{1,0:T(8,128)(2,1)S(1)}, bf16[864,512]{1,0:T(8,128)(2,1)}, u32[]{:S(2)}) copy-start(bf16[864,512]{1,0:T(8,128)(2,1)} %refs_2_.1) | copy-start | bytes 2654212
  34.5 22.3 %copy-start.1 = (bf16[864,512]{1,0:T(8,128)(2,1)S(1)}, bf16[864,512]{1,0:T(8,128)(2,1)}, u32[]{:S(2)}) copy-start(bf16[864,512]{1,0:T(8,128)(2,1)} %refs_3_.1) | copy-start | bytes 2654212
  35.1 28.6 %copy-start.8 = (s32[128]{0:T(128)S(1)}, s32[128]{0:T(128)}, u32[]{:S(2)}) copy-start(s32[128]{0:T(128)} %param.17) | copy-start | bytes 1540
  35.1 6.4 %collective-permute-start.12 = (f32[4,3,128,128]{3,2,1,0:T(8,128)S(1)}, f32[4,3,128,128]{3,2,1,0:T(8,128)S(1)}, u32[]{:S(2)}, u32[]{:S(2)}) collective-permute-start(f32[4,3,128,128]{3,2,1,0:T(8,128)S(1)} %pad_maximum_fusion.even), channel_id=1, source_target_pairs={{0,4},{4,0},{8,12},{12,8},{16,20},{20,16},{24,28},{28,24},{1,5},{5... | collective-permute-start | bytes 2359304 | tf_op jit(solution)/shard_map/ppermute | solution.py:23
  35.2 17.6 %collective-permute-start.10 = (bf16[3,864,128]{2,1,0:T(8,128)(2,1)S(1)}, bf16[3,864,128]{2,1,0:T(8,128)(2,1)S(1)}, u32[]{:S(2)}, u32[]{:S(2)}) collective-permute-start(bf16[3,864,128]{2,1,0:T(8,128)(2,1)S(1)} %pad_maximum_fusion.1.refs_2_), channel_id=1, source_target_pairs={{0,16},{4,20},{8,24},{12,28},{16,0},{20,4},{24,8},{28,12},{1,17},{... | collective-permute-start | bytes 1990664 | tf_op jit(solution)/shard_map/ppermute | solution.py:23
  36.7 17.0 %collective-permute-start.9 = (bf16[3,864,128]{2,1,0:T(8,128)(2,1)S(1)}, bf16[3,864,128]{2,1,0:T(8,128)(2,1)S(1)}, u32[]{:S(2)}, u32[]{:S(2)}) collective-permute-start(bf16[3,864,128]{2,1,0:T(8,128)(2,1)S(1)} %pad_maximum_fusion.1.refs_2_), channel_id=1, source_target_pairs={{0,8},{4,12},{8,0},{12,4},{16,24},{20,28},{24,16},{28,20},{1,9},{5... | collective-permute-start | bytes 1990664 | tf_op jit(solution)/shard_map/ppermute | solution.py:23
  38.2 14.5 %collective-permute-start.11 = (bf16[864,128]{1,0:T(8,128)(2,1)S(1)}, bf16[864,128]{1,0:T(8,128)(2,1)S(1)}, u32[]{:S(2)}, u32[]{:S(2)}) collective-permute-start(bf16[864,128]{1,0:T(8,128)(2,1)S(1)} %copy-done.10), channel_id=1, source_target_pairs={{0,1},{1,0},{2,3},{3,2},{4,5},{5,4},{6,7},{7,6},{8,9},{9,8},{10,11... | collective-permute-start | bytes 663560 | tf_op jit(solution)/shard_map/ppermute | solution.py:28
  41.5 14.9 %collective-permute-start.15 = (bf16[3,864,128]{2,1,0:T(8,128)(2,1)S(1)}, bf16[3,864,128]{2,1,0:T(8,128)(2,1)S(1)}, u32[]{:S(2)}, u32[]{:S(2)}) collective-permute-start(bf16[3,864,128]{2,1,0:T(8,128)(2,1)S(1)} %pad_maximum_fusion.1.refs_2_), channel_id=1, source_target_pairs={{0,4},{4,0},{8,12},{12,8},{16,20},{20,16},{24,28},{28,24},{1,5},{5... | collective-permute-start | bytes 1990664 | tf_op jit(solution)/shard_map/ppermute | solution.py:23
  53.7 2.7 %collective-permute-start.16 = (bf16[3,864,128]{2,1,0:T(8,128)(2,1)S(1)}, bf16[3,864,128]{2,1,0:T(8,128)(2,1)S(1)}, u32[]{:S(2)}, u32[]{:S(2)}) collective-permute-start(bf16[3,864,128]{2,1,0:T(8,128)(2,1)S(1)} %collective-permute-done.9.refs_4_), channel_id=1, source_target_pairs={{0,4},{4,0},{8,12},{12,8},{16,20},{20,16},{24,28},{28,24},{1,5},{5... | collective-permute-start | bytes 1990664 | tf_op jit(solution)/shard_map/ppermute | solution.py:23
  53.7 3.1 %collective-permute-start.17 = (bf16[3,864,128]{2,1,0:T(8,128)(2,1)S(1)}, bf16[3,864,128]{2,1,0:T(8,128)(2,1)S(1)}, u32[]{:S(2)}, u32[]{:S(2)}) collective-permute-start(bf16[3,864,128]{2,1,0:T(8,128)(2,1)S(1)} %collective-permute-done.10.refs_6_), channel_id=1, source_target_pairs={{0,4},{4,0},{8,12},{12,8},{16,20},{20,16},{24,28},{28,24},{1,5},{5... | collective-permute-start | bytes 1990664 | tf_op jit(solution)/shard_map/ppermute | solution.py:23
  54.3 7.4 %collective-permute-start.13 = (bf16[2,432,128]{2,1,0:T(8,128)(2,1)S(1)}, bf16[2,432,128]{2,1,0:T(8,128)(2,1)S(1)}, u32[]{:S(2)}, u32[]{:S(2)}) collective-permute-start(bf16[2,432,128]{2,1,0:T(8,128)(2,1)S(1)} %slice.52), channel_id=1, source_target_pairs={{0,16},{4,20},{8,24},{12,28},{16,0},{20,4},{24,8},{28,12},{1,17},{... | collective-permute-start | bytes 663560 | tf_op jit(solution)/shard_map/ppermute | solution.py:23
  54.8 7.1 %collective-permute-start.14 = (bf16[2,432,128]{2,1,0:T(8,128)(2,1)S(1)}, bf16[2,432,128]{2,1,0:T(8,128)(2,1)S(1)}, u32[]{:S(2)}, u32[]{:S(2)}) collective-permute-start(bf16[2,432,128]{2,1,0:T(8,128)(2,1)S(1)} %slice.53), channel_id=1, source_target_pairs={{0,8},{4,12},{8,0},{12,4},{16,24},{20,28},{24,16},{28,20},{1,9},{5... | collective-permute-start | bytes 663560 | tf_op jit(solution)/shard_map/ppermute | solution.py:23
  56.4 6.1 %collective-permute-start.18 = (bf16[1,864,128]{2,1,0:T(8,128)(2,1)S(1)}, bf16[1,864,128]{2,1,0:T(8,128)(2,1)S(1)}, u32[]{:S(2)}, u32[]{:S(2)}) collective-permute-start(bf16[1,864,128]{2,1,0:T(8,128)(2,1)S(1)} %bitcast.55), channel_id=1, source_target_pairs={{0,4},{4,0},{8,12},{12,8},{16,20},{20,16},{24,28},{28,24},{1,5},{5... | collective-permute-start | bytes 663560 | tf_op jit(solution)/shard_map/ppermute | solution.py:23
  61.9 1.5 %collective-permute-start.19 = (bf16[2,432,128]{2,1,0:T(8,128)(2,1)S(1)}, bf16[2,432,128]{2,1,0:T(8,128)(2,1)S(1)}, u32[]{:S(2)}, u32[]{:S(2)}) collective-permute-start(bf16[2,432,128]{2,1,0:T(8,128)(2,1)S(1)} %collective-permute-done.13.refs_6_), channel_id=1, source_target_pairs={{0,4},{4,0},{8,12},{12,8},{16,20},{20,16},{24,28},{28,24},{1,5},{5... | collective-permute-start | bytes 663560 | tf_op jit(solution)/shard_map/ppermute | solution.py:23
  61.9 1.8 %collective-permute-start.20 = (bf16[2,432,128]{2,1,0:T(8,128)(2,1)S(1)}, bf16[2,432,128]{2,1,0:T(8,128)(2,1)S(1)}, u32[]{:S(2)}, u32[]{:S(2)}) collective-permute-start(bf16[2,432,128]{2,1,0:T(8,128)(2,1)S(1)} %collective-permute-done.14.refs_8_), channel_id=1, source_target_pairs={{0,4},{4,0},{8,12},{12,8},{16,20},{20,16},{24,28},{28,24},{1,5},{5... | collective-permute-start | bytes 663560 | tf_op jit(solution)/shard_map/ppermute | solution.py:23
  63.7 39.4 %copy-start.6 = (f32[1024]{0:T(1024)S(1)}, f32[1024]{0:T(1024)}, u32[]{:S(2)}) copy-start(f32[1024]{0:T(1024)} %param.12) | copy-start | bytes 12292
  72.1 2.0 %collective-permute-start.21 = (bf16[4,4,128,128]{3,2,1,0:T(8,128)(2,1)S(1)}, bf16[4,4,128,128]{3,2,1,0:T(8,128)(2,1)S(1)}, u32[]{:S(2)}, u32[]{:S(2)}) collective-permute-start(bf16[4,4,128,128]{3,2,1,0:T(8,128)(2,1)S(1)} %get-tuple-element.90), channel_id=1, source_target_pairs={{0,4},{4,0},{8,12},{12,8},{16,20},{20,16},{24,28},{28,24},{1,5},{5... | collective-permute-start | bytes 1572872 | tf_op jit(solution)/shard_map/ppermute | solution.py:23
  74.3 6.0 %collective-permute-start.22 = (bf16[1,4,128,128]{3,2,1,0:T(8,128)(2,1)S(1)}, bf16[1,4,128,128]{3,2,1,0:T(8,128)(2,1)S(1)}, u32[]{:S(2)}, u32[]{:S(2)}) collective-permute-start(bf16[1,4,128,128]{3,2,1,0:T(8,128)(2,1)S(1)} %get-tuple-element.101), channel_id=1, source_target_pairs={{0,8},{4,12},{8,0},{12,4},{16,24},{20,28},{24,16},{28,20},{1,9},{5... | collective-permute-start | bytes 393224 | tf_op jit(solution)/shard_map/ppermute | solution.py:23
  75.9 8.1 %collective-permute-start.23 = (bf16[1,4,128,128]{3,2,1,0:T(8,128)(2,1)S(1)}, bf16[1,4,128,128]{3,2,1,0:T(8,128)(2,1)S(1)}, u32[]{:S(2)}, u32[]{:S(2)}) collective-permute-start(bf16[1,4,128,128]{3,2,1,0:T(8,128)(2,1)S(1)} %get-tuple-element.103), channel_id=1, source_target_pairs={{0,16},{4,20},{8,24},{12,28},{16,0},{20,4},{24,8},{28,12},{1,17},{... | collective-permute-start | bytes 393224 | tf_op jit(solution)/shard_map/ppermute | solution.py:23
  77.4 6.6 %collective-permute-start.24 = (bf16[1,4,128,128]{3,2,1,0:T(8,128)(2,1)S(1)}, bf16[1,4,128,128]{3,2,1,0:T(8,128)(2,1)S(1)}, u32[]{:S(2)}, u32[]{:S(2)}) collective-permute-start(bf16[1,4,128,128]{3,2,1,0:T(8,128)(2,1)S(1)} %get-tuple-element.102), channel_id=1, source_target_pairs={{0,24},{4,28},{8,16},{12,20},{16,8},{20,12},{24,0},{28,4},{1,25},{... | collective-permute-start | bytes 393224 | tf_op jit(solution)/shard_map/ppermute | solution.py:23
  84.1 5.8 %collective-permute-start.25 = (bf16[128,128]{1,0:T(8,128)(2,1)S(1)}, bf16[128,128]{1,0:T(8,128)(2,1)S(1)}, u32[]{:S(2)}, u32[]{:S(2)}) collective-permute-start(bf16[128,128]{1,0:T(8,128)(2,1)S(1)} %get-tuple-element.104), channel_id=1, source_target_pairs={{0,1},{1,0},{2,3},{3,2},{4,5},{5,4},{6,7},{7,6},{8,9},{9,8},{10,11... | collective-permute-start | bytes 98312 | tf_op jit(solution)/shard_map/ppermute | solution.py:28
  87.5 5.3 %collective-permute-start.26 = (bf16[128,128]{1,0:T(8,128)(2,1)S(1)}, bf16[128,128]{1,0:T(8,128)(2,1)S(1)}, u32[]{:S(2)}, u32[]{:S(2)}) collective-permute-start(bf16[128,128]{1,0:T(8,128)(2,1)S(1)} %get-tuple-element.106), channel_id=1, source_target_pairs={{0,2},{1,3},{2,0},{3,1},{4,6},{5,7},{6,4},{7,5},{8,10},{9,11},{10,... | collective-permute-start | bytes 98312 | tf_op jit(solution)/shard_map/ppermute | solution.py:28
  88.5 5.7 %collective-permute-start.27 = (bf16[128,128]{1,0:T(8,128)(2,1)S(1)}, bf16[128,128]{1,0:T(8,128)(2,1)S(1)}, u32[]{:S(2)}, u32[]{:S(2)}) collective-permute-start(bf16[128,128]{1,0:T(8,128)(2,1)S(1)} %get-tuple-element.105), channel_id=1, source_target_pairs={{0,3},{1,2},{2,1},{3,0},{4,7},{5,6},{6,5},{7,4},{8,11},{9,10},{10,... | collective-permute-start | bytes 98312 | tf_op jit(solution)/shard_map/ppermute | solution.py:28
  94.2 4.3 %collective-permute-start.28 = (f32[128,128]{1,0:T(8,128)S(1)}, f32[128,128]{1,0:T(8,128)S(1)}, u32[]{:S(2)}, u32[]{:S(2)}) collective-permute-start(f32[128,128]{1,0:T(8,128)S(1)} %fusion.5), channel_id=1, source_target_pairs={{0,8},{4,12},{8,0},{12,4},{16,24},{20,28},{24,16},{28,20},{1,9},{5... | collective-permute-start | bytes 196616 | tf_op jit(solution)/shard_map/ppermute | solution.py:23
  95.5 4.3 %collective-permute-start.29 = (f32[128,128]{1,0:T(8,128)S(1)}, f32[128,128]{1,0:T(8,128)S(1)}, u32[]{:S(2)}, u32[]{:S(2)}) collective-permute-start(f32[128,128]{1,0:T(8,128)S(1)} %fusion.5), channel_id=1, source_target_pairs={{0,16},{4,20},{8,24},{12,28},{16,0},{20,4},{24,8},{28,12},{1,17},{... | collective-permute-start | bytes 196616 | tf_op jit(solution)/shard_map/ppermute | solution.py:23
  96.3 5.2 %collective-permute-start.30 = (f32[128,128]{1,0:T(8,128)S(1)}, f32[128,128]{1,0:T(8,128)S(1)}, u32[]{:S(2)}, u32[]{:S(2)}) collective-permute-start(f32[128,128]{1,0:T(8,128)S(1)} %fusion.5), channel_id=1, source_target_pairs={{0,24},{4,28},{8,16},{12,20},{16,8},{20,12},{24,0},{28,4},{1,25},{... | collective-permute-start | bytes 196616 | tf_op jit(solution)/shard_map/ppermute | solution.py:23
  101.5 1.6 %collective-permute-start.31 = (f32[4,128,128]{2,1,0:T(8,128)S(1)}, f32[4,128,128]{2,1,0:T(8,128)S(1)}, u32[]{:S(2)}, u32[]{:S(2)}) collective-permute-start(f32[4,128,128]{2,1,0:T(8,128)S(1)} %pad_maximum_fusion.2.even), channel_id=1, source_target_pairs={{0,4},{4,0},{8,12},{12,8},{16,20},{20,16},{24,28},{28,24},{1,5},{5... | collective-permute-start | bytes 786440 | tf_op jit(solution)/shard_map/ppermute | solution.py:23

commit v8 on v7

--- a/solution.py
+++ b/solution.py
@@ -40,11 +40,14 @@
     return stages
 
 
-def replica_gather(piece, *beside):
+def replica_gather(piece, *beside, after=None):
     held = [piece]
     for masks in reversed(mask_stages(lax.axis_size("replica"))[1:]):
-        held = [held] + [[swap(h, mask) for h in held] for mask in masks]
-        held = [h for group in held for h in group]
+        last = held
+        if after is not None:
+            last, after = lax.optimization_barrier((held, after))
+        sent = [[swap(h, mask) for h in (held if mask != masks[-1] else last)] for mask in masks]
+        held = [h for group in [held] + sent for h in group]
     held, *beside = lax.optimization_barrier((held, *beside))
     order = sorted(range(len(held)), key=lambda i: gather_masks(lax.axis_size("replica"))[i])
     even = jnp.stack([held[i] for i in order])
@@ -684,10 +687,11 @@
     packed = pack(look_rows, emb_table, shards, replicas)
     parcels = [cross_over(p, k + 1) for k, p in enumerate(packed)]
     bias, head, label_row = (x.reshape(1, -1) for x in (cross_bias, head_weight, labels))
-    prepared = ready(live_counts, look_rows, bag_order, dense_emb, head, shards)
-    parcels, prepared, blocks = lax.optimization_barrier(
-        (parcels, prepared, cut(factors) if even_split else [])
+    parcels[0], blocks = lax.optimization_barrier(
+        (parcels[0], cut(factors) if even_split else [])
     )
+    counts, blocks = lax.optimization_barrier((live_counts, blocks))
+    prepared = ready(counts, look_rows, bag_order, dense_emb, head, shards)
     places, info, own_words, lead = prepared
     far, corner = [], []
     if even_split:
@@ -695,7 +699,11 @@
         corner = cross_over(blocks[1], 1)[None]
     counted = slots(info, own_words, parcels, bag_order.shape[2], rows, shards, replicas)
     pieces, far, counted, own_rows = replica_gather(
-        jnp.stack([p[:block] for p in parcels]), far, counted, split_own(emb_table, replicas)
+        jnp.stack([p[:block] for p in parcels]),
+        far,
+        counted,
+        split_own(emb_table, replicas),
+        after=prepared,
     )
     crossed = pool(info, places, counted, own_rows, pieces, lead, head)
     rank = cross_in.shape[1]

time: 105 us -> 102 us (0.971)
  starting transfers between devices: 38.5 us -> 36.8 us
  waiting for transfers between devices: 24.6 us -> 23.3 us
    ppermute x10, waiting for transfers between devices: 7.42 us -> 5.6 us  [cross_over(): return lax.ppermute(array, 'table', [(i, i ^ mask) for i in range(size)])]
    ppermute x22, starting transfers between devices: 19.3 us -> 17.6 us  [swap(): return lax.ppermute(array, 'replica', [(i, i ^ mask) for i in range(size)])]
  transfers between devices with their start and end apart: 32 -> 32, of which waited for: 18 -> 19; matrix products, arithmetic and copies ran while one was open for 1% -> 1% of each run, Pallas kernels for 23% -> 23%
where the time goes in v8:
time: 102 us
  starting transfers between devices  36.8 us (36%)
  Pallas kernels  35.2 us (35%)
  waiting for transfers between devices  23.3 us (23%)
  local copies, waits for them, and re-layouts  4.93 us (5%)
    ppermute x10, starting transfers between devices, cross_over(): return lax.ppermute(array, 'table', [(i, i ^ mask) for i in range(size)])  19.2 us
    ppermute x22, waiting for transfers between devices, swap(): return lax.ppermute(array, 'replica', [(i, i ^ mask) for i in range(size)])  17.7 us
    ppermute x22, starting transfers between devices, swap(): return lax.ppermute(array, 'replica', [(i, i ^ mask) for i in range(size)])  17.6 us
    pallas_call x1, Pallas kernels, pool(): pl.pallas_call(functools.partial(pool_kernel, shards), out_shape=[jax.Sha...  11.2 us
    pallas_call x1, Pallas kernels, dense_step(): pl.pallas_call(functools.partial(dense_kernel, shards, replicas, copies),...  8.44 us
    pallas_call x1, Pallas kernels, slots(): pl.pallas_call(functools.partial(slots_kernel, shards, replicas, bags), o...  6.23 us
    ppermute x10, waiting for transfers between devices, cross_over(): return lax.ppermute(array, 'table', [(i, i ^ mask) for i in range(size)])  5.6 us
    unnamed x22, local copies, waits for them, and re-layouts  4.11 us
  transfers between devices with their start and end apart: 32, of which 19 were waited for; matrix products, arithmetic and copies ran while one was open for 1% of the time, Pallas kernels for 23%

profile of v8, /device:TPU:0, one launch (start us, length us, event | category | flops | bytes accessed | tf_op | source)
XLA Modules:
  0.0 101.5 jit_solution(7703584386218193189)
XLA Ops:
  0.6 1.7 %pack.1 = (f32[148,128]{1,0:T(8,128)}, f32[148,128]{1,0:T(8,128)}, f32[148,128]{1,0:T(8,128)}) custom-call(s32[1,1,4,4,1248]{4,3,2,1,0:T(4,128)} %look_rows.3, f32[1024,128]{1,0:T(8,128)} %table.3), custom_call_target="tpu_custom_call" | custom-call | tf_op jit(solution)/shard_map/pack/pallas_call | solution.py:116
  2.4 3.1 %collective-permute-start = (f32[148,128]{1,0:T(8,128)}, f32[148,128]{1,0:T(8,128)S(1)}, u32[]{:S(2)}, u32[]{:S(2)}) collective-permute-start(f32[148,128]{1,0:T(8,128)} %get-tuple-element.48), channel_id=1, source_target_pairs={{0,1},{1,0},{2,3},{3,2},{4,5},{5,4},{6,7},{7,6},{8,9},{9,8},{10,11... | collective-permute-start | bytes 227336 | tf_op jit(solution)/shard_map/ppermute | solution.py:28
  5.5 2.5 %collective-permute-start.2 = (f32[148,128]{1,0:T(8,128)}, f32[148,128]{1,0:T(8,128)S(1)}, u32[]{:S(2)}, u32[]{:S(2)}) collective-permute-start(f32[148,128]{1,0:T(8,128)} %get-tuple-element.58), channel_id=1, source_target_pairs={{0,3},{1,2},{2,1},{3,0},{4,7},{5,6},{6,5},{7,4},{8,11},{9,10},{10,... | collective-permute-start | bytes 227336 | tf_op jit(solution)/shard_map/ppermute | solution.py:28
  8.0 0.7 reshape.77.head
  8.8 1.9 %cut.1 = (bf16[864,128]{1,0:T(8,128)(2,1)}, bf16[864,128]{1,0:T(8,128)(2,1)}) custom-call(bf16[864,512]{1,0:T(8,128)(2,1)} %refs_2_.1, bf16[864,512]{1,0:T(8,128)(2,1)} %refs_3_.1), custom_call_target="tpu_custom_call" | custom-call | tf_op jit(solution)/shard_map/cut/pallas_call | solution.py:150
  10.7 1.9 %collective-permute-start.6 = (bf16[864,128]{1,0:T(8,128)(2,1)}, bf16[864,128]{1,0:T(8,128)(2,1)S(1)}, u32[]{:S(2)}, u32[]{:S(2)}) collective-permute-start(bf16[864,128]{1,0:T(8,128)(2,1)} %get-tuple-element.62), channel_id=1, source_target_pairs={{0,1},{1,0},{2,3},{3,2},{4,5},{5,4},{6,7},{7,6},{8,9},{9,8},{10,11... | collective-permute-start | bytes 663560 | tf_op jit(solution)/shard_map/ppermute | solution.py:28
  12.5 1.7 %collective-permute-start.7 = (bf16[864,128]{1,0:T(8,128)(2,1)}, bf16[864,128]{1,0:T(8,128)(2,1)S(1)}, u32[]{:S(2)}, u32[]{:S(2)}) collective-permute-start(bf16[864,128]{1,0:T(8,128)(2,1)} %get-tuple-element.62), channel_id=1, source_target_pairs={{0,2},{1,3},{2,0},{3,1},{4,6},{5,7},{6,4},{7,5},{8,10},{9,11},{10,... | collective-permute-start | bytes 663560 | tf_op jit(solution)/shard_map/ppermute | solution.py:28
  14.2 0.9 collective-permute-start.8
  15.2 0.7 collective-permute-done.1.refs_1_
  15.9 1.6 %collective-permute-start.3 = (f32[3,128,128]{2,1,0:T(8,128)S(1)}, f32[3,128,128]{2,1,0:T(8,128)S(1)}, u32[]{:S(2)}, u32[]{:S(2)}) collective-permute-start(f32[3,128,128]{2,1,0:T(8,128)S(1)} %pad_maximum_fusion.3), channel_id=1, source_target_pairs={{0,8},{4,12},{8,0},{12,4},{16,24},{20,28},{24,16},{28,20},{1,9},{5... | collective-permute-start | bytes 589832 | tf_op jit(solution)/shard_map/ppermute | solution.py:23
  17.5 0.9 copy-done.3
  18.3 0.8 copy-done.4
  19.1 0.7 copy-done.5
  19.8 0.7 copy-done.7
  20.5 0.6 ready.1
  21.1 1.6 %collective-permute-start.5 = (f32[3,128,128]{2,1,0:T(8,128)S(1)}, f32[3,128,128]{2,1,0:T(8,128)S(1)}, u32[]{:S(2)}, u32[]{:S(2)}) collective-permute-start(f32[3,128,128]{2,1,0:T(8,128)S(1)} %pad_maximum_fusion.3), channel_id=1, source_target_pairs={{0,24},{4,28},{8,16},{12,20},{16,8},{20,12},{24,0},{28,4},{1,25},{... | collective-permute-start | bytes 589832 | tf_op jit(solution)/shard_map/ppermute | solution.py:23
  23.2 1.5 %collective-permute-start.4 = (f32[3,128,128]{2,1,0:T(8,128)S(1)}, f32[3,128,128]{2,1,0:T(8,128)S(1)}, u32[]{:S(2)}, u32[]{:S(2)}) collective-permute-start(f32[3,128,128]{2,1,0:T(8,128)S(1)} %pad_maximum_fusion.3), channel_id=1, source_target_pairs={{0,16},{4,20},{8,24},{12,28},{16,0},{20,4},{24,8},{28,12},{1,17},{... | collective-permute-start | bytes 589832 | tf_op jit(solution)/shard_map/ppermute | solution.py:23
  24.7 1.0 %copy-done.2 = f32[1024,128]{1,0:T(8,128)S(1)} copy-done((f32[1024,128]{1,0:T(8,128)S(1)}, f32[1024,128]{1,0:T(8,128)}, u32[]{:S(2)}) %copy-start.2) | copy-done | bytes 524312
  25.9 6.2 %slots.1.counted = bf16[16,1024,256]{2,1,0:T(8,128)(2,1)S(1)} custom-call(s32[1,128]{1,0:T(1,128)S(1)} %get-tuple-element.54.info, s32[8,1280]{1,0:T(8,128)S(1)} %get-tuple-element.59.own, f32[148,128]{1,0:T(8,128)S(1)} %collective-permute-done.refs_0_, f32[148,128]{1,0:T(8,128)S(1)} %collective-permute-done.1.refs_1_, ...), custom_call_target="tpu_custom_call" | custom-call | flops 1000 | bytes 1000 | tf_op jit(solution)/shard_map/slots/pallas_call | solution.py:298
  32.5 1.6 %collective-permute-start.10 = (bf16[3,864,128]{2,1,0:T(8,128)(2,1)S(1)}, bf16[3,864,128]{2,1,0:T(8,128)(2,1)S(1)}, u32[]{:S(2)}, u32[]{:S(2)}) collective-permute-start(bf16[3,864,128]{2,1,0:T(8,128)(2,1)S(1)} %pad_maximum_fusion.1.refs_2_), channel_id=1, source_target_pairs={{0,16},{4,20},{8,24},{12,28},{16,0},{20,4},{24,8},{28,12},{1,17},{... | collective-permute-start | bytes 1990664 | tf_op jit(solution)/shard_map/ppermute | solution.py:23
  34.1 0.8 collective-permute-start.9
  34.8 3.6 %collective-permute-start.11 = (bf16[864,128]{1,0:T(8,128)(2,1)S(1)}, bf16[864,128]{1,0:T(8,128)(2,1)S(1)}, u32[]{:S(2)}, u32[]{:S(2)}) collective-permute-start(bf16[864,128]{1,0:T(8,128)(2,1)S(1)} %copy-done.10), channel_id=1, source_target_pairs={{0,1},{1,0},{2,3},{3,2},{4,5},{5,4},{6,7},{7,6},{8,9},{9,8},{10,11... | collective-permute-start | bytes 663560 | tf_op jit(solution)/shard_map/ppermute | solution.py:28
  38.4 11.2 %pool.1 = (bf16[128,3456]{1,0:T(8,128)(2,1)S(1)}, bf16[128,3456]{1,0:T(8,128)(2,1)S(1)}) custom-call(s32[1,128]{1,0:T(1,128)S(1)} %get-tuple-element.54.info, s32[1,1664]{1,0:T(1,128)S(1)} %get-tuple-element.55.places, bf16[16,1024,256]{2,1,0:T(8,128)(2,1)S(1)} %slots.1.counted, bf16[1024,256]{1,0:T(8,128)(2,1)S(1)} %split_own.1.own, ...), custom_call_target="tpu_custom_call" | custom-call | flops 1000 | bytes 1000 | tf_op jit(solution)/shard_map/pool/pallas_call | solution.py:364
  49.8 1.2 %collective-permute-done.9.refs_4_ = bf16[3,864,128]{2,1,0:T(8,128)(2,1)S(1)} collective-permute-done((bf16[3,864,128]{2,1,0:T(8,128)(2,1)S(1)}, bf16[3,864,128]{2,1,0:T(8,128)(2,1)S(1)}, u32[]{:S(2)}, u32[]{:S(2)}) %collective-permute-start.9) | collective-permute-done | bytes 663584 | tf_op jit(solution)/shard_map/ppermute | solution.py:23
  52.2 1.4 %collective-permute-start.14 = (bf16[2,432,128]{2,1,0:T(8,128)(2,1)S(1)}, bf16[2,432,128]{2,1,0:T(8,128)(2,1)S(1)}, u32[]{:S(2)}, u32[]{:S(2)}) collective-permute-start(bf16[2,432,128]{2,1,0:T(8,128)(2,1)S(1)} %slice.53), channel_id=1, source_target_pairs={{0,8},{4,12},{8,0},{12,4},{16,24},{20,28},{24,16},{28,20},{1,9},{5... | collective-permute-start | bytes 663560 | tf_op jit(solution)/shard_map/ppermute | solution.py:23
  54.1 3.6 %first.3 = (f32[3328,128]{1,0:T(8,128)S(1)}, f32[128,128]{1,0:T(8,128)S(1)}) custom-call(bf16[128,3456]{1,0:T(8,128)(2,1)S(1)} %get-tuple-element.73.cross, bf16[128,3456]{1,0:T(8,128)(2,1)S(1)} %get-tuple-element.74.scaled, f32[1,3456]{1,0:T(1,128)S(1)} %reshape.79.bias, f32[1,3456]{1,0:T(1,128)S(1)} %reshape.77.head, bf16[864,512]{1,0:T(8,128)(2,1)S(1)} %copy-done, ...), custom_call_target="tpu_custom_call" | custom-call | flops 2000000000 | bytes 20000000 | tf_op jit(solution)/shard_map/first/pallas_call | solution.py:432
  57.8 1.2 %collective-permute-done.13.refs_6_ = bf16[2,432,128]{2,1,0:T(8,128)(2,1)S(1)} collective-permute-done((bf16[2,432,128]{2,1,0:T(8,128)(2,1)S(1)}, bf16[2,432,128]{2,1,0:T(8,128)(2,1)S(1)}, u32[]{:S(2)}, u32[]{:S(2)}) %collective-permute-start.13) | collective-permute-done | bytes 221216 | tf_op jit(solution)/shard_map/ppermute | solution.py:23
  59.7 1.0 collective-permute-done.19.refs_7_
  61.0 8.4 %dense.3 = (f32[1,128]{1,0:T(1,128)}, bf16[4,4,128,128]{3,2,1,0:T(8,128)(2,1)S(1)}, bf16[4,4,128,128]{3,2,1,0:T(8,128)(2,1)S(1)}) custom-call(s32[1,128]{1,0:T(1,128)S(1)} %get-tuple-element.54.info, s32[1,1664]{1,0:T(1,128)S(1)} %get-tuple-element.55.places, bf16[128,3456]{1,0:T(8,128)(2,1)S(1)} %get-tuple-element.73.cross, ...), custom_call_target="tpu_custom_call" | custom-call | flops 2000000000 | bytes 20000000 | tf_op jit(solution)/shard_map/dense/pallas_call | solution.py:535
  69.7 1.7 %collective-permute-done.21 = bf16[4,4,128,128]{3,2,1,0:T(8,128)(2,1)S(1)} collective-permute-done((bf16[4,4,128,128]{3,2,1,0:T(8,128)(2,1)S(1)}, bf16[4,4,128,128]{3,2,1,0:T(8,128)(2,1)S(1)}, u32[]{:S(2)}, u32[]{:S(2)}) %collective-permute-start.21) | collective-permute-done | bytes 524320 | tf_op jit(solution)/shard_map/ppermute | solution.py:23
  71.7 1.5 %collective-permute-start.22 = (bf16[1,4,128,128]{3,2,1,0:T(8,128)(2,1)S(1)}, bf16[1,4,128,128]{3,2,1,0:T(8,128)(2,1)S(1)}, u32[]{:S(2)}, u32[]{:S(2)}) collective-permute-start(bf16[1,4,128,128]{3,2,1,0:T(8,128)(2,1)S(1)} %get-tuple-element.97), channel_id=1, source_target_pairs={{0,8},{4,12},{8,0},{12,4},{16,24},{20,28},{24,16},{28,20},{1,9},{5... | collective-permute-start | bytes 393224 | tf_op jit(solution)/shard_map/ppermute | solution.py:23
  73.2 0.9 collective-permute-start.23
  74.0 1.2 %collective-permute-start.24 = (bf16[1,4,128,128]{3,2,1,0:T(8,128)(2,1)S(1)}, bf16[1,4,128,128]{3,2,1,0:T(8,128)(2,1)S(1)}, u32[]{:S(2)}, u32[]{:S(2)}) collective-permute-start(bf16[1,4,128,128]{3,2,1,0:T(8,128)(2,1)S(1)} %get-tuple-element.98), channel_id=1, source_target_pairs={{0,24},{4,28},{8,16},{12,20},{16,8},{20,12},{24,0},{28,4},{1,25},{... | collective-permute-start | bytes 393224 | tf_op jit(solution)/shard_map/ppermute | solution.py:23
  75.2 2.5 %collective-permute-done.22 = bf16[1,4,128,128]{3,2,1,0:T(8,128)(2,1)S(1)} collective-permute-done((bf16[1,4,128,128]{3,2,1,0:T(8,128)(2,1)S(1)}, bf16[1,4,128,128]{3,2,1,0:T(8,128)(2,1)S(1)}, u32[]{:S(2)}, u32[]{:S(2)}) %collective-permute-start.22) | collective-permute-done | bytes 131104 | tf_op jit(solution)/shard_map/ppermute | solution.py:23
  77.7 3.6 %collective-permute-done.23 = bf16[1,4,128,128]{3,2,1,0:T(8,128)(2,1)S(1)} collective-permute-done((bf16[1,4,128,128]{3,2,1,0:T(8,128)(2,1)S(1)}, bf16[1,4,128,128]{3,2,1,0:T(8,128)(2,1)S(1)}, u32[]{:S(2)}, u32[]{:S(2)}) %collective-permute-start.23) | collective-permute-done | bytes 131104 | tf_op jit(solution)/shard_map/ppermute | solution.py:23
  81.4 3.0 %collective-permute-start.25 = (bf16[128,128]{1,0:T(8,128)(2,1)S(1)}, bf16[128,128]{1,0:T(8,128)(2,1)S(1)}, u32[]{:S(2)}, u32[]{:S(2)}) collective-permute-start(bf16[128,128]{1,0:T(8,128)(2,1)S(1)} %get-tuple-element.100), channel_id=1, source_target_pairs={{0,1},{1,0},{2,3},{3,2},{4,5},{5,4},{6,7},{7,6},{8,9},{9,8},{10,11... | collective-permute-start | bytes 98312 | tf_op jit(solution)/shard_map/ppermute | solution.py:28
  84.4 1.1 %collective-permute-start.26 = (bf16[128,128]{1,0:T(8,128)(2,1)S(1)}, bf16[128,128]{1,0:T(8,128)(2,1)S(1)}, u32[]{:S(2)}, u32[]{:S(2)}) collective-permute-start(bf16[128,128]{1,0:T(8,128)(2,1)S(1)} %get-tuple-element.102), channel_id=1, source_target_pairs={{0,2},{1,3},{2,0},{3,1},{4,6},{5,7},{6,4},{7,5},{8,10},{9,11},{10,... | collective-permute-start | bytes 98312 | tf_op jit(solution)/shard_map/ppermute | solution.py:28
  85.5 1.4 %collective-permute-start.27 = (bf16[128,128]{1,0:T(8,128)(2,1)S(1)}, bf16[128,128]{1,0:T(8,128)(2,1)S(1)}, u32[]{:S(2)}, u32[]{:S(2)}) collective-permute-start(bf16[128,128]{1,0:T(8,128)(2,1)S(1)} %get-tuple-element.101), channel_id=1, source_target_pairs={{0,3},{1,2},{2,1},{3,0},{4,7},{5,6},{6,5},{7,4},{8,11},{9,10},{10,... | collective-permute-start | bytes 98312 | tf_op jit(solution)/shard_map/ppermute | solution.py:28
  86.9 2.9 %collective-permute-done.26 = bf16[128,128]{1,0:T(8,128)(2,1)S(1)} collective-permute-done((bf16[128,128]{1,0:T(8,128)(2,1)S(1)}, bf16[128,128]{1,0:T(8,128)(2,1)S(1)}, u32[]{:S(2)}, u32[]{:S(2)}) %collective-permute-start.26) | collective-permute-done | bytes 32800 | tf_op jit(solution)/shard_map/ppermute | solution.py:28
  89.7 1.5 %collective-permute-done.27 = bf16[128,128]{1,0:T(8,128)(2,1)S(1)} collective-permute-done((bf16[128,128]{1,0:T(8,128)(2,1)S(1)}, bf16[128,128]{1,0:T(8,128)(2,1)S(1)}, u32[]{:S(2)}, u32[]{:S(2)}) %collective-permute-start.27) | collective-permute-done | bytes 32800 | tf_op jit(solution)/shard_map/ppermute | solution.py:28
  91.2 1.3 %collective-permute-start.28 = (f32[128,128]{1,0:T(8,128)S(1)}, f32[128,128]{1,0:T(8,128)S(1)}, u32[]{:S(2)}, u32[]{:S(2)}) collective-permute-start(f32[128,128]{1,0:T(8,128)S(1)} %fusion.5), channel_id=1, source_target_pairs={{0,8},{4,12},{8,0},{12,4},{16,24},{20,28},{24,16},{28,20},{1,9},{5... | collective-permute-start | bytes 196616 | tf_op jit(solution)/shard_map/ppermute | solution.py:23
  92.5 0.8 collective-permute-start.29
  93.3 1.4 %collective-permute-start.30 = (f32[128,128]{1,0:T(8,128)S(1)}, f32[128,128]{1,0:T(8,128)S(1)}, u32[]{:S(2)}, u32[]{:S(2)}) collective-permute-start(f32[128,128]{1,0:T(8,128)S(1)} %fusion.5), channel_id=1, source_target_pairs={{0,24},{4,28},{8,16},{12,20},{16,8},{20,12},{24,0},{28,4},{1,25},{... | collective-permute-start | bytes 196616 | tf_op jit(solution)/shard_map/ppermute | solution.py:23
  94.8 0.8 collective-permute-done.28
  95.5 1.2 %collective-permute-done.29 = f32[128,128]{1,0:T(8,128)S(1)} collective-permute-done((f32[128,128]{1,0:T(8,128)S(1)}, f32[128,128]{1,0:T(8,128)S(1)}, u32[]{:S(2)}, u32[]{:S(2)}) %collective-permute-start.29) | collective-permute-done | bytes 65568 | tf_op jit(solution)/shard_map/ppermute | solution.py:23
  96.8 1.7 %collective-permute-done.30 = f32[128,128]{1,0:T(8,128)S(1)} collective-permute-done((f32[128,128]{1,0:T(8,128)S(1)}, f32[128,128]{1,0:T(8,128)S(1)}, u32[]{:S(2)}, u32[]{:S(2)}) %collective-permute-start.30) | collective-permute-done | bytes 65568 | tf_op jit(solution)/shard_map/ppermute | solution.py:23
  98.6 1.5 %collective-permute-done.31.odd = f32[4,128,128]{2,1,0:T(8,128)S(1)} collective-permute-done((f32[4,128,128]{2,1,0:T(8,128)S(1)}, f32[4,128,128]{2,1,0:T(8,128)S(1)}, u32[]{:S(2)}, u32[]{:S(2)}) %collective-permute-start.31) | collective-permute-done | bytes 262176 | tf_op jit(solution)/shard_map/ppermute | solution.py:23
  100.1 1.4 %finish.1 = (f32[1024,128]{1,0:T(8,128)}, f32[8,128]{1,0:T(8,128)}) custom-call(f32[8,128]{1,0:T(8,128)S(1)} %bitcast.57, f32[4,128,128]{2,1,0:T(8,128)S(1)} %pad_maximum_fusion.2.even, f32[4,128,128]{2,1,0:T(8,128)S(1)} %collective-permute-done.31.odd), custom_call_target="tpu_custom_call" | custom-call | tf_op jit(solution)/shard_map/finish/pallas_call | solution.py:654
  (63 shorter events, 4.6 us)
Async XLA Ops:
  2.4 8.3 %collective-permute-start = (f32[148,128]{1,0:T(8,128)}, f32[148,128]{1,0:T(8,128)S(1)}, u32[]{:S(2)}, u32[]{:S(2)}) collective-permute-start(f32[148,128]{1,0:T(8,128)} %get-tuple-element.48), channel_id=1, source_target_pairs={{0,1},{1,0},{2,3},{3,2},{4,5},{5,4},{6,7},{7,6},{8,9},{9,8},{10,11... | collective-permute-start | bytes 227336 | tf_op jit(solution)/shard_map/ppermute | solution.py:28
  5.5 9.7 %collective-permute-start.2 = (f32[148,128]{1,0:T(8,128)}, f32[148,128]{1,0:T(8,128)S(1)}, u32[]{:S(2)}, u32[]{:S(2)}) collective-permute-start(f32[148,128]{1,0:T(8,128)} %get-tuple-element.58), channel_id=1, source_target_pairs={{0,3},{1,2},{2,1},{3,0},{4,7},{5,6},{6,5},{7,4},{8,11},{9,10},{10,... | collective-permute-start | bytes 227336 | tf_op jit(solution)/shard_map/ppermute | solution.py:28
  7.9 7.9 %collective-permute-start.1 = (f32[148,128]{1,0:T(8,128)}, f32[148,128]{1,0:T(8,128)S(1)}, u32[]{:S(2)}, u32[]{:S(2)}) collective-permute-start(f32[148,128]{1,0:T(8,128)} %get-tuple-element.57), channel_id=1, source_target_pairs={{0,2},{1,3},{2,0},{3,1},{4,6},{5,7},{6,4},{7,5},{8,10},{9,11},{10,... | collective-permute-start | bytes 227336 | tf_op jit(solution)/shard_map/ppermute | solution.py:28
  10.7 24.2 %copy-start.10 = (bf16[864,128]{1,0:T(8,128)(2,1)S(1)}, bf16[864,128]{1,0:T(8,128)(2,1)}, u32[]{:S(2)}) copy-start(bf16[864,128]{1,0:T(8,128)(2,1)} %get-tuple-element.64) | copy-start | bytes 663556
  10.7 12.5 %collective-permute-start.6 = (bf16[864,128]{1,0:T(8,128)(2,1)}, bf16[864,128]{1,0:T(8,128)(2,1)S(1)}, u32[]{:S(2)}, u32[]{:S(2)}) collective-permute-start(bf16[864,128]{1,0:T(8,128)(2,1)} %get-tuple-element.62), channel_id=1, source_target_pairs={{0,1},{1,0},{2,3},{3,2},{4,5},{5,4},{6,7},{7,6},{8,9},{9,8},{10,11... | collective-permute-start | bytes 663560 | tf_op jit(solution)/shard_map/ppermute | solution.py:28
  12.5 19.6 %collective-permute-start.7 = (bf16[864,128]{1,0:T(8,128)(2,1)}, bf16[864,128]{1,0:T(8,128)(2,1)S(1)}, u32[]{:S(2)}, u32[]{:S(2)}) collective-permute-start(bf16[864,128]{1,0:T(8,128)(2,1)} %get-tuple-element.62), channel_id=1, source_target_pairs={{0,2},{1,3},{2,0},{3,1},{4,6},{5,7},{6,4},{7,5},{8,10},{9,11},{10,... | collective-permute-start | bytes 663560 | tf_op jit(solution)/shard_map/ppermute | solution.py:28
  14.2 17.9 %collective-permute-start.8 = (bf16[864,128]{1,0:T(8,128)(2,1)}, bf16[864,128]{1,0:T(8,128)(2,1)S(1)}, u32[]{:S(2)}, u32[]{:S(2)}) collective-permute-start(bf16[864,128]{1,0:T(8,128)(2,1)} %get-tuple-element.62), channel_id=1, source_target_pairs={{0,3},{1,2},{2,1},{3,0},{4,7},{5,6},{6,5},{7,4},{8,11},{9,10},{10,... | collective-permute-start | bytes 663560 | tf_op jit(solution)/shard_map/ppermute | solution.py:28
  15.9 16.3 %collective-permute-start.3 = (f32[3,128,128]{2,1,0:T(8,128)S(1)}, f32[3,128,128]{2,1,0:T(8,128)S(1)}, u32[]{:S(2)}, u32[]{:S(2)}) collective-permute-start(f32[3,128,128]{2,1,0:T(8,128)S(1)} %pad_maximum_fusion.3), channel_id=1, source_target_pairs={{0,8},{4,12},{8,0},{12,4},{16,24},{20,28},{24,16},{28,20},{1,9},{5... | collective-permute-start | bytes 589832 | tf_op jit(solution)/shard_map/ppermute | solution.py:23
  17.5 0.9 copy-start.3
  18.3 0.8 copy-start.4
  19.1 0.7 copy-start.5
  19.8 0.7 copy-start.7
  21.1 11.1 %collective-permute-start.5 = (f32[3,128,128]{2,1,0:T(8,128)S(1)}, f32[3,128,128]{2,1,0:T(8,128)S(1)}, u32[]{:S(2)}, u32[]{:S(2)}) collective-permute-start(f32[3,128,128]{2,1,0:T(8,128)S(1)} %pad_maximum_fusion.3), channel_id=1, source_target_pairs={{0,24},{4,28},{8,16},{12,20},{16,8},{20,12},{24,0},{28,4},{1,25},{... | collective-permute-start | bytes 589832 | tf_op jit(solution)/shard_map/ppermute | solution.py:23
  23.2 9.1 %collective-permute-start.4 = (f32[3,128,128]{2,1,0:T(8,128)S(1)}, f32[3,128,128]{2,1,0:T(8,128)S(1)}, u32[]{:S(2)}, u32[]{:S(2)}) collective-permute-start(f32[3,128,128]{2,1,0:T(8,128)S(1)} %pad_maximum_fusion.3), channel_id=1, source_target_pairs={{0,16},{4,20},{8,24},{12,28},{16,0},{20,4},{24,8},{28,12},{1,17},{... | collective-permute-start | bytes 589832 | tf_op jit(solution)/shard_map/ppermute | solution.py:23
  24.7 1.0 %copy-start.2 = (f32[1024,128]{1,0:T(8,128)S(1)}, f32[1024,128]{1,0:T(8,128)}, u32[]{:S(2)}) copy-start(f32[1024,128]{1,0:T(8,128)} %table.3) | copy-start | bytes 1572868
  32.1 21.5 %copy-start.9 = (f32[3456]{0:T(1024)S(1)}, f32[3456]{0:T(1024)}, u32[]{:S(2)}) copy-start(f32[3456]{0:T(1024)} %param.20) | copy-start | bytes 41476
  32.1 22.0 %copy-start = (bf16[864,512]{1,0:T(8,128)(2,1)S(1)}, bf16[864,512]{1,0:T(8,128)(2,1)}, u32[]{:S(2)}) copy-start(bf16[864,512]{1,0:T(8,128)(2,1)} %refs_2_.1) | copy-start | bytes 2654212
  32.1 22.0 %copy-start.1 = (bf16[864,512]{1,0:T(8,128)(2,1)S(1)}, bf16[864,512]{1,0:T(8,128)(2,1)}, u32[]{:S(2)}) copy-start(bf16[864,512]{1,0:T(8,128)(2,1)} %refs_3_.1) | copy-start | bytes 2654212
  32.4 28.6 %copy-start.8 = (s32[128]{0:T(128)S(1)}, s32[128]{0:T(128)}, u32[]{:S(2)}) copy-start(s32[128]{0:T(128)} %param.17) | copy-start | bytes 1540
  32.4 6.0 %collective-permute-start.12 = (f32[4,3,128,128]{3,2,1,0:T(8,128)S(1)}, f32[4,3,128,128]{3,2,1,0:T(8,128)S(1)}, u32[]{:S(2)}, u32[]{:S(2)}) collective-permute-start(f32[4,3,128,128]{3,2,1,0:T(8,128)S(1)} %pad_maximum_fusion.even), channel_id=1, source_target_pairs={{0,4},{4,0},{8,12},{12,8},{16,20},{20,16},{24,28},{28,24},{1,5},{5... | collective-permute-start | bytes 2359304 | tf_op jit(solution)/shard_map/ppermute | solution.py:23
  32.5 17.3 %collective-permute-start.10 = (bf16[3,864,128]{2,1,0:T(8,128)(2,1)S(1)}, bf16[3,864,128]{2,1,0:T(8,128)(2,1)S(1)}, u32[]{:S(2)}, u32[]{:S(2)}) collective-permute-start(bf16[3,864,128]{2,1,0:T(8,128)(2,1)S(1)} %pad_maximum_fusion.1.refs_2_), channel_id=1, source_target_pairs={{0,16},{4,20},{8,24},{12,28},{16,0},{20,4},{24,8},{28,12},{1,17},{... | collective-permute-start | bytes 1990664 | tf_op jit(solution)/shard_map/ppermute | solution.py:23
  34.1 17.0 %collective-permute-start.9 = (bf16[3,864,128]{2,1,0:T(8,128)(2,1)S(1)}, bf16[3,864,128]{2,1,0:T(8,128)(2,1)S(1)}, u32[]{:S(2)}, u32[]{:S(2)}) collective-permute-start(bf16[3,864,128]{2,1,0:T(8,128)(2,1)S(1)} %pad_maximum_fusion.1.refs_2_), channel_id=1, source_target_pairs={{0,8},{4,12},{8,0},{12,4},{16,24},{20,28},{24,16},{28,20},{1,9},{5... | collective-permute-start | bytes 1990664 | tf_op jit(solution)/shard_map/ppermute | solution.py:23
  34.8 14.8 %collective-permute-start.11 = (bf16[864,128]{1,0:T(8,128)(2,1)S(1)}, bf16[864,128]{1,0:T(8,128)(2,1)S(1)}, u32[]{:S(2)}, u32[]{:S(2)}) collective-permute-start(bf16[864,128]{1,0:T(8,128)(2,1)S(1)} %copy-done.10), channel_id=1, source_target_pairs={{0,1},{1,0},{2,3},{3,2},{4,5},{5,4},{6,7},{7,6},{8,9},{9,8},{10,11... | collective-permute-start | bytes 663560 | tf_op jit(solution)/shard_map/ppermute | solution.py:28
  38.4 15.2 %collective-permute-start.15 = (bf16[3,864,128]{2,1,0:T(8,128)(2,1)S(1)}, bf16[3,864,128]{2,1,0:T(8,128)(2,1)S(1)}, u32[]{:S(2)}, u32[]{:S(2)}) collective-permute-start(bf16[3,864,128]{2,1,0:T(8,128)(2,1)S(1)} %pad_maximum_fusion.1.refs_2_), channel_id=1, source_target_pairs={{0,4},{4,0},{8,12},{12,8},{16,20},{20,16},{24,28},{28,24},{1,5},{5... | collective-permute-start | bytes 1990664 | tf_op jit(solution)/shard_map/ppermute | solution.py:23
  51.0 2.7 %collective-permute-start.16 = (bf16[3,864,128]{2,1,0:T(8,128)(2,1)S(1)}, bf16[3,864,128]{2,1,0:T(8,128)(2,1)S(1)}, u32[]{:S(2)}, u32[]{:S(2)}) collective-permute-start(bf16[3,864,128]{2,1,0:T(8,128)(2,1)S(1)} %collective-permute-done.9.refs_4_), channel_id=1, source_target_pairs={{0,4},{4,0},{8,12},{12,8},{16,20},{20,16},{24,28},{28,24},{1,5},{5... | collective-permute-start | bytes 1990664 | tf_op jit(solution)/shard_map/ppermute | solution.py:23
  51.0 3.1 %collective-permute-start.17 = (bf16[3,864,128]{2,1,0:T(8,128)(2,1)S(1)}, bf16[3,864,128]{2,1,0:T(8,128)(2,1)S(1)}, u32[]{:S(2)}, u32[]{:S(2)}) collective-permute-start(bf16[3,864,128]{2,1,0:T(8,128)(2,1)S(1)} %collective-permute-done.10.refs_6_), channel_id=1, source_target_pairs={{0,4},{4,0},{8,12},{12,8},{16,20},{20,16},{24,28},{28,24},{1,5},{5... | collective-permute-start | bytes 1990664 | tf_op jit(solution)/shard_map/ppermute | solution.py:23
  51.6 7.4 %collective-permute-start.13 = (bf16[2,432,128]{2,1,0:T(8,128)(2,1)S(1)}, bf16[2,432,128]{2,1,0:T(8,128)(2,1)S(1)}, u32[]{:S(2)}, u32[]{:S(2)}) collective-permute-start(bf16[2,432,128]{2,1,0:T(8,128)(2,1)S(1)} %slice.52), channel_id=1, source_target_pairs={{0,16},{4,20},{8,24},{12,28},{16,0},{20,4},{24,8},{28,12},{1,17},{... | collective-permute-start | bytes 663560 | tf_op jit(solution)/shard_map/ppermute | solution.py:23
  52.2 7.1 %collective-permute-start.14 = (bf16[2,432,128]{2,1,0:T(8,128)(2,1)S(1)}, bf16[2,432,128]{2,1,0:T(8,128)(2,1)S(1)}, u32[]{:S(2)}, u32[]{:S(2)}) collective-permute-start(bf16[2,432,128]{2,1,0:T(8,128)(2,1)S(1)} %slice.53), channel_id=1, source_target_pairs={{0,8},{4,12},{8,0},{12,4},{16,24},{20,28},{24,16},{28,20},{1,9},{5... | collective-permute-start | bytes 663560 | tf_op jit(solution)/shard_map/ppermute | solution.py:23
  53.6 6.1 %collective-permute-start.18 = (bf16[1,864,128]{2,1,0:T(8,128)(2,1)S(1)}, bf16[1,864,128]{2,1,0:T(8,128)(2,1)S(1)}, u32[]{:S(2)}, u32[]{:S(2)}) collective-permute-start(bf16[1,864,128]{2,1,0:T(8,128)(2,1)S(1)} %bitcast.55), channel_id=1, source_target_pairs={{0,4},{4,0},{8,12},{12,8},{16,20},{20,16},{24,28},{28,24},{1,5},{5... | collective-permute-start | bytes 663560 | tf_op jit(solution)/shard_map/ppermute | solution.py:23
  59.2 1.5 %collective-permute-start.19 = (bf16[2,432,128]{2,1,0:T(8,128)(2,1)S(1)}, bf16[2,432,128]{2,1,0:T(8,128)(2,1)S(1)}, u32[]{:S(2)}, u32[]{:S(2)}) collective-permute-start(bf16[2,432,128]{2,1,0:T(8,128)(2,1)S(1)} %collective-permute-done.13.refs_6_), channel_id=1, source_target_pairs={{0,4},{4,0},{8,12},{12,8},{16,20},{20,16},{24,28},{28,24},{1,5},{5... | collective-permute-start | bytes 663560 | tf_op jit(solution)/shard_map/ppermute | solution.py:23
  59.2 1.8 %collective-permute-start.20 = (bf16[2,432,128]{2,1,0:T(8,128)(2,1)S(1)}, bf16[2,432,128]{2,1,0:T(8,128)(2,1)S(1)}, u32[]{:S(2)}, u32[]{:S(2)}) collective-permute-start(bf16[2,432,128]{2,1,0:T(8,128)(2,1)S(1)} %collective-permute-done.14.refs_8_), channel_id=1, source_target_pairs={{0,4},{4,0},{8,12},{12,8},{16,20},{20,16},{24,28},{28,24},{1,5},{5... | collective-permute-start | bytes 663560 | tf_op jit(solution)/shard_map/ppermute | solution.py:23
  61.0 39.1 %copy-start.6 = (f32[1024]{0:T(1024)S(1)}, f32[1024]{0:T(1024)}, u32[]{:S(2)}) copy-start(f32[1024]{0:T(1024)} %param.12) | copy-start | bytes 12292
  69.5 2.0 %collective-permute-start.21 = (bf16[4,4,128,128]{3,2,1,0:T(8,128)(2,1)S(1)}, bf16[4,4,128,128]{3,2,1,0:T(8,128)(2,1)S(1)}, u32[]{:S(2)}, u32[]{:S(2)}) collective-permute-start(bf16[4,4,128,128]{3,2,1,0:T(8,128)(2,1)S(1)} %get-tuple-element.86), channel_id=1, source_target_pairs={{0,4},{4,0},{8,12},{12,8},{16,20},{20,16},{24,28},{28,24},{1,5},{5... | collective-permute-start | bytes 1572872 | tf_op jit(solution)/shard_map/ppermute | solution.py:23
  71.7 6.1 %collective-permute-start.22 = (bf16[1,4,128,128]{3,2,1,0:T(8,128)(2,1)S(1)}, bf16[1,4,128,128]{3,2,1,0:T(8,128)(2,1)S(1)}, u32[]{:S(2)}, u32[]{:S(2)}) collective-permute-start(bf16[1,4,128,128]{3,2,1,0:T(8,128)(2,1)S(1)} %get-tuple-element.97), channel_id=1, source_target_pairs={{0,8},{4,12},{8,0},{12,4},{16,24},{20,28},{24,16},{28,20},{1,9},{5... | collective-permute-start | bytes 393224 | tf_op jit(solution)/shard_map/ppermute | solution.py:23
  73.2 8.1 %collective-permute-start.23 = (bf16[1,4,128,128]{3,2,1,0:T(8,128)(2,1)S(1)}, bf16[1,4,128,128]{3,2,1,0:T(8,128)(2,1)S(1)}, u32[]{:S(2)}, u32[]{:S(2)}) collective-permute-start(bf16[1,4,128,128]{3,2,1,0:T(8,128)(2,1)S(1)} %get-tuple-element.99), channel_id=1, source_target_pairs={{0,16},{4,20},{8,24},{12,28},{16,0},{20,4},{24,8},{28,12},{1,17},{... | collective-permute-start | bytes 393224 | tf_op jit(solution)/shard_map/ppermute | solution.py:23
  74.0 7.3 %collective-permute-start.24 = (bf16[1,4,128,128]{3,2,1,0:T(8,128)(2,1)S(1)}, bf16[1,4,128,128]{3,2,1,0:T(8,128)(2,1)S(1)}, u32[]{:S(2)}, u32[]{:S(2)}) collective-permute-start(bf16[1,4,128,128]{3,2,1,0:T(8,128)(2,1)S(1)} %get-tuple-element.98), channel_id=1, source_target_pairs={{0,24},{4,28},{8,16},{12,20},{16,8},{20,12},{24,0},{28,4},{1,25},{... | collective-permute-start | bytes 393224 | tf_op jit(solution)/shard_map/ppermute | solution.py:23
  81.4 5.5 %collective-permute-start.25 = (bf16[128,128]{1,0:T(8,128)(2,1)S(1)}, bf16[128,128]{1,0:T(8,128)(2,1)S(1)}, u32[]{:S(2)}, u32[]{:S(2)}) collective-permute-start(bf16[128,128]{1,0:T(8,128)(2,1)S(1)} %get-tuple-element.100), channel_id=1, source_target_pairs={{0,1},{1,0},{2,3},{3,2},{4,5},{5,4},{6,7},{7,6},{8,9},{9,8},{10,11... | collective-permute-start | bytes 98312 | tf_op jit(solution)/shard_map/ppermute | solution.py:28
  84.4 5.3 %collective-permute-start.26 = (bf16[128,128]{1,0:T(8,128)(2,1)S(1)}, bf16[128,128]{1,0:T(8,128)(2,1)S(1)}, u32[]{:S(2)}, u32[]{:S(2)}) collective-permute-start(bf16[128,128]{1,0:T(8,128)(2,1)S(1)} %get-tuple-element.102), channel_id=1, source_target_pairs={{0,2},{1,3},{2,0},{3,1},{4,6},{5,7},{6,4},{7,5},{8,10},{9,11},{10,... | collective-permute-start | bytes 98312 | tf_op jit(solution)/shard_map/ppermute | solution.py:28
  85.5 5.7 %collective-permute-start.27 = (bf16[128,128]{1,0:T(8,128)(2,1)S(1)}, bf16[128,128]{1,0:T(8,128)(2,1)S(1)}, u32[]{:S(2)}, u32[]{:S(2)}) collective-permute-start(bf16[128,128]{1,0:T(8,128)(2,1)S(1)} %get-tuple-element.101), channel_id=1, source_target_pairs={{0,3},{1,2},{2,1},{3,0},{4,7},{5,6},{6,5},{7,4},{8,11},{9,10},{10,... | collective-permute-start | bytes 98312 | tf_op jit(solution)/shard_map/ppermute | solution.py:28
  91.2 4.3 %collective-permute-start.28 = (f32[128,128]{1,0:T(8,128)S(1)}, f32[128,128]{1,0:T(8,128)S(1)}, u32[]{:S(2)}, u32[]{:S(2)}) collective-permute-start(f32[128,128]{1,0:T(8,128)S(1)} %fusion.5), channel_id=1, source_target_pairs={{0,8},{4,12},{8,0},{12,4},{16,24},{20,28},{24,16},{28,20},{1,9},{5... | collective-permute-start | bytes 196616 | tf_op jit(solution)/shard_map/ppermute | solution.py:23
  92.5 4.3 %collective-permute-start.29 = (f32[128,128]{1,0:T(8,128)S(1)}, f32[128,128]{1,0:T(8,128)S(1)}, u32[]{:S(2)}, u32[]{:S(2)}) collective-permute-start(f32[128,128]{1,0:T(8,128)S(1)} %fusion.5), channel_id=1, source_target_pairs={{0,16},{4,20},{8,24},{12,28},{16,0},{20,4},{24,8},{28,12},{1,17},{... | collective-permute-start | bytes 196616 | tf_op jit(solution)/shard_map/ppermute | solution.py:23
  93.3 5.2 %collective-permute-start.30 = (f32[128,128]{1,0:T(8,128)S(1)}, f32[128,128]{1,0:T(8,128)S(1)}, u32[]{:S(2)}, u32[]{:S(2)}) collective-permute-start(f32[128,128]{1,0:T(8,128)S(1)} %fusion.5), channel_id=1, source_target_pairs={{0,24},{4,28},{8,16},{12,20},{16,8},{20,12},{24,0},{28,4},{1,25},{... | collective-permute-start | bytes 196616 | tf_op jit(solution)/shard_map/ppermute | solution.py:23
  98.5 1.6 %collective-permute-start.31 = (f32[4,128,128]{2,1,0:T(8,128)S(1)}, f32[4,128,128]{2,1,0:T(8,128)S(1)}, u32[]{:S(2)}, u32[]{:S(2)}) collective-permute-start(f32[4,128,128]{2,1,0:T(8,128)S(1)} %pad_maximum_fusion.2.even), channel_id=1, source_target_pairs={{0,4},{4,0},{8,12},{12,8},{16,20},{20,16},{24,28},{28,24},{1,5},{5... | collective-permute-start | bytes 786440 | tf_op jit(solution)/shard_map/ppermute | solution.py:23

commit v9 on v8

--- a/solution.py
+++ b/solution.py
@@ -686,11 +686,12 @@
 
     packed = pack(look_rows, emb_table, shards, replicas)
     parcels = [cross_over(p, k + 1) for k, p in enumerate(packed)]
-    bias, head, label_row = (x.reshape(1, -1) for x in (cross_bias, head_weight, labels))
+    bias, label_row = cross_bias.reshape(1, -1), labels.reshape(1, -1)
     parcels[0], blocks = lax.optimization_barrier(
         (parcels[0], cut(factors) if even_split else [])
     )
-    counts, blocks = lax.optimization_barrier((live_counts, blocks))
+    counts, head, blocks = lax.optimization_barrier((live_counts, head_weight, blocks))
+    head = head.reshape(1, -1)
     prepared = ready(counts, look_rows, bag_order, dense_emb, head, shards)
     places, info, own_words, lead = prepared
     far, corner = [], []
@@ -698,13 +699,13 @@
         far = jnp.stack([cross_over(blocks[0], k) for k in range(1, shards)])
         corner = cross_over(blocks[1], 1)[None]
     counted = slots(info, own_words, parcels, bag_order.shape[2], rows, shards, replicas)
-    pieces, far, counted, own_rows = replica_gather(
+    pieces, far, counted = replica_gather(
         jnp.stack([p[:block] for p in parcels]),
         far,
         counted,
-        split_own(emb_table, replicas),
         after=prepared,
     )
+    own_rows = split_own(emb_table, replicas)
     crossed = pool(info, places, counted, own_rows, pieces, lead, head)
     rank = cross_in.shape[1]
     if even_split:

time: 102 us -> 102 us (level)
  waiting for transfers between devices: 23.3 us -> 25.6 us
  starting transfers between devices: 36.8 us -> 35.5 us
  local copies, waits for them, and re-layouts: 4.93 us -> 3.89 us
    ppermute x22, waiting for transfers between devices: 17.7 us -> 19.6 us  [swap(): return lax.ppermute(array, 'replica', [(i, i ^ mask) for i in range(size)])]
    unnamed x22, local copies, waits for them, and re-layouts: 4.11 us -> 3.07 us
where the time goes in v9:
time: 102 us
  starting transfers between devices  35.5 us (35%)
  Pallas kernels  35.2 us (35%)
  waiting for transfers between devices  25.6 us (25%)
  local copies, waits for them, and re-layouts  3.89 us (4%)
    ppermute x22, waiting for transfers between devices, swap(): return lax.ppermute(array, 'replica', [(i, i ^ mask) for i in range(size)])  19.6 us
    ppermute x10, starting transfers between devices, cross_over(): return lax.ppermute(array, 'table', [(i, i ^ mask) for i in range(size)])  18.5 us
    ppermute x22, starting transfers between devices, swap(): return lax.ppermute(array, 'replica', [(i, i ^ mask) for i in range(size)])  16.9 us
    pallas_call x1, Pallas kernels, pool(): pl.pallas_call(functools.partial(pool_kernel, shards), out_shape=[jax.Sha...  11.2 us
    pallas_call x1, Pallas kernels, dense_step(): pl.pallas_call(functools.partial(dense_kernel, shards, replicas, copies),...  8.44 us
    pallas_call x1, Pallas kernels, slots(): pl.pallas_call(functools.partial(slots_kernel, shards, replicas, bags), o...  6.23 us
    ppermute x10, waiting for transfers between devices, cross_over(): return lax.ppermute(array, 'table', [(i, i ^ mask) for i in range(size)])  5.99 us
    pallas_call x1, Pallas kernels, first_step(): pl.pallas_call(functools.partial(first_kernel, copies), out_shape=(jax.Sh...  3.65 us
  transfers between devices with their start and end apart: 32, of which 19 were waited for; matrix products, arithmetic and copies ran while one was open for 1% of the time, Pallas kernels for 23%

profile of v9, /device:TPU:0, one launch (start us, length us, event | category | flops | bytes accessed | tf_op | source)
XLA Modules:
  0.0 101.6 jit_solution(17304895368210461135)
XLA Ops:
  0.6 1.8 %pack.1 = (f32[148,128]{1,0:T(8,128)}, f32[148,128]{1,0:T(8,128)}, f32[148,128]{1,0:T(8,128)}) custom-call(s32[1,1,4,4,1248]{4,3,2,1,0:T(4,128)} %look_rows.3, f32[1024,128]{1,0:T(8,128)} %table.3), custom_call_target="tpu_custom_call" | custom-call | tf_op jit(solution)/shard_map/pack/pallas_call | solution.py:116
  2.4 3.1 %collective-permute-start = (f32[148,128]{1,0:T(8,128)}, f32[148,128]{1,0:T(8,128)S(1)}, u32[]{:S(2)}, u32[]{:S(2)}) collective-permute-start(f32[148,128]{1,0:T(8,128)} %get-tuple-element.48), channel_id=1, source_target_pairs={{0,1},{1,0},{2,3},{3,2},{4,5},{5,4},{6,7},{7,6},{8,9},{9,8},{10,11... | collective-permute-start | bytes 227336 | tf_op jit(solution)/shard_map/ppermute | solution.py:28
  5.5 2.5 %collective-permute-start.2 = (f32[148,128]{1,0:T(8,128)}, f32[148,128]{1,0:T(8,128)S(1)}, u32[]{:S(2)}, u32[]{:S(2)}) collective-permute-start(f32[148,128]{1,0:T(8,128)} %get-tuple-element.59), channel_id=1, source_target_pairs={{0,3},{1,2},{2,1},{3,0},{4,7},{5,6},{6,5},{7,4},{8,11},{9,10},{10,... | collective-permute-start | bytes 227336 | tf_op jit(solution)/shard_map/ppermute | solution.py:28
  8.1 1.9 %cut.1 = (bf16[864,128]{1,0:T(8,128)(2,1)}, bf16[864,128]{1,0:T(8,128)(2,1)}) custom-call(bf16[864,512]{1,0:T(8,128)(2,1)} %refs_2_.1, bf16[864,512]{1,0:T(8,128)(2,1)} %refs_3_.1), custom_call_target="tpu_custom_call" | custom-call | tf_op jit(solution)/shard_map/cut/pallas_call | solution.py:150
  10.0 1.9 %collective-permute-start.6 = (bf16[864,128]{1,0:T(8,128)(2,1)}, bf16[864,128]{1,0:T(8,128)(2,1)S(1)}, u32[]{:S(2)}, u32[]{:S(2)}) collective-permute-start(bf16[864,128]{1,0:T(8,128)(2,1)} %get-tuple-element.63), channel_id=1, source_target_pairs={{0,1},{1,0},{2,3},{3,2},{4,5},{5,4},{6,7},{7,6},{8,9},{9,8},{10,11... | collective-permute-start | bytes 663560 | tf_op jit(solution)/shard_map/ppermute | solution.py:28
  11.9 1.7 %collective-permute-start.7 = (bf16[864,128]{1,0:T(8,128)(2,1)}, bf16[864,128]{1,0:T(8,128)(2,1)S(1)}, u32[]{:S(2)}, u32[]{:S(2)}) collective-permute-start(bf16[864,128]{1,0:T(8,128)(2,1)} %get-tuple-element.63), channel_id=1, source_target_pairs={{0,2},{1,3},{2,0},{3,1},{4,6},{5,7},{6,4},{7,5},{8,10},{9,11},{10,... | collective-permute-start | bytes 663560 | tf_op jit(solution)/shard_map/ppermute | solution.py:28
  13.5 0.9 collective-permute-start.8
  14.5 1.5 %collective-permute-done.1.refs_1_ = f32[148,128]{1,0:T(8,128)S(1)} collective-permute-done((f32[148,128]{1,0:T(8,128)}, f32[148,128]{1,0:T(8,128)S(1)}, u32[]{:S(2)}, u32[]{:S(2)}) %collective-permute-start.1) | collective-permute-done | bytes 75808 | tf_op jit(solution)/shard_map/ppermute | solution.py:28
  15.9 0.7 reshape.77.head
  16.7 1.6 %collective-permute-start.3 = (f32[3,128,128]{2,1,0:T(8,128)S(1)}, f32[3,128,128]{2,1,0:T(8,128)S(1)}, u32[]{:S(2)}, u32[]{:S(2)}) collective-permute-start(f32[3,128,128]{2,1,0:T(8,128)S(1)} %pad_maximum_fusion.3), channel_id=1, source_target_pairs={{0,8},{4,12},{8,0},{12,4},{16,24},{20,28},{24,16},{28,20},{1,9},{5... | collective-permute-start | bytes 589832 | tf_op jit(solution)/shard_map/ppermute | solution.py:23
  18.3 0.9 copy-done.3
  19.1 0.8 copy-done.4
  19.9 0.7 copy-done.5
  21.9 1.6 %collective-permute-start.5 = (f32[3,128,128]{2,1,0:T(8,128)S(1)}, f32[3,128,128]{2,1,0:T(8,128)S(1)}, u32[]{:S(2)}, u32[]{:S(2)}) collective-permute-start(f32[3,128,128]{2,1,0:T(8,128)S(1)} %pad_maximum_fusion.3), channel_id=1, source_target_pairs={{0,24},{4,28},{8,16},{12,20},{16,8},{20,12},{24,0},{28,4},{1,25},{... | collective-permute-start | bytes 589832 | tf_op jit(solution)/shard_map/ppermute | solution.py:23
  23.4 0.9 collective-permute-start.4
  24.4 6.2 %slots.1.counted = bf16[16,1024,256]{2,1,0:T(8,128)(2,1)S(1)} custom-call(s32[1,128]{1,0:T(1,128)S(1)} %get-tuple-element.55.info, s32[8,1280]{1,0:T(8,128)S(1)} %get-tuple-element.60.own, f32[148,128]{1,0:T(8,128)S(1)} %collective-permute-done.refs_0_, f32[148,128]{1,0:T(8,128)S(1)} %collective-permute-done.1.refs_1_, ...), custom_call_target="tpu_custom_call" | custom-call | flops 1000 | bytes 1000 | tf_op jit(solution)/shard_map/slots/pallas_call | solution.py:298
  30.9 2.2 %collective-permute-done.4 = f32[3,128,128]{2,1,0:T(8,128)S(1)} collective-permute-done((f32[3,128,128]{2,1,0:T(8,128)S(1)}, f32[3,128,128]{2,1,0:T(8,128)S(1)}, u32[]{:S(2)}, u32[]{:S(2)}) %collective-permute-start.4) | collective-permute-done | bytes 196640 | tf_op jit(solution)/shard_map/ppermute | solution.py:23
  33.3 0.9 collective-permute-start.10
  34.1 1.2 %collective-permute-start.9 = (bf16[3,864,128]{2,1,0:T(8,128)(2,1)S(1)}, bf16[3,864,128]{2,1,0:T(8,128)(2,1)S(1)}, u32[]{:S(2)}, u32[]{:S(2)}) collective-permute-start(bf16[3,864,128]{2,1,0:T(8,128)(2,1)S(1)} %pad_maximum_fusion.1.refs_2_), channel_id=1, source_target_pairs={{0,8},{4,12},{8,0},{12,4},{16,24},{20,28},{24,16},{28,20},{1,9},{5... | collective-permute-start | bytes 1990664 | tf_op jit(solution)/shard_map/ppermute | solution.py:23
  35.4 3.1 %collective-permute-start.11 = (bf16[864,128]{1,0:T(8,128)(2,1)S(1)}, bf16[864,128]{1,0:T(8,128)(2,1)S(1)}, u32[]{:S(2)}, u32[]{:S(2)}) collective-permute-start(bf16[864,128]{1,0:T(8,128)(2,1)S(1)} %copy-done.10), channel_id=1, source_target_pairs={{0,1},{1,0},{2,3},{3,2},{4,5},{5,4},{6,7},{7,6},{8,9},{9,8},{10,11... | collective-permute-start | bytes 663560 | tf_op jit(solution)/shard_map/ppermute | solution.py:28
  38.7 11.2 %pool.1 = (bf16[128,3456]{1,0:T(8,128)(2,1)S(1)}, bf16[128,3456]{1,0:T(8,128)(2,1)S(1)}) custom-call(s32[1,128]{1,0:T(1,128)S(1)} %get-tuple-element.55.info, s32[1,1664]{1,0:T(1,128)S(1)} %get-tuple-element.56.places, bf16[16,1024,256]{2,1,0:T(8,128)(2,1)S(1)} %slots.1.counted, bf16[1024,256]{1,0:T(8,128)(2,1)S(1)} %split_own.1.own, ...), custom_call_target="tpu_custom_call" | custom-call | flops 1000 | bytes 1000 | tf_op jit(solution)/shard_map/pool/pallas_call | solution.py:364
  49.9 0.7 collective-permute-done.10.refs_6_
  51.7 1.3 %collective-permute-start.13 = (bf16[2,432,128]{2,1,0:T(8,128)(2,1)S(1)}, bf16[2,432,128]{2,1,0:T(8,128)(2,1)S(1)}, u32[]{:S(2)}, u32[]{:S(2)}) collective-permute-start(bf16[2,432,128]{2,1,0:T(8,128)(2,1)S(1)} %slice.52), channel_id=1, source_target_pairs={{0,16},{4,20},{8,24},{12,28},{16,0},{20,4},{24,8},{28,12},{1,17},{... | collective-permute-start | bytes 663560 | tf_op jit(solution)/shard_map/ppermute | solution.py:23
  52.9 0.8 collective-permute-start.14
  54.2 3.6 %first.3 = (f32[3328,128]{1,0:T(8,128)S(1)}, f32[128,128]{1,0:T(8,128)S(1)}) custom-call(bf16[128,3456]{1,0:T(8,128)(2,1)S(1)} %get-tuple-element.73.cross, bf16[128,3456]{1,0:T(8,128)(2,1)S(1)} %get-tuple-element.74.scaled, f32[1,3456]{1,0:T(1,128)S(1)} %reshape.79.bias, f32[1,3456]{1,0:T(1,128)S(1)} %reshape.77.head, bf16[864,512]{1,0:T(8,128)(2,1)S(1)} %copy-done, ...), custom_call_target="tpu_custom_call" | custom-call | flops 2000000000 | bytes 20000000 | tf_op jit(solution)/shard_map/first/pallas_call | solution.py:432
  57.8 1.2 %collective-permute-done.13.refs_6_ = bf16[2,432,128]{2,1,0:T(8,128)(2,1)S(1)} collective-permute-done((bf16[2,432,128]{2,1,0:T(8,128)(2,1)S(1)}, bf16[2,432,128]{2,1,0:T(8,128)(2,1)S(1)}, u32[]{:S(2)}, u32[]{:S(2)}) %collective-permute-start.13) | collective-permute-done | bytes 221216 | tf_op jit(solution)/shard_map/ppermute | solution.py:23
  59.1 0.9 collective-permute-done.14.refs_8_
  60.5 1.0 collective-permute-done.19.refs_7_
  61.8 8.4 %dense.3 = (f32[1,128]{1,0:T(1,128)}, bf16[4,4,128,128]{3,2,1,0:T(8,128)(2,1)S(1)}, bf16[4,4,128,128]{3,2,1,0:T(8,128)(2,1)S(1)}) custom-call(s32[1,128]{1,0:T(1,128)S(1)} %get-tuple-element.55.info, s32[1,1664]{1,0:T(1,128)S(1)} %get-tuple-element.56.places, bf16[128,3456]{1,0:T(8,128)(2,1)S(1)} %get-tuple-element.73.cross, ...), custom_call_target="tpu_custom_call" | custom-call | flops 2000000000 | bytes 20000000 | tf_op jit(solution)/shard_map/dense/pallas_call | solution.py:535
  70.5 1.7 %collective-permute-done.21 = bf16[4,4,128,128]{3,2,1,0:T(8,128)(2,1)S(1)} collective-permute-done((bf16[4,4,128,128]{3,2,1,0:T(8,128)(2,1)S(1)}, bf16[4,4,128,128]{3,2,1,0:T(8,128)(2,1)S(1)}, u32[]{:S(2)}, u32[]{:S(2)}) %collective-permute-start.21) | collective-permute-done | bytes 524320 | tf_op jit(solution)/shard_map/ppermute | solution.py:23
  72.5 0.9 collective-permute-start.22
  73.4 1.2 %collective-permute-start.23 = (bf16[1,4,128,128]{3,2,1,0:T(8,128)(2,1)S(1)}, bf16[1,4,128,128]{3,2,1,0:T(8,128)(2,1)S(1)}, u32[]{:S(2)}, u32[]{:S(2)}) collective-permute-start(bf16[1,4,128,128]{3,2,1,0:T(8,128)(2,1)S(1)} %get-tuple-element.99), channel_id=1, source_target_pairs={{0,16},{4,20},{8,24},{12,28},{16,0},{20,4},{24,8},{28,12},{1,17},{... | collective-permute-start | bytes 393224 | tf_op jit(solution)/shard_map/ppermute | solution.py:23
  74.6 1.4 %collective-permute-start.24 = (bf16[1,4,128,128]{3,2,1,0:T(8,128)(2,1)S(1)}, bf16[1,4,128,128]{3,2,1,0:T(8,128)(2,1)S(1)}, u32[]{:S(2)}, u32[]{:S(2)}) collective-permute-start(bf16[1,4,128,128]{3,2,1,0:T(8,128)(2,1)S(1)} %get-tuple-element.98), channel_id=1, source_target_pairs={{0,24},{4,28},{8,16},{12,20},{16,8},{20,12},{24,0},{28,4},{1,25},{... | collective-permute-start | bytes 393224 | tf_op jit(solution)/shard_map/ppermute | solution.py:23
  76.0 2.8 %collective-permute-done.22 = bf16[1,4,128,128]{3,2,1,0:T(8,128)(2,1)S(1)} collective-permute-done((bf16[1,4,128,128]{3,2,1,0:T(8,128)(2,1)S(1)}, bf16[1,4,128,128]{3,2,1,0:T(8,128)(2,1)S(1)}, u32[]{:S(2)}, u32[]{:S(2)}) %collective-permute-start.22) | collective-permute-done | bytes 131104 | tf_op jit(solution)/shard_map/ppermute | solution.py:23
  78.9 2.6 %collective-permute-done.23 = bf16[1,4,128,128]{3,2,1,0:T(8,128)(2,1)S(1)} collective-permute-done((bf16[1,4,128,128]{3,2,1,0:T(8,128)(2,1)S(1)}, bf16[1,4,128,128]{3,2,1,0:T(8,128)(2,1)S(1)}, u32[]{:S(2)}, u32[]{:S(2)}) %collective-permute-start.23) | collective-permute-done | bytes 131104 | tf_op jit(solution)/shard_map/ppermute | solution.py:23
  81.6 2.8 %collective-permute-start.25 = (bf16[128,128]{1,0:T(8,128)(2,1)S(1)}, bf16[128,128]{1,0:T(8,128)(2,1)S(1)}, u32[]{:S(2)}, u32[]{:S(2)}) collective-permute-start(bf16[128,128]{1,0:T(8,128)(2,1)S(1)} %get-tuple-element.100), channel_id=1, source_target_pairs={{0,1},{1,0},{2,3},{3,2},{4,5},{5,4},{6,7},{7,6},{8,9},{9,8},{10,11... | collective-permute-start | bytes 98312 | tf_op jit(solution)/shard_map/ppermute | solution.py:28
  84.4 1.1 %collective-permute-start.26 = (bf16[128,128]{1,0:T(8,128)(2,1)S(1)}, bf16[128,128]{1,0:T(8,128)(2,1)S(1)}, u32[]{:S(2)}, u32[]{:S(2)}) collective-permute-start(bf16[128,128]{1,0:T(8,128)(2,1)S(1)} %get-tuple-element.102), channel_id=1, source_target_pairs={{0,2},{1,3},{2,0},{3,1},{4,6},{5,7},{6,4},{7,5},{8,10},{9,11},{10,... | collective-permute-start | bytes 98312 | tf_op jit(solution)/shard_map/ppermute | solution.py:28
  85.5 1.4 %collective-permute-start.27 = (bf16[128,128]{1,0:T(8,128)(2,1)S(1)}, bf16[128,128]{1,0:T(8,128)(2,1)S(1)}, u32[]{:S(2)}, u32[]{:S(2)}) collective-permute-start(bf16[128,128]{1,0:T(8,128)(2,1)S(1)} %get-tuple-element.101), channel_id=1, source_target_pairs={{0,3},{1,2},{2,1},{3,0},{4,7},{5,6},{6,5},{7,4},{8,11},{9,10},{10,... | collective-permute-start | bytes 98312 | tf_op jit(solution)/shard_map/ppermute | solution.py:28
  86.9 2.9 %collective-permute-done.26 = bf16[128,128]{1,0:T(8,128)(2,1)S(1)} collective-permute-done((bf16[128,128]{1,0:T(8,128)(2,1)S(1)}, bf16[128,128]{1,0:T(8,128)(2,1)S(1)}, u32[]{:S(2)}, u32[]{:S(2)}) %collective-permute-start.26) | collective-permute-done | bytes 32800 | tf_op jit(solution)/shard_map/ppermute | solution.py:28
  89.8 1.5 %collective-permute-done.27 = bf16[128,128]{1,0:T(8,128)(2,1)S(1)} collective-permute-done((bf16[128,128]{1,0:T(8,128)(2,1)S(1)}, bf16[128,128]{1,0:T(8,128)(2,1)S(1)}, u32[]{:S(2)}, u32[]{:S(2)}) %collective-permute-start.27) | collective-permute-done | bytes 32800 | tf_op jit(solution)/shard_map/ppermute | solution.py:28
  91.3 1.3 %collective-permute-start.28 = (f32[128,128]{1,0:T(8,128)S(1)}, f32[128,128]{1,0:T(8,128)S(1)}, u32[]{:S(2)}, u32[]{:S(2)}) collective-permute-start(f32[128,128]{1,0:T(8,128)S(1)} %fusion.5), channel_id=1, source_target_pairs={{0,8},{4,12},{8,0},{12,4},{16,24},{20,28},{24,16},{28,20},{1,9},{5... | collective-permute-start | bytes 196616 | tf_op jit(solution)/shard_map/ppermute | solution.py:23
  92.5 0.8 collective-permute-start.29
  93.4 1.4 %collective-permute-start.30 = (f32[128,128]{1,0:T(8,128)S(1)}, f32[128,128]{1,0:T(8,128)S(1)}, u32[]{:S(2)}, u32[]{:S(2)}) collective-permute-start(f32[128,128]{1,0:T(8,128)S(1)} %fusion.5), channel_id=1, source_target_pairs={{0,24},{4,28},{8,16},{12,20},{16,8},{20,12},{24,0},{28,4},{1,25},{... | collective-permute-start | bytes 196616 | tf_op jit(solution)/shard_map/ppermute | solution.py:23
  94.8 0.8 collective-permute-done.28
  95.6 1.2 %collective-permute-done.29 = f32[128,128]{1,0:T(8,128)S(1)} collective-permute-done((f32[128,128]{1,0:T(8,128)S(1)}, f32[128,128]{1,0:T(8,128)S(1)}, u32[]{:S(2)}, u32[]{:S(2)}) %collective-permute-start.29) | collective-permute-done | bytes 65568 | tf_op jit(solution)/shard_map/ppermute | solution.py:23
  96.8 1.7 %collective-permute-done.30 = f32[128,128]{1,0:T(8,128)S(1)} collective-permute-done((f32[128,128]{1,0:T(8,128)S(1)}, f32[128,128]{1,0:T(8,128)S(1)}, u32[]{:S(2)}, u32[]{:S(2)}) %collective-permute-start.30) | collective-permute-done | bytes 65568 | tf_op jit(solution)/shard_map/ppermute | solution.py:23
  98.6 1.5 %collective-permute-done.31.odd = f32[4,128,128]{2,1,0:T(8,128)S(1)} collective-permute-done((f32[4,128,128]{2,1,0:T(8,128)S(1)}, f32[4,128,128]{2,1,0:T(8,128)S(1)}, u32[]{:S(2)}, u32[]{:S(2)}) %collective-permute-start.31) | collective-permute-done | bytes 262176 | tf_op jit(solution)/shard_map/ppermute | solution.py:23
  100.2 1.4 %finish.1 = (f32[1024,128]{1,0:T(8,128)}, f32[8,128]{1,0:T(8,128)}) custom-call(f32[8,128]{1,0:T(8,128)S(1)} %bitcast.57, f32[4,128,128]{2,1,0:T(8,128)S(1)} %pad_maximum_fusion.2.even, f32[4,128,128]{2,1,0:T(8,128)S(1)} %collective-permute-done.31.odd), custom_call_target="tpu_custom_call" | custom-call | tf_op jit(solution)/shard_map/finish/pallas_call | solution.py:654
  (63 shorter events, 5.0 us)
Async XLA Ops:
  0.6 37.8 %copy-start.2 = (f32[1024,128]{1,0:T(8,128)S(1)}, f32[1024,128]{1,0:T(8,128)}, u32[]{:S(2)}) copy-start(f32[1024,128]{1,0:T(8,128)} %table.3) | copy-start | bytes 1572868
  2.4 7.6 %collective-permute-start = (f32[148,128]{1,0:T(8,128)}, f32[148,128]{1,0:T(8,128)S(1)}, u32[]{:S(2)}, u32[]{:S(2)}) collective-permute-start(f32[148,128]{1,0:T(8,128)} %get-tuple-element.48), channel_id=1, source_target_pairs={{0,1},{1,0},{2,3},{3,2},{4,5},{5,4},{6,7},{7,6},{8,9},{9,8},{10,11... | collective-permute-start | bytes 227336 | tf_op jit(solution)/shard_map/ppermute | solution.py:28
  5.5 8.9 %collective-permute-start.2 = (f32[148,128]{1,0:T(8,128)}, f32[148,128]{1,0:T(8,128)S(1)}, u32[]{:S(2)}, u32[]{:S(2)}) collective-permute-start(f32[148,128]{1,0:T(8,128)} %get-tuple-element.59), channel_id=1, source_target_pairs={{0,3},{1,2},{2,1},{3,0},{4,7},{5,6},{6,5},{7,4},{8,11},{9,10},{10,... | collective-permute-start | bytes 227336 | tf_op jit(solution)/shard_map/ppermute | solution.py:28
  8.0 7.9 %collective-permute-start.1 = (f32[148,128]{1,0:T(8,128)}, f32[148,128]{1,0:T(8,128)S(1)}, u32[]{:S(2)}, u32[]{:S(2)}) collective-permute-start(f32[148,128]{1,0:T(8,128)} %get-tuple-element.58), channel_id=1, source_target_pairs={{0,2},{1,3},{2,0},{3,1},{4,6},{5,7},{6,4},{7,5},{8,10},{9,11},{10,... | collective-permute-start | bytes 227336 | tf_op jit(solution)/shard_map/ppermute | solution.py:28
  10.0 25.4 %copy-start.10 = (bf16[864,128]{1,0:T(8,128)(2,1)S(1)}, bf16[864,128]{1,0:T(8,128)(2,1)}, u32[]{:S(2)}) copy-start(bf16[864,128]{1,0:T(8,128)(2,1)} %get-tuple-element.65) | copy-start | bytes 663556
  10.0 13.5 %collective-permute-start.6 = (bf16[864,128]{1,0:T(8,128)(2,1)}, bf16[864,128]{1,0:T(8,128)(2,1)S(1)}, u32[]{:S(2)}, u32[]{:S(2)}) collective-permute-start(bf16[864,128]{1,0:T(8,128)(2,1)} %get-tuple-element.63), channel_id=1, source_target_pairs={{0,1},{1,0},{2,3},{3,2},{4,5},{5,4},{6,7},{7,6},{8,9},{9,8},{10,11... | collective-permute-start | bytes 663560 | tf_op jit(solution)/shard_map/ppermute | solution.py:28
  11.9 19.0 %collective-permute-start.7 = (bf16[864,128]{1,0:T(8,128)(2,1)}, bf16[864,128]{1,0:T(8,128)(2,1)S(1)}, u32[]{:S(2)}, u32[]{:S(2)}) collective-permute-start(bf16[864,128]{1,0:T(8,128)(2,1)} %get-tuple-element.63), channel_id=1, source_target_pairs={{0,2},{1,3},{2,0},{3,1},{4,6},{5,7},{6,4},{7,5},{8,10},{9,11},{10,... | collective-permute-start | bytes 663560 | tf_op jit(solution)/shard_map/ppermute | solution.py:28
  13.5 17.3 %collective-permute-start.8 = (bf16[864,128]{1,0:T(8,128)(2,1)}, bf16[864,128]{1,0:T(8,128)(2,1)S(1)}, u32[]{:S(2)}, u32[]{:S(2)}) collective-permute-start(bf16[864,128]{1,0:T(8,128)(2,1)} %get-tuple-element.63), channel_id=1, source_target_pairs={{0,3},{1,2},{2,1},{3,0},{4,7},{5,6},{6,5},{7,4},{8,11},{9,10},{10,... | collective-permute-start | bytes 663560 | tf_op jit(solution)/shard_map/ppermute | solution.py:28
  16.7 14.2 %collective-permute-start.3 = (f32[3,128,128]{2,1,0:T(8,128)S(1)}, f32[3,128,128]{2,1,0:T(8,128)S(1)}, u32[]{:S(2)}, u32[]{:S(2)}) collective-permute-start(f32[3,128,128]{2,1,0:T(8,128)S(1)} %pad_maximum_fusion.3), channel_id=1, source_target_pairs={{0,8},{4,12},{8,0},{12,4},{16,24},{20,28},{24,16},{28,20},{1,9},{5... | collective-permute-start | bytes 589832 | tf_op jit(solution)/shard_map/ppermute | solution.py:23
  18.3 0.9 copy-start.3
  19.1 0.8 copy-start.4
  19.9 0.7 copy-start.5
  20.6 0.7 copy-start.7
  21.9 9.0 %collective-permute-start.5 = (f32[3,128,128]{2,1,0:T(8,128)S(1)}, f32[3,128,128]{2,1,0:T(8,128)S(1)}, u32[]{:S(2)}, u32[]{:S(2)}) collective-permute-start(f32[3,128,128]{2,1,0:T(8,128)S(1)} %pad_maximum_fusion.3), channel_id=1, source_target_pairs={{0,24},{4,28},{8,16},{12,20},{16,8},{20,12},{24,0},{28,4},{1,25},{... | collective-permute-start | bytes 589832 | tf_op jit(solution)/shard_map/ppermute | solution.py:23
  23.4 9.7 %collective-permute-start.4 = (f32[3,128,128]{2,1,0:T(8,128)S(1)}, f32[3,128,128]{2,1,0:T(8,128)S(1)}, u32[]{:S(2)}, u32[]{:S(2)}) collective-permute-start(f32[3,128,128]{2,1,0:T(8,128)S(1)} %pad_maximum_fusion.3), channel_id=1, source_target_pairs={{0,16},{4,20},{8,24},{12,28},{16,0},{20,4},{24,8},{28,12},{1,17},{... | collective-permute-start | bytes 589832 | tf_op jit(solution)/shard_map/ppermute | solution.py:23
  30.6 23.2 %copy-start.9 = (f32[3456]{0:T(1024)S(1)}, f32[3456]{0:T(1024)}, u32[]{:S(2)}) copy-start(f32[3456]{0:T(1024)} %param.20) | copy-start | bytes 41476
  30.6 23.6 %copy-start = (bf16[864,512]{1,0:T(8,128)(2,1)S(1)}, bf16[864,512]{1,0:T(8,128)(2,1)}, u32[]{:S(2)}) copy-start(bf16[864,512]{1,0:T(8,128)(2,1)} %refs_2_.1) | copy-start | bytes 2654212
  30.6 23.6 %copy-start.1 = (bf16[864,512]{1,0:T(8,128)(2,1)S(1)}, bf16[864,512]{1,0:T(8,128)(2,1)}, u32[]{:S(2)}) copy-start(bf16[864,512]{1,0:T(8,128)(2,1)} %refs_3_.1) | copy-start | bytes 2654212
  33.2 5.5 %collective-permute-start.12 = (f32[4,3,128,128]{3,2,1,0:T(8,128)S(1)}, f32[4,3,128,128]{3,2,1,0:T(8,128)S(1)}, u32[]{:S(2)}, u32[]{:S(2)}) collective-permute-start(f32[4,3,128,128]{3,2,1,0:T(8,128)S(1)} %pad_maximum_fusion.even), channel_id=1, source_target_pairs={{0,4},{4,0},{8,12},{12,8},{16,20},{20,16},{24,28},{28,24},{1,5},{5... | collective-permute-start | bytes 2359304 | tf_op jit(solution)/shard_map/ppermute | solution.py:23
  33.3 17.3 %collective-permute-start.10 = (bf16[3,864,128]{2,1,0:T(8,128)(2,1)S(1)}, bf16[3,864,128]{2,1,0:T(8,128)(2,1)S(1)}, u32[]{:S(2)}, u32[]{:S(2)}) collective-permute-start(bf16[3,864,128]{2,1,0:T(8,128)(2,1)S(1)} %pad_maximum_fusion.1.refs_2_), channel_id=1, source_target_pairs={{0,16},{4,20},{8,24},{12,28},{16,0},{20,4},{24,8},{28,12},{1,17},{... | collective-permute-start | bytes 1990664 | tf_op jit(solution)/shard_map/ppermute | solution.py:23
  34.1 17.0 %collective-permute-start.9 = (bf16[3,864,128]{2,1,0:T(8,128)(2,1)S(1)}, bf16[3,864,128]{2,1,0:T(8,128)(2,1)S(1)}, u32[]{:S(2)}, u32[]{:S(2)}) collective-permute-start(bf16[3,864,128]{2,1,0:T(8,128)(2,1)S(1)} %pad_maximum_fusion.1.refs_2_), channel_id=1, source_target_pairs={{0,8},{4,12},{8,0},{12,4},{16,24},{20,28},{24,16},{28,20},{1,9},{5... | collective-permute-start | bytes 1990664 | tf_op jit(solution)/shard_map/ppermute | solution.py:23
  35.4 14.5 %collective-permute-start.11 = (bf16[864,128]{1,0:T(8,128)(2,1)S(1)}, bf16[864,128]{1,0:T(8,128)(2,1)S(1)}, u32[]{:S(2)}, u32[]{:S(2)}) collective-permute-start(bf16[864,128]{1,0:T(8,128)(2,1)S(1)} %copy-done.10), channel_id=1, source_target_pairs={{0,1},{1,0},{2,3},{3,2},{4,5},{5,4},{6,7},{7,6},{8,9},{9,8},{10,11... | collective-permute-start | bytes 663560 | tf_op jit(solution)/shard_map/ppermute | solution.py:28
  38.6 23.2 %copy-start.8 = (s32[128]{0:T(128)S(1)}, s32[128]{0:T(128)}, u32[]{:S(2)}) copy-start(s32[128]{0:T(128)} %param.17) | copy-start | bytes 1540
  38.6 15.2 %collective-permute-start.15 = (bf16[3,864,128]{2,1,0:T(8,128)(2,1)S(1)}, bf16[3,864,128]{2,1,0:T(8,128)(2,1)S(1)}, u32[]{:S(2)}, u32[]{:S(2)}) collective-permute-start(bf16[3,864,128]{2,1,0:T(8,128)(2,1)S(1)} %pad_maximum_fusion.1.refs_2_), channel_id=1, source_target_pairs={{0,4},{4,0},{8,12},{12,8},{16,20},{20,16},{24,28},{28,24},{1,5},{5... | collective-permute-start | bytes 1990664 | tf_op jit(solution)/shard_map/ppermute | solution.py:23
  51.1 2.8 %collective-permute-start.16 = (bf16[3,864,128]{2,1,0:T(8,128)(2,1)S(1)}, bf16[3,864,128]{2,1,0:T(8,128)(2,1)S(1)}, u32[]{:S(2)}, u32[]{:S(2)}) collective-permute-start(bf16[3,864,128]{2,1,0:T(8,128)(2,1)S(1)} %collective-permute-done.9.refs_4_), channel_id=1, source_target_pairs={{0,4},{4,0},{8,12},{12,8},{16,20},{20,16},{24,28},{28,24},{1,5},{5... | collective-permute-start | bytes 1990664 | tf_op jit(solution)/shard_map/ppermute | solution.py:23
  51.1 3.1 %collective-permute-start.17 = (bf16[3,864,128]{2,1,0:T(8,128)(2,1)S(1)}, bf16[3,864,128]{2,1,0:T(8,128)(2,1)S(1)}, u32[]{:S(2)}, u32[]{:S(2)}) collective-permute-start(bf16[3,864,128]{2,1,0:T(8,128)(2,1)S(1)} %collective-permute-done.10.refs_6_), channel_id=1, source_target_pairs={{0,4},{4,0},{8,12},{12,8},{16,20},{20,16},{24,28},{28,24},{1,5},{5... | collective-permute-start | bytes 1990664 | tf_op jit(solution)/shard_map/ppermute | solution.py:23
  51.7 7.4 %collective-permute-start.13 = (bf16[2,432,128]{2,1,0:T(8,128)(2,1)S(1)}, bf16[2,432,128]{2,1,0:T(8,128)(2,1)S(1)}, u32[]{:S(2)}, u32[]{:S(2)}) collective-permute-start(bf16[2,432,128]{2,1,0:T(8,128)(2,1)S(1)} %slice.52), channel_id=1, source_target_pairs={{0,16},{4,20},{8,24},{12,28},{16,0},{20,4},{24,8},{28,12},{1,17},{... | collective-permute-start | bytes 663560 | tf_op jit(solution)/shard_map/ppermute | solution.py:23
  52.9 7.1 %collective-permute-start.14 = (bf16[2,432,128]{2,1,0:T(8,128)(2,1)S(1)}, bf16[2,432,128]{2,1,0:T(8,128)(2,1)S(1)}, u32[]{:S(2)}, u32[]{:S(2)}) collective-permute-start(bf16[2,432,128]{2,1,0:T(8,128)(2,1)S(1)} %slice.53), channel_id=1, source_target_pairs={{0,8},{4,12},{8,0},{12,4},{16,24},{20,28},{24,16},{28,20},{1,9},{5... | collective-permute-start | bytes 663560 | tf_op jit(solution)/shard_map/ppermute | solution.py:23
  53.8 6.7 %collective-permute-start.18 = (bf16[1,864,128]{2,1,0:T(8,128)(2,1)S(1)}, bf16[1,864,128]{2,1,0:T(8,128)(2,1)S(1)}, u32[]{:S(2)}, u32[]{:S(2)}) collective-permute-start(bf16[1,864,128]{2,1,0:T(8,128)(2,1)S(1)} %bitcast.55), channel_id=1, source_target_pairs={{0,4},{4,0},{8,12},{12,8},{16,20},{20,16},{24,28},{28,24},{1,5},{5... | collective-permute-start | bytes 663560 | tf_op jit(solution)/shard_map/ppermute | solution.py:23
  60.0 1.5 %collective-permute-start.19 = (bf16[2,432,128]{2,1,0:T(8,128)(2,1)S(1)}, bf16[2,432,128]{2,1,0:T(8,128)(2,1)S(1)}, u32[]{:S(2)}, u32[]{:S(2)}) collective-permute-start(bf16[2,432,128]{2,1,0:T(8,128)(2,1)S(1)} %collective-permute-done.13.refs_6_), channel_id=1, source_target_pairs={{0,4},{4,0},{8,12},{12,8},{16,20},{20,16},{24,28},{28,24},{1,5},{5... | collective-permute-start | bytes 663560 | tf_op jit(solution)/shard_map/ppermute | solution.py:23
  60.0 1.8 %collective-permute-start.20 = (bf16[2,432,128]{2,1,0:T(8,128)(2,1)S(1)}, bf16[2,432,128]{2,1,0:T(8,128)(2,1)S(1)}, u32[]{:S(2)}, u32[]{:S(2)}) collective-permute-start(bf16[2,432,128]{2,1,0:T(8,128)(2,1)S(1)} %collective-permute-done.14.refs_8_), channel_id=1, source_target_pairs={{0,4},{4,0},{8,12},{12,8},{16,20},{20,16},{24,28},{28,24},{1,5},{5... | collective-permute-start | bytes 663560 | tf_op jit(solution)/shard_map/ppermute | solution.py:23
  61.8 38.4 %copy-start.6 = (f32[1024]{0:T(1024)S(1)}, f32[1024]{0:T(1024)}, u32[]{:S(2)}) copy-start(f32[1024]{0:T(1024)} %param.12) | copy-start | bytes 12292
  70.3 2.0 %collective-permute-start.21 = (bf16[4,4,128,128]{3,2,1,0:T(8,128)(2,1)S(1)}, bf16[4,4,128,128]{3,2,1,0:T(8,128)(2,1)S(1)}, u32[]{:S(2)}, u32[]{:S(2)}) collective-permute-start(bf16[4,4,128,128]{3,2,1,0:T(8,128)(2,1)S(1)} %get-tuple-element.86), channel_id=1, source_target_pairs={{0,4},{4,0},{8,12},{12,8},{16,20},{20,16},{24,28},{28,24},{1,5},{5... | collective-permute-start | bytes 1572872 | tf_op jit(solution)/shard_map/ppermute | solution.py:23
  72.5 6.4 %collective-permute-start.22 = (bf16[1,4,128,128]{3,2,1,0:T(8,128)(2,1)S(1)}, bf16[1,4,128,128]{3,2,1,0:T(8,128)(2,1)S(1)}, u32[]{:S(2)}, u32[]{:S(2)}) collective-permute-start(bf16[1,4,128,128]{3,2,1,0:T(8,128)(2,1)S(1)} %get-tuple-element.97), channel_id=1, source_target_pairs={{0,8},{4,12},{8,0},{12,4},{16,24},{20,28},{24,16},{28,20},{1,9},{5... | collective-permute-start | bytes 393224 | tf_op jit(solution)/shard_map/ppermute | solution.py:23
  73.4 8.1 %collective-permute-start.23 = (bf16[1,4,128,128]{3,2,1,0:T(8,128)(2,1)S(1)}, bf16[1,4,128,128]{3,2,1,0:T(8,128)(2,1)S(1)}, u32[]{:S(2)}, u32[]{:S(2)}) collective-permute-start(bf16[1,4,128,128]{3,2,1,0:T(8,128)(2,1)S(1)} %get-tuple-element.99), channel_id=1, source_target_pairs={{0,16},{4,20},{8,24},{12,28},{16,0},{20,4},{24,8},{28,12},{1,17},{... | collective-permute-start | bytes 393224 | tf_op jit(solution)/shard_map/ppermute | solution.py:23
  74.6 6.9 %collective-permute-start.24 = (bf16[1,4,128,128]{3,2,1,0:T(8,128)(2,1)S(1)}, bf16[1,4,128,128]{3,2,1,0:T(8,128)(2,1)S(1)}, u32[]{:S(2)}, u32[]{:S(2)}) collective-permute-start(bf16[1,4,128,128]{3,2,1,0:T(8,128)(2,1)S(1)} %get-tuple-element.98), channel_id=1, source_target_pairs={{0,24},{4,28},{8,16},{12,20},{16,8},{20,12},{24,0},{28,4},{1,25},{... | collective-permute-start | bytes 393224 | tf_op jit(solution)/shard_map/ppermute | solution.py:23
  81.6 5.3 %collective-permute-start.25 = (bf16[128,128]{1,0:T(8,128)(2,1)S(1)}, bf16[128,128]{1,0:T(8,128)(2,1)S(1)}, u32[]{:S(2)}, u32[]{:S(2)}) collective-permute-start(bf16[128,128]{1,0:T(8,128)(2,1)S(1)} %get-tuple-element.100), channel_id=1, source_target_pairs={{0,1},{1,0},{2,3},{3,2},{4,5},{5,4},{6,7},{7,6},{8,9},{9,8},{10,11... | collective-permute-start | bytes 98312 | tf_op jit(solution)/shard_map/ppermute | solution.py:28
  84.4 5.3 %collective-permute-start.26 = (bf16[128,128]{1,0:T(8,128)(2,1)S(1)}, bf16[128,128]{1,0:T(8,128)(2,1)S(1)}, u32[]{:S(2)}, u32[]{:S(2)}) collective-permute-start(bf16[128,128]{1,0:T(8,128)(2,1)S(1)} %get-tuple-element.102), channel_id=1, source_target_pairs={{0,2},{1,3},{2,0},{3,1},{4,6},{5,7},{6,4},{7,5},{8,10},{9,11},{10,... | collective-permute-start | bytes 98312 | tf_op jit(solution)/shard_map/ppermute | solution.py:28
  85.5 5.7 %collective-permute-start.27 = (bf16[128,128]{1,0:T(8,128)(2,1)S(1)}, bf16[128,128]{1,0:T(8,128)(2,1)S(1)}, u32[]{:S(2)}, u32[]{:S(2)}) collective-permute-start(bf16[128,128]{1,0:T(8,128)(2,1)S(1)} %get-tuple-element.101), channel_id=1, source_target_pairs={{0,3},{1,2},{2,1},{3,0},{4,7},{5,6},{6,5},{7,4},{8,11},{9,10},{10,... | collective-permute-start | bytes 98312 | tf_op jit(solution)/shard_map/ppermute | solution.py:28
  91.3 4.3 %collective-permute-start.28 = (f32[128,128]{1,0:T(8,128)S(1)}, f32[128,128]{1,0:T(8,128)S(1)}, u32[]{:S(2)}, u32[]{:S(2)}) collective-permute-start(f32[128,128]{1,0:T(8,128)S(1)} %fusion.5), channel_id=1, source_target_pairs={{0,8},{4,12},{8,0},{12,4},{16,24},{20,28},{24,16},{28,20},{1,9},{5... | collective-permute-start | bytes 196616 | tf_op jit(solution)/shard_map/ppermute | solution.py:23
  92.5 4.3 %collective-permute-start.29 = (f32[128,128]{1,0:T(8,128)S(1)}, f32[128,128]{1,0:T(8,128)S(1)}, u32[]{:S(2)}, u32[]{:S(2)}) collective-permute-start(f32[128,128]{1,0:T(8,128)S(1)} %fusion.5), channel_id=1, source_target_pairs={{0,16},{4,20},{8,24},{12,28},{16,0},{20,4},{24,8},{28,12},{1,17},{... | collective-permute-start | bytes 196616 | tf_op jit(solution)/shard_map/ppermute | solution.py:23
  93.4 5.2 %collective-permute-start.30 = (f32[128,128]{1,0:T(8,128)S(1)}, f32[128,128]{1,0:T(8,128)S(1)}, u32[]{:S(2)}, u32[]{:S(2)}) collective-permute-start(f32[128,128]{1,0:T(8,128)S(1)} %fusion.5), channel_id=1, source_target_pairs={{0,24},{4,28},{8,16},{12,20},{16,8},{20,12},{24,0},{28,4},{1,25},{... | collective-permute-start | bytes 196616 | tf_op jit(solution)/shard_map/ppermute | solution.py:23
  98.6 1.6 %collective-permute-start.31 = (f32[4,128,128]{2,1,0:T(8,128)S(1)}, f32[4,128,128]{2,1,0:T(8,128)S(1)}, u32[]{:S(2)}, u32[]{:S(2)}) collective-permute-start(f32[4,128,128]{2,1,0:T(8,128)S(1)} %pad_maximum_fusion.2.even), channel_id=1, source_target_pairs={{0,4},{4,0},{8,12},{12,8},{16,20},{20,16},{24,28},{28,24},{1,5},{5... | collective-permute-start | bytes 786440 | tf_op jit(solution)/shard_map/ppermute | solution.py:23
